TPU v7x, 32 devices: a whole 2x2x4 slice. The times are simulated.
32 devices in a mesh: fsdp: 8 (over y, x, core), tensor: 4 (over z).
Axes of the slice: x: 2, y: 2, z: 4, core: 2. Of those that a mesh axis runs over, the one named last changes fastest.
Arguments:
- images: bfloat16 [8, 576, 768], P('fsdp'), may hold values from -6 to 6
- cotangent: bfloat16 [8, 576, 768], P('fsdp'), may hold values from -6 to 6
- qkv_weight: float32 [3, 768, 768], P(None, 'fsdp', 'tensor'), may hold values from -0.21875 to 0.21875
- out_weight: float32 [768, 768], P('tensor', 'fsdp'), may hold values from -0.875 to 0.875
- up_weight: float32 [768, 3072], P('fsdp', 'tensor'), may hold values from -0.21875 to 0.21875
- down_weight: float32 [3072, 768], P('tensor', 'fsdp'), may hold values from -0.109375 to 0.109375
- vectors: float32 [8, 768], P(None, ('fsdp', 'tensor')), may hold values from -1.2 to 1.8, as said below
- up_bias: float32 [3072], P(('fsdp', 'tensor')), may hold values from -1.8 to 1.8
- qkv_first: float32 [3, 768, 768], P(None, 'fsdp', 'tensor'), may hold values from -31.3616 to 31.3616
- qkv_second: float32 [3, 768, 768], P(None, 'fsdp', 'tensor'), may hold values from 1.12896 to 18.06336
- out_first: float32 [768, 768], P('tensor', 'fsdp'), may hold values from -8.960457 to 8.960457
- out_second: float32 [768, 768], P('tensor', 'fsdp'), may hold values from 0.09216 to 1.47456
- up_first: float32 [768, 3072], P('fsdp', 'tensor'), may hold values from -13.440685 to 13.440685
- up_second: float32 [768, 3072], P('fsdp', 'tensor'), may hold values from 0.20736 to 3.31776
- down_first: float32 [3072, 768], P('tensor', 'fsdp'), may hold values from -29.121485 to 29.121485
- down_second: float32 [3072, 768], P('tensor', 'fsdp'), may hold values from 0.96768 to 15.48288
- vector_first: float32 [8, 768], P(None, ('fsdp', 'tensor')), may hold values from -44.802284 to 44.802284
- vector_second: float32 [8, 768], P(None, ('fsdp', 'tensor')), may hold values from 2.304 to 36.864
- bias_first: float32 [3072], P(('fsdp', 'tensor')), may hold values from -13.440685 to 13.440685
- bias_second: float32 [3072], P(('fsdp', 'tensor')), may hold values from 0.20736 to 3.31776
Outputs:
- output: bfloat16 [8, 576, 768], P('fsdp', 'tensor')
- input_grad: float32 [8, 576, 768], P('fsdp', 'tensor')
- qkv_new: float32 [3, 768, 768], P(None, 'fsdp', 'tensor')
- qkv_first_new: float32 [3, 768, 768], P(None, 'fsdp', 'tensor')
- qkv_second_new: float32 [3, 768, 768], P(None, 'fsdp', 'tensor')
- out_new: float32 [768, 768], P('tensor', 'fsdp')
- out_first_new: float32 [768, 768], P('tensor', 'fsdp')
- out_second_new: float32 [768, 768], P('tensor', 'fsdp')
- up_new: float32 [768, 3072], P('fsdp', 'tensor')
- up_first_new: float32 [768, 3072], P('fsdp', 'tensor')
- up_second_new: float32 [768, 3072], P('fsdp', 'tensor')
- down_new: float32 [3072, 768], P('tensor', 'fsdp')
- down_first_new: float32 [3072, 768], P('tensor', 'fsdp')
- down_second_new: float32 [3072, 768], P('tensor', 'fsdp')
- vectors_new: float32 [8, 768], P(None, ('fsdp', 'tensor'))
- vector_first_new: float32 [8, 768], P(None, ('fsdp', 'tensor'))
- vector_second_new: float32 [8, 768], P(None, ('fsdp', 'tensor'))
- bias_new: float32 [3072], P(('fsdp', 'tensor'))
- bias_first_new: float32 [3072], P(('fsdp', 'tensor'))
- bias_second_new: float32 [3072], P(('fsdp', 'tensor'))
Inputs may be any that keep to these rules, and one draw needn't show every extreme that they name: `vectors`: rows 0 and 2 are gains about 1, the other rows biases about 0.
All inputs are finite; a program needn't handle non-finite values.
Results may differ from a plain program's by a relative error of at most 0.013.
Values may be sent and summed in bfloat16 or wider, within the bound.
No kernel may reach another device: no remote copies, remote signals or barrier semaphores. Data moves between devices by JAX's collectives and lax.ppermute only.
A program may use at most 128 MiB of HBM per device.

v0:
```python
import math

import jax
import jax.numpy as jnp
from jax import lax
from jax.sharding import PartitionSpec as P

HD = 64
STEP = 10


norm_eps = 1e-06
beta_one = 0.9
beta_two = 0.999
adam_eps = 1e-08
gelu_coef = math.sqrt(2.0 / math.pi)


def cut_along(value, dim, peers):
    before, after = (value.shape[:dim], value.shape[dim + 1 :])
    return jnp.moveaxis(value.reshape(*before, peers, -1, *after), dim, 0)


def summed_on_arrival(value, axis, dim):
    peers = lax.axis_size(axis)
    blocks = lax.all_to_all(cut_along(value, dim, peers), axis, 0, 0, tiled=True)
    return jnp.sum(blocks.astype(jnp.float32), axis=0)


def norm_forward(values, gain_vec, shift_vec):
    row_mean = jnp.mean(values, axis=-1, keepdims=True)
    centred = values - row_mean
    row_var = jnp.mean(centred * centred, axis=-1, keepdims=True)
    inverse = lax.rsqrt(row_var + norm_eps)
    normed = centred * inverse
    return (normed * gain_vec + shift_vec, normed, inverse)


def norm_backward(grad_out, normed, inverse, gain_vec):
    scaled = grad_out * gain_vec
    return inverse * (
        scaled
        - jnp.mean(scaled, axis=-1, keepdims=True)
        - normed * jnp.mean(scaled * normed, axis=-1, keepdims=True)
    )


def gelu_slope(pre_act):
    inner = gelu_coef * (pre_act + 0.044715 * pre_act * pre_act * pre_act)
    tangent = jnp.tanh(inner)
    return 0.5 * (1.0 + tangent) + 0.5 * pre_act * (1.0 - tangent * tangent) * gelu_coef * (
        1.0 + 3.0 * 0.044715 * pre_act * pre_act
    )


def adamw(weight, gradient, first, second, rate, decay):
    first_new = beta_one * first + (1.0 - beta_one) * gradient
    second_new = beta_two * second + (1.0 - beta_two) * gradient * gradient
    first_hat = first_new / (1.0 - beta_one**STEP)
    second_hat = second_new / (1.0 - beta_two**STEP)
    weight_new = weight - rate * (first_hat / (jnp.sqrt(second_hat) + adam_eps) + decay * weight)
    return (weight_new, first_new, second_new)


def body(
    images,
    cotangent,
    qkv_weight,
    out_weight,
    up_weight,
    down_weight,
    vectors,
    up_bias,
    qkv_first,
    qkv_second,
    out_first,
    out_second,
    up_first,
    up_second,
    down_first,
    down_second,
    vector_first,
    vector_second,
    bias_first,
    bias_second,
):
    tensor_size = lax.axis_size("tensor")
    tensor_rank = lax.axis_index("tensor")
    image_count, seq_len, model_width = images.shape
    row_total = image_count * seq_len
    seq_part = seq_len // tensor_size
    own_total = image_count * seq_part
    score_scale = float(HD) ** (-0.5)
    qkv_low = qkv_weight.astype(jnp.bfloat16)
    out_low = out_weight.astype(jnp.bfloat16)
    up_low = up_weight.astype(jnp.bfloat16)
    down_low = down_weight.astype(jnp.bfloat16)
    qkv_full, out_full = (
        lax.all_gather(qkv_low, "fsdp", axis=1, tiled=True),
        lax.all_gather(out_low, "fsdp", axis=1, tiled=True),
    )
    full_vectors, full_bias = (
        lax.all_gather(vectors, ("fsdp", "tensor"), axis=1, tiled=True),
        lax.all_gather(up_bias, ("fsdp", "tensor"), axis=0, tiled=True),
    )
    heads_width = qkv_full.shape[2]
    heads_local = heads_width // HD

    def own_rows(values):
        cube = values.reshape(image_count, seq_len, -1)
        return lax.dynamic_slice_in_dim(cube, tensor_rank * seq_part, seq_part, 1).reshape(
            own_total, -1
        )

    query_bias = lax.dynamic_slice_in_dim(
        full_vectors[4], tensor_rank * heads_width, heads_width, 0
    )
    value_bias = lax.dynamic_slice_in_dim(
        full_vectors[5], tensor_rank * heads_width, heads_width, 0
    )
    flat_rows = images.reshape(row_total, model_width).astype(jnp.float32)
    first_norm, normed_one, inverse_one = norm_forward(flat_rows, full_vectors[0], full_vectors[1])
    first_low = first_norm.astype(jnp.bfloat16)
    projected = jnp.einsum("rd,kde->kre", first_low, qkv_full, preferred_element_type=jnp.float32)
    queries = (projected[0] + query_bias).astype(jnp.bfloat16)
    keys_low = projected[1].astype(jnp.bfloat16)
    values_low = (projected[2] + value_bias).astype(jnp.bfloat16)
    query_img = queries.reshape(image_count, seq_len, heads_local, HD)
    key_img = keys_low.reshape(image_count, seq_len, heads_local, HD)
    value_img = values_low.reshape(image_count, seq_len, heads_local, HD)

    def attend(pieces):
        query_one, key_one, value_one = pieces
        scores = (
            jnp.einsum("shd,thd->hst", query_one, key_one, preferred_element_type=jnp.float32)
            * score_scale
        )
        row_max = jnp.max(scores, axis=-1, keepdims=True)
        expos = jnp.exp(scores - row_max)
        summed = jnp.sum(expos, axis=-1, keepdims=True)
        soft_probs = (expos / summed).astype(jnp.bfloat16)
        attended = jnp.einsum(
            "hst,thd->shd", soft_probs, value_one, preferred_element_type=jnp.float32
        )
        return (attended, (row_max + jnp.log(summed))[..., 0])

    attended, log_sums = lax.map(attend, (query_img, key_img, value_img))
    attn_low = attended.reshape(row_total, heads_width).astype(jnp.bfloat16)
    attn_part = jnp.dot(attn_low, out_full, preferred_element_type=jnp.float32)
    attn_sum = lax.psum(attn_part.astype(jnp.bfloat16), "tensor").astype(jnp.float32)
    hidden_state = flat_rows + attn_sum + full_vectors[6]
    second_norm, normed_two, inverse_two = norm_forward(
        hidden_state, full_vectors[2], full_vectors[3]
    )
    second_low = second_norm.astype(jnp.bfloat16)
    normed_two_own = own_rows(normed_two)
    up_full, down_full = (
        lax.all_gather(up_low, "fsdp", axis=0, tiled=True),
        lax.all_gather(down_low, "fsdp", axis=1, tiled=True),
    )
    hidden_width = up_full.shape[1]
    up_local = lax.dynamic_slice_in_dim(full_bias, tensor_rank * hidden_width, hidden_width, 0)
    pre_act = jnp.dot(second_low, up_full, preferred_element_type=jnp.float32) + up_local
    act_low = jax.nn.gelu(pre_act, approximate=True).astype(jnp.bfloat16)
    mlp_part = jnp.dot(act_low, down_full, preferred_element_type=jnp.float32)
    mlp_sum = lax.psum(mlp_part.astype(jnp.bfloat16), "tensor").astype(jnp.float32)
    result_own = own_rows(hidden_state + mlp_sum + full_vectors[7])
    output = result_own.reshape(image_count, seq_part, model_width).astype(jnp.bfloat16)
    cotan_low = cotangent.reshape(row_total, model_width)
    cotan_rows = cotan_low.astype(jnp.float32)
    down_grad = jnp.einsum("rf,rd->fd", act_low, cotan_low, preferred_element_type=jnp.float32)
    grad_act = jnp.einsum("rd,fd->rf", cotan_low, down_full, preferred_element_type=jnp.float32)
    grad_pre = (grad_act * gelu_slope(pre_act)).astype(jnp.bfloat16)
    up_grad = jnp.einsum("rd,rf->df", second_low, grad_pre, preferred_element_type=jnp.float32)
    up_bias_part = jnp.sum(grad_pre.astype(jnp.float32), axis=0)
    up_owned, down_owned = (
        summed_on_arrival(up_grad.astype(jnp.bfloat16), "fsdp", 0),
        summed_on_arrival(down_grad.astype(jnp.bfloat16), "fsdp", 1),
    )
    second_part = jnp.einsum("rf,df->rd", grad_pre, up_full, preferred_element_type=jnp.float32)
    cotan_own = own_rows(cotan_rows)
    grad_second = lax.psum(second_part.astype(jnp.bfloat16), "tensor").astype(jnp.float32)
    grad_hidden = cotan_rows + norm_backward(grad_second, normed_two, inverse_two, full_vectors[2])
    grad_attn_low = grad_hidden.astype(jnp.bfloat16)
    grad_second_own = own_rows(grad_second)
    grad_hidden_own = own_rows(grad_hidden)
    out_grad = jnp.einsum("re,rd->ed", attn_low, grad_attn_low, preferred_element_type=jnp.float32)
    grad_attended = jnp.einsum(
        "rd,ed->re", grad_attn_low, out_full, preferred_element_type=jnp.float32
    ).astype(jnp.bfloat16)
    grad_img = grad_attended.reshape(image_count, seq_len, heads_local, HD)

    def attend_back(pieces):
        query_one, key_one, value_one, grad_one, log_one = pieces
        scores = (
            jnp.einsum("shd,thd->hst", query_one, key_one, preferred_element_type=jnp.float32)
            * score_scale
        )
        soft_probs = jnp.exp(scores - log_one[..., None])
        probs_low = soft_probs.astype(jnp.bfloat16)
        grad_value = jnp.einsum(
            "hst,shd->thd", probs_low, grad_one, preferred_element_type=jnp.float32
        )
        grad_probs = jnp.einsum(
            "shd,thd->hst", grad_one, value_one, preferred_element_type=jnp.float32
        )
        grad_scores = soft_probs * (
            grad_probs - jnp.sum(grad_probs * soft_probs, axis=-1, keepdims=True)
        )
        scores_low = grad_scores.astype(jnp.bfloat16)
        grad_query = (
            jnp.einsum("hst,thd->shd", scores_low, key_one, preferred_element_type=jnp.float32)
            * score_scale
        )
        grad_key = (
            jnp.einsum("hst,shd->thd", scores_low, query_one, preferred_element_type=jnp.float32)
            * score_scale
        )
        return (
            grad_query.astype(jnp.bfloat16),
            grad_key.astype(jnp.bfloat16),
            grad_value.astype(jnp.bfloat16),
        )

    grad_query, grad_key, grad_value = lax.map(
        attend_back, (query_img, key_img, value_img, grad_img, log_sums)
    )
    grad_stack = jnp.stack(
        [
            grad_query.reshape(row_total, heads_width),
            grad_key.reshape(row_total, heads_width),
            grad_value.reshape(row_total, heads_width),
        ]
    )
    qkv_grad = jnp.einsum("rd,kre->kde", first_low, grad_stack, preferred_element_type=jnp.float32)
    query_bias_part = jnp.sum(grad_stack[0].astype(jnp.float32), axis=0)
    value_bias_part = jnp.sum(grad_stack[2].astype(jnp.float32), axis=0)
    first_part = jnp.einsum("kre,kde->rd", grad_stack, qkv_full, preferred_element_type=jnp.float32)
    grad_first_own = own_rows(
        lax.psum(first_part.astype(jnp.bfloat16), "tensor").astype(jnp.float32)
    )
    normed_one_own = own_rows(normed_one)
    input_own = grad_hidden_own + norm_backward(
        grad_first_own, normed_one_own, own_rows(inverse_one), full_vectors[0]
    )
    input_grad = input_own.reshape(image_count, seq_part, model_width)
    qkv_owned, out_owned = (
        summed_on_arrival(qkv_grad.astype(jnp.bfloat16), "fsdp", 1),
        summed_on_arrival(out_grad.astype(jnp.bfloat16), "fsdp", 1),
    )

    def place_heads(part_vec):
        return lax.dynamic_update_slice_in_dim(
            jnp.zeros((model_width,), jnp.float32), part_vec, tensor_rank * heads_width, 0
        )

    vector_grad = jnp.stack(
        [
            jnp.sum(grad_first_own * normed_one_own, axis=0),
            jnp.sum(grad_first_own, axis=0),
            jnp.sum(grad_second_own * normed_two_own, axis=0),
            jnp.sum(grad_second_own, axis=0),
            place_heads(query_bias_part),
            place_heads(value_bias_part),
            jnp.sum(grad_hidden_own, axis=0),
            jnp.sum(cotan_own, axis=0),
        ]
    )
    bias_grad = lax.dynamic_update_slice_in_dim(
        jnp.zeros(full_bias.shape, jnp.float32), up_bias_part, tensor_rank * hidden_width, 0
    )
    vector_owned, bias_owned = (
        lax.psum_scatter(vector_grad, ("fsdp", "tensor"), scatter_dimension=1, tiled=True),
        lax.psum_scatter(bias_grad, ("fsdp", "tensor"), scatter_dimension=0, tiled=True),
    )
    qkv_state = adamw(qkv_weight, qkv_owned, qkv_first, qkv_second, 0.08, 0.1)
    out_state = adamw(out_weight, out_owned, out_first, out_second, 0.3, 0.1)
    up_state = adamw(up_weight, up_owned, up_first, up_second, 0.08, 0.1)
    down_state = adamw(down_weight, down_owned, down_first, down_second, 0.045, 0.1)
    vec_state = adamw(vectors, vector_owned, vector_first, vector_second, 0.5, 0.0)
    bias_state = adamw(up_bias, bias_owned, bias_first, bias_second, 0.7, 0.0)
    return (
        output,
        input_grad,
        qkv_state[0],
        qkv_state[1],
        qkv_state[2],
        out_state[0],
        out_state[1],
        out_state[2],
        up_state[0],
        up_state[1],
        up_state[2],
        down_state[0],
        down_state[1],
        down_state[2],
        vec_state[0],
        vec_state[1],
        vec_state[2],
        bias_state[0],
        bias_state[1],
        bias_state[2],
    )


def solution(mesh):
    return jax.shard_map(
        body,
        mesh=mesh,
        in_specs=(
            P("fsdp", None, None),
            P("fsdp", None, None),
            P(None, "fsdp", "tensor"),
            P("tensor", "fsdp"),
            P("fsdp", "tensor"),
            P("tensor", "fsdp"),
            P(None, ("fsdp", "tensor")),
            P(("fsdp", "tensor")),
            P(None, "fsdp", "tensor"),
            P(None, "fsdp", "tensor"),
            P("tensor", "fsdp"),
            P("tensor", "fsdp"),
            P("fsdp", "tensor"),
            P("fsdp", "tensor"),
            P("tensor", "fsdp"),
            P("tensor", "fsdp"),
            P(None, ("fsdp", "tensor")),
            P(None, ("fsdp", "tensor")),
            P(("fsdp", "tensor")),
            P(("fsdp", "tensor")),
        ),
        out_specs=(
            P("fsdp", "tensor", None),
            P("fsdp", "tensor", None),
            P(None, "fsdp", "tensor"),
            P(None, "fsdp", "tensor"),
            P(None, "fsdp", "tensor"),
            P("tensor", "fsdp"),
            P("tensor", "fsdp"),
            P("tensor", "fsdp"),
            P("fsdp", "tensor"),
            P("fsdp", "tensor"),
            P("fsdp", "tensor"),
            P("tensor", "fsdp"),
            P("tensor", "fsdp"),
            P("tensor", "fsdp"),
            P(None, ("fsdp", "tensor")),
            P(None, ("fsdp", "tensor")),
            P(None, ("fsdp", "tensor")),
            P(("fsdp", "tensor")),
            P(("fsdp", "tensor")),
            P(("fsdp", "tensor")),
        ),
        check_vma=False,
    )
```

profile of v0, /device:TPU:0, one launch (start us, length us, event | category | flops | bytes accessed | tf_op | source)
XLA Modules:
  0.0 410.1 jit_solution(12190590792771839715)
XLA Ops:
  8.1 1.4 convert_reduce_fusion.3
  9.5 1.6 fusion.11
  11.1 70.7 %all-gather = f32[32,24,8]{1,2,0:T(8,128)S(1)} all-gather(f32[1,24,8]{1,2,0:T(8,128)S(1)} %bitcast.130), channel_id=1, replica_groups=mesh['fsdp'=8,'tensor'=4] {'fsdp','tensor'}, dimensions={0}, use_global_device_ids=true | all-gather | bytes 25344 | tf_op jit(solution)/shard_map/all_gather | solution.py:103
  82.8 12.4 %all_gather.19 = bf16[3,768,192]{2,0,1:T(4,128)(2,1)S(1)} all-gather(bf16[3,96,192]{2,0,1:T(4,128)(2,1)S(1)} %copy.73), channel_id=1, replica_groups=mesh['fsdp'=8,'tensor'=4] {'fsdp'}, dimensions={1}, use_global_device_ids=true | all-gather | bytes 995328 | tf_op jit(solution)/shard_map/all_gather | solution.py:99
  95.2 2.1 copy.74
  97.2 2.2 fusion.54
  100.8 8.4 %all_gather.20 = bf16[192,768]{0,1:T(8,128)(2,1)S(1)} all-gather(bf16[192,96]{0,1:T(8,128)(2,1)S(1)} %copy.76), channel_id=1, replica_groups=mesh['fsdp'=8,'tensor'=4] {'fsdp'}, dimensions={1}, use_global_device_ids=true | all-gather | bytes 331776 | tf_op jit(solution)/shard_map/all_gather | solution.py:100
  113.2 1.4 convolution_convert_fusion.5
  115.8 38.0 %all-reduce = f32[3072]{0:T(1024)S(1)} all-reduce(f32[3072]{0:T(1024)S(1)} %dynamic-update-slice), channel_id=1, replica_groups=mesh['fsdp'=8,'tensor'=4] {'fsdp','tensor'}, use_global_device_ids=true, to_apply=%add | all-reduce | flops 3072 | bytes 24576
  153.9 5.6 %all-reduce.9.cloned.1.call-done = bf16[576,768]{1,0:T(8,128)(2,1)} async-done(((bf16[576,768]{1,0:T(8,128)(2,1)}), bf16[576,768]{1,0:T(8,128)(2,1)}) %all-reduce.9.cloned.1.call-update) | async-done | bytes 884752 | tf_op jit(solution)/shard_map/psum | solution.py:150
  159.5 3.0 fusion.78
  162.8 1.4 subtract_multiply_fusion
  164.3 2.8 fusion.55
  167.1 1.4 convolution_convert_fusion
  168.5 20.4 %all_to_all.20 = bf16[8,768,96]{1,2,0:T(8,128)(2,1)S(1)} all-to-all(bf16[8,768,96]{1,2,0:T(8,128)(2,1)S(1)} %bitcast.117), channel_id=1, replica_groups=mesh['fsdp'=8,'tensor'=4] {'fsdp'}, dimensions={0} | all-to-all | bytes 2359296 | tf_op jit(solution)/shard_map/all_to_all | solution.py:26
  194.3 17.3 %all-gather.6.cloned.1.call-done = bf16[768,768]{0,1:T(8,128)(2,1)} async-done(((bf16[768,96]{0,1:T(8,128)(2,1)}), bf16[768,768]{0,1:T(8,128)(2,1)}) %all-gather.6.cloned.1.call-update) | async-done | bytes 1179664 | tf_op jit(solution)/shard_map/all_gather | solution.py:159
  211.6 4.2 %convert_reduce_fusion.4 = (f32[768]{0:T(1024)}, bf16[576,768]{1,0:T(8,128)(2,1)S(1)}) fusion(f32[576,768]{1,0:T(8,128)} %copy-done.61, f32[768]{0:T(1024)S(1)} %copy-done.55, bf16[768,768]{0,1:T(8,128)(2,1)} %all-gather.6.cloned.1.call-done, bf16[1,576,768]{2,1,0:T(8,128)(2,1)S(1)} %copy-done.6), kind=kOutput, calls=%fused_computation.42 | convolution fusion | flops 689208576 | bytes 4724736 | tf_op jit(solution)/shard_map/rd,fd->rf/dot_general | solution.py:172
  216.7 1.8 convolution_convert_fusion.3
  219.3 3.4 convolution_convert_fusion.1
  222.6 4.4 %all-to-all-start.2 = ((bf16[8,96,768]{2,1,0:T(8,128)(2,1)}), bf16[8,96,768]{2,1,0:T(8,128)(2,1)}, u32[]{:S(2)}, u32[]{:S(2)}) async-start(bf16[8,96,768]{2,1,0:T(8,128)(2,1)} %bitcast.116), calls=%async_computation.2 | async-start | bytes 2359296 | tf_op jit(solution)/shard_map/all_to_all | solution.py:26
  227.7 1.4 dynamic_update_slice.26
  229.1 3.7 convolution_convert_fusion.4
  232.8 32.6 %all-reduce.11.cloned.1.call-done = bf16[576,768]{1,0:T(8,128)(2,1)} async-done(((bf16[576,768]{1,0:T(8,128)(2,1)}), bf16[576,768]{1,0:T(8,128)(2,1)}) %all-reduce.11.cloned.1.call-update) | async-done | bytes 884752 | tf_op jit(solution)/shard_map/psum | solution.py:182
  265.4 1.9 multiply_reduce_fusion.4
  267.3 2.2 multiply_add_fusion.1
  274.4 1.6 convert_reduce_fusion.7
  276.7 1.9 bitcast_convert_fusion
  278.6 2.1 convolution_convert_fusion.6
  280.7 2.2 reshape.221
  282.8 1.9 copy.101
  289.6 4.1 all-to-all-start.1
  293.7 3.6 fusion.28
  297.3 3.2 reshape.220
  300.6 2.6 copy.100
  305.2 4.5 %all-to-all-start = ((bf16[8,3,96,192]{2,3,1,0:T(8,128)(2,1)}), bf16[8,3,96,192]{2,3,1,0:T(8,128)(2,1)}, u32[]{:S(2)}, u32[]{:S(2)}) async-start(bf16[8,3,96,192]{2,3,1,0:T(8,128)(2,1)} %bitcast.106), calls=%async_computation | async-start | bytes 2359296 | tf_op jit(solution)/shard_map/all_to_all | solution.py:26
  309.7 1.5 convert_reduce_fusion.1
  311.3 2.2 multiply_subtract_fusion.1
  315.3 11.1 %all-to-all-done = bf16[8,3,96,192]{2,3,1,0:T(8,128)(2,1)} async-done(((bf16[8,3,96,192]{2,3,1,0:T(8,128)(2,1)}), bf16[8,3,96,192]{2,3,1,0:T(8,128)(2,1)}, u32[]{:S(2)}, u32[]{:S(2)}) %all-to-all-start) | async-done | bytes 884768 | tf_op jit(solution)/shard_map/all_to_all | solution.py:26
  326.4 1.5 convert_reduce_fusion.2
  327.9 2.2 multiply_subtract_fusion.2
  330.1 1.8 copy.88
  332.0 1.8 copy.89
  333.8 1.8 copy.90
  335.7 18.2 %all-reduce.13.cloned.1.call-done = (bf16[576,768]{1,0:T(8,128)(2,1)}, bf16[576,768]{1,0:T(8,128)(2,1)}) async-done(((bf16[576,768]{1,0:T(8,128)(2,1)}, bf16[576,768]{1,0:T(8,128)(2,1)}), (bf16[576,768]{1,0:T(8,128)(2,1)}, bf16[576,768]{1,0:T(8,128)(2,1)})) %all-reduce.13.cloned.1.call-update) | async-done | bytes 1769488 | tf_op jit(solution)/shard_map/psum | solution.py:166
  355.8 2.1 dynamic-slice_reduce_fusion.2
  357.8 1.7 fusion.56
  360.3 40.0 %all-reduce.3 = (f32[8,768]{1,0:T(8,128)S(1)}, f32[3072]{0:T(1024)S(1)}) all-reduce(f32[8,768]{1,0:T(8,128)S(1)} %stack.42, f32[3072]{0:T(1024)} %dynamic_update_slice.26), channel_id=2, replica_groups=mesh['fsdp'=8,'tensor'=4] {'fsdp','tensor'}, use_global_device_ids=true, to_apply=%region_27.28.clone | all-reduce | flops 9216 | bytes 73728
  400.3 1.4 multiply_subtract_fusion.4
  (205 shorter events, 33.7 us)
Async XLA Ops:
  8.0 74.5 %copy-start.12 = (f32[3,96,192]{2,1,0:T(8,128)S(1)}, f32[3,96,192]{2,1,0:T(8,128)}, u32[]{:S(2)}) copy-start(f32[3,96,192]{2,1,0:T(8,128)} %param.22) | copy-start | bytes 663556
  8.0 151.4 %all-reduce.9.cloned.1.call-start = ((), (), s32[]{:S(2)}) async-start(), calls=%async_computation.4 | async-start | bytes 1769472 | tf_op jit(solution)/shard_map/psum | solution.py:150
  9.5 150.0 %copy-start.36 = (f32[576]{0:T(1024)}, f32[576]{0:T(1024)S(1)}, u32[]{:S(2)}) copy-start(f32[576]{0:T(1024)S(1)} %broadcast_multiply_fusion.3) | copy-start | bytes 6916
  11.1 180.0 %copy-start.38 = (f32[576]{0:T(1024)}, f32[576]{0:T(1024)S(1)}, u32[]{:S(2)}) copy-start(f32[576]{0:T(1024)S(1)} %add_rsqrt_fusion.1) | copy-start | bytes 6916
  82.6 14.6 %copy-start.32 = (f32[768]{0:T(1024)}, f32[768]{0:T(1024)S(1)}, u32[]{:S(2)}) copy-start(f32[768]{0:T(1024)S(1)} %get-tuple-element.118) | copy-start | bytes 9220
  82.6 14.6 %copy-start.50 = (f32[768]{0:T(1024)}, f32[768]{0:T(1024)S(1)}, u32[]{:S(2)}) copy-start(f32[768]{0:T(1024)S(1)} %get-tuple-element.117) | copy-start | bytes 9220
  82.6 81.7 %copy-start.34 = (f32[768]{0:T(1024)}, f32[768]{0:T(1024)S(1)}, u32[]{:S(2)}) copy-start(f32[768]{0:T(1024)S(1)} %get-tuple-element.113) | copy-start | bytes 9220
  82.6 81.7 %copy-start.51 = (f32[768]{0:T(1024)}, f32[768]{0:T(1024)S(1)}, u32[]{:S(2)}) copy-start(f32[768]{0:T(1024)S(1)} %get-tuple-element.115) | copy-start | bytes 9220
  82.8 14.5 %copy-start.1 = (bf16[1,576,768]{2,1,0:T(8,128)(2,1)S(1)}, bf16[1,576,768]{2,1,0:T(8,128)(2,1)}, u32[]{:S(2)}) copy-start(bf16[1,576,768]{2,1,0:T(8,128)(2,1)} %param.20) | copy-start | bytes 2654212
  99.5 10.5 %copy-start.8 = (bf16[1,576,192]{1,2,0:T(8,128)(2,1)}, bf16[1,576,192]{1,2,0:T(8,128)(2,1)S(1)}, u32[]{:S(2)}) copy-start(bf16[1,576,192]{1,2,0:T(8,128)(2,1)S(1)} %slice.65) | copy-start | bytes 663556
  99.6 10.5 %copy-start.2 = (f32[1,576,192]{1,2,0:T(8,128)}, f32[1,576,192]{1,2,0:T(8,128)S(1)}, u32[]{:S(2)}) copy-start(f32[1,576,192]{1,2,0:T(8,128)S(1)} %get-tuple-element.146) | copy-start | bytes 1327108
  99.6 11.3 %copy-start.10 = (f32[1,576,192]{1,2,0:T(8,128)}, f32[1,576,192]{1,2,0:T(8,128)S(1)}, u32[]{:S(2)}) copy-start(f32[1,576,192]{1,2,0:T(8,128)S(1)} %get-tuple-element.145) | copy-start | bytes 1327108
  100.6 10.2 %copy-start.47 = (f32[3,64]{1,0:T(4,128)}, f32[3,64]{1,0:T(4,128)S(1)}, u32[]{:S(2)}) copy-start(f32[3,64]{1,0:T(4,128)S(1)} %add.262) | copy-start | bytes 2308
  100.8 9.2 %copy-start.40 = (f32[3,64]{1,0:T(4,128)}, f32[3,64]{1,0:T(4,128)S(1)}, u32[]{:S(2)}) copy-start(f32[3,64]{1,0:T(4,128)S(1)} %add.265) | copy-start | bytes 2308
  109.2 4.0 copy-start.4
  113.2 46.3 %copy-start.14 = (bf16[3,64,576]{2,1,0:T(8,128)(2,1)}, bf16[3,64,576]{2,1,0:T(8,128)(2,1)S(1)}, u32[]{:S(2)}) copy-start(bf16[3,64,576]{2,1,0:T(8,128)(2,1)S(1)} %fusion.32) | copy-start | bytes 663556
  114.6 49.6 %all-gather.4.cloned.1.call-start = ((), (), s32[]{:S(2)}) async-start(), calls=%async_computation.5 | async-start | bytes 1327104 | tf_op jit(solution)/shard_map/all_gather | solution.py:158
  115.4 96.2 %all-gather.6.cloned.1.call-start = ((), (), s32[]{:S(2)}) async-start(), calls=%async_computation.6 | async-start | bytes 1327104 | tf_op jit(solution)/shard_map/all_gather | solution.py:159
  153.9 13.2 %copy-start.54 = (f32[768]{0:T(1024)}, f32[768]{0:T(1024)S(1)}, u32[]{:S(2)}) copy-start(f32[768]{0:T(1024)S(1)} %dynamic_slice.37) | copy-start | bytes 9220
  168.5 20.6 %copy-start.18 = (f32[768,96]{0,1:T(8,128)S(1)}, f32[768,96]{0,1:T(8,128)}, u32[]{:S(2)}) copy-start(f32[768,96]{0,1:T(8,128)} %param.25) | copy-start | bytes 884740
  168.5 20.5 %copy-start.19 = (f32[768,96]{0,1:T(8,128)S(1)}, f32[768,96]{0,1:T(8,128)}, u32[]{:S(2)}) copy-start(f32[768,96]{0,1:T(8,128)} %param.34) | copy-start | bytes 884740
  168.5 20.5 %copy-start.20 = (f32[768,96]{0,1:T(8,128)S(1)}, f32[768,96]{0,1:T(8,128)}, u32[]{:S(2)}) copy-start(f32[768,96]{0,1:T(8,128)} %param.35) | copy-start | bytes 884740
  190.2 75.2 %all-reduce.11.cloned.1.call-start = ((), (), s32[]{:S(2)}) async-start(), calls=%async_computation.7 | async-start | bytes 1769472 | tf_op jit(solution)/shard_map/psum | solution.py:182
  192.7 18.9 %copy-start.55 = (f32[768]{0:T(1024)S(1)}, f32[768]{0:T(1024)}, u32[]{:S(2)}) copy-start(f32[768]{0:T(1024)} %copy-done.54) | copy-start | bytes 9220
  211.6 5.1 %copy-start.59 = (bf16[768,768]{1,0:T(8,128)(2,1)S(1)}, bf16[768,768]{1,0:T(8,128)(2,1)}, u32[]{:S(2)}) copy-start(bf16[768,768]{1,0:T(8,128)(2,1)} %all-gather.4.cloned.1.call-done) | copy-start | bytes 3538948
  222.6 5.1 %copy-start.57 = (f32[768]{0:T(1024)S(1)}, f32[768]{0:T(1024)}, u32[]{:S(2)}) copy-start(f32[768]{0:T(1024)} %get-tuple-element.159) | copy-start | bytes 9220
  222.6 6.5 %copy-start.56 = (f32[768]{0:T(1024)S(1)}, f32[768]{0:T(1024)}, u32[]{:S(2)}) copy-start(f32[768]{0:T(1024)} %copy-done.54) | copy-start | bytes 9220
  222.6 6.5 %copy-start.60 = (bf16[768,768]{0,1:T(8,128)(2,1)S(1)}, bf16[768,768]{0,1:T(8,128)(2,1)}, u32[]{:S(2)}) copy-start(bf16[768,768]{0,1:T(8,128)(2,1)} %all-gather.6.cloned.1.call-done) | copy-start | bytes 3538948
  222.6 67.0 %all-to-all-start.2 = ((bf16[8,96,768]{2,1,0:T(8,128)(2,1)}), bf16[8,96,768]{2,1,0:T(8,128)(2,1)}, u32[]{:S(2)}, u32[]{:S(2)}) async-start(bf16[8,96,768]{2,1,0:T(8,128)(2,1)} %bitcast.116), calls=%async_computation.2 | async-start | bytes 2359296 | tf_op jit(solution)/shard_map/all_to_all | solution.py:26
  227.0 126.8 %all-reduce.13.cloned.1.call-start = ((), (), s32[]{:S(2)}) async-start(), calls=%async_computation.8 | async-start | bytes 3538944 | tf_op jit(solution)/shard_map/psum | solution.py:166
  229.1 36.3 %copy-start.30 = (f32[576]{0:T(1024)S(1)}, f32[576]{0:T(1024)}, u32[]{:S(2)}) copy-start(f32[576]{0:T(1024)} %copy-done.29) | copy-start | bytes 6916
  229.1 36.3 %copy-start.35 = (f32[768]{0:T(1024)S(1)}, f32[768]{0:T(1024)}, u32[]{:S(2)}) copy-start(f32[768]{0:T(1024)} %copy-done.34) | copy-start | bytes 9220
  265.4 4.7 %slice-start = ((s8[4423680]{0:T(1024)(128)(4,1)}), s8[4194304]{0:T(1024)(128)(4,1)S(1)}, s32[]{:S(2)}) async-start(s8[4423680]{0:T(1024)(128)(4,1)} %bitcast.104), calls=%async_computation.9 | async-start | bytes 8388608
  278.6 6.2 %copy-start.49 = (f32[3,64]{1,0:T(4,128)S(1)}, f32[3,64]{1,0:T(4,128)}, u32[]{:S(2)}) copy-start(f32[3,64]{1,0:T(4,128)} %get-tuple-element.157) | copy-start | bytes 2308
  285.4 8.3 %copy-start.33 = (f32[768]{0:T(1024)S(1)}, f32[768]{0:T(1024)}, u32[]{:S(2)}) copy-start(f32[768]{0:T(1024)} %copy-done.32) | copy-start | bytes 9220
  285.4 8.3 %copy-start.37 = (f32[576]{0:T(1024)S(1)}, f32[576]{0:T(1024)}, u32[]{:S(2)}) copy-start(f32[576]{0:T(1024)} %copy-done.36) | copy-start | bytes 6916
  285.4 8.3 %copy-start.39 = (f32[576]{0:T(1024)S(1)}, f32[576]{0:T(1024)}, u32[]{:S(2)}) copy-start(f32[576]{0:T(1024)} %copy-done.38) | copy-start | bytes 6916
  289.6 15.6 %all-to-all-start.1 = ((bf16[8,192,96]{2,1,0:T(8,128)(2,1)}), bf16[8,192,96]{2,1,0:T(8,128)(2,1)}, u32[]{:S(2)}, u32[]{:S(2)}) async-start(bf16[8,192,96]{2,1,0:T(8,128)(2,1)} %bitcast.115), calls=%async_computation.1 | async-start | bytes 786432 | tf_op jit(solution)/shard_map/all_to_all | solution.py:26
  297.3 6.4 %copy-start.52 = (f32[1,192]{1,0:T(1,128)S(1)}, f32[1,192]{1,0:T(1,128)}, u32[]{:S(2)}) copy-start(f32[1,192]{1,0:T(1,128)} %stack.39) | copy-start | bytes 2308
  297.3 7.7 %copy-start.53 = (f32[1,192]{1,0:T(1,128)S(1)}, f32[1,192]{1,0:T(1,128)}, u32[]{:S(2)}) copy-start(f32[1,192]{1,0:T(1,128)} %stack.38) | copy-start | bytes 2308
  305.2 6.1 %copy-start.46 = (f32[1,768]{1,0:T(1,128)}, f32[1,768]{1,0:T(1,128)S(1)}, u32[]{:S(2)}) copy-start(f32[1,768]{1,0:T(1,128)S(1)} %dynamic_update_slice.24) | copy-start | bytes 9220
  305.2 21.2 %all-to-all-start = ((bf16[8,3,96,192]{2,3,1,0:T(8,128)(2,1)}), bf16[8,3,96,192]{2,3,1,0:T(8,128)(2,1)}, u32[]{:S(2)}, u32[]{:S(2)}) async-start(bf16[8,3,96,192]{2,3,1,0:T(8,128)(2,1)} %bitcast.106), calls=%async_computation | async-start | bytes 2359296 | tf_op jit(solution)/shard_map/all_to_all | solution.py:26
  309.7 4.9 %copy-start.17 = (f32[192,96]{1,0:T(8,128)S(1)}, f32[192,96]{1,0:T(8,128)}, u32[]{:S(2)}) copy-start(f32[192,96]{1,0:T(8,128)} %param.23) | copy-start | bytes 221188
  309.7 4.9 %copy-start.26 = (f32[192,96]{1,0:T(8,128)S(1)}, f32[192,96]{1,0:T(8,128)}, u32[]{:S(2)}) copy-start(f32[192,96]{1,0:T(8,128)} %param.30) | copy-start | bytes 221188
  309.7 4.9 %copy-start.27 = (f32[192,96]{1,0:T(8,128)S(1)}, f32[192,96]{1,0:T(8,128)}, u32[]{:S(2)}) copy-start(f32[192,96]{1,0:T(8,128)} %param.31) | copy-start | bytes 221188
  332.0 25.9 %copy-start.42 = (f32[768]{0:T(1024)S(1)}, f32[768]{0:T(1024)}, u32[]{:S(2)}) copy-start(f32[768]{0:T(1024)} %get-tuple-element.114) | copy-start | bytes 9220
  333.8 25.7 %copy-start.45 = (f32[1,768]{1,0:T(1,128)S(1)}, f32[1,768]{1,0:T(1,128)}, u32[]{:S(2)}) copy-start(f32[1,768]{1,0:T(1,128)} %stack.41) | copy-start | bytes 9220
  335.7 64.7 %copy-start.44 = (f32[8,24]{1,0:T(8,128)S(1)}, f32[8,24]{1,0:T(8,128)}, u32[]{:S(2)}) copy-start(f32[8,24]{1,0:T(8,128)} %param.26) | copy-start | bytes 2308
  (25 other events, 46.5 us)
Sparse Core Ops, SparseCore 0:
  114.8 44.6 all-reduce.8
  218.6 46.7 all-reduce.10
  278.7 75.0 all-reduce.12
Sparse Core Ops, SparseCore 1:
  117.6 21.4 all-gather.3
  190.3 21.2 all-gather.5
where the time goes:
time: 412 us; the launch traced here: 410 us
  blocking collectives  190 us (46%)
  waiting for transfers between devices  84.8 us (21%)
  other arithmetic  35.9 us (9%)
  local copies, waits for them, and re-layouts  35.5 us (9%)
  matrix products  34.9 us (8%)
  between operations  16.1 us (4%)
  starting transfers between devices  13.2 us (3%)
    unnamed x2, blocking collectives  78 us
    all_gather x1, blocking collectives, body(): lax.all_gather(vectors, ('fsdp', 'tensor'), axis=1, tiled=True)  70.7 us
    psum x1, waiting for transfers between devices, body(): lax.psum(second_part.astype(jnp.bfloat16), 'tensor').astype(jnp.float32)  32.6 us
    all_to_all x1, blocking collectives, summed_on_arrival(): lax.all_to_all(cut_along(value, dim, peers), axis, 0, 0, tiled=True)  20.4 us
    psum x1, waiting for transfers between devices, body(): lax.psum(mlp_part.astype(jnp.bfloat16), 'tensor').astype(jnp.float32)  18.2 us
    all_gather x1, waiting for transfers between devices, body(): lax.all_gather(down_low, 'fsdp', axis=1, tiled=True)  17.3 us
    unnamed x141, local copies, waits for them, and re-layouts  13.7 us
    all_to_all x3, starting transfers between devices, summed_on_arrival(): lax.all_to_all(cut_along(value, dim, peers), axis, 0, 0, tiled=True)  13 us
  transfers between devices with their start and end apart: 8, of which 5 were waited for; matrix products, arithmetic and copies ran while one was open for 17% of the time, Pallas kernels for 0%

commit v1 on v0

v1 whole, which is shorter than its diff:
```python
import functools
import math

import jax
import jax.numpy as jnp
from jax import lax
from jax.experimental import pallas as pl
from jax.experimental.pallas import tpu as pltpu
from jax.sharding import PartitionSpec as P

HD = 64
STEP = 10


norm_eps = 1e-06
beta_one = 0.9
beta_two = 0.999
adam_eps = 1e-08
gelu_coef = math.sqrt(2.0 / math.pi)
score_scale = float(HD) ** (-0.5)
low = jnp.bfloat16
wide = jnp.float32
VMEM_LIMIT = 48 * 1024 * 1024

NN = (((1,), (0,)), ((), ()))
NT = (((1,), (1,)), ((), ()))
TN = (((0,), (0,)), ((), ()))


def dot(left, right, dims=NN):
    return lax.dot_general(left, right, dims, preferred_element_type=wide)


def kernel_call(body, outs, args, scratch=(), flops=0, moved=0):
    smem = pl.BlockSpec(memory_space=pltpu.SMEM)
    vmem = pl.BlockSpec(memory_space=pltpu.VMEM)
    return pl.pallas_call(
        body,
        out_shape=[jax.ShapeDtypeStruct(s, d) for s, d in outs],
        in_specs=[smem] + [vmem] * (len(args) - 1),
        out_specs=[vmem] * len(outs),
        scratch_shapes=list(scratch),
        compiler_params=pltpu.CompilerParams(vmem_limit_bytes=VMEM_LIMIT),
        cost_estimate=pl.CostEstimate(flops=flops, bytes_accessed=moved, transcendentals=0),
    )(*args)


def flip(value, axis, mask):
    size = lax.axis_size(axis)
    return lax.ppermute(value, axis, [(i, i ^ mask) for i in range(size)])


def gather_parts(shard, dim):
    if lax.axis_size("fsdp") != 8:
        return [lax.all_gather(shard, "fsdp", axis=dim, tiled=True)]
    chips = [shard] + [flip(shard, "fsdp", mask) for mask in (2, 4, 6)]
    others = [flip(part, "fsdp", 1) for part in chips]
    return [part for pair in zip(chips, others) for part in pair]


def fsdp_sum(keep, send):
    got = flip(send, "fsdp", 1)
    total = keep.astype(wide) + got.astype(wide)
    sent = [flip(total[j].astype(low), "fsdp", 2 * j) for j in (1, 2, 3)]
    return total[0] + sum(part.astype(wide) for part in sent)


def summed_on_arrival(value, dim):
    peers = lax.axis_size("fsdp")
    before, after = (value.shape[:dim], value.shape[dim + 1 :])
    blocks = jnp.moveaxis(value.reshape(*before, peers, -1, *after), dim, 0)
    blocks = lax.all_to_all(blocks, "fsdp", 0, 0, tiled=True)
    return jnp.sum(blocks.astype(wide), axis=0)


def norm_parts(values):
    row_mean = jnp.mean(values, axis=-1, keepdims=True)
    centred = values - row_mean
    row_var = jnp.mean(centred * centred, axis=-1, keepdims=True)
    inverse = lax.rsqrt(row_var + norm_eps)
    return centred * inverse, inverse


def norm_backward(grad_out, normed, inverse, gain_vec):
    scaled = grad_out * gain_vec
    return inverse * (
        scaled
        - jnp.mean(scaled, axis=-1, keepdims=True)
        - normed * jnp.mean(scaled * normed, axis=-1, keepdims=True)
    )


def place_rows(at_ref, parts, target, lead):
    if len(parts) == 1:
        target[...] = parts[0][...]
        return
    for slot, part in enumerate(parts):
        height = part.shape[lead]
        start = pl.multiple_of((at_ref[0] ^ slot) * height, 32)
        if lead == 0:
            target[pl.ds(start, height), :] = part[...]
        else:
            target[:, pl.ds(start, height), :] = part[...]


def take_rows(at_ref, source, slot, height):
    start = pl.multiple_of((at_ref[0] ^ slot) * height, 32)
    return source[pl.ds(start, height), :]


def pack_heads(value):
    half = value.shape[0] // 2
    side = value[:, 128:]
    return value[:, :128], jnp.concatenate([side[:half], side[half:]], axis=1)


def unpack_heads(packed):
    rows = packed.shape[0] * 2 // 3
    head, side = packed[:rows], packed[rows:]
    return jnp.concatenate([head, jnp.concatenate([side[:, :64], side[:, 64:]], axis=0)], axis=1)


def attend_kernel(n_parts, at_ref, x_ref, vec_ref, qv_ref, *refs):
    parts = refs[:n_parts]
    a1_ref, qkv_ref, lse_ref, o_ref, w_ref, ot_ref = refs[n_parts:]
    place_rows(at_ref, parts, w_ref, 1)
    normed, _ = norm_parts(x_ref[...].astype(wide))
    a1 = (normed * vec_ref[0:1, :] + vec_ref[1:2, :]).astype(low)
    a1_ref[...] = a1
    q = (dot(a1, w_ref[0]) + qv_ref[0:1, :]).astype(low)
    k = dot(a1, w_ref[1]).astype(low)
    v = (dot(a1, w_ref[2]) + qv_ref[1:2, :]).astype(low)
    qkv_ref[0] = q
    qkv_ref[1] = k
    qkv_ref[2] = v
    vt = v.T
    for head in range(q.shape[1] // HD):
        cols = slice(head * HD, (head + 1) * HD)
        scores = dot(k[:, cols], q[:, cols], NT) * score_scale
        top = jnp.max(scores, axis=0, keepdims=True)
        expos = jnp.exp(scores - top)
        summed = jnp.sum(expos, axis=0, keepdims=True)
        lse_ref[head : head + 1, :] = top + jnp.log(summed)
        ot_ref[cols, :] = dot(vt[cols, :], expos.astype(low)) / summed
    o = ot_ref[...].T.astype(low)
    head_part, side_part = pack_heads(o)
    rows = o.shape[0]
    o_ref[0:rows, :] = head_part
    o_ref[rows:, :] = side_part


def mlp_kernel(n_parts, at_ref, x_ref, c_ref, vec_ref, ub_ref, o_ref, *refs):
    parts = refs[:n_parts]
    (dn2_ref, a2_ref, g_ref, du_ref, own_ref, stat_ref, sums_ref, gub_ref,
     w_ref, h_ref, n_ref, s_ref) = refs[n_parts:]
    ranks = o_ref.shape[0]
    rows, width = x_ref.shape
    part_rows = rows // ranks
    hidden = ub_ref.shape[1]
    heads_width = width // ranks
    if n_parts == 1:
        w_ref[...] = parts[0][...]
    else:
        for slot, part in enumerate(parts):
            height = part.shape[1]
            start = pl.multiple_of((at_ref[0] ^ slot) * height, 32)
            w_ref[:, pl.ds(start, height), :] = part[...]
    rank = at_ref[1]
    o = jnp.concatenate([unpack_heads(o_ref[j]) for j in range(ranks)], axis=1)
    hidden_state = x_ref[...].astype(wide) + dot(o, w_ref[2], NT) + vec_ref[6:7, :]
    h_ref[...] = hidden_state
    normed, inverse = norm_parts(hidden_state)
    n_ref[...] = normed
    s_ref[...] = jnp.broadcast_to(inverse, s_ref.shape)
    a2 = (normed * vec_ref[2:3, :] + vec_ref[3:4, :]).astype(low)
    a2_ref[...] = a2
    pre = dot(a2, w_ref[0]) + ub_ref[...]
    square = pre * pre
    tangent = jnp.tanh(gelu_coef * pre * (1.0 + 0.044715 * square))
    half = 0.5 * (1.0 + tangent)
    g_ref[...] = (pre * half).astype(low)
    slope = half + 0.5 * pre * (1.0 - tangent * tangent) * gelu_coef * (1.0 + 3.0 * 0.044715 * square)
    du = (dot(c_ref[...], w_ref[1]) * slope).astype(low)
    du_ref[...] = du
    gub_ref[...] = jnp.sum(du.astype(wide), axis=0, keepdims=True)
    dn2 = dot(du, w_ref[0], NT)
    sums_ref[0:1, :] = jnp.sum(dn2 * normed, axis=0, keepdims=True)
    sums_ref[1:2, :] = jnp.sum(dn2, axis=0, keepdims=True)
    for j in range(ranks):
        dn2_ref[j ^ rank] = dn2[j * part_rows : (j + 1) * part_rows].astype(low)
    own = pl.ds(pl.multiple_of(rank * part_rows, 16), part_rows)
    own_ref[0] = h_ref[own, :]
    own_ref[1] = n_ref[own, :]
    stat_ref[...] = s_ref[own, :]
    cotan = c_ref[own, :].astype(wide)
    sums_ref[2:3, :] = jnp.sum(cotan, axis=0, keepdims=True)


def mlp_out_kernel(at_ref, g_ref, w_ref, out_ref):
    rank = at_ref[1]
    part_rows = out_ref.shape[1]
    out = dot(g_ref[...], w_ref[1], NT).astype(low)
    for j in range(4):
        out_ref[j ^ rank] = out[j * part_rows : (j + 1) * part_rows]


def mix_kernel(at_ref, own_ref, stat_ref, c_ref, vec_ref, wo_ref, *refs):
    chunks = refs[:4]
    dh_ref, dz_ref, do_ref, gbo_ref = refs[4:]
    rank = at_ref[1]
    part_rows = stat_ref.shape[0]
    grad = sum(ref[...].astype(wide) for ref in chunks)
    own = pl.ds(pl.multiple_of(rank * part_rows, 16), part_rows)
    cotan = c_ref[own, :].astype(wide)
    dh = cotan + norm_backward(grad, own_ref[1], stat_ref[:, 0:1], vec_ref[2:3, :])
    dh_ref[...] = dh
    gbo_ref[...] = jnp.sum(dh, axis=0, keepdims=True)
    dz = dh.astype(low)
    dz_ref[...] = dz
    do = dot(dz, wo_ref[2]).astype(low)
    ranks = do_ref.shape[0]
    heads_width = do.shape[1] // ranks
    for j in range(ranks):
        head_part, side_part = pack_heads(do[:, j * heads_width : (j + 1) * heads_width])
        do_ref[j ^ rank, 0:part_rows, :] = head_part
        do_ref[j ^ rank, part_rows:, :] = side_part


def attend_back_kernel(fast, at_ref, x_ref, a1_ref, qkv_ref, lse_ref, w_ref, *refs):
    chunks = refs[:4]
    if fast:
        dn1_ref, keep_ref, send_ref, sums_ref, qvsum_ref = refs[4:9]
    else:
        dn1_ref, whole_ref, sums_ref, qvsum_ref = refs[4:8]
    do_ref, dqt_ref, d_ref, g_ref = refs[-4:]
    rank = at_ref[1]
    rows, width = x_ref.shape
    part_rows = rows // 4
    for j in range(4):
        do_ref[pl.ds(pl.multiple_of((rank ^ j) * part_rows, 16), part_rows), :] = unpack_heads(chunks[j][...])
    q, k, v, do = qkv_ref[0], qkv_ref[1], qkv_ref[2], do_ref[...]
    kt = k.T
    for head in range(q.shape[1] // HD):
        cols = slice(head * HD, (head + 1) * HD)
        scores = dot(k[:, cols], q[:, cols], NT) * score_scale
        probs = jnp.exp(scores - lse_ref[head : head + 1, :])
        grad_probs = dot(v[:, cols], do[:, cols], NT)
        d_ref[2, :, cols] = dot(probs.astype(low), do[:, cols]).astype(low)
        both = probs * grad_probs
        grad_scores = (both - probs * jnp.sum(both, axis=0, keepdims=True)).astype(low)
        d_ref[1, :, cols] = (dot(grad_scores, q[:, cols]) * score_scale).astype(low)
        dqt_ref[cols, :] = dot(kt[cols, :], grad_scores) * score_scale
    d_ref[0] = dqt_ref[...].T.astype(low)
    qvsum_ref[0:1, :] = jnp.sum(d_ref[0].astype(wide), axis=0, keepdims=True)
    qvsum_ref[1:2, :] = jnp.sum(d_ref[2].astype(wide), axis=0, keepdims=True)
    dn1 = dot(d_ref[0], w_ref[0], NT) + dot(d_ref[1], w_ref[1], NT) + dot(d_ref[2], w_ref[2], NT)
    for j in range(4):
        dn1_ref[j ^ rank] = dn1[j * part_rows : (j + 1) * part_rows].astype(low)
    normed, _ = norm_parts(x_ref[...].astype(wide))
    sums_ref[0:1, :] = jnp.sum(dn1 * normed, axis=0, keepdims=True)
    sums_ref[1:2, :] = jnp.sum(dn1, axis=0, keepdims=True)
    a1t = a1_ref[...].T
    for which in range(3):
        grad = dot(a1t, d_ref[which])
        if fast:
            g_ref[...] = grad.astype(low)
            height = width // 8
            for slot in range(4):
                keep_ref[slot, which] = take_rows(at_ref, g_ref, 2 * slot, height)
                send_ref[slot, which] = take_rows(at_ref, g_ref, 2 * slot + 1, height)
        else:
            whole_ref[which] = grad.astype(low)


def weight_grad_kernel(fast, at_ref, left_ref, right_ref, *refs):
    grad = dot(left_ref[...].T, right_ref[...]).astype(low)
    if not fast:
        refs[0][...] = grad
        return
    keep_ref, send_ref, g_ref = refs
    g_ref[...] = grad
    height = grad.shape[0] // 8
    for slot in range(4):
        keep_ref[slot] = take_rows(at_ref, g_ref, 2 * slot, height)
        send_ref[slot] = take_rows(at_ref, g_ref, 2 * slot + 1, height)


def input_kernel(at_ref, x_ref, dh_ref, vec_ref, *refs):
    chunks, out_ref = refs[:4], refs[4]
    part_rows = dh_ref.shape[0]
    own = pl.ds(pl.multiple_of(at_ref[1] * part_rows, 16), part_rows)
    normed, inverse = norm_parts(x_ref[own, :].astype(wide))
    grad = sum(ref[...].astype(wide) for ref in chunks)
    out_ref[...] = dh_ref[...] + norm_backward(grad, normed, inverse, vec_ref[0:1, :])


def adamw(weight, gradient, first, second, rate, decay):
    first_new = beta_one * first + (1.0 - beta_one) * gradient
    second_new = beta_two * second + (1.0 - beta_two) * gradient * gradient
    first_hat = first_new / (1.0 - beta_one**STEP)
    second_hat = second_new / (1.0 - beta_two**STEP)
    weight_new = weight - rate * (first_hat / (jnp.sqrt(second_hat) + adam_eps) + decay * weight)
    return (weight_new, first_new, second_new)


def body(
    images,
    cotangent,
    qkv_weight,
    out_weight,
    up_weight,
    down_weight,
    vectors,
    up_bias,
    qkv_first,
    qkv_second,
    out_first,
    out_second,
    up_first,
    up_second,
    down_first,
    down_second,
    vector_first,
    vector_second,
    bias_first,
    bias_second,
):
    fsdp_size = lax.axis_size("fsdp")
    tensor_size = lax.axis_size("tensor")
    devices = fsdp_size * tensor_size
    fast = fsdp_size == 8
    rank = lax.axis_index("tensor")
    at = jnp.stack([lax.axis_index("fsdp"), rank]).astype(jnp.int32)
    _, rows, width = images.shape
    hidden = up_weight.shape[1]
    heads_width = width // tensor_size
    part_rows = rows // tensor_size
    height = width // fsdp_size
    x = images.reshape(rows, width)
    c = cotangent.reshape(rows, width)

    cols = vectors.shape[1]
    ends = up_bias.shape[0]
    mine = jnp.concatenate([vectors.reshape(-1), up_bias])
    small = lax.all_to_all(
        jnp.broadcast_to(mine[None], (devices, mine.shape[0])), ("fsdp", "tensor"), 0, 0, tiled=True
    )
    vec = small[:, : 8 * cols].reshape(devices, 8, cols).transpose(1, 0, 2).reshape(8, width)
    full_bias = small[:, 8 * cols :].reshape(1, devices * ends)
    up_local = lax.dynamic_slice_in_dim(full_bias, rank * hidden, hidden, 1)
    qv_bias = lax.dynamic_slice_in_dim(vec[4:6], rank * heads_width, heads_width, 1)

    qkv_parts = gather_parts(qkv_weight.astype(low), 1)
    out_t = out_weight.astype(low).T
    out_slots = jnp.stack([out_t] + [flip(out_t, "tensor", mask) for mask in (1, 2, 3)])
    out_rows = jnp.concatenate([lax.dynamic_index_in_dim(out_slots, rank ^ j, 0, False) for j in range(4)], axis=1)
    shard = jnp.stack([up_weight.astype(low), down_weight.astype(low).T, out_rows])
    shard, qkv_parts = lax.optimization_barrier((shard, qkv_parts))
    rest_parts = gather_parts(shard, 1)

    n = len(qkv_parts)
    a1, qkv, lse, o_mine, qkv_full = kernel_call(
        functools.partial(attend_kernel, n),
        [
            ((rows, width), low),
            ((3, rows, heads_width), low),
            ((8, rows), wide),
            ((rows * 3 // 2, 128), low),
            ((3, width, heads_width), low),
        ],
        (at, x, vec, qv_bias, *qkv_parts),
        [pltpu.VMEM((heads_width, rows), wide)],
        flops=2 * rows * width * heads_width * 3 + 4 * rows * rows * heads_width,
        moved=8 << 20,
    )
    o_all = lax.all_gather(o_mine, "tensor", axis=0)

    dn2, a2, g, du, own, stat, sums_two, gub, w_full = kernel_call(
        functools.partial(mlp_kernel, n),
        [
            ((4, part_rows, width), low),
            ((rows, width), low),
            ((rows, hidden), low),
            ((rows, hidden), low),
            ((2, part_rows, width), wide),
            ((part_rows, 128), wide),
            ((8, width), wide),
            ((1, hidden), wide),
            ((3, width, hidden), low),
        ],
        (at, x, c, vec, up_local, o_all, *rest_parts),
        [pltpu.VMEM((rows, width), wide), pltpu.VMEM((rows, width), wide), pltpu.VMEM((rows, 128), wide)],
        flops=2 * rows * width * (width + 3 * hidden),
        moved=16 << 20,
    )

    dn2_got = [dn2[0]] + [flip(dn2[j], "tensor", j) for j in (1, 2, 3)]

    def weight_grad(left, right):
        shape = (left.shape[1], right.shape[1])
        cut = (4, height, shape[1])
        outs = [(cut, low), (cut, low)] if fast else [(shape, low)]
        got = kernel_call(
            functools.partial(weight_grad_kernel, fast),
            outs,
            (at, left, right),
            [pltpu.VMEM(shape, low)] if fast else [],
            flops=2 * left.shape[0] * shape[0] * shape[1],
            moved=4 << 20,
        )
        return fsdp_sum(*got) if fast else summed_on_arrival(got[0], 0)

    up_owned = weight_grad(a2, du)
    down_owned = weight_grad(c, g).T

    (mlp,) = kernel_call(
        mlp_out_kernel,
        [((4, part_rows, width), low)],
        (at, g, w_full),
        flops=2 * rows * width * hidden,
        moved=3 << 20,
    )

    dh, dz, do, gbo = kernel_call(
        mix_kernel,
        [
            ((part_rows, width), wide),
            ((part_rows, width), low),
            ((4, part_rows * 3 // 2, 128), low),
            ((1, width), wide),
        ],
        (at, own, stat, c, vec, w_full, *dn2_got),
        flops=2 * part_rows * width * width,
        moved=4 << 20,
    )
    do_got = [do[0]] + [flip(do[j], "tensor", j) for j in (1, 2, 3)]

    cut = (4, 3, height, heads_width)
    outs = [((4, part_rows, width), low)]
    outs += [(cut, low), (cut, low)] if fast else [((3, width, heads_width), low)]
    outs += [((8, width), wide), ((8, heads_width), wide)]
    back = kernel_call(
        functools.partial(attend_back_kernel, fast),
        outs,
        (at, x, a1, qkv, lse, qkv_full, *do_got),
        [
            pltpu.VMEM((rows, heads_width), low),
            pltpu.VMEM((heads_width, rows), wide),
            pltpu.VMEM((3, rows, heads_width), low),
            pltpu.VMEM((width, heads_width), low),
        ],
        flops=10 * rows * rows * heads_width + 4 * rows * width * heads_width * 3,
        moved=8 << 20,
    )
    dn1, sums_one, qv_sums = back[0], back[-2], back[-1]
    dn1_got = [dn1[0]] + [flip(dn1[j], "tensor", j) for j in (1, 2, 3)]
    qkv_owned = fsdp_sum(back[1], back[2]) if fast else summed_on_arrival(back[1], 1)

    def place(value, total):
        return lax.dynamic_update_slice_in_dim(
            jnp.zeros((value.shape[0], total), wide), value, rank * value.shape[1], 1
        )

    vector_grad = jnp.concatenate(
        [sums_one[0:2], sums_two[0:2], place(qv_sums[0:2], width), gbo, sums_two[2:3]], axis=0
    )
    bias_grad = place(gub, hidden * tensor_size)
    blocks = jnp.concatenate(
        [
            vector_grad.reshape(8, devices, cols).transpose(1, 0, 2).reshape(devices, 8 * cols),
            bias_grad.reshape(devices, ends),
        ],
        axis=1,
    )
    owned = jnp.sum(lax.all_to_all(blocks, ("fsdp", "tensor"), 0, 0, tiled=True), axis=0)
    vector_owned = owned[: 8 * cols].reshape(8, cols)
    bias_owned = owned[8 * cols :]

    mlp_got = [mlp[0]] + [flip(mlp[j], "tensor", j) for j in (1, 2, 3)]
    output = (own[0] + sum(part.astype(wide) for part in mlp_got) + vec[7]).astype(low)
    dz_all = lax.all_gather(dz, "tensor", axis=0, tiled=True)
    o_flat = unpack_heads(o_mine)
    out_owned = weight_grad(dz_all, o_flat).T

    (input_own,) = kernel_call(
        input_kernel,
        [((part_rows, width), wide)],
        (at, x, dh, vec, *dn1_got),
        moved=3 << 20,
    )

    qkv_state = adamw(qkv_weight, qkv_owned, qkv_first, qkv_second, 0.08, 0.1)
    out_state = adamw(out_weight, out_owned, out_first, out_second, 0.3, 0.1)
    up_state = adamw(up_weight, up_owned, up_first, up_second, 0.08, 0.1)
    down_state = adamw(down_weight, down_owned, down_first, down_second, 0.045, 0.1)
    vec_state = adamw(vectors, vector_owned, vector_first, vector_second, 0.5, 0.0)
    bias_state = adamw(up_bias, bias_owned, bias_first, bias_second, 0.7, 0.0)
    return (
        output[None],
        input_own[None],
        *qkv_state,
        *out_state,
        *up_state,
        *down_state,
        *vec_state,
        *bias_state,
    )


def solution(mesh):
    weights = (P(None, "fsdp", "tensor"), P("tensor", "fsdp"), P("fsdp", "tensor"), P("tensor", "fsdp"))
    vector, bias = P(None, ("fsdp", "tensor")), P(("fsdp", "tensor"))
    twice = [spec for spec in (*weights, vector, bias) for _ in range(2)]
    thrice = [spec for spec in (*weights, vector, bias) for _ in range(3)]
    return jax.shard_map(
        body,
        mesh=mesh,
        in_specs=(P("fsdp", None, None), P("fsdp", None, None), *weights, vector, bias, *twice),
        out_specs=(P("fsdp", "tensor", None), P("fsdp", "tensor", None), *thrice),
        check_vma=False,
    )
```

time: 412 us -> 220 us (0.53)
  blocking collectives: 190 us -> 54.8 us
  waiting for transfers between devices: 84.8 us -> 37.3 us
  starting transfers between devices: 13.2 us -> 53.6 us
  matrix products: 34.9 us -> 0 us
  Pallas kernels: 0 us -> 30.8 us
  other arithmetic: 35.9 us -> 15.5 us
  between operations: 16.1 us -> 1.5 us
  local copies, waits for them, and re-layouts: 35.5 us -> 23.9 us
    unnamed x2 -> x0, blocking collectives: 78 us -> none
    psum x3 -> x0, waiting for transfers between devices: 56.4 us -> none  [the longest x1 32.6 us: body(): lax.psum(second_part.astype(jnp.bfloat16), 'tensor').astype(jnp.float32)]
    ppermute x0 -> x45, starting transfers between devices: none -> 45.6 us  [flip(): return lax.ppermute(value, axis, [(i, i ^ mask) for i in range(size)])]
    all_gather x3 -> x2, blocking collectives: 91.5 us -> 54.8 us  [the longest x1 33.6 us: body(): dz_all = lax.all_gather(dz, 'tensor', axis=0, tiled=True)]
    dot_general x17 -> x0, matrix products: 32.7 us -> none  [the longest x1 4.17 us: body(): jnp.einsum('rd,fd->rf', cotan_low, down_full, preferred_element_type=jnp....]
    pallas_call x0 -> x9, Pallas kernels: none -> 30.8 us  [kernel_call(): pl.pallas_call(body, out_shape=[jax.ShapeDtypeStruct(s, d) for s, d in ou...]
    ppermute x0 -> x45, waiting for transfers between devices: none -> 30.1 us  [flip(): return lax.ppermute(value, axis, [(i, i ^ mask) for i in range(size)])]
    all_to_all x1 -> x0, blocking collectives: 20.4 us -> none  [summed_on_arrival(): lax.all_to_all(cut_along(value, dim, peers), axis, 0, 0, tiled=True)]
  transfers between devices with their start and end apart: 8 -> 47, of which waited for: 5 -> 13; matrix products, arithmetic and copies ran while one was open for 17% -> 13% of each run, Pallas kernels for 0% -> 10%
where the time goes in v1:
time: 220 us; the launch traced here: 217 us
  blocking collectives  54.8 us (25%)
  starting transfers between devices  53.6 us (24%)
  waiting for transfers between devices  37.3 us (17%)
  Pallas kernels  30.8 us (14%)
  local copies, waits for them, and re-layouts  23.9 us (11%)
  other arithmetic  15.5 us (7%)
    ppermute x45, starting transfers between devices, flip(): return lax.ppermute(value, axis, [(i, i ^ mask) for i in range(size)])  45.6 us
    all_gather x1, blocking collectives, body(): dz_all = lax.all_gather(dz, 'tensor', axis=0, tiled=True)  33.6 us
    pallas_call x9, Pallas kernels, kernel_call(): pl.pallas_call(body, out_shape=[jax.ShapeDtypeStruct(s, d) for s, d in ou...  30.8 us
    ppermute x45, waiting for transfers between devices, flip(): return lax.ppermute(value, axis, [(i, i ^ mask) for i in range(size)])  30.1 us
    all_gather x1, blocking collectives, body(): o_all = lax.all_gather(o_mine, 'tensor', axis=0)  21.3 us
    unnamed x97, local copies, waits for them, and re-layouts  16 us
    all_to_all x1, waiting for transfers between devices, body(): lax.all_to_all(blocks, ('fsdp', 'tensor'), 0, 0, tiled=True)  6.51 us
    sub x6, other arithmetic, adamw(): weight - rate * (first_hat / (jnp.sqrt(second_hat) + adam_eps) + decay *...  6.29 us
  transfers between devices with their start and end apart: 47, of which 13 were waited for; matrix products, arithmetic and copies ran while one was open for 13% of the time, Pallas kernels for 10%

profile of v1, /device:TPU:0, one launch (start us, length us, event | category | flops | bytes accessed | tf_op | source)
XLA Modules:
  0.0 217.5 jit_solution(2138330857132665886)
XLA Ops:
  1.7 3.1 %collective-permute-start = (bf16[96,192]{0,1:T(8,128)(2,1)S(1)}, bf16[96,192]{0,1:T(8,128)(2,1)S(1)}, u32[]{:S(2)}, u32[]{:S(2)}) collective-permute-start(bf16[96,192]{0,1:T(8,128)(2,1)S(1)} %get-tuple-element.216), channel_id=1, source_target_pairs={{0,1},{1,0},{2,3},{3,2},{4,5},{5,4},{6,7},{7,6},{8,9},{9,8},{10,11... | collective-permute-start | bytes 110600 | tf_op jit(solution)/shard_map/ppermute | solution.py:50
  4.8 2.6 %collective-permute-start.1 = (bf16[96,192]{0,1:T(8,128)(2,1)S(1)}, bf16[96,192]{0,1:T(8,128)(2,1)S(1)}, u32[]{:S(2)}, u32[]{:S(2)}) collective-permute-start(bf16[96,192]{0,1:T(8,128)(2,1)S(1)} %get-tuple-element.216), channel_id=1, source_target_pairs={{0,2},{1,3},{2,0},{3,1},{4,6},{5,7},{6,4},{7,5},{8,10},{9,11},{10,... | collective-permute-start | bytes 110600 | tf_op jit(solution)/shard_map/ppermute | solution.py:50
  8.3 1.8 collective-permute-start.4
  10.1 1.5 collective-permute-start.6
  13.8 4.0 %all-to-all-start = ((f32[32,1,288]{2,1,0:T(1,128)}), f32[32,1,288]{2,1,0:T(1,128)S(1)}, u32[]{:S(2)}, u32[]{:S(2)}) async-start(f32[32,1,288]{2,1,0:T(1,128)} %broadcast_in_dim.18), calls=%async_computation | async-start | bytes 98304 | tf_op jit(solution)/shard_map/all_to_all | solution.py:345
  21.1 2.7 %collective-permute-start.8 = (bf16[3,96,192]{2,1,0:T(8,128)(2,1)S(1)}, bf16[3,96,192]{2,1,0:T(8,128)(2,1)S(1)}, u32[]{:S(2)}, u32[]{:S(2)}) collective-permute-start(bf16[3,96,192]{2,1,0:T(8,128)(2,1)S(1)} %convert_element_type.141.refs_0_), channel_id=1, source_target_pairs={{0,24},{4,28},{8,16},{12,20},{16,8},{20,12},{24,0},{28,4},{1,25},{... | collective-permute-start | bytes 331784 | tf_op jit(solution)/shard_map/ppermute | solution.py:50
  26.0 2.1 collective-permute-done.8.refs_6_
  28.1 1.3 collective-permute-done.9.refs_7_
  30.1 1.6 collective-permute-start.11
  31.7 1.5 collective-permute-start.13
  37.5 4.0 %shard_map.347 = (bf16[576,768]{1,0:T(8,128)(2,1)S(1)}, bf16[3,576,192]{2,1,0:T(8,128)(2,1)S(1)}, f32[8,576]{1,0:T(8,128)S(1)}, bf16[864,128]{1,0:T(8,128)(2,1)S(1)}, bf16[3,768,192]{2,1,0:T(8,128)(2,1)S(1)}) custom-call(s32[2]{0:T(128)S(1)} %pad_add_fusion.at_ref, bf16[576,768]{1,0:T(8,128)(2,1)S(1)} %bitcast.162, f32[8,768]{1,0:T(8,128)S(1)} %reshape.107.vec_ref, ...), custom_call_target="tpu_custom_call" | custom-call | flops 764411904 | bytes 8388608 | tf_op jit(solution)/shard_map/pallas_call | solution.py:37
  44.2 8.9 %collective-permute-done.13.refs_4_ = bf16[3,96,768]{2,1,0:T(8,128)(2,1)S(1)} collective-permute-done((bf16[3,96,768]{2,1,0:T(8,128)(2,1)S(1)}, bf16[3,96,768]{2,1,0:T(8,128)(2,1)S(1)}, u32[]{:S(2)}, u32[]{:S(2)}) %collective-permute-start.13) | collective-permute-done | bytes 442400 | tf_op jit(solution)/shard_map/ppermute | solution.py:50
  53.7 21.3 %all-gather = bf16[3456,128]{1,0:T(8,128)(2,1)} all-gather(bf16[864,128]{1,0:T(8,128)(2,1)S(1)} %get-tuple-element.66), channel_id=2, replica_groups=mesh['fsdp'=8,'tensor'=4] {'tensor'}, dimensions={0}, use_global_device_ids=true | all-gather | bytes 1105920 | tf_op jit(solution)/shard_map/all_gather | solution.py:376
  75.0 8.1 %shard_map.348 = (bf16[4,144,768]{2,1,0:T(8,128)(2,1)S(1)}, bf16[576,768]{1,0:T(8,128)(2,1)S(1)}, bf16[576,768]{1,0:T(8,128)(2,1)}, bf16[576,768]{1,0:T(8,128)(2...) custom-call(s32[2]{0:T(128)S(1)} %pad_add_fusion.at_ref, ...), custom_call_target="tpu_custom_call" | custom-call | flops 2717908992 | bytes 16777216 | tf_op jit(solution)/shard_map/pallas_call | solution.py:37
  84.3 2.3 %collective-permute-start.21 = (bf16[144,768]{1,0:T(8,128)(2,1)}, bf16[144,768]{1,0:T(8,128)(2,1)}, u32[]{:S(2)}, u32[]{:S(2)}) collective-permute-start(bf16[144,768]{1,0:T(8,128)(2,1)} %get-tuple-element.185), channel_id=1, source_target_pairs={{0,2},{1,3},{2,0},{3,1},{4,6},{5,7},{6,4},{7,5},{8,10},{9,11},{10,... | collective-permute-start | bytes 663560 | tf_op jit(solution)/shard_map/ppermute | solution.py:50
  86.5 2.1 collective-permute-start.22
  89.9 2.6 %shard_map.355 = (bf16[4,96,768]{2,1,0:T(8,128)(2,1)S(1)}, bf16[4,96,768]{2,1,0:T(8,128)(2,1)}) custom-call(s32[2]{0:T(128)S(1)} %pad_add_fusion.at_ref, bf16[576,768]{1,0:T(8,128)(2,1)S(1)} %bitcast.159, bf16[576,768]{1,0:T(8,128)(2,1)S(1)} %copy-done.5), custom_call_target="tpu_custom_call" | custom-call | flops 679477248 | bytes 4194304 | tf_op jit(solution)/shard_map/pallas_call | solution.py:37
  92.5 1.2 copy-done.24
  93.7 1.2 copy-done.25
  94.9 2.6 %shard_map.354 = (bf16[4,96,768]{2,1,0:T(8,128)(2,1)S(1)}, bf16[4,96,768]{2,1,0:T(8,128)(2,1)}) custom-call(s32[2]{0:T(128)S(1)} %pad_add_fusion.at_ref, bf16[576,768]{1,0:T(8,128)(2,1)S(1)} %copy-done.24, bf16[576,768]{1,0:T(8,128)(2,1)S(1)} %copy-done.25), custom_call_target="tpu_custom_call" | custom-call | flops 679477248 | bytes 4194304 | tf_op jit(solution)/shard_map/pallas_call | solution.py:37
  98.0 1.4 shard_map.349
  99.6 3.3 %collective-permute-done.21.refs_2_ = bf16[144,768]{1,0:T(8,128)(2,1)} collective-permute-done((bf16[144,768]{1,0:T(8,128)(2,1)}, bf16[144,768]{1,0:T(8,128)(2,1)}, u32[]{:S(2)}, u32[]{:S(2)}) %collective-permute-start.21) | collective-permute-done | bytes 221216 | tf_op jit(solution)/shard_map/ppermute | solution.py:50
  102.8 1.9 collective-permute-start.19
  104.7 2.9 %shard_map.350 = (f32[144,768]{1,0:T(8,128)S(1)}, bf16[144,768]{1,0:T(8,128)(2,1)S(1)}, bf16[4,216,128]{2,1,0:T(8,128)(2,1)S(1)}, f32[1,768]{1,0:T(1,128)S(1)}) custom-call(s32[2]{0:T(128)S(1)} %pad_add_fusion.at_ref, f32[2,144,768]{2,1,0:T(8,128)S(1)} %copy-done.1, f32[144,128]{1,0:T(8,128)S(1)} %copy-done.11, bf16[576,768]{1,0:T(8,128)(2,1)S(1)} %bitcast.160, ...), custom_call_target="tpu_custom_call" | custom-call | flops 169869312 | bytes 4194304 | tf_op jit(solution)/shard_map/pallas_call | solution.py:37
  107.7 33.6 %all_gather.11.left_ref = bf16[576,768]{1,0:T(8,128)(2,1)S(1)} all-gather(bf16[144,768]{1,0:T(8,128)(2,1)S(1)} %get-tuple-element.82), channel_id=1, replica_groups=mesh['fsdp'=8,'tensor'=4] {'tensor'}, dimensions={0}, use_global_device_ids=true | all-gather | bytes 1105920 | tf_op jit(solution)/shard_map/all_gather | solution.py:481
  141.3 1.5 collective-permute-start.23
  142.9 2.9 %collective-permute-start.25 = (bf16[216,128]{1,0:T(8,128)(2,1)S(1)}, bf16[216,128]{1,0:T(8,128)(2,1)S(1)}, u32[]{:S(2)}, u32[]{:S(2)}) collective-permute-start(bf16[216,128]{1,0:T(8,128)(2,1)S(1)} %get-tuple-element.204), channel_id=1, source_target_pairs={{0,3},{1,2},{2,1},{3,0},{4,7},{5,6},{6,5},{7,4},{8,11},{9,10},{10,... | collective-permute-start | bytes 165896 | tf_op jit(solution)/shard_map/ppermute | solution.py:50
  146.6 1.8 shard_map.353
  149.1 5.6 %shard_map.351 = (bf16[4,144,768]{2,1,0:T(8,128)(2,1)S(1)}, bf16[4,3,96,192]{3,2,1,0:T(8,128)(2,1)S(1)}, bf16[4,3,96,192]{3,2,1,0:T(8,128)(2,1)S(1)}, f32[8,768]{1,0:T(8,128)S(1)}, f32[8,192]{1,0:T(8,128)S(1)}) custom-call(s32[2]{0:T(128)S(1)} %pad_add_fusion.at_ref, bf16[576,768]{1,0:T(8,128)(2,1)S(1)} %bitcast.163, bf16[576,768]{1,0:T(8,128)(2,1)S(1)} %copy-done.20, ...), custom_call_target="tpu_custom_call" | custom-call | flops 1656225792 | bytes 8388608 | tf_op jit(solution)/shard_map/pallas_call | solution.py:37
  157.7 4.0 %all-to-all-start.1 = ((f32[32,1,288]{2,1,0:T(1,128)}), f32[32,1,288]{2,1,0:T(1,128)S(1)}, u32[]{:S(2)}, u32[]{:S(2)}) async-start(f32[32,1,288]{2,1,0:T(1,128)} %copy.76), calls=%async_computation.1 | async-start | bytes 98304 | tf_op jit(solution)/shard_map/all_to_all | solution.py:475
  162.6 6.5 %all-to-all-done.1 = f32[32,1,288]{2,1,0:T(1,128)S(1)} async-done(((f32[32,1,288]{2,1,0:T(1,128)}), f32[32,1,288]{2,1,0:T(1,128)S(1)}, u32[]{:S(2)}, u32[]{:S(2)}) %all-to-all-start.1) | async-done | bytes 36896 | tf_op jit(solution)/shard_map/all_to_all | solution.py:475
  172.2 2.3 %collective-permute-start.36 = (bf16[96,192]{1,0:T(8,128)(2,1)S(1)}, bf16[96,192]{1,0:T(8,128)(2,1)S(1)}, u32[]{:S(2)}, u32[]{:S(2)}) collective-permute-start(bf16[96,192]{1,0:T(8,128)(2,1)S(1)} %get-tuple-element.209), channel_id=1, source_target_pairs={{0,24},{4,28},{8,16},{12,20},{16,8},{20,12},{24,0},{28,4},{1,25},{... | collective-permute-start | bytes 110600 | tf_op jit(solution)/shard_map/ppermute | solution.py:50
  177.2 2.5 %collective-permute-start.28 = (bf16[144,768]{1,0:T(8,128)(2,1)}, bf16[144,768]{1,0:T(8,128)(2,1)S(1)}, u32[]{:S(2)}, u32[]{:S(2)}) collective-permute-start(bf16[144,768]{1,0:T(8,128)(2,1)} %get-tuple-element.180), channel_id=1, source_target_pairs={{0,3},{1,2},{2,1},{3,0},{4,7},{5,6},{6,5},{7,4},{8,11},{9,10},{10,... | collective-permute-start | bytes 663560 | tf_op jit(solution)/shard_map/ppermute | solution.py:50
  179.6 1.8 multiply_subtract_fusion.3
  181.4 1.6 copy.77
  183.0 1.6 copy.78
  184.7 1.6 copy.79
  186.3 8.0 %collective-permute-done.27.refs_2_ = bf16[144,768]{1,0:T(8,128)(2,1)S(1)} collective-permute-done((bf16[144,768]{1,0:T(8,128)(2,1)}, bf16[144,768]{1,0:T(8,128)(2,1)S(1)}, u32[]{:S(2)}, u32[]{:S(2)}) %collective-permute-start.27) | collective-permute-done | bytes 221216 | tf_op jit(solution)/shard_map/ppermute | solution.py:50
  194.3 1.7 shard_map.352
  196.1 1.2 convert_add_fusion
  197.3 1.3 collective-permute-start.42
  199.5 1.4 collective-permute-start.44
  200.9 1.2 convert_add_fusion.1
  202.1 1.3 collective-permute-start.38
  204.6 1.4 collective-permute-start.40
  206.0 2.6 %collective-permute-done.43 = bf16[96,768]{1,0:T(8,128)(2,1)S(1)} collective-permute-done((bf16[96,768]{1,0:T(8,128)(2,1)S(1)}, bf16[96,768]{1,0:T(8,128)(2,1)S(1)}, u32[]{:S(2)}, u32[]{:S(2)}) %collective-permute-start.43) | collective-permute-done | bytes 147488 | tf_op jit(solution)/shard_map/ppermute | solution.py:50
  210.3 2.9 %collective-permute-start.32 = (bf16[3,96,192]{2,1,0:T(8,128)(2,1)S(1)}, bf16[3,96,192]{2,1,0:T(8,128)(2,1)S(1)}, u32[]{:S(2)}, u32[]{:S(2)}) collective-permute-start(bf16[3,96,192]{2,1,0:T(8,128)(2,1)S(1)} %get-tuple-element.198), channel_id=1, source_target_pairs={{0,24},{4,28},{8,16},{12,20},{16,8},{20,12},{24,0},{28,4},{1,25},{... | collective-permute-start | bytes 331784 | tf_op jit(solution)/shard_map/ppermute | solution.py:50
  214.4 1.9 collective-permute-done.32
  (225 shorter events, 37.8 us)
Async XLA Ops:
  1.7 19.4 %collective-permute-start = (bf16[96,192]{0,1:T(8,128)(2,1)S(1)}, bf16[96,192]{0,1:T(8,128)(2,1)S(1)}, u32[]{:S(2)}, u32[]{:S(2)}) collective-permute-start(bf16[96,192]{0,1:T(8,128)(2,1)S(1)} %get-tuple-element.216), channel_id=1, source_target_pairs={{0,1},{1,0},{2,3},{3,2},{4,5},{5,4},{6,7},{7,6},{8,9},{9,8},{10,11... | collective-permute-start | bytes 110600 | tf_op jit(solution)/shard_map/ppermute | solution.py:50
  4.8 19.0 %collective-permute-start.1 = (bf16[96,192]{0,1:T(8,128)(2,1)S(1)}, bf16[96,192]{0,1:T(8,128)(2,1)S(1)}, u32[]{:S(2)}, u32[]{:S(2)}) collective-permute-start(bf16[96,192]{0,1:T(8,128)(2,1)S(1)} %get-tuple-element.216), channel_id=1, source_target_pairs={{0,2},{1,3},{2,0},{3,1},{4,6},{5,7},{6,4},{7,5},{8,10},{9,11},{10,... | collective-permute-start | bytes 110600 | tf_op jit(solution)/shard_map/ppermute | solution.py:50
  7.3 16.4 %collective-permute-start.2 = (bf16[96,192]{0,1:T(8,128)(2,1)S(1)}, bf16[96,192]{0,1:T(8,128)(2,1)S(1)}, u32[]{:S(2)}, u32[]{:S(2)}) collective-permute-start(bf16[96,192]{0,1:T(8,128)(2,1)S(1)} %get-tuple-element.216), channel_id=1, source_target_pairs={{0,3},{1,2},{2,1},{3,0},{4,7},{5,6},{6,5},{7,4},{8,11},{9,10},{10,... | collective-permute-start | bytes 110600 | tf_op jit(solution)/shard_map/ppermute | solution.py:50
  8.3 17.1 %collective-permute-start.4 = (bf16[3,96,192]{2,1,0:T(8,128)(2,1)S(1)}, bf16[3,96,192]{2,1,0:T(8,128)(2,1)S(1)}, u32[]{:S(2)}, u32[]{:S(2)}) collective-permute-start(bf16[3,96,192]{2,1,0:T(8,128)(2,1)S(1)} %convert_element_type.141.refs_0_), channel_id=1, source_target_pairs={{0,8},{4,12},{8,0},{12,4},{16,24},{20,28},{24,16},{28,20},{1,9},{5... | collective-permute-start | bytes 331784 | tf_op jit(solution)/shard_map/ppermute | solution.py:50
  10.1 15.4 %collective-permute-start.6 = (bf16[3,96,192]{2,1,0:T(8,128)(2,1)S(1)}, bf16[3,96,192]{2,1,0:T(8,128)(2,1)S(1)}, u32[]{:S(2)}, u32[]{:S(2)}) collective-permute-start(bf16[3,96,192]{2,1,0:T(8,128)(2,1)S(1)} %convert_element_type.141.refs_0_), channel_id=1, source_target_pairs={{0,16},{4,20},{8,24},{12,28},{16,0},{20,4},{24,8},{28,12},{1,17},{... | collective-permute-start | bytes 331784 | tf_op jit(solution)/shard_map/ppermute | solution.py:50
  13.8 11.4 %all-to-all-start = ((f32[32,1,288]{2,1,0:T(1,128)}), f32[32,1,288]{2,1,0:T(1,128)S(1)}, u32[]{:S(2)}, u32[]{:S(2)}) async-start(f32[32,1,288]{2,1,0:T(1,128)} %broadcast_in_dim.18), calls=%async_computation | async-start | bytes 98304 | tf_op jit(solution)/shard_map/all_to_all | solution.py:345
  21.1 7.0 %collective-permute-start.8 = (bf16[3,96,192]{2,1,0:T(8,128)(2,1)S(1)}, bf16[3,96,192]{2,1,0:T(8,128)(2,1)S(1)}, u32[]{:S(2)}, u32[]{:S(2)}) collective-permute-start(bf16[3,96,192]{2,1,0:T(8,128)(2,1)S(1)} %convert_element_type.141.refs_0_), channel_id=1, source_target_pairs={{0,24},{4,28},{8,16},{12,20},{16,8},{20,12},{24,0},{28,4},{1,25},{... | collective-permute-start | bytes 331784 | tf_op jit(solution)/shard_map/ppermute | solution.py:50
  23.7 4.4 %collective-permute-start.3 = (bf16[3,96,192]{2,1,0:T(8,128)(2,1)S(1)}, bf16[3,96,192]{2,1,0:T(8,128)(2,1)S(1)}, u32[]{:S(2)}, u32[]{:S(2)}) collective-permute-start(bf16[3,96,192]{2,1,0:T(8,128)(2,1)S(1)} %convert_element_type.141.refs_0_), channel_id=1, source_target_pairs={{0,4},{4,0},{8,12},{12,8},{16,20},{20,16},{24,28},{28,24},{1,5},{5... | collective-permute-start | bytes 331784 | tf_op jit(solution)/shard_map/ppermute | solution.py:50
  25.4 2.7 %collective-permute-start.5 = (bf16[3,96,192]{2,1,0:T(8,128)(2,1)S(1)}, bf16[3,96,192]{2,1,0:T(8,128)(2,1)S(1)}, u32[]{:S(2)}, u32[]{:S(2)}) collective-permute-start(bf16[3,96,192]{2,1,0:T(8,128)(2,1)S(1)} %collective-permute-done.4.refs_2_), channel_id=1, source_target_pairs={{0,4},{4,0},{8,12},{12,8},{16,20},{20,16},{24,28},{28,24},{1,5},{5... | collective-permute-start | bytes 331784 | tf_op jit(solution)/shard_map/ppermute | solution.py:50
  25.5 2.6 %collective-permute-start.7 = (bf16[3,96,192]{2,1,0:T(8,128)(2,1)S(1)}, bf16[3,96,192]{2,1,0:T(8,128)(2,1)S(1)}, u32[]{:S(2)}, u32[]{:S(2)}) collective-permute-start(bf16[3,96,192]{2,1,0:T(8,128)(2,1)S(1)} %collective-permute-done.6.refs_4_), channel_id=1, source_target_pairs={{0,4},{4,0},{8,12},{12,8},{16,20},{20,16},{24,28},{28,24},{1,5},{5... | collective-permute-start | bytes 331784 | tf_op jit(solution)/shard_map/ppermute | solution.py:50
  28.0 1.4 collective-permute-start.9
  30.1 13.6 %collective-permute-start.11 = (bf16[3,96,768]{2,1,0:T(8,128)(2,1)S(1)}, bf16[3,96,768]{2,1,0:T(8,128)(2,1)S(1)}, u32[]{:S(2)}, u32[]{:S(2)}) collective-permute-start(bf16[3,96,768]{2,1,0:T(8,128)(2,1)S(1)} %pad_maximum_fusion.refs_0_), channel_id=1, source_target_pairs={{0,8},{4,12},{8,0},{12,4},{16,24},{20,28},{24,16},{28,20},{1,9},{5... | collective-permute-start | bytes 1327112 | tf_op jit(solution)/shard_map/ppermute | solution.py:50
  31.7 21.4 %collective-permute-start.13 = (bf16[3,96,768]{2,1,0:T(8,128)(2,1)S(1)}, bf16[3,96,768]{2,1,0:T(8,128)(2,1)S(1)}, u32[]{:S(2)}, u32[]{:S(2)}) collective-permute-start(bf16[3,96,768]{2,1,0:T(8,128)(2,1)S(1)} %pad_maximum_fusion.refs_0_), channel_id=1, source_target_pairs={{0,16},{4,20},{8,24},{12,28},{16,0},{20,4},{24,8},{28,12},{1,17},{... | collective-permute-start | bytes 1327112 | tf_op jit(solution)/shard_map/ppermute | solution.py:50
  33.1 20.0 %collective-permute-start.15 = (bf16[3,96,768]{2,1,0:T(8,128)(2,1)S(1)}, bf16[3,96,768]{2,1,0:T(8,128)(2,1)}, u32[]{:S(2)}, u32[]{:S(2)}) collective-permute-start(bf16[3,96,768]{2,1,0:T(8,128)(2,1)S(1)} %pad_maximum_fusion.refs_0_), channel_id=1, source_target_pairs={{0,24},{4,28},{8,16},{12,20},{16,8},{20,12},{24,0},{28,4},{1,25},{... | collective-permute-start | bytes 1327112 | tf_op jit(solution)/shard_map/ppermute | solution.py:50
  35.6 39.3 %collective-permute-start.10 = (bf16[3,96,768]{2,1,0:T(8,128)(2,1)S(1)}, bf16[3,96,768]{2,1,0:T(8,128)(2,1)S(1)}, u32[]{:S(2)}, u32[]{:S(2)}) collective-permute-start(bf16[3,96,768]{2,1,0:T(8,128)(2,1)S(1)} %pad_maximum_fusion.refs_0_), channel_id=1, source_target_pairs={{0,4},{4,0},{8,12},{12,8},{16,20},{20,16},{24,28},{28,24},{1,5},{5... | collective-permute-start | bytes 1327112 | tf_op jit(solution)/shard_map/ppermute | solution.py:50
  43.7 31.3 %collective-permute-start.12 = (bf16[3,96,768]{2,1,0:T(8,128)(2,1)S(1)}, bf16[3,96,768]{2,1,0:T(8,128)(2,1)S(1)}, u32[]{:S(2)}, u32[]{:S(2)}) collective-permute-start(bf16[3,96,768]{2,1,0:T(8,128)(2,1)S(1)} %collective-permute-done.11.refs_2_), channel_id=1, source_target_pairs={{0,4},{4,0},{8,12},{12,8},{16,20},{20,16},{24,28},{28,24},{1,5},{5... | collective-permute-start | bytes 1327112 | tf_op jit(solution)/shard_map/ppermute | solution.py:50
  53.1 21.8 %collective-permute-start.14 = (bf16[3,96,768]{2,1,0:T(8,128)(2,1)S(1)}, bf16[3,96,768]{2,1,0:T(8,128)(2,1)S(1)}, u32[]{:S(2)}, u32[]{:S(2)}) collective-permute-start(bf16[3,96,768]{2,1,0:T(8,128)(2,1)S(1)} %collective-permute-done.13.refs_4_), channel_id=1, source_target_pairs={{0,4},{4,0},{8,12},{12,8},{16,20},{20,16},{24,28},{28,24},{1,5},{5... | collective-permute-start | bytes 1327112 | tf_op jit(solution)/shard_map/ppermute | solution.py:50
  53.1 21.8 %collective-permute-start.16 = (bf16[3,96,768]{2,1,0:T(8,128)(2,1)}, bf16[3,96,768]{2,1,0:T(8,128)(2,1)S(1)}, u32[]{:S(2)}, u32[]{:S(2)}) collective-permute-start(bf16[3,96,768]{2,1,0:T(8,128)(2,1)} %collective-permute-done.15.refs_6_), channel_id=1, source_target_pairs={{0,4},{4,0},{8,12},{12,8},{16,20},{20,16},{24,28},{28,24},{1,5},{5... | collective-permute-start | bytes 1327112 | tf_op jit(solution)/shard_map/ppermute | solution.py:50
  84.3 15.2 %collective-permute-start.20 = (bf16[144,768]{1,0:T(8,128)(2,1)}, bf16[144,768]{1,0:T(8,128)(2,1)}, u32[]{:S(2)}, u32[]{:S(2)}) collective-permute-start(bf16[144,768]{1,0:T(8,128)(2,1)} %get-tuple-element.186), channel_id=1, source_target_pairs={{0,1},{1,0},{2,3},{3,2},{4,5},{5,4},{6,7},{7,6},{8,9},{9,8},{10,11... | collective-permute-start | bytes 663560 | tf_op jit(solution)/shard_map/ppermute | solution.py:50
  84.3 18.6 %collective-permute-start.21 = (bf16[144,768]{1,0:T(8,128)(2,1)}, bf16[144,768]{1,0:T(8,128)(2,1)}, u32[]{:S(2)}, u32[]{:S(2)}) collective-permute-start(bf16[144,768]{1,0:T(8,128)(2,1)} %get-tuple-element.185), channel_id=1, source_target_pairs={{0,2},{1,3},{2,0},{3,1},{4,6},{5,7},{6,4},{7,5},{8,10},{9,11},{10,... | collective-permute-start | bytes 663560 | tf_op jit(solution)/shard_map/ppermute | solution.py:50
  86.5 16.3 %collective-permute-start.22 = (bf16[144,768]{1,0:T(8,128)(2,1)}, bf16[144,768]{1,0:T(8,128)(2,1)}, u32[]{:S(2)}, u32[]{:S(2)}) collective-permute-start(bf16[144,768]{1,0:T(8,128)(2,1)} %get-tuple-element.184), channel_id=1, source_target_pairs={{0,3},{1,2},{2,1},{3,0},{4,7},{5,6},{6,5},{7,4},{8,11},{9,10},{10,... | collective-permute-start | bytes 663560 | tf_op jit(solution)/shard_map/ppermute | solution.py:50
  92.5 103.5 %collective-permute-start.41 = (bf16[4,96,768]{2,1,0:T(8,128)(2,1)}, bf16[4,96,768]{2,1,0:T(8,128)(2,1)}, u32[]{:S(2)}, u32[]{:S(2)}) collective-permute-start(bf16[4,96,768]{2,1,0:T(8,128)(2,1)} %get-tuple-element.90), channel_id=1, source_target_pairs={{0,4},{4,0},{8,12},{12,8},{16,20},{20,16},{24,28},{28,24},{1,5},{5... | collective-permute-start | bytes 1769480 | tf_op jit(solution)/shard_map/ppermute | solution.py:50
  97.5 103.4 %collective-permute-start.37 = (bf16[4,96,768]{2,1,0:T(8,128)(2,1)}, bf16[4,96,768]{2,1,0:T(8,128)(2,1)}, u32[]{:S(2)}, u32[]{:S(2)}) collective-permute-start(bf16[4,96,768]{2,1,0:T(8,128)(2,1)} %get-tuple-element.88), channel_id=1, source_target_pairs={{0,4},{4,0},{8,12},{12,8},{16,20},{20,16},{24,28},{28,24},{1,5},{5... | collective-permute-start | bytes 1769480 | tf_op jit(solution)/shard_map/ppermute | solution.py:50
  99.5 41.8 %collective-permute-start.17 = (bf16[144,768]{1,0:T(8,128)(2,1)S(1)}, bf16[144,768]{1,0:T(8,128)(2,1)S(1)}, u32[]{:S(2)}, u32[]{:S(2)}) collective-permute-start(bf16[144,768]{1,0:T(8,128)(2,1)S(1)} %get-tuple-element.188), channel_id=1, source_target_pairs={{0,1},{1,0},{2,3},{3,2},{4,5},{5,4},{6,7},{7,6},{8,9},{9,8},{10,11... | collective-permute-start | bytes 663560 | tf_op jit(solution)/shard_map/ppermute | solution.py:50
  102.8 40.0 %collective-permute-start.18 = (bf16[144,768]{1,0:T(8,128)(2,1)S(1)}, bf16[144,768]{1,0:T(8,128)(2,1)S(1)}, u32[]{:S(2)}, u32[]{:S(2)}) collective-permute-start(bf16[144,768]{1,0:T(8,128)(2,1)S(1)} %get-tuple-element.190), channel_id=1, source_target_pairs={{0,2},{1,3},{2,0},{3,1},{4,6},{5,7},{6,4},{7,5},{8,10},{9,11},{10,... | collective-permute-start | bytes 663560 | tf_op jit(solution)/shard_map/ppermute | solution.py:50
  102.8 40.0 %collective-permute-start.19 = (bf16[144,768]{1,0:T(8,128)(2,1)S(1)}, bf16[144,768]{1,0:T(8,128)(2,1)S(1)}, u32[]{:S(2)}, u32[]{:S(2)}) collective-permute-start(bf16[144,768]{1,0:T(8,128)(2,1)S(1)} %get-tuple-element.189), channel_id=1, source_target_pairs={{0,3},{1,2},{2,1},{3,0},{4,7},{5,6},{6,5},{7,4},{8,11},{9,10},{10,... | collective-permute-start | bytes 663560 | tf_op jit(solution)/shard_map/ppermute | solution.py:50
  107.7 41.4 %copy-start.22 = (bf16[3,576,192]{2,1,0:T(8,128)(2,1)S(1)}, bf16[3,576,192]{2,1,0:T(8,128)(2,1)}, u32[]{:S(2)}) copy-start(bf16[3,576,192]{2,1,0:T(8,128)(2,1)} %copy-done.21) | copy-start | bytes 1990660
  141.3 7.1 %collective-permute-start.23 = (bf16[216,128]{1,0:T(8,128)(2,1)S(1)}, bf16[216,128]{1,0:T(8,128)(2,1)S(1)}, u32[]{:S(2)}, u32[]{:S(2)}) collective-permute-start(bf16[216,128]{1,0:T(8,128)(2,1)S(1)} %get-tuple-element.206), channel_id=1, source_target_pairs={{0,1},{1,0},{2,3},{3,2},{4,5},{5,4},{6,7},{7,6},{8,9},{9,8},{10,11... | collective-permute-start | bytes 165896 | tf_op jit(solution)/shard_map/ppermute | solution.py:50
  142.8 6.2 %collective-permute-start.24 = (bf16[216,128]{1,0:T(8,128)(2,1)S(1)}, bf16[216,128]{1,0:T(8,128)(2,1)S(1)}, u32[]{:S(2)}, u32[]{:S(2)}) collective-permute-start(bf16[216,128]{1,0:T(8,128)(2,1)S(1)} %get-tuple-element.205), channel_id=1, source_target_pairs={{0,2},{1,3},{2,0},{3,1},{4,6},{5,7},{6,4},{7,5},{8,10},{9,11},{10,... | collective-permute-start | bytes 165896 | tf_op jit(solution)/shard_map/ppermute | solution.py:50
  142.9 6.2 %collective-permute-start.25 = (bf16[216,128]{1,0:T(8,128)(2,1)S(1)}, bf16[216,128]{1,0:T(8,128)(2,1)S(1)}, u32[]{:S(2)}, u32[]{:S(2)}) collective-permute-start(bf16[216,128]{1,0:T(8,128)(2,1)S(1)} %get-tuple-element.204), channel_id=1, source_target_pairs={{0,3},{1,2},{2,1},{3,0},{4,7},{5,6},{6,5},{7,4},{8,11},{9,10},{10,... | collective-permute-start | bytes 165896 | tf_op jit(solution)/shard_map/ppermute | solution.py:50
  148.3 21.6 %collective-permute-start.33 = (bf16[4,96,192]{2,1,0:T(8,128)(2,1)}, bf16[4,96,192]{2,1,0:T(8,128)(2,1)}, u32[]{:S(2)}, u32[]{:S(2)}) collective-permute-start(bf16[4,96,192]{2,1,0:T(8,128)(2,1)} %get-tuple-element.84), channel_id=1, source_target_pairs={{0,4},{4,0},{8,12},{12,8},{16,20},{20,16},{24,28},{28,24},{1,5},{5... | collective-permute-start | bytes 442376 | tf_op jit(solution)/shard_map/ppermute | solution.py:50
  157.7 11.4 %all-to-all-start.1 = ((f32[32,1,288]{2,1,0:T(1,128)}), f32[32,1,288]{2,1,0:T(1,128)S(1)}, u32[]{:S(2)}, u32[]{:S(2)}) async-start(f32[32,1,288]{2,1,0:T(1,128)} %copy.76), calls=%async_computation.1 | async-start | bytes 98304 | tf_op jit(solution)/shard_map/all_to_all | solution.py:475
  171.0 4.3 %collective-permute-start.34 = (bf16[96,192]{1,0:T(8,128)(2,1)S(1)}, bf16[96,192]{1,0:T(8,128)(2,1)S(1)}, u32[]{:S(2)}, u32[]{:S(2)}) collective-permute-start(bf16[96,192]{1,0:T(8,128)(2,1)S(1)} %get-tuple-element.208), channel_id=1, source_target_pairs={{0,8},{4,12},{8,0},{12,4},{16,24},{20,28},{24,16},{28,20},{1,9},{5... | collective-permute-start | bytes 110600 | tf_op jit(solution)/shard_map/ppermute | solution.py:50
  171.7 4.5 %collective-permute-start.35 = (bf16[96,192]{1,0:T(8,128)(2,1)S(1)}, bf16[96,192]{1,0:T(8,128)(2,1)S(1)}, u32[]{:S(2)}, u32[]{:S(2)}) collective-permute-start(bf16[96,192]{1,0:T(8,128)(2,1)S(1)} %get-tuple-element.210), channel_id=1, source_target_pairs={{0,16},{4,20},{8,24},{12,28},{16,0},{20,4},{24,8},{28,12},{1,17},{... | collective-permute-start | bytes 110600 | tf_op jit(solution)/shard_map/ppermute | solution.py:50
  172.2 5.0 %collective-permute-start.36 = (bf16[96,192]{1,0:T(8,128)(2,1)S(1)}, bf16[96,192]{1,0:T(8,128)(2,1)S(1)}, u32[]{:S(2)}, u32[]{:S(2)}) collective-permute-start(bf16[96,192]{1,0:T(8,128)(2,1)S(1)} %get-tuple-element.209), channel_id=1, source_target_pairs={{0,24},{4,28},{8,16},{12,20},{16,8},{20,12},{24,0},{28,4},{1,25},{... | collective-permute-start | bytes 110600 | tf_op jit(solution)/shard_map/ppermute | solution.py:50
  175.2 11.0 %collective-permute-start.26 = (bf16[144,768]{1,0:T(8,128)(2,1)}, bf16[144,768]{1,0:T(8,128)(2,1)S(1)}, u32[]{:S(2)}, u32[]{:S(2)}) collective-permute-start(bf16[144,768]{1,0:T(8,128)(2,1)} %get-tuple-element.182), channel_id=1, source_target_pairs={{0,1},{1,0},{2,3},{3,2},{4,5},{5,4},{6,7},{7,6},{8,9},{9,8},{10,11... | collective-permute-start | bytes 663560 | tf_op jit(solution)/shard_map/ppermute | solution.py:50
  176.1 18.2 %collective-permute-start.27 = (bf16[144,768]{1,0:T(8,128)(2,1)}, bf16[144,768]{1,0:T(8,128)(2,1)S(1)}, u32[]{:S(2)}, u32[]{:S(2)}) collective-permute-start(bf16[144,768]{1,0:T(8,128)(2,1)} %get-tuple-element.181), channel_id=1, source_target_pairs={{0,2},{1,3},{2,0},{3,1},{4,6},{5,7},{6,4},{7,5},{8,10},{9,11},{10,... | collective-permute-start | bytes 663560 | tf_op jit(solution)/shard_map/ppermute | solution.py:50
  177.2 17.2 %collective-permute-start.28 = (bf16[144,768]{1,0:T(8,128)(2,1)}, bf16[144,768]{1,0:T(8,128)(2,1)S(1)}, u32[]{:S(2)}, u32[]{:S(2)}) collective-permute-start(bf16[144,768]{1,0:T(8,128)(2,1)} %get-tuple-element.180), channel_id=1, source_target_pairs={{0,3},{1,2},{2,1},{3,0},{4,7},{5,6},{6,5},{7,4},{8,11},{9,10},{10,... | collective-permute-start | bytes 663560 | tf_op jit(solution)/shard_map/ppermute | solution.py:50
  186.3 17.2 %collective-permute-start.29 = (bf16[4,3,96,192]{3,2,1,0:T(8,128)(2,1)}, bf16[4,3,96,192]{3,2,1,0:T(8,128)(2,1)S(1)}, u32[]{:S(2)}, u32[]{:S(2)}) collective-permute-start(bf16[4,3,96,192]{3,2,1,0:T(8,128)(2,1)} %copy-done.12), channel_id=1, source_target_pairs={{0,4},{4,0},{8,12},{12,8},{16,20},{20,16},{24,28},{28,24},{1,5},{5... | collective-permute-start | bytes 1327112 | tf_op jit(solution)/shard_map/ppermute | solution.py:50
  197.3 7.2 %collective-permute-start.42 = (bf16[96,768]{1,0:T(8,128)(2,1)S(1)}, bf16[96,768]{1,0:T(8,128)(2,1)S(1)}, u32[]{:S(2)}, u32[]{:S(2)}) collective-permute-start(bf16[96,768]{1,0:T(8,128)(2,1)S(1)} %get-tuple-element.191), channel_id=1, source_target_pairs={{0,8},{4,12},{8,0},{12,4},{16,24},{20,28},{24,16},{28,20},{1,9},{5... | collective-permute-start | bytes 442376 | tf_op jit(solution)/shard_map/ppermute | solution.py:50
  198.7 10.0 %collective-permute-start.43 = (bf16[96,768]{1,0:T(8,128)(2,1)S(1)}, bf16[96,768]{1,0:T(8,128)(2,1)S(1)}, u32[]{:S(2)}, u32[]{:S(2)}) collective-permute-start(bf16[96,768]{1,0:T(8,128)(2,1)S(1)} %get-tuple-element.193), channel_id=1, source_target_pairs={{0,16},{4,20},{8,24},{12,28},{16,0},{20,4},{24,8},{28,12},{1,17},{... | collective-permute-start | bytes 442376 | tf_op jit(solution)/shard_map/ppermute | solution.py:50
  199.5 9.1 %collective-permute-start.44 = (bf16[96,768]{1,0:T(8,128)(2,1)S(1)}, bf16[96,768]{1,0:T(8,128)(2,1)S(1)}, u32[]{:S(2)}, u32[]{:S(2)}) collective-permute-start(bf16[96,768]{1,0:T(8,128)(2,1)S(1)} %get-tuple-element.192), channel_id=1, source_target_pairs={{0,24},{4,28},{8,16},{12,20},{16,8},{20,12},{24,0},{28,4},{1,25},{... | collective-permute-start | bytes 442376 | tf_op jit(solution)/shard_map/ppermute | solution.py:50
  202.1 8.2 %collective-permute-start.38 = (bf16[96,768]{1,0:T(8,128)(2,1)S(1)}, bf16[96,768]{1,0:T(8,128)(2,1)S(1)}, u32[]{:S(2)}, u32[]{:S(2)}) collective-permute-start(bf16[96,768]{1,0:T(8,128)(2,1)S(1)} %get-tuple-element.194), channel_id=1, source_target_pairs={{0,8},{4,12},{8,0},{12,4},{16,24},{20,28},{24,16},{28,20},{1,9},{5... | collective-permute-start | bytes 442376 | tf_op jit(solution)/shard_map/ppermute | solution.py:50
  203.5 9.8 %collective-permute-start.39 = (bf16[96,768]{1,0:T(8,128)(2,1)S(1)}, bf16[96,768]{1,0:T(8,128)(2,1)S(1)}, u32[]{:S(2)}, u32[]{:S(2)}) collective-permute-start(bf16[96,768]{1,0:T(8,128)(2,1)S(1)} %get-tuple-element.196), channel_id=1, source_target_pairs={{0,16},{4,20},{8,24},{12,28},{16,0},{20,4},{24,8},{28,12},{1,17},{... | collective-permute-start | bytes 442376 | tf_op jit(solution)/shard_map/ppermute | solution.py:50
  204.6 8.7 %collective-permute-start.40 = (bf16[96,768]{1,0:T(8,128)(2,1)S(1)}, bf16[96,768]{1,0:T(8,128)(2,1)S(1)}, u32[]{:S(2)}, u32[]{:S(2)}) collective-permute-start(bf16[96,768]{1,0:T(8,128)(2,1)S(1)} %get-tuple-element.195), channel_id=1, source_target_pairs={{0,24},{4,28},{8,16},{12,20},{16,8},{20,12},{24,0},{28,4},{1,25},{... | collective-permute-start | bytes 442376 | tf_op jit(solution)/shard_map/ppermute | solution.py:50
  208.6 5.8 %collective-permute-start.30 = (bf16[3,96,192]{2,1,0:T(8,128)(2,1)S(1)}, bf16[3,96,192]{2,1,0:T(8,128)(2,1)S(1)}, u32[]{:S(2)}, u32[]{:S(2)}) collective-permute-start(bf16[3,96,192]{2,1,0:T(8,128)(2,1)S(1)} %get-tuple-element.197), channel_id=1, source_target_pairs={{0,8},{4,12},{8,0},{12,4},{16,24},{20,28},{24,16},{28,20},{1,9},{5... | collective-permute-start | bytes 331784 | tf_op jit(solution)/shard_map/ppermute | solution.py:50
  208.6 5.8 %collective-permute-start.31 = (bf16[3,96,192]{2,1,0:T(8,128)(2,1)S(1)}, bf16[3,96,192]{2,1,0:T(8,128)(2,1)S(1)}, u32[]{:S(2)}, u32[]{:S(2)}) collective-permute-start(bf16[3,96,192]{2,1,0:T(8,128)(2,1)S(1)} %get-tuple-element.199), channel_id=1, source_target_pairs={{0,16},{4,20},{8,24},{12,28},{16,0},{20,4},{24,8},{28,12},{1,17},{... | collective-permute-start | bytes 331784 | tf_op jit(solution)/shard_map/ppermute | solution.py:50
  210.3 6.0 %collective-permute-start.32 = (bf16[3,96,192]{2,1,0:T(8,128)(2,1)S(1)}, bf16[3,96,192]{2,1,0:T(8,128)(2,1)S(1)}, u32[]{:S(2)}, u32[]{:S(2)}) collective-permute-start(bf16[3,96,192]{2,1,0:T(8,128)(2,1)S(1)} %get-tuple-element.198), channel_id=1, source_target_pairs={{0,24},{4,28},{8,16},{12,20},{16,8},{20,12},{24,0},{28,4},{1,25},{... | collective-permute-start | bytes 331784 | tf_op jit(solution)/shard_map/ppermute | solution.py:50
  (44 other events, 365.7 us)

commit v2 on v1

v2 whole, which is shorter than its diff:
```python
import functools
import math

import jax
import jax.numpy as jnp
from jax import lax
from jax.experimental import pallas as pl
from jax.experimental.pallas import tpu as pltpu
from jax.sharding import PartitionSpec as P

HD = 64
STEP = 10


norm_eps = 1e-06
beta_one = 0.9
beta_two = 0.999
adam_eps = 1e-08
gelu_coef = math.sqrt(2.0 / math.pi)
score_scale = float(HD) ** (-0.5)
low = jnp.bfloat16
wide = jnp.float32
VMEM_LIMIT = 24 * 1024 * 1024

NN = (((1,), (0,)), ((), ()))
NT = (((1,), (1,)), ((), ()))
TN = (((0,), (0,)), ((), ()))


def dot(left, right, dims=NN):
    return lax.dot_general(left, right, dims, preferred_element_type=wide)


def kernel_call(body, outs, args, scratch=()):
    smem = pl.BlockSpec(memory_space=pltpu.SMEM)
    vmem = pl.BlockSpec(memory_space=pltpu.VMEM)
    return pl.pallas_call(
        body,
        out_shape=[jax.ShapeDtypeStruct(s, d) for s, d in outs],
        in_specs=[smem] + [vmem] * (len(args) - 1),
        out_specs=[vmem] * len(outs),
        scratch_shapes=list(scratch),
        compiler_params=pltpu.CompilerParams(vmem_limit_bytes=VMEM_LIMIT),
        cost_estimate=pl.CostEstimate(flops=0, bytes_accessed=0, transcendentals=0),
    )(*args)


def flip(value, axis, mask):
    size = lax.axis_size(axis)
    return lax.ppermute(value, axis, [(i, i ^ mask) for i in range(size)])


def after(value, *others):
    return lax.optimization_barrier((value, *others))[0]


def chips_of(shard):
    return lax.optimization_barrier([shard] + [flip(shard, "fsdp", mask) for mask in (2, 4, 6)])


def cores_of(chips):
    others = [flip(part, "fsdp", 1) for part in chips]
    return [part for pair in zip(chips, others) for part in pair]


def summed_on_arrival(value, dim):
    peers = lax.axis_size("fsdp")
    before, behind = (value.shape[:dim], value.shape[dim + 1 :])
    blocks = jnp.moveaxis(value.reshape(*before, peers, -1, *behind), dim, 0)
    blocks = lax.all_to_all(blocks, "fsdp", 0, 0, tiled=True)
    return [jnp.sum(blocks.astype(wide), axis=0)]


def rank_gather(value):
    one, two = flip(value, "tensor", 1), flip(value, "tensor", 2)
    return [value, one, two, flip(two, "tensor", 1)]


def rank_sum(at, slots):
    three = flip(slots[3], "tensor", 1)
    one = flip(slots[1], "tensor", 1)
    (two,) = kernel_call(add_kernel, [(three.shape, low)], (at, slots[2], three))
    return [slots[0], one, flip(two, "tensor", 2)]


def to_ranks(slots):
    return [slots[0]] + [flip(slots[j], "tensor", j) for j in (1, 2, 3)]


def norm_parts(values):
    row_mean = jnp.mean(values, axis=-1, keepdims=True)
    centred = values - row_mean
    row_var = jnp.mean(centred * centred, axis=-1, keepdims=True)
    inverse = lax.rsqrt(row_var + norm_eps)
    return centred * inverse, inverse


def norm_backward(grad_out, normed, inverse, gain_vec):
    scaled = grad_out * gain_vec
    return inverse * (
        scaled
        - jnp.mean(scaled, axis=-1, keepdims=True)
        - normed * jnp.mean(scaled * normed, axis=-1, keepdims=True)
    )


def place_rows(at_ref, parts, target):
    if len(parts) == 1:
        target[...] = parts[0][...]
        return
    for slot, part in enumerate(parts):
        height = part.shape[1]
        start = pl.multiple_of((at_ref[0] ^ slot) * height, 32)
        target[:, pl.ds(start, height), :] = part[...]


def take_rows(at_ref, source, slot, height):
    start = pl.multiple_of((at_ref[0] ^ slot) * height, 32)
    return source[pl.ds(start, height), :]


def rank_rows(at_ref, slot, height):
    return pl.ds(pl.multiple_of((at_ref[1] ^ slot) * height, 16), height)


def pack_heads(value):
    half = value.shape[0] // 2
    side = value[:, 128:]
    return value[:, :128], jnp.concatenate([side[:half], side[half:]], axis=1)


def unpack_heads(packed):
    rows = packed.shape[0] * 2 // 3
    head, side = packed[:rows], packed[rows:]
    return jnp.concatenate([head, jnp.concatenate([side[:, :64], side[:, 64:]], axis=0)], axis=1)


def two_halves(value):
    upper = value.astype(low)
    return jnp.concatenate([upper.astype(wide), value - upper.astype(wide)], axis=0)


def small_pack_kernel(at_ref, vec_ref, bias_ref, out_ref):
    cols, ends = vec_ref.shape[1], bias_ref.shape[1]
    tile = jnp.concatenate(
        [vec_ref[...], jnp.zeros((8, 128 - cols - ends), wide), jnp.broadcast_to(bias_ref[...], (8, ends))], axis=1
    )
    for j in range(out_ref.shape[0]):
        out_ref[j] = tile


def small_unpack_kernel(cols, at_ref, small_ref, vec_ref, qv_ref, bias_ref):
    devices = small_ref.shape[0]
    ends = bias_ref.shape[1] * 4 // devices
    share = devices // 4
    vec_ref[...] = jnp.concatenate([small_ref[j, :, :cols] for j in range(devices)], axis=1)
    mine = [small_ref[at_ref[1] * share + j] for j in range(share)]
    qv_ref[...] = jnp.concatenate([tile[:, :cols] for tile in mine], axis=1)
    bias_ref[...] = jnp.concatenate([tile[0:1, 128 - ends :] for tile in mine], axis=1)


def round_kernel(turned, at_ref, in_ref, out_ref):
    value = in_ref[...]
    out_ref[...] = (value.T if turned else value).astype(low)


def add_kernel(at_ref, left_ref, right_ref, out_ref):
    out_ref[...] = (left_ref[...].astype(wide) + right_ref[...].astype(wide)).astype(out_ref.dtype)


def pair_kernel(at_ref, keep_ref, got_ref, stay_ref, go_ref):
    stay_ref[...] = keep_ref[0].astype(wide) + got_ref[0].astype(wide)
    go_ref[...] = (keep_ref[1].astype(wide) + got_ref[1].astype(wide)).astype(low)


def across_kernel(at_ref, stay_ref, got_ref, mine_ref, go_ref):
    mine_ref[...] = stay_ref[0] + got_ref[0].astype(wide)
    go_ref[...] = (stay_ref[1] + got_ref[1].astype(wide)).astype(low)


def quad_kernel(at_ref, keep_ref, got_ref, mine_ref, *go_refs):
    mine_ref[...] = keep_ref[0, 0].astype(wide) + got_ref[0, 0].astype(wide)
    for j, ref in enumerate(go_refs, 1):
        at = (j // 2, j % 2)
        ref[...] = (keep_ref[at].astype(wide) + got_ref[at].astype(wide)).astype(low)


def ranks_kernel(at_ref, left_ref, right_ref, *out_refs):
    total = left_ref[...] + right_ref[...].astype(wide)
    width = total.shape[1] // 4
    for j, ref in enumerate(out_refs):
        ref[...] = total[:, j * width : (j + 1) * width].astype(low)


def output_kernel(at_ref, own_ref, vec_ref, one_ref, two_ref, three_ref, out_ref):
    total = one_ref[...].astype(wide) + two_ref[...].astype(wide) + three_ref[...].astype(wide)
    out_ref[...] = (own_ref[0] + total + vec_ref[7:8, :]).astype(low)


def sums_pack_kernel(cols, ends, at_ref, one_ref, two_ref, qv_ref, gbo_ref, gub_ref, out_ref):
    devices = out_ref.shape[0]
    share = devices // 4
    middle = jnp.zeros((8, 128 - cols - ends), wide)
    for j in range(devices):
        span = slice(j * cols, (j + 1) * cols)
        mine = (at_ref[1] == j // share).astype(wide)
        k = j % share
        rows = [
            one_ref[0:2, span],
            two_ref[0:2, span],
            qv_ref[0:2, k * cols : (k + 1) * cols] * mine,
            gbo_ref[0:1, span],
            two_ref[2:3, span],
        ]
        bias = gub_ref[0:1, k * ends : (k + 1) * ends] * mine
        out_ref[j] = jnp.concatenate(
            [jnp.concatenate(rows, axis=0), middle, jnp.broadcast_to(bias, (8, ends))], axis=1
        )


def small_adam_kernel(at_ref, got_ref, *refs):
    (w_ref, m_ref, s_ref, b_ref, bm_ref, bs_ref), outs = refs[:6], refs[6:]
    total = jnp.sum(got_ref[...], axis=0)
    cols, ends = w_ref.shape[1], b_ref.shape[1]
    states = adamw(w_ref[...], total[:, :cols], m_ref[...], s_ref[...], 0.5, 0.0)
    states += adamw(b_ref[...], total[0:1, 128 - ends :], bm_ref[...], bs_ref[...], 0.7, 0.0)
    for ref, value in zip(outs, states):
        ref[...] = value


def adam_kernel(n_parts, turned, rate, decay, at_ref, *refs):
    parts, (w_ref, m_ref, s_ref) = refs[:n_parts], refs[n_parts : n_parts + 3]
    total = sum(ref[...].astype(wide) for ref in parts)
    if turned:
        total = total.T
    states = adamw(w_ref[...], total, m_ref[...], s_ref[...], rate, decay)
    for ref, value in zip(refs[n_parts + 3 :], states):
        ref[...] = value


def weights_kernel(at_ref, up_ref, down_ref, *refs):
    parts, out_ref = refs[:4], refs[4]
    height = up_ref.shape[0]
    out_ref[0] = up_ref[...].astype(low)
    out_ref[1] = down_ref[...].astype(low)
    out_ref[2] = jnp.concatenate([ref[...] for ref in parts], axis=1)


def attend_kernel(n_parts, at_ref, x_ref, vec_ref, qv_ref, *refs):
    parts = refs[:n_parts]
    a1_ref, qkv_ref, lse_ref, o_ref, w_ref, ot_ref = refs[n_parts:]
    if n_parts == 1:
        w_ref[...] = parts[0][...]
    else:
        height = w_ref.shape[1] // n_parts
        for slot, part in enumerate(parts):
            start = pl.multiple_of((at_ref[0] ^ slot) * height, 32)
            for j in range(3):
                w_ref[j, pl.ds(start, height), :] = part[j]
    normed, _ = norm_parts(x_ref[...].astype(wide))
    a1 = (normed * vec_ref[0:1, :] + vec_ref[1:2, :]).astype(low)
    a1_ref[...] = a1
    q = (dot(a1, w_ref[0]) + qv_ref[4:5, :]).astype(low)
    k = dot(a1, w_ref[1]).astype(low)
    v = (dot(a1, w_ref[2]) + qv_ref[5:6, :]).astype(low)
    qkv_ref[0] = q
    qkv_ref[1] = k
    qkv_ref[2] = v
    vt = v.T
    for head in range(q.shape[1] // HD):
        cols = slice(head * HD, (head + 1) * HD)
        scores = dot(k[:, cols], q[:, cols], NT) * score_scale
        top = jnp.max(scores, axis=0, keepdims=True)
        expos = jnp.exp(scores - top)
        summed = jnp.sum(expos, axis=0, keepdims=True)
        lse_ref[head : head + 1, :] = top + jnp.log(summed)
        ot_ref[cols, :] = dot(vt[cols, :], expos.astype(low)) / summed
    o = ot_ref[...].T.astype(low)
    head_part, side_part = pack_heads(o)
    rows = o.shape[0]
    o_ref[0:rows, :] = head_part
    o_ref[rows:, :] = side_part


def mlp_kernel(n_parts, at_ref, x_ref, c_ref, vec_ref, ub_ref, *refs):
    heads, parts = refs[:4], refs[4 : 4 + n_parts]
    dn2_refs = refs[4 + n_parts : 8 + n_parts]
    (a2_ref, g_ref, du_ref, own_ref, stat_ref, sums_ref, gub_ref, oo_ref,
     w_ref, h_ref, n_ref, s_ref, o_ref) = refs[8 + n_parts :]
    part_rows = dn2_refs[0].shape[0]
    place_rows(at_ref, parts, w_ref)
    o_ref[...] = jnp.concatenate([unpack_heads(ref[...]) for ref in heads], axis=1)
    hidden_state = x_ref[...].astype(wide) + dot(o_ref[...], w_ref[2], NT) + vec_ref[6:7, :]
    h_ref[...] = hidden_state
    normed, inverse = norm_parts(hidden_state)
    n_ref[...] = normed
    s_ref[...] = jnp.broadcast_to(inverse, s_ref.shape)
    a2 = (normed * vec_ref[2:3, :] + vec_ref[3:4, :]).astype(low)
    a2_ref[...] = a2
    pre = dot(a2, w_ref[0]) + ub_ref[...]
    square = pre * pre
    tangent = jnp.tanh(gelu_coef * pre * (1.0 + 0.044715 * square))
    half = 0.5 * (1.0 + tangent)
    g_ref[...] = (pre * half).astype(low)
    slope = half + 0.5 * pre * (1.0 - tangent * tangent) * gelu_coef * (1.0 + 3.0 * 0.044715 * square)
    du = (dot(c_ref[...], w_ref[1]) * slope).astype(low)
    du_ref[...] = du
    gub_ref[...] = jnp.sum(du.astype(wide), axis=0, keepdims=True)
    own = rank_rows(at_ref, 0, part_rows)
    own_ref[0] = h_ref[own, :]
    own_ref[1] = n_ref[own, :]
    stat_ref[...] = s_ref[own, :]
    oo_ref[...] = o_ref[own, :]
    dn2 = dot(du, w_ref[0], NT)
    h_ref[...] = dn2
    sums_ref[0:1, :] = jnp.sum(dn2 * normed, axis=0, keepdims=True)
    sums_ref[1:2, :] = jnp.sum(dn2, axis=0, keepdims=True)
    for j, ref in enumerate(dn2_refs):
        ref[...] = h_ref[rank_rows(at_ref, j, part_rows), :].astype(low)
    sums_ref[2:3, :] = jnp.sum(c_ref[own, :].astype(wide), axis=0, keepdims=True)


def mlp_out_kernel(at_ref, g_ref, w_ref, *refs):
    slots, out_ref = refs[:4], refs[4]
    out_ref[...] = dot(g_ref[...], w_ref[1], NT)
    for j, ref in enumerate(slots):
        ref[...] = out_ref[rank_rows(at_ref, j, ref.shape[0]), :].astype(low)


def mix_kernel(at_ref, own_ref, stat_ref, c_ref, vec_ref, w_ref, *refs):
    chunks = refs[:3]
    dh_ref, dz_ref, gbo_ref = refs[3:6]
    do_refs = refs[6:]
    part_rows = stat_ref.shape[0]
    grad = sum(ref[...].astype(wide) for ref in chunks)
    cotan = c_ref[rank_rows(at_ref, 0, part_rows), :].astype(wide)
    dh = cotan + norm_backward(grad, own_ref[1], stat_ref[:, 0:1], vec_ref[2:3, :])
    dh_ref[...] = dh
    gbo_ref[...] = jnp.sum(dh, axis=0, keepdims=True)
    dz = dh.astype(low)
    dz_ref[...] = dz
    do = dot(dz, w_ref[2]).astype(low)
    heads_width = do.shape[1] // 4
    for j, ref in enumerate(do_refs):
        head_part, side_part = pack_heads(do[:, j * heads_width : (j + 1) * heads_width])
        ref[0:part_rows, :] = head_part
        ref[part_rows:, :] = side_part


def attend_back_kernel(fast, at_ref, x_ref, a1_ref, qkv_ref, lse_ref, w_ref, *refs):
    chunks, dn1_refs = refs[:4], refs[4:8]
    if fast:
        keep_ref, send_ref, sums_ref, qvsum_ref = refs[8:12]
    else:
        whole_ref, sums_ref, qvsum_ref = refs[8:11]
    do_ref, dqt_ref, d_ref, g_ref, dn1_ref = refs[-5:]
    rows, width = x_ref.shape
    part_rows = rows // 4
    for j in range(4):
        do_ref[rank_rows(at_ref, j, part_rows), :] = unpack_heads(chunks[j][...])
    q, k, v, do = qkv_ref[0], qkv_ref[1], qkv_ref[2], do_ref[...]
    kt = k.T
    for head in range(q.shape[1] // HD):
        cols = slice(head * HD, (head + 1) * HD)
        scores = dot(k[:, cols], q[:, cols], NT) * score_scale
        probs = jnp.exp(scores - lse_ref[head : head + 1, :])
        grad_probs = dot(v[:, cols], do[:, cols], NT)
        d_ref[2, :, cols] = dot(probs.astype(low), do[:, cols]).astype(low)
        both = probs * grad_probs
        grad_scores = (both - probs * jnp.sum(both, axis=0, keepdims=True)).astype(low)
        d_ref[1, :, cols] = (dot(grad_scores, q[:, cols]) * score_scale).astype(low)
        dqt_ref[cols, :] = dot(kt[cols, :], grad_scores) * score_scale
    d_ref[0] = dqt_ref[...].T.astype(low)
    qvsum_ref[0:1, :] = jnp.sum(d_ref[0].astype(wide), axis=0, keepdims=True)
    qvsum_ref[1:2, :] = jnp.sum(d_ref[2].astype(wide), axis=0, keepdims=True)
    dn1 = dot(d_ref[0], w_ref[0], NT) + dot(d_ref[1], w_ref[1], NT) + dot(d_ref[2], w_ref[2], NT)
    dn1_ref[...] = dn1
    for j, ref in enumerate(dn1_refs):
        ref[...] = dn1_ref[rank_rows(at_ref, j, part_rows), :].astype(low)
    normed, _ = norm_parts(x_ref[...].astype(wide))
    sums_ref[0:1, :] = jnp.sum(dn1 * normed, axis=0, keepdims=True)
    sums_ref[1:2, :] = jnp.sum(dn1, axis=0, keepdims=True)
    a1t = a1_ref[...].T
    for which in range(3):
        grad = dot(a1t, d_ref[which])
        if fast:
            g_ref[...] = grad.astype(low)
            height = width // 8
            for slot in range(4):
                mask = (0, 4, 2, 6)[slot]
                keep_ref[slot // 2, slot % 2, which] = take_rows(at_ref, g_ref, mask, height)
                send_ref[slot // 2, slot % 2, which] = take_rows(at_ref, g_ref, mask ^ 1, height)
        else:
            whole_ref[which] = grad.astype(low)


def weight_grad_kernel(fast, masks, at_ref, left_ref, right_ref, *refs):
    grad = dot(left_ref[...].T, right_ref[...]).astype(low)
    if not fast:
        refs[0][...] = grad
        return
    keep_ref, send_ref, g_ref = refs
    g_ref[...] = grad
    height = grad.shape[0] // 8
    for slot, mask in enumerate(masks):
        keep_ref[slot // 2, slot % 2] = take_rows(at_ref, g_ref, mask, height)
        send_ref[slot // 2, slot % 2] = take_rows(at_ref, g_ref, mask ^ 1, height)


def input_kernel(at_ref, x_ref, dh_ref, vec_ref, *refs):
    chunks, out_ref = refs[:3], refs[3]
    part_rows = dh_ref.shape[0]
    normed, inverse = norm_parts(x_ref[rank_rows(at_ref, 0, part_rows), :].astype(wide))
    grad = sum(ref[...].astype(wide) for ref in chunks)
    out_ref[...] = dh_ref[...] + norm_backward(grad, normed, inverse, vec_ref[0:1, :])


def adamw(weight, gradient, first, second, rate, decay):
    first_new = beta_one * first + (1.0 - beta_one) * gradient
    second_new = beta_two * second + (1.0 - beta_two) * gradient * gradient
    first_hat = first_new / (1.0 - beta_one**STEP)
    second_hat = second_new / (1.0 - beta_two**STEP)
    weight_new = weight - rate * (first_hat / (jnp.sqrt(second_hat) + adam_eps) + decay * weight)
    return (weight_new, first_new, second_new)


def body(
    images,
    cotangent,
    qkv_weight,
    out_weight,
    up_weight,
    down_weight,
    vectors,
    up_bias,
    qkv_first,
    qkv_second,
    out_first,
    out_second,
    up_first,
    up_second,
    down_first,
    down_second,
    vector_first,
    vector_second,
    bias_first,
    bias_second,
):
    fsdp_size = lax.axis_size("fsdp")
    tensor_size = lax.axis_size("tensor")
    devices = fsdp_size * tensor_size
    fast = fsdp_size == 8
    at = jnp.stack([lax.axis_index("fsdp"), lax.axis_index("tensor")]).astype(jnp.int32)
    _, rows, width = images.shape
    hidden = up_weight.shape[1]
    heads_width = width // tensor_size
    part_rows = rows // tensor_size
    height = width // fsdp_size
    x = images.reshape(rows, width)
    c = cotangent.reshape(rows, width)
    cols, ends = vectors.shape[1], up_bias.shape[0]
    both_axes = ("fsdp", "tensor")

    (tiles,) = kernel_call(
        small_pack_kernel, [((devices, 8, 128), wide)], (at, vectors, up_bias[None])
    )
    small = lax.all_to_all(tiles, both_axes, 0, 0, tiled=True)
    vec, qv, up_local = kernel_call(
        functools.partial(small_unpack_kernel, cols),
        [((8, width), wide), ((8, heads_width), wide), ((1, hidden), wide)],
        (at, small),
    )

    (qkv_low,) = kernel_call(
        functools.partial(round_kernel, False), [(qkv_weight.shape, low)], (at, after(qkv_weight, tiles))
    )
    (out_t,) = kernel_call(
        functools.partial(round_kernel, True), [((height, heads_width), low)], (at, after(out_weight, qkv_low))
    )
    if fast:
        chips = chips_of(qkv_low)
        qkv_parts = cores_of(chips)
    else:
        chips = qkv_parts = [lax.all_gather(qkv_low, "fsdp", axis=1, tiled=True)]
    (shard,) = kernel_call(
        weights_kernel,
        [((3, height, width), low)],
        (at, after(up_weight, chips[-1]), down_weight.T, *to_ranks([out_t] * 4)),
    )
    if fast:
        chips = chips_of(shard)

    n = len(qkv_parts)
    a1, qkv, lse, o_mine, qkv_full = kernel_call(
        functools.partial(attend_kernel, n),
        [
            ((rows, width), low),
            ((3, rows, heads_width), low),
            ((8, rows), wide),
            ((rows * 3 // 2, 128), low),
            ((3, width, heads_width), low),
        ],
        (at, x, vec, qv, *qkv_parts),
        [pltpu.VMEM((heads_width, rows), wide)],
    )
    o_parts = rank_gather(o_mine)
    if fast:
        chips = lax.optimization_barrier((*chips, o_parts[1]))[:4]
        rest_parts = cores_of(chips)
    else:
        rest_parts = [lax.all_gather(shard, "fsdp", axis=1, tiled=True)]

    block = ((part_rows, width), low)
    *dn2, a2, g, du, own, stat, sums_two, gub, o_own, w_full = kernel_call(
        functools.partial(mlp_kernel, n),
        [
            *[block] * 4,
            ((rows, width), low),
            ((rows, hidden), low),
            ((rows, hidden), low),
            ((2, part_rows, width), wide),
            ((part_rows, 128), wide),
            ((8, width), wide),
            ((1, hidden), wide),
            block,
            ((3, width, hidden), low),
        ],
        (at, x, c, vec, up_local, *o_parts, *rest_parts),
        [
            pltpu.VMEM((rows, width), wide),
            pltpu.VMEM((rows, width), wide),
            pltpu.VMEM((rows, 128), wide),
            pltpu.VMEM((rows, width), low),
        ],
    )
    dn2_got = rank_sum(at, dn2)

    def weight_grad(left, right, masks):
        shape = (left.shape[1], right.shape[1])
        cut = (2, 2, height, shape[1])
        return kernel_call(
            functools.partial(weight_grad_kernel, fast, masks),
            [(cut, low), (cut, low)] if fast else [(shape, low)],
            (at, left, right),
            [pltpu.VMEM(shape, low)] if fast else [],
        )

    def over_cores(grads):
        keep, send = grads
        half = keep.shape[1:]
        return kernel_call(pair_kernel, [(half, wide), (half, low)], (at, keep, flip(send, "fsdp", 1)))

    def over_first(stay, go, mask):
        block = stay.shape[1:]
        return kernel_call(across_kernel, [(block, wide), (block, low)], (at, stay, flip(go, "fsdp", mask)))

    along_x, along_y = (0, 4, 2, 6), (0, 2, 4, 6)
    up_sums = weight_grad(a2, du, along_x)
    down_sums = weight_grad(c, g, along_y)
    if fast:
        up_sums, down_sums = over_cores(up_sums), over_cores(down_sums)
    mlp = kernel_call(
        mlp_out_kernel,
        [block] * 4,
        (at, g, w_full),
        [pltpu.VMEM((rows, width), wide)],
    )
    held = lax.optimization_barrier((dn2_got, up_sums, down_sums, mlp))
    dn2_got, up_sums, down_sums, mlp = held
    dh, dz, gbo, *do = kernel_call(
        mix_kernel,
        [
            ((part_rows, width), wide),
            block,
            ((1, width), wide),
            *[((part_rows * 3 // 2, 128), low)] * 4,
        ],
        (at, own, stat, c, vec, w_full, *dn2_got),
    )
    do_got = to_ranks(do)
    out_grads = weight_grad(dz, o_own, along_x)
    if fast:
        up_sums, down_sums = over_first(*up_sums, 2), over_first(*down_sums, 4)
    held = lax.optimization_barrier((do_got, mlp, out_grads, up_sums, down_sums))
    do_got, mlp, out_grads, up_sums, down_sums = held
    mlp_got = rank_sum(at, mlp)
    (output,) = kernel_call(output_kernel, [block], (at, own, vec, *mlp_got))
    if fast:
        up_sums = [up_sums[0], flip(up_sums[1], "fsdp", 4)]
        down_sums = [down_sums[0], flip(down_sums[1], "fsdp", 2)]
        out_sums = over_first(*over_cores(out_grads), 2)
        out_sums = [out_sums[0], flip(out_sums[1], "fsdp", 4)]
    else:
        up_sums = summed_on_arrival(up_sums[0], 0)
        down_sums = summed_on_arrival(down_sums[0], 0)
        out_sums = summed_on_arrival(out_grads[0], 0)
        out_sums = [out_sums[0], jnp.zeros(out_sums[0].shape, low)]
    out_sums = to_ranks(
        kernel_call(ranks_kernel, [((height, heads_width), low)] * 4, (at, *out_sums))
    )

    cut = (2, 2, 3, height, heads_width)
    outs = [block] * 4
    outs += [(cut, low), (cut, low)] if fast else [((3, width, heads_width), low)]
    outs += [((8, width), wide), ((8, heads_width), wide)]
    back = kernel_call(
        functools.partial(attend_back_kernel, fast),
        outs,
        (at, x, a1, qkv, lse, qkv_full, *do_got),
        [
            pltpu.VMEM((rows, heads_width), low),
            pltpu.VMEM((heads_width, rows), wide),
            pltpu.VMEM((3, rows, heads_width), low),
            pltpu.VMEM((width, heads_width), low),
            pltpu.VMEM((rows, width), wide),
        ],
    )
    dn1, sums_one, qv_sums = back[:4], back[-2], back[-1]
    dn1_got = rank_sum(at, dn1)
    if fast:
        got = flip(back[5], "fsdp", 1)
        blk = (3, height, heads_width)
        mine, *go = kernel_call(quad_kernel, [(blk, wide)] + [(blk, low)] * 3, (at, back[4], got))
        qkv_sums = [mine] + [flip(part, "fsdp", mask) for part, mask in zip(go, (4, 2, 6))]
    else:
        qkv_sums = summed_on_arrival(back[4], 1)

    (tiles,) = kernel_call(
        functools.partial(sums_pack_kernel, cols, ends),
        [((devices, 8, 128), wide)],
        (at, sums_one, sums_two, qv_sums, gbo, gub),
    )
    tiles = lax.all_to_all(tiles, both_axes, 0, 0, tiled=True)
    *vec_state, bias_new, bias_m, bias_s = kernel_call(
        small_adam_kernel,
        [(vectors.shape, wide)] * 3 + [((1, ends), wide)] * 3,
        (at, tiles, vectors, vector_first, vector_second, up_bias[None], bias_first[None], bias_second[None]),
    )

    def update(sums, weight, first, second, rate, decay, turned=False):
        return kernel_call(
            functools.partial(adam_kernel, len(sums), turned, rate, decay),
            [(weight.shape, wide)] * 3,
            (at, *sums, weight, first, second),
        )

    up_state = update(up_sums, up_weight, up_first, up_second, 0.08, 0.1)
    down_state = update(down_sums, down_weight.T, down_first.T, down_second.T, 0.045, 0.1)
    down_state = [value.T for value in down_state]
    out_state = update(out_sums, out_weight, out_first, out_second, 0.3, 0.1, True)
    qkv_state = update(qkv_sums, qkv_weight, qkv_first, qkv_second, 0.08, 0.1)

    (input_own,) = kernel_call(
        input_kernel,
        [((part_rows, width), wide)],
        (at, x, dh, vec, *dn1_got),
    )
    return (
        output[None],
        input_own[None],
        *qkv_state,
        *out_state,
        *up_state,
        *down_state,
        *vec_state,
        bias_new[0],
        bias_m[0],
        bias_s[0],
    )


def solution(mesh):
    weights = (P(None, "fsdp", "tensor"), P("tensor", "fsdp"), P("fsdp", "tensor"), P("tensor", "fsdp"))
    vector, bias = P(None, ("fsdp", "tensor")), P(("fsdp", "tensor"))
    twice = [spec for spec in (*weights, vector, bias) for _ in range(2)]
    thrice = [spec for spec in (*weights, vector, bias) for _ in range(3)]
    return jax.shard_map(
        body,
        mesh=mesh,
        in_specs=(P("fsdp", None, None), P("fsdp", None, None), *weights, vector, bias, *twice),
        out_specs=(P("fsdp", "tensor", None), P("fsdp", "tensor", None), *thrice),
        check_vma=False,
    )
```

time: 220 us -> 179 us (0.81)
  blocking collectives: 54.8 us -> 0 us
  Pallas kernels: 30.8 us -> 51.9 us
  other arithmetic: 15.5 us -> 0.08 us
  local copies, waits for them, and re-layouts: 23.9 us -> 28 us
  starting transfers between devices: 53.6 us -> 56.4 us
  waiting for transfers between devices: 37.3 us -> 39.9 us
    all_gather x2 -> x0, blocking collectives: 54.8 us -> none  [the longest x1 33.6 us: body(): dz_all = lax.all_gather(dz, 'tensor', axis=0, tiled=True)]
    pallas_call x9 -> x32, Pallas kernels: 30.8 us -> 51.9 us  [kernel_call(): pl.pallas_call(body, out_shape=[jax.ShapeDtypeStruct(s, d) for s, d in ou...]
    unnamed x97 -> x110, local copies, waits for them, and re-layouts: 16 us -> 28 us
    ppermute x45 -> x48, waiting for transfers between devices: 30.1 us -> 39.9 us  [flip(): return lax.ppermute(value, axis, [(i, i ^ mask) for i in range(size)])]
    all_to_all x2, waiting for transfers between devices: 7.22 us -> 0.01 us  [the longest x1 0.01 us: body(): small = lax.all_to_all(tiles, both_axes, 0, 0, tiled=True)]
    sub x6 -> x0, other arithmetic: 6.29 us -> none  [adamw(): weight - rate * (first_hat / (jnp.sqrt(second_hat) + adam_eps) + decay *...]
    add x4 -> x0, other arithmetic: 3.59 us -> none  [fsdp_sum(): total = keep.astype(wide) + got.astype(wide)]
    reshape x8 -> x0, local copies, waits for them, and re-layouts: 2.31 us -> none  [the longest x2 1.11 us: body(): small[:, :8 * cols].reshape(devices, 8, cols).transpose(1, 0, 2)]
  transfers between devices with their start and end apart: 47 -> 50, of which waited for: 13 -> 14; matrix products, arithmetic and copies ran while one was open for 13% -> 0% of each run, Pallas kernels for 10% -> 23%
where the time goes in v2:
time: 179 us; the launch traced here: 178 us
  starting transfers between devices  56.4 us (32%)
  Pallas kernels  51.9 us (29%)
  waiting for transfers between devices  39.9 us (22%)
  local copies, waits for them, and re-layouts  28 us (16%)
    pallas_call x32, Pallas kernels, kernel_call(): pl.pallas_call(body, out_shape=[jax.ShapeDtypeStruct(s, d) for s, d in ou...  51.9 us
    ppermute x48, starting transfers between devices, flip(): return lax.ppermute(value, axis, [(i, i ^ mask) for i in range(size)])  46.8 us
    ppermute x48, waiting for transfers between devices, flip(): return lax.ppermute(value, axis, [(i, i ^ mask) for i in range(size)])  39.9 us
    unnamed x110, local copies, waits for them, and re-layouts  28 us
    all_to_all x1, starting transfers between devices, body(): small = lax.all_to_all(tiles, both_axes, 0, 0, tiled=True)  5.99 us
    all_to_all x1, starting transfers between devices, body(): tiles = lax.all_to_all(tiles, both_axes, 0, 0, tiled=True)  3.64 us
  transfers between devices with their start and end apart: 50, of which 14 were waited for; matrix products, arithmetic and copies ran while one was open for 0% of the time, Pallas kernels for 23%

profile of v2, /device:TPU:0, one launch (start us, length us, event | category | flops | bytes accessed | tf_op | source)
XLA Modules:
  0.0 177.5 jit_solution(7058482006301931693)
XLA Ops:
  2.2 1.3 shard_map.347
  5.0 4.0 %collective-permute-start.2 = (bf16[3,96,192]{2,1,0:T(8,128)(2,1)S(1)}, bf16[3,96,192]{2,1,0:T(8,128)(2,1)S(1)}, u32[]{:S(2)}, u32[]{:S(2)}) collective-permute-start(bf16[3,96,192]{2,1,0:T(8,128)(2,1)S(1)} %shard_map.349.refs_0_), channel_id=1, source_target_pairs={{0,24},{4,28},{8,16},{12,20},{16,8},{20,12},{24,0},{28,4},{1,25},{... | collective-permute-start | bytes 331784 | tf_op jit(solution)/shard_map/ppermute | solution.py:50
  11.1 4.1 %collective-permute-start.12 = (bf16[96,192]{1,0:T(8,128)(2,1)S(1)}, bf16[96,192]{1,0:T(8,128)(2,1)S(1)}, u32[]{:S(2)}, u32[]{:S(2)}) collective-permute-start(bf16[96,192]{1,0:T(8,128)(2,1)S(1)} %shard_map.351.refs_0_), channel_id=1, source_target_pairs={{0,3},{1,2},{2,1},{3,0},{4,7},{5,6},{6,5},{7,4},{8,11},{9,10},{10,... | collective-permute-start | bytes 110600 | tf_op jit(solution)/shard_map/ppermute | solution.py:50
  15.9 6.0 %all-to-all-start = ((f32[32,8,128]{2,1,0:T(8,128)}), f32[32,8,128]{2,1,0:T(8,128)S(1)}, u32[]{:S(2)}, u32[]{:S(2)}) async-start(f32[32,8,128]{2,1,0:T(8,128)} %shard_map.347), calls=%async_computation | async-start | bytes 262144 | tf_op jit(solution)/shard_map/all_to_all | solution.py:467
  25.0 2.7 %collective-permute-start.15 = (bf16[3,96,768]{2,1,0:T(8,128)(2,1)S(1)}, bf16[3,96,768]{2,1,0:T(8,128)(2,1)S(1)}, u32[]{:S(2)}, u32[]{:S(2)}) collective-permute-start(bf16[3,96,768]{2,1,0:T(8,128)(2,1)S(1)} %shard_map.352.refs_4_), channel_id=1, source_target_pairs={{0,24},{4,28},{8,16},{12,20},{16,8},{20,12},{24,0},{28,4},{1,25},{... | collective-permute-start | bytes 1327112 | tf_op jit(solution)/shard_map/ppermute | solution.py:50
  34.6 4.4 %shard_map.350 = (bf16[576,768]{1,0:T(8,128)(2,1)S(1)}, bf16[3,576,192]{2,1,0:T(8,128)(2,1)S(1)}, f32[8,576]{1,0:T(8,128)S(1)}, bf16[864,128]{1,0:T(8,128)(2,1)S(1)}, bf16[3,768,192]{2,1,0:T(8,128)(2,1)S(1)}) custom-call(s32[2]{0:T(128)S(1)} %pad_add_fusion.at_ref, bf16[576,768]{1,0:T(8,128)(2,1)S(1)} %bitcast.18, f32[8,768]{1,0:T(8,128)S(1)} %get-tuple-element.144.vec_ref, ...), custom_call_target="tpu_custom_call" | custom-call | tf_op jit(solution)/shard_map/pallas_call | solution.py:37
  39.0 1.9 %collective-permute-start.7 = (bf16[864,128]{1,0:T(8,128)(2,1)S(1)}, bf16[864,128]{1,0:T(8,128)(2,1)S(1)}, u32[]{:S(2)}, u32[]{:S(2)}) collective-permute-start(bf16[864,128]{1,0:T(8,128)(2,1)S(1)} %get-tuple-element.152.refs_0_), channel_id=1, source_target_pairs={{0,1},{1,0},{2,3},{3,2},{4,5},{5,4},{6,7},{7,6},{8,9},{9,8},{10,11... | collective-permute-start | bytes 663560 | tf_op jit(solution)/shard_map/ppermute | solution.py:50
  40.9 2.4 %collective-permute-start.8 = (bf16[864,128]{1,0:T(8,128)(2,1)S(1)}, bf16[864,128]{1,0:T(8,128)(2,1)S(1)}, u32[]{:S(2)}, u32[]{:S(2)}) collective-permute-start(bf16[864,128]{1,0:T(8,128)(2,1)S(1)} %get-tuple-element.152.refs_0_), channel_id=1, source_target_pairs={{0,2},{1,3},{2,0},{3,1},{4,6},{5,7},{6,4},{7,5},{8,10},{9,11},{10,... | collective-permute-start | bytes 663560 | tf_op jit(solution)/shard_map/ppermute | solution.py:50
  43.3 5.0 %collective-permute-done.14.refs_8_ = bf16[3,96,768]{2,1,0:T(8,128)(2,1)} collective-permute-done((bf16[3,96,768]{2,1,0:T(8,128)(2,1)S(1)}, bf16[3,96,768]{2,1,0:T(8,128)(2,1)}, u32[]{:S(2)}, u32[]{:S(2)}) %collective-permute-start.14) | collective-permute-done | bytes 442400 | tf_op jit(solution)/shard_map/ppermute | solution.py:50
  48.2 3.1 %collective-permute-done.7.refs_1_ = bf16[864,128]{1,0:T(8,128)(2,1)S(1)} collective-permute-done((bf16[864,128]{1,0:T(8,128)(2,1)S(1)}, bf16[864,128]{1,0:T(8,128)(2,1)S(1)}, u32[]{:S(2)}, u32[]{:S(2)}) %collective-permute-start.7) | collective-permute-done | bytes 221216 | tf_op jit(solution)/shard_map/ppermute | solution.py:50
  54.3 6.2 %collective-permute-done.9.refs_3_ = bf16[864,128]{1,0:T(8,128)(2,1)S(1)} collective-permute-done((bf16[864,128]{1,0:T(8,128)(2,1)S(1)}, bf16[864,128]{1,0:T(8,128)(2,1)S(1)}, u32[]{:S(2)}, u32[]{:S(2)}) %collective-permute-start.9) | collective-permute-done | bytes 221216 | tf_op jit(solution)/shard_map/ppermute | solution.py:50
  61.5 5.8 %shard_map.353 = (bf16[144,768]{1,0:T(8,128)(2,1)S(1)}, bf16[144,768]{1,0:T(8,128)(2,1)S(1)}, bf16[144,768]{1,0:T(8,128)(2,1)S(1)}, bf16[144,768]{1,0:T(8,128)(2...) custom-call(s32[2]{0:T(128)S(1)} %pad_add_fusion.at_ref, ...), custom_call_target="tpu_custom_call" | custom-call | tf_op jit(solution)/shard_map/pallas_call | solution.py:37
  67.3 1.7 shard_map.357
  69.1 1.7 shard_map.355
  72.1 1.4 collective-permute-start.20
  73.4 6.3 %collective-permute-done.21.right_ref = bf16[144,768]{1,0:T(8,128)(2,1)S(1)} collective-permute-done((bf16[144,768]{1,0:T(8,128)(2,1)S(1)}, bf16[144,768]{1,0:T(8,128)(2,1)S(1)}, u32[]{:S(2)}, u32[]{:S(2)}) %collective-permute-start.21) | collective-permute-done | bytes 221216 | tf_op jit(solution)/shard_map/ppermute | solution.py:50
  80.3 1.6 collective-permute-start.22
  81.9 2.2 %shard_map.359 = (bf16[144,768]{1,0:T(8,128)(2,1)S(1)}, bf16[144,768]{1,0:T(8,128)(2,1)}, bf16[144,768]{1,0:T(8,128)(2,1)S(1)}, bf16[144,768]{1,0:T(8,128)(2,1)S(1)}) custom-call(s32[2]{0:T(128)S(1)} %pad_add_fusion.at_ref, bf16[576,768]{1,0:T(8,128)(2,1)S(1)} %get-tuple-element.176.right_ref.g_ref, bf16[3,768,768]{2,1,0:T(8,128)(2,1)S(1)} %get-tuple-element.165.w_ref), custom_call_target="tpu_custom_call" | custom-call | tf_op jit(solution)/shard_map/pallas_call | solution.py:37
  85.9 5.8 %collective-permute-done.22.refs_2_ = bf16[144,768]{1,0:T(8,128)(2,1)S(1)} collective-permute-done((bf16[144,768]{1,0:T(8,128)(2,1)S(1)}, bf16[144,768]{1,0:T(8,128)(2,1)S(1)}, u32[]{:S(2)}, u32[]{:S(2)}) %collective-permute-start.22) | collective-permute-done | bytes 221216 | tf_op jit(solution)/shard_map/ppermute | solution.py:50
  91.8 1.7 collective-permute-start.28
  93.5 1.5 collective-permute-start.29
  97.0 2.9 %collective-permute-start.26 = (bf16[216,128]{1,0:T(8,128)(2,1)S(1)}, bf16[216,128]{1,0:T(8,128)(2,1)S(1)}, u32[]{:S(2)}, u32[]{:S(2)}) collective-permute-start(bf16[216,128]{1,0:T(8,128)(2,1)S(1)} %get-tuple-element.190), channel_id=1, source_target_pairs={{0,2},{1,3},{2,0},{3,1},{4,6},{5,7},{6,4},{7,5},{8,10},{9,11},{10,... | collective-permute-start | bytes 165896 | tf_op jit(solution)/shard_map/ppermute | solution.py:50
  99.9 1.5 collective-permute-start.27
  103.9 2.0 %collective-permute-done.27.refs_3_ = bf16[216,128]{1,0:T(8,128)(2,1)S(1)} collective-permute-done((bf16[216,128]{1,0:T(8,128)(2,1)S(1)}, bf16[216,128]{1,0:T(8,128)(2,1)S(1)}, u32[]{:S(2)}, u32[]{:S(2)}) %collective-permute-start.27) | collective-permute-done | bytes 55328 | tf_op jit(solution)/shard_map/ppermute | solution.py:50
  105.9 6.1 %shard_map.366 = (bf16[144,768]{1,0:T(8,128)(2,1)S(1)}, bf16[144,768]{1,0:T(8,128)(2,1)}, bf16[144,768]{1,0:T(8,128)(2,1)S(1)}, bf16[144,768]{1,0:T(8,128)(2,1)S...) custom-call(s32[2]{0:T(128)S(1)} %pad_add_fusion.at_ref, ...), custom_call_target="tpu_custom_call" | custom-call | tf_op jit(solution)/shard_map/pallas_call | solution.py:37
  115.3 2.0 %collective-permute-start.34 = (bf16[144,768]{1,0:T(8,128)(2,1)S(1)}, bf16[144,768]{1,0:T(8,128)(2,1)S(1)}, u32[]{:S(2)}, u32[]{:S(2)}) collective-permute-start(bf16[144,768]{1,0:T(8,128)(2,1)S(1)} %get-tuple-element.224), channel_id=1, source_target_pairs={{0,1},{1,0},{2,3},{3,2},{4,5},{5,4},{6,7},{7,6},{8,9},{9,8},{10,11... | collective-permute-start | bytes 663560 | tf_op jit(solution)/shard_map/ppermute | solution.py:50
  117.3 2.9 %collective-permute-done.46.refs_1_ = bf16[96,768]{1,0:T(8,128)(2,1)S(1)} collective-permute-done((bf16[96,768]{1,0:T(8,128)(2,1)S(1)}, bf16[96,768]{1,0:T(8,128)(2,1)S(1)}, u32[]{:S(2)}, u32[]{:S(2)}) %collective-permute-start.46) | collective-permute-done | bytes 147488 | tf_op jit(solution)/shard_map/ppermute | solution.py:50
  120.3 1.5 collective-permute-start.47
  121.7 1.4 collective-permute-done.31.right_ref
  125.1 1.3 shard_map.364
  126.4 1.3 shard_map.372
  129.2 1.3 shard_map.367
  131.3 2.0 %collective-permute-start.35 = (bf16[144,768]{1,0:T(8,128)(2,1)}, bf16[144,768]{1,0:T(8,128)(2,1)}, u32[]{:S(2)}, u32[]{:S(2)}) collective-permute-start(bf16[144,768]{1,0:T(8,128)(2,1)} %shard_map.367), channel_id=1, source_target_pairs={{0,2},{1,3},{2,0},{3,1},{4,6},{5,7},{6,4},{7,5},{8,10},{9,11},{10,... | collective-permute-start | bytes 663560 | tf_op jit(solution)/shard_map/ppermute | solution.py:50
  133.3 1.4 shard_map.377
  134.7 3.6 %all-to-all-start.1 = ((f32[32,8,128]{2,1,0:T(8,128)}), f32[32,8,128]{2,1,0:T(8,128)S(1)}, u32[]{:S(2)}, u32[]{:S(2)}) async-start(f32[32,8,128]{2,1,0:T(8,128)} %shard_map.377), calls=%async_computation.1 | async-start | bytes 262144 | tf_op jit(solution)/shard_map/all_to_all | solution.py:633
  140.5 1.3 shard_map.369
  141.8 1.8 collective-permute-start.37
  143.6 1.5 collective-permute-start.38
  145.3 1.3 shard_map.373
  146.5 2.1 %collective-permute-done.32.three_ref = bf16[144,768]{1,0:T(8,128)(2,1)} collective-permute-done((bf16[144,768]{1,0:T(8,128)(2,1)}, bf16[144,768]{1,0:T(8,128)(2,1)}, u32[]{:S(2)}, u32[]{:S(2)}) %collective-permute-start.32) | collective-permute-done | bytes 221216 | tf_op jit(solution)/shard_map/ppermute | solution.py:50
  148.6 2.7 %collective-permute-done.35.refs_2_ = bf16[144,768]{1,0:T(8,128)(2,1)} collective-permute-done((bf16[144,768]{1,0:T(8,128)(2,1)}, bf16[144,768]{1,0:T(8,128)(2,1)}, u32[]{:S(2)}, u32[]{:S(2)}) %collective-permute-start.35) | collective-permute-done | bytes 221216 | tf_op jit(solution)/shard_map/ppermute | solution.py:50
  152.0 1.7 collective-permute-start.45
  156.5 1.6 shard_map.376
  161.9 1.6 shard_map.375
  165.7 1.8 %shard_map.365 = bf16[144,768]{1,0:T(8,128)(2,1)} custom-call(s32[2]{0:T(128)S(1)} %pad_add_fusion.at_ref, f32[2,144,768]{2,1,0:T(8,128)S(1)} %get-tuple-element.163.own_ref, f32[8,768]{1,0:T(8,128)S(1)} %get-tuple-element.144.vec_ref, bf16[144,768]{1,0:T(8,128)(2,1)S(1)} %copy-done.32, bf16[144,768]{1,0:T(8,128)(2,1)} %collective-permute-done.30.two_ref, ...), custom_call_target="tpu_custom_call" | custom-call | tf_op jit(solution)/shard_map/pallas_call | solution.py:37
  169.5 2.2 %shard_map.368 = f32[144,768]{1,0:T(8,128)} custom-call(s32[2]{0:T(128)S(1)} %pad_add_fusion.at_ref, bf16[576,768]{1,0:T(8,128)(2,1)S(1)} %bitcast.21, f32[144,768]{1,0:T(8,128)S(1)} %copy-done.16, f32[8,768]{1,0:T(8,128)S(1)} %get-tuple-element.144.vec_ref, bf16[144,768]{1,0:T(8,128)(2,1)S(1)} %copy-done.34, ...), custom_call_target="tpu_custom_call" | custom-call | tf_op jit(solution)/shard_map/pallas_call | solution.py:37
  173.7 2.1 %shard_map.370 = (f32[3,96,192]{2,1,0:T(8,128)}, f32[3,96,192]{2,1,0:T(8,128)}, f32[3,96,192]{2,1,0:T(8,128)}) custom-call(s32[2]{0:T(128)S(1)} %pad_add_fusion.at_ref, f32[3,96,192]{2,1,0:T(8,128)S(1)} %copy-done.30, bf16[3,96,192]{2,1,0:T(8,128)(2,1)S(1)} %copy-done.40, bf16[3,96,192]{2,1,0:T(8,128)(2,1)} %collective-permute-done.38.refs_2_, ...), custom_call_target="tpu_custom_call" | custom-call | tf_op jit(solution)/shard_map/pallas_call | solution.py:37
  175.8 1.7 shard_map.374
  (195 shorter events, 51.3 us)
Async XLA Ops:
  5.0 10.2 %collective-permute-start.2 = (bf16[3,96,192]{2,1,0:T(8,128)(2,1)S(1)}, bf16[3,96,192]{2,1,0:T(8,128)(2,1)S(1)}, u32[]{:S(2)}, u32[]{:S(2)}) collective-permute-start(bf16[3,96,192]{2,1,0:T(8,128)(2,1)S(1)} %shard_map.349.refs_0_), channel_id=1, source_target_pairs={{0,24},{4,28},{8,16},{12,20},{16,8},{20,12},{24,0},{28,4},{1,25},{... | collective-permute-start | bytes 331784 | tf_op jit(solution)/shard_map/ppermute | solution.py:50
  9.0 12.9 %collective-permute-start.1 = (bf16[3,96,192]{2,1,0:T(8,128)(2,1)S(1)}, bf16[3,96,192]{2,1,0:T(8,128)(2,1)S(1)}, u32[]{:S(2)}, u32[]{:S(2)}) collective-permute-start(bf16[3,96,192]{2,1,0:T(8,128)(2,1)S(1)} %shard_map.349.refs_0_), channel_id=1, source_target_pairs={{0,16},{4,20},{8,24},{12,28},{16,0},{20,4},{24,8},{28,12},{1,17},{... | collective-permute-start | bytes 331784 | tf_op jit(solution)/shard_map/ppermute | solution.py:50
  9.5 12.4 %collective-permute-start = (bf16[3,96,192]{2,1,0:T(8,128)(2,1)S(1)}, bf16[3,96,192]{2,1,0:T(8,128)(2,1)S(1)}, u32[]{:S(2)}, u32[]{:S(2)}) collective-permute-start(bf16[3,96,192]{2,1,0:T(8,128)(2,1)S(1)} %shard_map.349.refs_0_), channel_id=1, source_target_pairs={{0,8},{4,12},{8,0},{12,4},{16,24},{20,28},{24,16},{28,20},{1,9},{5... | collective-permute-start | bytes 331784 | tf_op jit(solution)/shard_map/ppermute | solution.py:50
  11.1 11.3 %collective-permute-start.12 = (bf16[96,192]{1,0:T(8,128)(2,1)S(1)}, bf16[96,192]{1,0:T(8,128)(2,1)S(1)}, u32[]{:S(2)}, u32[]{:S(2)}) collective-permute-start(bf16[96,192]{1,0:T(8,128)(2,1)S(1)} %shard_map.351.refs_0_), channel_id=1, source_target_pairs={{0,3},{1,2},{2,1},{3,0},{4,7},{5,6},{6,5},{7,4},{8,11},{9,10},{10,... | collective-permute-start | bytes 110600 | tf_op jit(solution)/shard_map/ppermute | solution.py:50
  15.2 7.2 %collective-permute-start.11 = (bf16[96,192]{1,0:T(8,128)(2,1)S(1)}, bf16[96,192]{1,0:T(8,128)(2,1)S(1)}, u32[]{:S(2)}, u32[]{:S(2)}) collective-permute-start(bf16[96,192]{1,0:T(8,128)(2,1)S(1)} %shard_map.351.refs_0_), channel_id=1, source_target_pairs={{0,2},{1,3},{2,0},{3,1},{4,6},{5,7},{6,4},{7,5},{8,10},{9,11},{10,... | collective-permute-start | bytes 110600 | tf_op jit(solution)/shard_map/ppermute | solution.py:50
  15.2 7.2 %collective-permute-start.10 = (bf16[96,192]{1,0:T(8,128)(2,1)S(1)}, bf16[96,192]{1,0:T(8,128)(2,1)S(1)}, u32[]{:S(2)}, u32[]{:S(2)}) collective-permute-start(bf16[96,192]{1,0:T(8,128)(2,1)S(1)} %shard_map.351.refs_0_), channel_id=1, source_target_pairs={{0,1},{1,0},{2,3},{3,2},{4,5},{5,4},{6,7},{7,6},{8,9},{9,8},{10,11... | collective-permute-start | bytes 110600 | tf_op jit(solution)/shard_map/ppermute | solution.py:50
  15.9 14.6 %all-to-all-start = ((f32[32,8,128]{2,1,0:T(8,128)}), f32[32,8,128]{2,1,0:T(8,128)S(1)}, u32[]{:S(2)}, u32[]{:S(2)}) async-start(f32[32,8,128]{2,1,0:T(8,128)} %shard_map.347), calls=%async_computation | async-start | bytes 262144 | tf_op jit(solution)/shard_map/all_to_all | solution.py:467
  21.9 6.7 %collective-permute-start.3 = (bf16[3,96,192]{2,1,0:T(8,128)(2,1)S(1)}, bf16[3,96,192]{2,1,0:T(8,128)(2,1)S(1)}, u32[]{:S(2)}, u32[]{:S(2)}) collective-permute-start(bf16[3,96,192]{2,1,0:T(8,128)(2,1)S(1)} %shard_map.349.refs_0_), channel_id=1, source_target_pairs={{0,4},{4,0},{8,12},{12,8},{16,20},{20,16},{24,28},{28,24},{1,5},{5... | collective-permute-start | bytes 331784 | tf_op jit(solution)/shard_map/ppermute | solution.py:50
  22.2 7.1 %collective-permute-start.4 = (bf16[3,96,192]{2,1,0:T(8,128)(2,1)S(1)}, bf16[3,96,192]{2,1,0:T(8,128)(2,1)S(1)}, u32[]{:S(2)}, u32[]{:S(2)}) collective-permute-start(bf16[3,96,192]{2,1,0:T(8,128)(2,1)S(1)} %collective-permute-done.refs_2_), channel_id=1, source_target_pairs={{0,4},{4,0},{8,12},{12,8},{16,20},{20,16},{24,28},{28,24},{1,5},{5... | collective-permute-start | bytes 331784 | tf_op jit(solution)/shard_map/ppermute | solution.py:50
  25.0 18.2 %collective-permute-start.15 = (bf16[3,96,768]{2,1,0:T(8,128)(2,1)S(1)}, bf16[3,96,768]{2,1,0:T(8,128)(2,1)S(1)}, u32[]{:S(2)}, u32[]{:S(2)}) collective-permute-start(bf16[3,96,768]{2,1,0:T(8,128)(2,1)S(1)} %shard_map.352.refs_4_), channel_id=1, source_target_pairs={{0,24},{4,28},{8,16},{12,20},{16,8},{20,12},{24,0},{28,4},{1,25},{... | collective-permute-start | bytes 1327112 | tf_op jit(solution)/shard_map/ppermute | solution.py:50
  27.8 20.5 %collective-permute-start.14 = (bf16[3,96,768]{2,1,0:T(8,128)(2,1)S(1)}, bf16[3,96,768]{2,1,0:T(8,128)(2,1)}, u32[]{:S(2)}, u32[]{:S(2)}) collective-permute-start(bf16[3,96,768]{2,1,0:T(8,128)(2,1)S(1)} %shard_map.352.refs_4_), channel_id=1, source_target_pairs={{0,16},{4,20},{8,24},{12,28},{16,0},{20,4},{24,8},{28,12},{1,17},{... | collective-permute-start | bytes 1327112 | tf_op jit(solution)/shard_map/ppermute | solution.py:50
  28.3 19.9 %collective-permute-start.13 = (bf16[3,96,768]{2,1,0:T(8,128)(2,1)S(1)}, bf16[3,96,768]{2,1,0:T(8,128)(2,1)}, u32[]{:S(2)}, u32[]{:S(2)}) collective-permute-start(bf16[3,96,768]{2,1,0:T(8,128)(2,1)S(1)} %shard_map.352.refs_4_), channel_id=1, source_target_pairs={{0,8},{4,12},{8,0},{12,4},{16,24},{20,28},{24,16},{28,20},{1,9},{5... | collective-permute-start | bytes 1327112 | tf_op jit(solution)/shard_map/ppermute | solution.py:50
  39.0 12.3 %collective-permute-start.7 = (bf16[864,128]{1,0:T(8,128)(2,1)S(1)}, bf16[864,128]{1,0:T(8,128)(2,1)S(1)}, u32[]{:S(2)}, u32[]{:S(2)}) collective-permute-start(bf16[864,128]{1,0:T(8,128)(2,1)S(1)} %get-tuple-element.152.refs_0_), channel_id=1, source_target_pairs={{0,1},{1,0},{2,3},{3,2},{4,5},{5,4},{6,7},{7,6},{8,9},{9,8},{10,11... | collective-permute-start | bytes 663560 | tf_op jit(solution)/shard_map/ppermute | solution.py:50
  40.9 13.1 %collective-permute-start.8 = (bf16[864,128]{1,0:T(8,128)(2,1)S(1)}, bf16[864,128]{1,0:T(8,128)(2,1)S(1)}, u32[]{:S(2)}, u32[]{:S(2)}) collective-permute-start(bf16[864,128]{1,0:T(8,128)(2,1)S(1)} %get-tuple-element.152.refs_0_), channel_id=1, source_target_pairs={{0,2},{1,3},{2,0},{3,1},{4,6},{5,7},{6,4},{7,5},{8,10},{9,11},{10,... | collective-permute-start | bytes 663560 | tf_op jit(solution)/shard_map/ppermute | solution.py:50
  51.3 9.1 %collective-permute-start.16 = (bf16[3,96,768]{2,1,0:T(8,128)(2,1)S(1)}, bf16[3,96,768]{2,1,0:T(8,128)(2,1)S(1)}, u32[]{:S(2)}, u32[]{:S(2)}) collective-permute-start(bf16[3,96,768]{2,1,0:T(8,128)(2,1)S(1)} %shard_map.352.refs_4_), channel_id=1, source_target_pairs={{0,4},{4,0},{8,12},{12,8},{16,20},{20,16},{24,28},{28,24},{1,5},{5... | collective-permute-start | bytes 1327112 | tf_op jit(solution)/shard_map/ppermute | solution.py:50
  51.3 9.1 %collective-permute-start.17 = (bf16[3,96,768]{2,1,0:T(8,128)(2,1)}, bf16[3,96,768]{2,1,0:T(8,128)(2,1)S(1)}, u32[]{:S(2)}, u32[]{:S(2)}) collective-permute-start(bf16[3,96,768]{2,1,0:T(8,128)(2,1)} %collective-permute-done.13.refs_6_), channel_id=1, source_target_pairs={{0,4},{4,0},{8,12},{12,8},{16,20},{20,16},{24,28},{28,24},{1,5},{5... | collective-permute-start | bytes 1327112 | tf_op jit(solution)/shard_map/ppermute | solution.py:50
  51.8 8.6 %collective-permute-start.18 = (bf16[3,96,768]{2,1,0:T(8,128)(2,1)}, bf16[3,96,768]{2,1,0:T(8,128)(2,1)S(1)}, u32[]{:S(2)}, u32[]{:S(2)}) collective-permute-start(bf16[3,96,768]{2,1,0:T(8,128)(2,1)} %collective-permute-done.14.refs_8_), channel_id=1, source_target_pairs={{0,4},{4,0},{8,12},{12,8},{16,20},{20,16},{24,28},{28,24},{1,5},{5... | collective-permute-start | bytes 1327112 | tf_op jit(solution)/shard_map/ppermute | solution.py:50
  51.8 8.6 %collective-permute-start.19 = (bf16[3,96,768]{2,1,0:T(8,128)(2,1)S(1)}, bf16[3,96,768]{2,1,0:T(8,128)(2,1)S(1)}, u32[]{:S(2)}, u32[]{:S(2)}) collective-permute-start(bf16[3,96,768]{2,1,0:T(8,128)(2,1)S(1)} %collective-permute-done.15.refs_10_), channel_id=1, source_target_pairs={{0,4},{4,0},{8,12},{12,8},{16,20},{20,16},{24,28},{28,24},{1,5},{5... | collective-permute-start | bytes 1327112 | tf_op jit(solution)/shard_map/ppermute | solution.py:50
  53.9 6.5 %collective-permute-start.9 = (bf16[864,128]{1,0:T(8,128)(2,1)S(1)}, bf16[864,128]{1,0:T(8,128)(2,1)S(1)}, u32[]{:S(2)}, u32[]{:S(2)}) collective-permute-start(bf16[864,128]{1,0:T(8,128)(2,1)S(1)} %collective-permute-done.8.refs_2_), channel_id=1, source_target_pairs={{0,1},{1,0},{2,3},{3,2},{4,5},{5,4},{6,7},{7,6},{8,9},{9,8},{10,11... | collective-permute-start | bytes 663560 | tf_op jit(solution)/shard_map/ppermute | solution.py:50
  69.0 15.1 %collective-permute-start.24 = (bf16[2,2,96,768]{3,2,1,0:T(8,128)(2,1)S(1)}, bf16[2,2,96,768]{3,2,1,0:T(8,128)(2,1)S(1)}, u32[]{:S(2)}, u32[]{:S(2)}) collective-permute-start(bf16[2,2,96,768]{3,2,1,0:T(8,128)(2,1)S(1)} %get-tuple-element.178), channel_id=1, source_target_pairs={{0,4},{4,0},{8,12},{12,8},{16,20},{20,16},{24,28},{28,24},{1,5},{5... | collective-permute-start | bytes 1769480 | tf_op jit(solution)/shard_map/ppermute | solution.py:50
  70.9 13.9 %collective-permute-start.23 = (bf16[2,2,96,768]{3,2,1,0:T(8,128)(2,1)S(1)}, bf16[2,2,96,768]{3,2,1,0:T(8,128)(2,1)S(1)}, u32[]{:S(2)}, u32[]{:S(2)}) collective-permute-start(bf16[2,2,96,768]{3,2,1,0:T(8,128)(2,1)S(1)} %get-tuple-element.173), channel_id=1, source_target_pairs={{0,4},{4,0},{8,12},{12,8},{16,20},{20,16},{24,28},{28,24},{1,5},{5... | collective-permute-start | bytes 1769480 | tf_op jit(solution)/shard_map/ppermute | solution.py:50
  71.4 8.3 %collective-permute-start.21 = (bf16[144,768]{1,0:T(8,128)(2,1)S(1)}, bf16[144,768]{1,0:T(8,128)(2,1)S(1)}, u32[]{:S(2)}, u32[]{:S(2)}) collective-permute-start(bf16[144,768]{1,0:T(8,128)(2,1)S(1)} %get-tuple-element.169), channel_id=1, source_target_pairs={{0,1},{1,0},{2,3},{3,2},{4,5},{5,4},{6,7},{7,6},{8,9},{9,8},{10,11... | collective-permute-start | bytes 663560 | tf_op jit(solution)/shard_map/ppermute | solution.py:50
  72.1 13.8 %collective-permute-start.20 = (bf16[144,768]{1,0:T(8,128)(2,1)S(1)}, bf16[144,768]{1,0:T(8,128)(2,1)S(1)}, u32[]{:S(2)}, u32[]{:S(2)}) collective-permute-start(bf16[144,768]{1,0:T(8,128)(2,1)S(1)} %get-tuple-element.167), channel_id=1, source_target_pairs={{0,1},{1,0},{2,3},{3,2},{4,5},{5,4},{6,7},{7,6},{8,9},{9,8},{10,11... | collective-permute-start | bytes 663560 | tf_op jit(solution)/shard_map/ppermute | solution.py:50
  80.3 11.5 %collective-permute-start.22 = (bf16[144,768]{1,0:T(8,128)(2,1)S(1)}, bf16[144,768]{1,0:T(8,128)(2,1)S(1)}, u32[]{:S(2)}, u32[]{:S(2)}) collective-permute-start(bf16[144,768]{1,0:T(8,128)(2,1)S(1)} %shard_map.354), channel_id=1, source_target_pairs={{0,2},{1,3},{2,0},{3,1},{4,6},{5,7},{6,4},{7,5},{8,10},{9,11},{10,... | collective-permute-start | bytes 663560 | tf_op jit(solution)/shard_map/ppermute | solution.py:50
  91.8 10.8 %collective-permute-start.28 = (bf16[2,96,768]{2,1,0:T(8,128)(2,1)S(1)}, bf16[2,96,768]{2,1,0:T(8,128)(2,1)S(1)}, u32[]{:S(2)}, u32[]{:S(2)}) collective-permute-start(bf16[2,96,768]{2,1,0:T(8,128)(2,1)S(1)} %get-tuple-element.201), channel_id=1, source_target_pairs={{0,8},{4,12},{8,0},{12,4},{16,24},{20,28},{24,16},{28,20},{1,9},{5... | collective-permute-start | bytes 884744 | tf_op jit(solution)/shard_map/ppermute | solution.py:50
  93.5 9.7 %collective-permute-start.29 = (bf16[2,96,768]{2,1,0:T(8,128)(2,1)S(1)}, bf16[2,96,768]{2,1,0:T(8,128)(2,1)S(1)}, u32[]{:S(2)}, u32[]{:S(2)}) collective-permute-start(bf16[2,96,768]{2,1,0:T(8,128)(2,1)S(1)} %get-tuple-element.205), channel_id=1, source_target_pairs={{0,16},{4,20},{8,24},{12,28},{16,0},{20,4},{24,8},{28,12},{1,17},{... | collective-permute-start | bytes 884744 | tf_op jit(solution)/shard_map/ppermute | solution.py:50
  97.0 6.8 %collective-permute-start.25 = (bf16[216,128]{1,0:T(8,128)(2,1)S(1)}, bf16[216,128]{1,0:T(8,128)(2,1)S(1)}, u32[]{:S(2)}, u32[]{:S(2)}) collective-permute-start(bf16[216,128]{1,0:T(8,128)(2,1)S(1)} %get-tuple-element.189), channel_id=1, source_target_pairs={{0,1},{1,0},{2,3},{3,2},{4,5},{5,4},{6,7},{7,6},{8,9},{9,8},{10,11... | collective-permute-start | bytes 165896 | tf_op jit(solution)/shard_map/ppermute | solution.py:50
  97.0 6.8 %collective-permute-start.26 = (bf16[216,128]{1,0:T(8,128)(2,1)S(1)}, bf16[216,128]{1,0:T(8,128)(2,1)S(1)}, u32[]{:S(2)}, u32[]{:S(2)}) collective-permute-start(bf16[216,128]{1,0:T(8,128)(2,1)S(1)} %get-tuple-element.190), channel_id=1, source_target_pairs={{0,2},{1,3},{2,0},{3,1},{4,6},{5,7},{6,4},{7,5},{8,10},{9,11},{10,... | collective-permute-start | bytes 165896 | tf_op jit(solution)/shard_map/ppermute | solution.py:50
  99.9 6.0 %collective-permute-start.27 = (bf16[216,128]{1,0:T(8,128)(2,1)S(1)}, bf16[216,128]{1,0:T(8,128)(2,1)S(1)}, u32[]{:S(2)}, u32[]{:S(2)}) collective-permute-start(bf16[216,128]{1,0:T(8,128)(2,1)S(1)} %get-tuple-element.191), channel_id=1, source_target_pairs={{0,3},{1,2},{2,1},{3,0},{4,7},{5,6},{6,5},{7,4},{8,11},{9,10},{10,... | collective-permute-start | bytes 165896 | tf_op jit(solution)/shard_map/ppermute | solution.py:50
  105.9 7.5 %collective-permute-start.40 = (bf16[2,2,96,768]{3,2,1,0:T(8,128)(2,1)S(1)}, bf16[2,2,96,768]{3,2,1,0:T(8,128)(2,1)S(1)}, u32[]{:S(2)}, u32[]{:S(2)}) collective-permute-start(bf16[2,2,96,768]{3,2,1,0:T(8,128)(2,1)S(1)} %get-tuple-element.235), channel_id=1, source_target_pairs={{0,4},{4,0},{8,12},{12,8},{16,20},{20,16},{24,28},{28,24},{1,5},{5... | collective-permute-start | bytes 1769480 | tf_op jit(solution)/shard_map/ppermute | solution.py:50
  112.8 17.7 %collective-permute-start.36 = (bf16[2,2,3,96,192]{4,3,2,1,0:T(8,128)(2,1)S(1)}, bf16[2,2,3,96,192]{4,3,2,1,0:T(8,128)(2,1)S(1)}, u32[]{:S(2)}, u32[]{:S(2)}) collective-permute-start(bf16[2,2,3,96,192]{4,3,2,1,0:T(8,128)(2,1)S(1)} %get-tuple-element.226), channel_id=1, source_target_pairs={{0,4},{4,0},{8,12},{12,8},{16,20},{20,16},{24,28},{28,24},{1,5},{5... | collective-permute-start | bytes 1327112 | tf_op jit(solution)/shard_map/ppermute | solution.py:50
  114.1 9.9 %collective-permute-start.41 = (bf16[2,96,768]{2,1,0:T(8,128)(2,1)S(1)}, bf16[2,96,768]{2,1,0:T(8,128)(2,1)S(1)}, u32[]{:S(2)}, u32[]{:S(2)}) collective-permute-start(bf16[2,96,768]{2,1,0:T(8,128)(2,1)S(1)} %get-tuple-element.237), channel_id=1, source_target_pairs={{0,8},{4,12},{8,0},{12,4},{16,24},{20,28},{24,16},{28,20},{1,9},{5... | collective-permute-start | bytes 884744 | tf_op jit(solution)/shard_map/ppermute | solution.py:50
  114.8 8.3 %collective-permute-start.31 = (bf16[144,768]{1,0:T(8,128)(2,1)S(1)}, bf16[144,768]{1,0:T(8,128)(2,1)S(1)}, u32[]{:S(2)}, u32[]{:S(2)}) collective-permute-start(bf16[144,768]{1,0:T(8,128)(2,1)S(1)} %get-tuple-element.211), channel_id=1, source_target_pairs={{0,1},{1,0},{2,3},{3,2},{4,5},{5,4},{6,7},{7,6},{8,9},{9,8},{10,11... | collective-permute-start | bytes 663560 | tf_op jit(solution)/shard_map/ppermute | solution.py:50
  114.8 5.5 %collective-permute-start.46 = (bf16[96,768]{1,0:T(8,128)(2,1)S(1)}, bf16[96,768]{1,0:T(8,128)(2,1)S(1)}, u32[]{:S(2)}, u32[]{:S(2)}) collective-permute-start(bf16[96,768]{1,0:T(8,128)(2,1)S(1)} %get-tuple-element.248), channel_id=1, source_target_pairs={{0,16},{4,20},{8,24},{12,28},{16,0},{20,4},{24,8},{28,12},{1,17},{... | collective-permute-start | bytes 442376 | tf_op jit(solution)/shard_map/ppermute | solution.py:50
  115.3 13.0 %collective-permute-start.34 = (bf16[144,768]{1,0:T(8,128)(2,1)S(1)}, bf16[144,768]{1,0:T(8,128)(2,1)S(1)}, u32[]{:S(2)}, u32[]{:S(2)}) collective-permute-start(bf16[144,768]{1,0:T(8,128)(2,1)S(1)} %get-tuple-element.224), channel_id=1, source_target_pairs={{0,1},{1,0},{2,3},{3,2},{4,5},{5,4},{6,7},{7,6},{8,9},{9,8},{10,11... | collective-permute-start | bytes 663560 | tf_op jit(solution)/shard_map/ppermute | solution.py:50
  120.3 7.4 %collective-permute-start.47 = (bf16[96,768]{1,0:T(8,128)(2,1)S(1)}, bf16[96,768]{1,0:T(8,128)(2,1)S(1)}, u32[]{:S(2)}, u32[]{:S(2)}) collective-permute-start(bf16[96,768]{1,0:T(8,128)(2,1)S(1)} %get-tuple-element.253), channel_id=1, source_target_pairs={{0,8},{4,12},{8,0},{12,4},{16,24},{20,28},{24,16},{28,20},{1,9},{5... | collective-permute-start | bytes 442376 | tf_op jit(solution)/shard_map/ppermute | solution.py:50
  123.1 18.7 %collective-permute-start.30 = (bf16[144,768]{1,0:T(8,128)(2,1)}, bf16[144,768]{1,0:T(8,128)(2,1)}, u32[]{:S(2)}, u32[]{:S(2)}) collective-permute-start(bf16[144,768]{1,0:T(8,128)(2,1)} %get-tuple-element.209), channel_id=1, source_target_pairs={{0,1},{1,0},{2,3},{3,2},{4,5},{5,4},{6,7},{7,6},{8,9},{9,8},{10,11... | collective-permute-start | bytes 663560 | tf_op jit(solution)/shard_map/ppermute | solution.py:50
  124.1 19.5 %collective-permute-start.33 = (bf16[144,768]{1,0:T(8,128)(2,1)}, bf16[144,768]{1,0:T(8,128)(2,1)}, u32[]{:S(2)}, u32[]{:S(2)}) collective-permute-start(bf16[144,768]{1,0:T(8,128)(2,1)} %get-tuple-element.222), channel_id=1, source_target_pairs={{0,1},{1,0},{2,3},{3,2},{4,5},{5,4},{6,7},{7,6},{8,9},{9,8},{10,11... | collective-permute-start | bytes 663560 | tf_op jit(solution)/shard_map/ppermute | solution.py:50
  127.7 17.4 %collective-permute-start.42 = (bf16[96,768]{1,0:T(8,128)(2,1)}, bf16[96,768]{1,0:T(8,128)(2,1)S(1)}, u32[]{:S(2)}, u32[]{:S(2)}) collective-permute-start(bf16[96,768]{1,0:T(8,128)(2,1)} %get-tuple-element.239), channel_id=1, source_target_pairs={{0,16},{4,20},{8,24},{12,28},{16,0},{20,4},{24,8},{28,12},{1,17},{... | collective-permute-start | bytes 442376 | tf_op jit(solution)/shard_map/ppermute | solution.py:50
  128.3 20.4 %collective-permute-start.32 = (bf16[144,768]{1,0:T(8,128)(2,1)}, bf16[144,768]{1,0:T(8,128)(2,1)}, u32[]{:S(2)}, u32[]{:S(2)}) collective-permute-start(bf16[144,768]{1,0:T(8,128)(2,1)} %shard_map.364), channel_id=1, source_target_pairs={{0,2},{1,3},{2,0},{3,1},{4,6},{5,7},{6,4},{7,5},{8,10},{9,11},{10,... | collective-permute-start | bytes 663560 | tf_op jit(solution)/shard_map/ppermute | solution.py:50
  131.3 20.0 %collective-permute-start.35 = (bf16[144,768]{1,0:T(8,128)(2,1)}, bf16[144,768]{1,0:T(8,128)(2,1)}, u32[]{:S(2)}, u32[]{:S(2)}) collective-permute-start(bf16[144,768]{1,0:T(8,128)(2,1)} %shard_map.367), channel_id=1, source_target_pairs={{0,2},{1,3},{2,0},{3,1},{4,6},{5,7},{6,4},{7,5},{8,10},{9,11},{10,... | collective-permute-start | bytes 663560 | tf_op jit(solution)/shard_map/ppermute | solution.py:50
  134.7 28.8 %all-to-all-start.1 = ((f32[32,8,128]{2,1,0:T(8,128)}), f32[32,8,128]{2,1,0:T(8,128)S(1)}, u32[]{:S(2)}, u32[]{:S(2)}) async-start(f32[32,8,128]{2,1,0:T(8,128)} %shard_map.377), calls=%async_computation.1 | async-start | bytes 262144 | tf_op jit(solution)/shard_map/all_to_all | solution.py:633
  141.8 9.6 %collective-permute-start.37 = (bf16[3,96,192]{2,1,0:T(8,128)(2,1)S(1)}, bf16[3,96,192]{2,1,0:T(8,128)(2,1)S(1)}, u32[]{:S(2)}, u32[]{:S(2)}) collective-permute-start(bf16[3,96,192]{2,1,0:T(8,128)(2,1)S(1)} %get-tuple-element.228), channel_id=1, source_target_pairs={{0,16},{4,20},{8,24},{12,28},{16,0},{20,4},{24,8},{28,12},{1,17},{... | collective-permute-start | bytes 331784 | tf_op jit(solution)/shard_map/ppermute | solution.py:50
  143.6 28.1 %collective-permute-start.38 = (bf16[3,96,192]{2,1,0:T(8,128)(2,1)}, bf16[3,96,192]{2,1,0:T(8,128)(2,1)}, u32[]{:S(2)}, u32[]{:S(2)}) collective-permute-start(bf16[3,96,192]{2,1,0:T(8,128)(2,1)} %get-tuple-element.229), channel_id=1, source_target_pairs={{0,8},{4,12},{8,0},{12,4},{16,24},{20,28},{24,16},{28,20},{1,9},{5... | collective-permute-start | bytes 331784 | tf_op jit(solution)/shard_map/ppermute | solution.py:50
  145.0 26.7 %collective-permute-start.39 = (bf16[3,96,192]{2,1,0:T(8,128)(2,1)}, bf16[3,96,192]{2,1,0:T(8,128)(2,1)}, u32[]{:S(2)}, u32[]{:S(2)}) collective-permute-start(bf16[3,96,192]{2,1,0:T(8,128)(2,1)} %get-tuple-element.230), channel_id=1, source_target_pairs={{0,24},{4,28},{8,16},{12,20},{16,8},{20,12},{24,0},{28,4},{1,25},{... | collective-permute-start | bytes 331784 | tf_op jit(solution)/shard_map/ppermute | solution.py:50
  148.6 27.1 %collective-permute-start.43 = (bf16[96,192]{1,0:T(8,128)(2,1)}, bf16[96,192]{1,0:T(8,128)(2,1)}, u32[]{:S(2)}, u32[]{:S(2)}) collective-permute-start(bf16[96,192]{1,0:T(8,128)(2,1)} %get-tuple-element.241), channel_id=1, source_target_pairs={{0,1},{1,0},{2,3},{3,2},{4,5},{5,4},{6,7},{7,6},{8,9},{9,8},{10,11... | collective-permute-start | bytes 110600 | tf_op jit(solution)/shard_map/ppermute | solution.py:50
  151.4 24.4 %collective-permute-start.44 = (bf16[96,192]{1,0:T(8,128)(2,1)}, bf16[96,192]{1,0:T(8,128)(2,1)}, u32[]{:S(2)}, u32[]{:S(2)}) collective-permute-start(bf16[96,192]{1,0:T(8,128)(2,1)} %get-tuple-element.242), channel_id=1, source_target_pairs={{0,2},{1,3},{2,0},{3,1},{4,6},{5,7},{6,4},{7,5},{8,10},{9,11},{10,... | collective-permute-start | bytes 110600 | tf_op jit(solution)/shard_map/ppermute | solution.py:50
  152.0 23.8 %collective-permute-start.45 = (bf16[96,192]{1,0:T(8,128)(2,1)}, bf16[96,192]{1,0:T(8,128)(2,1)}, u32[]{:S(2)}, u32[]{:S(2)}) collective-permute-start(bf16[96,192]{1,0:T(8,128)(2,1)} %get-tuple-element.243), channel_id=1, source_target_pairs={{0,3},{1,2},{2,1},{3,0},{4,7},{5,6},{6,5},{7,4},{8,11},{9,10},{10,... | collective-permute-start | bytes 110600 | tf_op jit(solution)/shard_map/ppermute | solution.py:50
  (57 other events, 764.7 us)

commit v3 on v2

--- a/solution.py
+++ b/solution.py
@@ -31,18 +31,29 @@
     return lax.dot_general(left, right, dims, preferred_element_type=wide)
 
 
-def kernel_call(body, outs, args, scratch=()):
-    smem = pl.BlockSpec(memory_space=pltpu.SMEM)
-    vmem = pl.BlockSpec(memory_space=pltpu.VMEM)
+def kernel_call(body, outs, args, scratch=(), hbm=(), free=(), hbm_outs=False):
+    def spec(i):
+        space = pltpu.HBM if i in hbm else pl.ANY if i in free else pltpu.VMEM
+        return pl.BlockSpec(memory_space=space)
+
+    out_space = pltpu.HBM if hbm_outs else pltpu.VMEM
+    args = [pltpu.with_memory_space_constraint(arg, pltpu.HBM) if i in hbm else arg for i, arg in enumerate(args)]
     return pl.pallas_call(
         body,
         out_shape=[jax.ShapeDtypeStruct(s, d) for s, d in outs],
-        in_specs=[smem] + [vmem] * (len(args) - 1),
-        out_specs=[vmem] * len(outs),
+        in_specs=[pl.BlockSpec(memory_space=pltpu.SMEM)] + [spec(i) for i in range(1, len(args))],
+        out_specs=[pl.BlockSpec(memory_space=out_space)] * len(outs),
         scratch_shapes=list(scratch),
         compiler_params=pltpu.CompilerParams(vmem_limit_bytes=VMEM_LIMIT),
         cost_estimate=pl.CostEstimate(flops=0, bytes_accessed=0, transcendentals=0),
     )(*args)
+
+
+def fetch(pairs, sems):
+    copies = [pltpu.make_async_copy(source, target, sems.at[i]) for i, (source, target) in enumerate(pairs)]
+    for copy in copies:
+        copy.start()
+    return copies
 
 
 def flip(value, axis, mask):
@@ -76,11 +87,11 @@
     return [value, one, two, flip(two, "tensor", 1)]
 
 
-def rank_sum(at, slots):
-    three = flip(slots[3], "tensor", 1)
+def rank_sum(at, slots, *gates):
+    three = after(flip(slots[3], "tensor", 1), *gates)
     one = flip(slots[1], "tensor", 1)
     (two,) = kernel_call(add_kernel, [(three.shape, low)], (at, slots[2], three))
-    return [slots[0], one, flip(two, "tensor", 2)]
+    return [slots[0], one, flip(two, "tensor", 2)], two
 
 
 def to_ranks(slots):
@@ -104,14 +115,12 @@
     )
 
 
-def place_rows(at_ref, parts, target):
+def place_rows(at_ref, parts, target, sems):
     if len(parts) == 1:
-        target[...] = parts[0][...]
-        return
-    for slot, part in enumerate(parts):
-        height = part.shape[1]
-        start = pl.multiple_of((at_ref[0] ^ slot) * height, 32)
-        target[:, pl.ds(start, height), :] = part[...]
+        return fetch([(parts[0], target)], sems)
+    height = parts[0].shape[1]
+    spots = [pl.ds(pl.multiple_of((at_ref[0] ^ slot) * height, 32), height) for slot in range(len(parts))]
+    return fetch([(part, target.at[:, spot, :]) for part, spot in zip(parts, spots)], sems)
 
 
 def take_rows(at_ref, source, slot, height):
@@ -140,13 +149,22 @@
     return jnp.concatenate([upper.astype(wide), value - upper.astype(wide)], axis=0)
 
 
-def small_pack_kernel(at_ref, vec_ref, bias_ref, out_ref):
-    cols, ends = vec_ref.shape[1], bias_ref.shape[1]
+def first_kernel(at_ref, *refs):
+    ins, (tile_ref, low_ref, turned_ref), bufs, sems = refs[:4], refs[4:7], refs[7:11], refs[11]
+    copies = fetch(list(zip(ins, bufs)), sems)
+    vec_buf, bias_buf, qkv_buf, out_buf = bufs
+    copies[0].wait()
+    copies[1].wait()
+    cols, ends = vec_buf.shape[1], bias_buf.shape[1]
     tile = jnp.concatenate(
-        [vec_ref[...], jnp.zeros((8, 128 - cols - ends), wide), jnp.broadcast_to(bias_ref[...], (8, ends))], axis=1
-    )
-    for j in range(out_ref.shape[0]):
-        out_ref[j] = tile
+        [vec_buf[...], jnp.zeros((8, 128 - cols - ends), wide), jnp.broadcast_to(bias_buf[...], (8, ends))], axis=1
+    )
+    for j in range(tile_ref.shape[0]):
+        tile_ref[j] = tile
+    copies[2].wait()
+    low_ref[...] = qkv_buf[...].astype(low)
+    copies[3].wait()
+    turned_ref[...] = out_buf[...].T.astype(low)
 
 
 def small_unpack_kernel(cols, at_ref, small_ref, vec_ref, qv_ref, bias_ref):
@@ -159,35 +177,19 @@
     bias_ref[...] = jnp.concatenate([tile[0:1, 128 - ends :] for tile in mine], axis=1)
 
 
-def round_kernel(turned, at_ref, in_ref, out_ref):
-    value = in_ref[...]
-    out_ref[...] = (value.T if turned else value).astype(low)
-
-
 def add_kernel(at_ref, left_ref, right_ref, out_ref):
     out_ref[...] = (left_ref[...].astype(wide) + right_ref[...].astype(wide)).astype(out_ref.dtype)
 
 
-def pair_kernel(at_ref, keep_ref, got_ref, stay_ref, go_ref):
-    stay_ref[...] = keep_ref[0].astype(wide) + got_ref[0].astype(wide)
-    go_ref[...] = (keep_ref[1].astype(wide) + got_ref[1].astype(wide)).astype(low)
-
-
-def across_kernel(at_ref, stay_ref, got_ref, mine_ref, go_ref):
-    mine_ref[...] = stay_ref[0] + got_ref[0].astype(wide)
-    go_ref[...] = (stay_ref[1] + got_ref[1].astype(wide)).astype(low)
-
-
-def quad_kernel(at_ref, keep_ref, got_ref, mine_ref, *go_refs):
-    mine_ref[...] = keep_ref[0, 0].astype(wide) + got_ref[0, 0].astype(wide)
-    for j, ref in enumerate(go_refs, 1):
-        at = (j // 2, j % 2)
-        ref[...] = (keep_ref[at].astype(wide) + got_ref[at].astype(wide)).astype(low)
-
-
-def ranks_kernel(at_ref, left_ref, right_ref, *out_refs):
-    total = left_ref[...] + right_ref[...].astype(wide)
-    width = total.shape[1] // 4
+def quad_kernel(at_ref, keep_ref, got_ref, *out_refs):
+    for j, ref in enumerate(out_refs):
+        ref[...] = (keep_ref[j].astype(wide) + got_ref[j].astype(wide)).astype(ref.dtype)
+
+
+def ranks_kernel(at_ref, *refs):
+    parts, out_refs = refs[:-4], refs[-4:]
+    width = out_refs[0].shape[1]
+    total = sum(ref[:, : 4 * width].astype(wide) for ref in parts)
     for j, ref in enumerate(out_refs):
         ref[...] = total[:, j * width : (j + 1) * width].astype(low)
 
@@ -218,48 +220,63 @@
         )
 
 
+def stored(values, bufs, refs, sems):
+    for value, buf in zip(values, bufs):
+        buf[...] = value
+    for copy in fetch(list(zip(bufs, refs)), sems):
+        copy.wait()
+
+
 def small_adam_kernel(at_ref, got_ref, *refs):
-    (w_ref, m_ref, s_ref, b_ref, bm_ref, bs_ref), outs = refs[:6], refs[6:]
+    ins, outs, bufs, in_sems, out_sems = refs[:6], refs[6:12], refs[12:18], refs[18], refs[19]
+    copies = fetch(list(zip(ins, bufs)), in_sems)
     total = jnp.sum(got_ref[...], axis=0)
-    cols, ends = w_ref.shape[1], b_ref.shape[1]
-    states = adamw(w_ref[...], total[:, :cols], m_ref[...], s_ref[...], 0.5, 0.0)
-    states += adamw(b_ref[...], total[0:1, 128 - ends :], bm_ref[...], bs_ref[...], 0.7, 0.0)
-    for ref, value in zip(outs, states):
-        ref[...] = value
-
-
-def adam_kernel(n_parts, turned, rate, decay, at_ref, *refs):
-    parts, (w_ref, m_ref, s_ref) = refs[:n_parts], refs[n_parts : n_parts + 3]
-    total = sum(ref[...].astype(wide) for ref in parts)
-    if turned:
-        total = total.T
-    states = adamw(w_ref[...], total, m_ref[...], s_ref[...], rate, decay)
-    for ref, value in zip(refs[n_parts + 3 :], states):
-        ref[...] = value
+    for copy in copies:
+        copy.wait()
+    cols, ends = bufs[0].shape[1], bufs[3].shape[1]
+    vectors, biases = [buf[...] for buf in bufs[:3]], [buf[...] for buf in bufs[3:]]
+    states = adamw(vectors[0], total[:, :cols], vectors[1], vectors[2], 0.5, 0.0)
+    states += adamw(biases[0], total[0:1, 128 - ends :], biases[1], biases[2], 0.7, 0.0)
+    stored(states, bufs, outs, out_sems)
+
+
+def adam_kernel(n_parts, turned, rates, at_ref, *refs):
+    count = len(rates)
+    parts, refs = refs[: n_parts * count], refs[n_parts * count :]
+    ins, outs, bufs = refs[: 3 * count], refs[3 * count : 6 * count], refs[6 * count : 9 * count]
+    in_sems, out_sems = refs[9 * count :]
+    copies = fetch(list(zip(ins, bufs)), in_sems)
+    states = []
+    for j, (rate, decay) in enumerate(rates):
+        total = sum(ref[...].astype(wide) for ref in parts[j * n_parts : (j + 1) * n_parts])
+        if turned:
+            total = total.T
+        for copy in copies[3 * j : 3 * j + 3]:
+            copy.wait()
+        weight, first, second = (buf[...] for buf in bufs[3 * j : 3 * j + 3])
+        states += adamw(weight, total, first, second, rate, decay)
+    stored(states, bufs, outs, out_sems)
 
 
 def weights_kernel(at_ref, up_ref, down_ref, *refs):
-    parts, out_ref = refs[:4], refs[4]
-    height = up_ref.shape[0]
-    out_ref[0] = up_ref[...].astype(low)
-    out_ref[1] = down_ref[...].astype(low)
+    parts, (out_ref, up_buf, down_buf, sems) = refs[:4], refs[4:]
+    copies = fetch([(up_ref, up_buf), (down_ref, down_buf)], sems)
     out_ref[2] = jnp.concatenate([ref[...] for ref in parts], axis=1)
+    copies[0].wait()
+    out_ref[0] = up_buf[...].astype(low)
+    copies[1].wait()
+    out_ref[1] = down_buf[...].astype(low)
 
 
 def attend_kernel(n_parts, at_ref, x_ref, vec_ref, qv_ref, *refs):
     parts = refs[:n_parts]
-    a1_ref, qkv_ref, lse_ref, o_ref, w_ref, ot_ref = refs[n_parts:]
-    if n_parts == 1:
-        w_ref[...] = parts[0][...]
-    else:
-        height = w_ref.shape[1] // n_parts
-        for slot, part in enumerate(parts):
-            start = pl.multiple_of((at_ref[0] ^ slot) * height, 32)
-            for j in range(3):
-                w_ref[j, pl.ds(start, height), :] = part[j]
+    a1_ref, qkv_ref, lse_ref, o_ref, w_ref, ot_ref, sems = refs[n_parts:]
+    copies = place_rows(at_ref, parts, w_ref, sems)
     normed, _ = norm_parts(x_ref[...].astype(wide))
     a1 = (normed * vec_ref[0:1, :] + vec_ref[1:2, :]).astype(low)
     a1_ref[...] = a1
+    for copy in copies:
+        copy.wait()
     q = (dot(a1, w_ref[0]) + qv_ref[4:5, :]).astype(low)
     k = dot(a1, w_ref[1]).astype(low)
     v = (dot(a1, w_ref[2]) + qv_ref[5:6, :]).astype(low)
@@ -286,10 +303,12 @@
     heads, parts = refs[:4], refs[4 : 4 + n_parts]
     dn2_refs = refs[4 + n_parts : 8 + n_parts]
     (a2_ref, g_ref, du_ref, own_ref, stat_ref, sums_ref, gub_ref, oo_ref,
-     w_ref, h_ref, n_ref, s_ref, o_ref) = refs[8 + n_parts :]
+     w_ref, h_ref, n_ref, s_ref, o_ref, sems) = refs[8 + n_parts :]
     part_rows = dn2_refs[0].shape[0]
-    place_rows(at_ref, parts, w_ref)
+    copies = place_rows(at_ref, parts, w_ref, sems)
     o_ref[...] = jnp.concatenate([unpack_heads(ref[...]) for ref in heads], axis=1)
+    for copy in copies:
+        copy.wait()
     hidden_state = x_ref[...].astype(wide) + dot(o_ref[...], w_ref[2], NT) + vec_ref[6:7, :]
     h_ref[...] = hidden_state
     normed, inverse = norm_parts(hidden_state)
@@ -347,12 +366,9 @@
         ref[part_rows:, :] = side_part
 
 
-def attend_back_kernel(fast, at_ref, x_ref, a1_ref, qkv_ref, lse_ref, w_ref, *refs):
+def attend_back_kernel(fast, at_ref, x_ref, a1_ref, qkv_ref, lse_ref, w_ref, out_grad_ref, *refs):
     chunks, dn1_refs = refs[:4], refs[4:8]
-    if fast:
-        keep_ref, send_ref, sums_ref, qvsum_ref = refs[8:12]
-    else:
-        whole_ref, sums_ref, qvsum_ref = refs[8:11]
+    grad_refs, (sums_ref, qvsum_ref) = refs[8:-7], refs[-7:-5]
     do_ref, dqt_ref, d_ref, g_ref, dn1_ref = refs[-5:]
     rows, width = x_ref.shape
     part_rows = rows // 4
@@ -360,51 +376,55 @@
         do_ref[rank_rows(at_ref, j, part_rows), :] = unpack_heads(chunks[j][...])
     q, k, v, do = qkv_ref[0], qkv_ref[1], qkv_ref[2], do_ref[...]
     kt = k.T
+    heads_width = q.shape[1]
     for head in range(q.shape[1] // HD):
         cols = slice(head * HD, (head + 1) * HD)
         scores = dot(k[:, cols], q[:, cols], NT) * score_scale
         probs = jnp.exp(scores - lse_ref[head : head + 1, :])
         grad_probs = dot(v[:, cols], do[:, cols], NT)
-        d_ref[2, :, cols] = dot(probs.astype(low), do[:, cols]).astype(low)
+        d_ref[:, 2 * heads_width + head * HD : 2 * heads_width + (head + 1) * HD] = dot(
+            probs.astype(low), do[:, cols]
+        ).astype(low)
         both = probs * grad_probs
         grad_scores = (both - probs * jnp.sum(both, axis=0, keepdims=True)).astype(low)
-        d_ref[1, :, cols] = (dot(grad_scores, q[:, cols]) * score_scale).astype(low)
+        d_ref[:, heads_width + head * HD : heads_width + (head + 1) * HD] = (
+            dot(grad_scores, q[:, cols]) * score_scale
+        ).astype(low)
         dqt_ref[cols, :] = dot(kt[cols, :], grad_scores) * score_scale
-    d_ref[0] = dqt_ref[...].T.astype(low)
-    qvsum_ref[0:1, :] = jnp.sum(d_ref[0].astype(wide), axis=0, keepdims=True)
-    qvsum_ref[1:2, :] = jnp.sum(d_ref[2].astype(wide), axis=0, keepdims=True)
-    dn1 = dot(d_ref[0], w_ref[0], NT) + dot(d_ref[1], w_ref[1], NT) + dot(d_ref[2], w_ref[2], NT)
+    d_ref[:, :heads_width] = dqt_ref[...].T.astype(low)
+    dq, dk, dv = (d_ref[:, j * heads_width : (j + 1) * heads_width] for j in range(3))
+    qvsum_ref[0:1, :] = jnp.sum(dq.astype(wide), axis=0, keepdims=True)
+    qvsum_ref[1:2, :] = jnp.sum(dv.astype(wide), axis=0, keepdims=True)
+    dn1 = dot(dq, w_ref[0], NT) + dot(dk, w_ref[1], NT) + dot(dv, w_ref[2], NT)
     dn1_ref[...] = dn1
     for j, ref in enumerate(dn1_refs):
         ref[...] = dn1_ref[rank_rows(at_ref, j, part_rows), :].astype(low)
     normed, _ = norm_parts(x_ref[...].astype(wide))
     sums_ref[0:1, :] = jnp.sum(dn1 * normed, axis=0, keepdims=True)
     sums_ref[1:2, :] = jnp.sum(dn1, axis=0, keepdims=True)
-    a1t = a1_ref[...].T
-    for which in range(3):
-        grad = dot(a1t, d_ref[which])
-        if fast:
-            g_ref[...] = grad.astype(low)
-            height = width // 8
-            for slot in range(4):
-                mask = (0, 4, 2, 6)[slot]
-                keep_ref[slot // 2, slot % 2, which] = take_rows(at_ref, g_ref, mask, height)
-                send_ref[slot // 2, slot % 2, which] = take_rows(at_ref, g_ref, mask ^ 1, height)
-        else:
-            whole_ref[which] = grad.astype(low)
-
-
-def weight_grad_kernel(fast, masks, at_ref, left_ref, right_ref, *refs):
-    grad = dot(left_ref[...].T, right_ref[...]).astype(low)
-    if not fast:
-        refs[0][...] = grad
-        return
-    keep_ref, send_ref, g_ref = refs
-    g_ref[...] = grad
-    height = grad.shape[0] // 8
-    for slot, mask in enumerate(masks):
-        keep_ref[slot // 2, slot % 2] = take_rows(at_ref, g_ref, mask, height)
-        send_ref[slot // 2, slot % 2] = take_rows(at_ref, g_ref, mask ^ 1, height)
+    grad = jnp.concatenate([out_grad_ref[...], dot(a1_ref[...].T, d_ref[...]).astype(low)], axis=1)
+    if fast:
+        g_ref[...] = grad
+        cut_blocks(at_ref, g_ref, *grad_refs)
+    else:
+        grad_refs[0][...] = grad
+
+
+def cut_blocks(at_ref, source, keep_refs, send_refs):
+    height = source.shape[0] // 8
+    for slot in range(4):
+        keep_refs[slot] = take_rows(at_ref, source, 2 * slot, height)
+        send_refs[slot] = take_rows(at_ref, source, 2 * slot + 1, height)
+
+
+def weight_grad_kernel(at_ref, left_ref, right_ref, out_ref):
+    out_ref[...] = dot(left_ref[...].T, right_ref[...]).astype(low)
+
+
+def mlp_grad_kernel(at_ref, a2_ref, du_ref, c_ref, g_ref, keep_ref, send_ref, grad_ref):
+    for j, (left, right) in enumerate(((a2_ref, du_ref), (c_ref, g_ref))):
+        grad_ref[j] = dot(left[...].T, right[...]).astype(low)
+        cut_blocks(at_ref, grad_ref.at[j], keep_ref.at[:, j], send_ref.at[:, j])
 
 
 def input_kernel(at_ref, x_ref, dh_ref, vec_ref, *refs):
@@ -461,8 +481,18 @@
     cols, ends = vectors.shape[1], up_bias.shape[0]
     both_axes = ("fsdp", "tensor")
 
-    (tiles,) = kernel_call(
-        small_pack_kernel, [((devices, 8, 128), wide)], (at, vectors, up_bias[None])
+    tiles, qkv_low, out_t = kernel_call(
+        first_kernel,
+        [((devices, 8, 128), wide), (qkv_weight.shape, low), ((height, heads_width), low)],
+        (at, vectors, up_bias[None], qkv_weight, out_weight),
+        [
+            pltpu.VMEM(vectors.shape, wide),
+            pltpu.VMEM((1, ends), wide),
+            pltpu.VMEM(qkv_weight.shape, wide),
+            pltpu.VMEM(out_weight.shape, wide),
+            pltpu.SemaphoreType.DMA((4,)),
+        ],
+        hbm=(1, 2, 3, 4),
     )
     small = lax.all_to_all(tiles, both_axes, 0, 0, tiled=True)
     vec, qv, up_local = kernel_call(
@@ -471,12 +501,6 @@
         (at, small),
     )
 
-    (qkv_low,) = kernel_call(
-        functools.partial(round_kernel, False), [(qkv_weight.shape, low)], (at, after(qkv_weight, tiles))
-    )
-    (out_t,) = kernel_call(
-        functools.partial(round_kernel, True), [((height, heads_width), low)], (at, after(out_weight, qkv_low))
-    )
     if fast:
         chips = chips_of(qkv_low)
         qkv_parts = cores_of(chips)
@@ -486,6 +510,12 @@
         weights_kernel,
         [((3, height, width), low)],
         (at, after(up_weight, chips[-1]), down_weight.T, *to_ranks([out_t] * 4)),
+        [
+            pltpu.VMEM(up_weight.shape, wide),
+            pltpu.VMEM(up_weight.shape, wide),
+            pltpu.SemaphoreType.DMA((2,)),
+        ],
+        hbm=(1, 2),
     )
     if fast:
         chips = chips_of(shard)
@@ -501,7 +531,8 @@
             ((3, width, heads_width), low),
         ],
         (at, x, vec, qv, *qkv_parts),
-        [pltpu.VMEM((heads_width, rows), wide)],
+        [pltpu.VMEM((heads_width, rows), wide), pltpu.SemaphoreType.DMA((n,))],
+        free=(4,), hbm=range(5, 4 + n),
     )
     o_parts = rank_gather(o_mine)
     if fast:
@@ -531,42 +562,39 @@
             pltpu.VMEM((rows, width), wide),
             pltpu.VMEM((rows, 128), wide),
             pltpu.VMEM((rows, width), low),
+            pltpu.SemaphoreType.DMA((n,)),
         ],
-    )
-    dn2_got = rank_sum(at, dn2)
-
-    def weight_grad(left, right, masks):
-        shape = (left.shape[1], right.shape[1])
-        cut = (2, 2, height, shape[1])
+        free=range(9, 9 + n),
+    )
+
+    def over_cores(keep, send):
+        cut = keep.shape[1:]
         return kernel_call(
-            functools.partial(weight_grad_kernel, fast, masks),
-            [(cut, low), (cut, low)] if fast else [(shape, low)],
-            (at, left, right),
-            [pltpu.VMEM(shape, low)] if fast else [],
+            quad_kernel, [(cut, wide)] + [(cut, low)] * 3, (at, keep, flip(send, "fsdp", 1))
         )
 
-    def over_cores(grads):
-        keep, send = grads
-        half = keep.shape[1:]
-        return kernel_call(pair_kernel, [(half, wide), (half, low)], (at, keep, flip(send, "fsdp", 1)))
-
-    def over_first(stay, go, mask):
-        block = stay.shape[1:]
-        return kernel_call(across_kernel, [(block, wide), (block, low)], (at, stay, flip(go, "fsdp", mask)))
-
-    along_x, along_y = (0, 4, 2, 6), (0, 2, 4, 6)
-    up_sums = weight_grad(a2, du, along_x)
-    down_sums = weight_grad(c, g, along_y)
+    def over_chips(mine, *go):
+        return [mine] + [flip(part, "fsdp", mask) for part, mask in zip(go, (2, 4, 6))]
+
     if fast:
-        up_sums, down_sums = over_cores(up_sums), over_cores(down_sums)
+        cut = (4, 2, height, hidden)
+        keep, send = kernel_call(
+            mlp_grad_kernel, [(cut, low)] * 2, (at, a2, du, c, g), [pltpu.VMEM((2, width, hidden), low)]
+        )
+        dn2_got, dn2_pair = rank_sum(at, dn2, keep, send)
+        mlp_sums = over_chips(*over_cores(keep, after(send, dn2_pair)))
+    else:
+        (up_grad,) = kernel_call(weight_grad_kernel, [((width, hidden), low)], (at, a2, du))
+        (down_grad,) = kernel_call(weight_grad_kernel, [((width, hidden), low)], (at, c, g))
+        dn2_got, dn2_pair = rank_sum(at, dn2)
+        mlp_sums = summed_on_arrival(jnp.stack([up_grad, down_grad]), 1)
     mlp = kernel_call(
         mlp_out_kernel,
         [block] * 4,
-        (at, g, w_full),
+        (at, after(g, dn2_got[1]), w_full),
         [pltpu.VMEM((rows, width), wide)],
     )
-    held = lax.optimization_barrier((dn2_got, up_sums, down_sums, mlp))
-    dn2_got, up_sums, down_sums, mlp = held
+    dn2_got = lax.optimization_barrier((dn2_got, mlp, mlp_sums))[0]
     dh, dz, gbo, *do = kernel_call(
         mix_kernel,
         [
@@ -578,78 +606,81 @@
         (at, own, stat, c, vec, w_full, *dn2_got),
     )
     do_got = to_ranks(do)
-    out_grads = weight_grad(dz, o_own, along_x)
-    if fast:
-        up_sums, down_sums = over_first(*up_sums, 2), over_first(*down_sums, 4)
-    held = lax.optimization_barrier((do_got, mlp, out_grads, up_sums, down_sums))
-    do_got, mlp, out_grads, up_sums, down_sums = held
-    mlp_got = rank_sum(at, mlp)
-    (output,) = kernel_call(output_kernel, [block], (at, own, vec, *mlp_got))
-    if fast:
-        up_sums = [up_sums[0], flip(up_sums[1], "fsdp", 4)]
-        down_sums = [down_sums[0], flip(down_sums[1], "fsdp", 2)]
-        out_sums = over_first(*over_cores(out_grads), 2)
-        out_sums = [out_sums[0], flip(out_sums[1], "fsdp", 4)]
-    else:
-        up_sums = summed_on_arrival(up_sums[0], 0)
-        down_sums = summed_on_arrival(down_sums[0], 0)
-        out_sums = summed_on_arrival(out_grads[0], 0)
-        out_sums = [out_sums[0], jnp.zeros(out_sums[0].shape, low)]
-    out_sums = to_ranks(
-        kernel_call(ranks_kernel, [((height, heads_width), low)] * 4, (at, *out_sums))
-    )
-
-    cut = (2, 2, 3, height, heads_width)
-    outs = [block] * 4
-    outs += [(cut, low), (cut, low)] if fast else [((3, width, heads_width), low)]
-    outs += [((8, width), wide), ((8, heads_width), wide)]
-    back = kernel_call(
+    (out_grad,) = kernel_call(weight_grad_kernel, [((width, width), low)], (at, dz, o_own))
+
+    def update(sums, weight, first, second, rate, decay):
+        return adamw(weight, sum(part.astype(wide) for part in sums), first, second, rate, decay)
+
+    mlp_sums = lax.optimization_barrier((mlp_sums, dz))[0]
+    up_state = update([part[0] for part in mlp_sums], up_weight, up_first, up_second, 0.08, 0.1)
+    down_state = update(
+        [part[1] for part in mlp_sums], down_weight.T, down_first.T, down_second.T, 0.045, 0.1
+    )
+    mlp_three, mlp_one = flip(mlp[3], "tensor", 1), flip(mlp[1], "tensor", 1)
+    (mlp_two,) = kernel_call(add_kernel, [block], (at, mlp[2], mlp_three))
+    do_got = lax.optimization_barrier((do_got, out_grad, mlp_one, mlp_two, up_state, down_state))[0]
+    down_state = [value.T for value in down_state]
+
+    lanes = width + 3 * heads_width
+    cut = (4, height, lanes)
+    grads = [(cut, low)] * 2 if fast else [((width, lanes), low)]
+    *dn1, sums_one, qv_sums = kernel_call(
         functools.partial(attend_back_kernel, fast),
-        outs,
-        (at, x, a1, qkv, lse, qkv_full, *do_got),
+        [*[block] * 4, *grads, ((8, width), wide), ((8, heads_width), wide)],
+        (at, x, a1, qkv, lse, qkv_full, out_grad, *do_got),
         [
             pltpu.VMEM((rows, heads_width), low),
             pltpu.VMEM((heads_width, rows), wide),
-            pltpu.VMEM((3, rows, heads_width), low),
-            pltpu.VMEM((width, heads_width), low),
+            pltpu.VMEM((rows, 3 * heads_width), low),
+            pltpu.VMEM((width, lanes), low),
             pltpu.VMEM((rows, width), wide),
         ],
     )
-    dn1, sums_one, qv_sums = back[:4], back[-2], back[-1]
-    dn1_got = rank_sum(at, dn1)
+    dn1, grads = dn1[:4], dn1[4:]
+
     if fast:
-        got = flip(back[5], "fsdp", 1)
-        blk = (3, height, heads_width)
-        mine, *go = kernel_call(quad_kernel, [(blk, wide)] + [(blk, low)] * 3, (at, back[4], got))
-        qkv_sums = [mine] + [flip(part, "fsdp", mask) for part, mask in zip(go, (4, 2, 6))]
+        sums = over_cores(*grads)
+        dn1_got, dn1_pair = rank_sum(at, dn1, *sums)
+        sums = over_chips(*sums)
     else:
-        qkv_sums = summed_on_arrival(back[4], 1)
-
+        dn1_got, dn1_pair = rank_sum(at, dn1)
+        sums = summed_on_arrival(grads[0], 0)
+
+    sums_one, mlp_two = lax.optimization_barrier((sums_one, mlp_two, dn1_pair))[:2]
     (tiles,) = kernel_call(
         functools.partial(sums_pack_kernel, cols, ends),
         [((devices, 8, 128), wide)],
         (at, sums_one, sums_two, qv_sums, gbo, gub),
     )
+    (output,) = kernel_call(output_kernel, [block], (at, own, vec, mlp[0], mlp_one, flip(mlp_two, "tensor", 2)))
+    out_sums = to_ranks(kernel_call(ranks_kernel, [((height, heads_width), low)] * 4, (at, *sums)))
     tiles = lax.all_to_all(tiles, both_axes, 0, 0, tiled=True)
+    small_state = (vectors, vector_first, vector_second, up_bias[None], bias_first[None], bias_second[None])
     *vec_state, bias_new, bias_m, bias_s = kernel_call(
         small_adam_kernel,
-        [(vectors.shape, wide)] * 3 + [((1, ends), wide)] * 3,
-        (at, tiles, vectors, vector_first, vector_second, up_bias[None], bias_first[None], bias_second[None]),
-    )
-
-    def update(sums, weight, first, second, rate, decay, turned=False):
-        return kernel_call(
-            functools.partial(adam_kernel, len(sums), turned, rate, decay),
-            [(weight.shape, wide)] * 3,
-            (at, *sums, weight, first, second),
-        )
-
-    up_state = update(up_sums, up_weight, up_first, up_second, 0.08, 0.1)
-    down_state = update(down_sums, down_weight.T, down_first.T, down_second.T, 0.045, 0.1)
-    down_state = [value.T for value in down_state]
-    out_state = update(out_sums, out_weight, out_first, out_second, 0.3, 0.1, True)
+        [(value.shape, wide) for value in small_state],
+        (at, tiles, *small_state),
+        [pltpu.VMEM(value.shape, wide) for value in small_state] + [pltpu.SemaphoreType.DMA((6,))] * 2,
+        hbm=range(2, 8),
+        hbm_outs=True,
+    )
+
+    qkv_sums = [
+        jnp.stack([part[:, width + j * heads_width : width + (j + 1) * heads_width] for j in range(3)]) for part in sums
+    ]
     qkv_state = update(qkv_sums, qkv_weight, qkv_first, qkv_second, 0.08, 0.1)
-
+    out_state = (out_weight, out_first, out_second)
+    sems = pltpu.SemaphoreType.DMA((3,))
+    out_state = kernel_call(
+        functools.partial(adam_kernel, 4, True, ((0.3, 0.1),)),
+        [(value.shape, wide) for value in out_state],
+        (at, *out_sums, *out_state),
+        [pltpu.VMEM(value.shape, wide) for value in out_state] + [sems, sems],
+        hbm=range(5, 8),
+        hbm_outs=True,
+    )
+
+    dn1_got = lax.optimization_barrier((dn1_got, output, qkv_state))[0]
     (input_own,) = kernel_call(
         input_kernel,
         [((part_rows, width), wide)],

time: 179 us -> 156 us (0.87)
  local copies, waits for them, and re-layouts: 28 us -> 6.75 us
  Pallas kernels: 51.9 us -> 43.1 us
  waiting for transfers between devices: 39.9 us -> 43.4 us
  other arithmetic: 0.08 us -> 2.8 us
    unnamed x110 -> x60, local copies, waits for them, and re-layouts: 28 us -> 5.75 us
    pallas_call x32 -> x21, Pallas kernels: 51.9 us -> 43.1 us  [kernel_call(): pl.pallas_call(body, out_shape=[jax.ShapeDtypeStruct(s, d) for s, d in ou...]
    ppermute x48 -> x43, starting transfers between devices: 46.8 us -> 50.2 us  [flip(): return lax.ppermute(value, axis, [(i, i ^ mask) for i in range(size)])]
    sub x0 -> x2, other arithmetic: none -> 2.72 us  [adamw(): weight - rate * (first_hat / (jnp.sqrt(second_hat) + adam_eps) + decay *...]
    ppermute x48 -> x43, waiting for transfers between devices: 39.9 us -> 42.1 us  [flip(): return lax.ppermute(value, axis, [(i, i ^ mask) for i in range(size)])]
  transfers between devices with their start and end apart: 50 -> 45, of which waited for: 14 -> 15; matrix products, arithmetic and copies ran while one was open for 0% -> 2% of each run, Pallas kernels for 23% -> 16%
where the time goes in v3:
time: 156 us
  starting transfers between devices  58.1 us (37%)
  waiting for transfers between devices  43.4 us (28%)
  Pallas kernels  43.1 us (28%)
  local copies, waits for them, and re-layouts  6.75 us (4%)
  other arithmetic  2.8 us (2%)
    ppermute x43, starting transfers between devices, flip(): return lax.ppermute(value, axis, [(i, i ^ mask) for i in range(size)])  50.2 us
    pallas_call x21, Pallas kernels, kernel_call(): pl.pallas_call(body, out_shape=[jax.ShapeDtypeStruct(s, d) for s, d in ou...  43.1 us
    ppermute x43, waiting for transfers between devices, flip(): return lax.ppermute(value, axis, [(i, i ^ mask) for i in range(size)])  42.1 us
    unnamed x60, local copies, waits for them, and re-layouts  5.75 us
    all_to_all x1, starting transfers between devices, body(): small = lax.all_to_all(tiles, both_axes, 0, 0, tiled=True)  5.32 us
  transfers between devices with their start and end apart: 45, of which 15 were waited for; matrix products, arithmetic and copies ran while one was open for 2% of the time, Pallas kernels for 16%

profile of v3, /device:TPU:0, one launch (start us, length us, event | category | flops | bytes accessed | tf_op | source)
XLA Modules:
  0.0 155.6 jit_solution(16342121914219740230)
XLA Ops:
  0.7 2.2 %shard_map.347 = (f32[32,8,128]{2,1,0:T(8,128)}, bf16[3,96,192]{2,1,0:T(8,128)(2,1)S(1)}, bf16[96,192]{1,0:T(8,128)(2,1)S(1)}) custom-call(s32[2]{0:T(128)S(1)} %pad_add_fusion.at_ref, f32[8,24]{1,0:T(8,128)} %refs_0_.3, f32[1,96]{1,0:T(1,128)} %bitcast.74, f32[3,96,192]{2,1,0:T(8,128)} %refs_2_.2, f32[192,96]{1,0:T(8,128)} %refs_4_.1), custom_call_target="tpu_custom_call" | custom-call | tf_op jit(solution)/shard_map/pallas_call | solution.py:41
  3.0 4.0 %collective-permute-start.2 = (bf16[3,96,192]{2,1,0:T(8,128)(2,1)S(1)}, bf16[3,96,192]{2,1,0:T(8,128)(2,1)S(1)}, u32[]{:S(2)}, u32[]{:S(2)}) collective-permute-start(bf16[3,96,192]{2,1,0:T(8,128)(2,1)S(1)} %get-tuple-element.124.refs_0_), channel_id=1, source_target_pairs={{0,24},{4,28},{8,16},{12,20},{16,8},{20,12},{24,0},{28,4},{1,25},{... | collective-permute-start | bytes 331784 | tf_op jit(solution)/shard_map/ppermute | solution.py:61
  7.6 4.0 %collective-permute-start.12 = (bf16[96,192]{1,0:T(8,128)(2,1)S(1)}, bf16[96,192]{1,0:T(8,128)(2,1)S(1)}, u32[]{:S(2)}, u32[]{:S(2)}) collective-permute-start(bf16[96,192]{1,0:T(8,128)(2,1)S(1)} %get-tuple-element.130.refs_0_), channel_id=1, source_target_pairs={{0,3},{1,2},{2,1},{3,0},{4,7},{5,6},{6,5},{7,4},{8,11},{9,10},{10,... | collective-permute-start | bytes 110600 | tf_op jit(solution)/shard_map/ppermute | solution.py:61
  11.6 1.6 %collective-permute-start.10 = (bf16[96,192]{1,0:T(8,128)(2,1)S(1)}, bf16[96,192]{1,0:T(8,128)(2,1)S(1)}, u32[]{:S(2)}, u32[]{:S(2)}) collective-permute-start(bf16[96,192]{1,0:T(8,128)(2,1)S(1)} %get-tuple-element.130.refs_0_), channel_id=1, source_target_pairs={{0,1},{1,0},{2,3},{3,2},{4,5},{5,4},{6,7},{7,6},{8,9},{9,8},{10,11... | collective-permute-start | bytes 110600 | tf_op jit(solution)/shard_map/ppermute | solution.py:61
  13.2 5.3 %all-to-all-start = ((f32[32,8,128]{2,1,0:T(8,128)}), f32[32,8,128]{2,1,0:T(8,128)S(1)}, u32[]{:S(2)}, u32[]{:S(2)}) async-start(f32[32,8,128]{2,1,0:T(8,128)} %get-tuple-element.119), calls=%async_computation | async-start | bytes 262144 | tf_op jit(solution)/shard_map/all_to_all | solution.py:497
  19.2 1.6 %shard_map.350.refs_4_ = bf16[3,96,768]{2,1,0:T(8,128)(2,1)S(1)} custom-call(s32[2]{0:T(128)S(1)} %pad_add_fusion.at_ref, f32[96,768]{1,0:T(8,128)} %up_ref, f32[96,768]{1,0:T(8,128)} %bitcast.68, bf16[96,192]{1,0:T(8,128)(2,1)S(1)} %get-tuple-element.130.refs_0_, bf16[96,192]{1,0:T(8,128)(2,1)S(1)} %collective-permute-done.10.refs_1_, ...), custom_call_target="tpu_custom_call" | custom-call | tf_op jit(solution)/shard_map/pallas_call | solution.py:41
  20.8 2.7 %collective-permute-start.15 = (bf16[3,96,768]{2,1,0:T(8,128)(2,1)S(1)}, bf16[3,96,768]{2,1,0:T(8,128)(2,1)S(1)}, u32[]{:S(2)}, u32[]{:S(2)}) collective-permute-start(bf16[3,96,768]{2,1,0:T(8,128)(2,1)S(1)} %shard_map.350.refs_4_), channel_id=1, source_target_pairs={{0,24},{4,28},{8,16},{12,20},{16,8},{20,12},{24,0},{28,4},{1,25},{... | collective-permute-start | bytes 1327112 | tf_op jit(solution)/shard_map/ppermute | solution.py:61
  25.7 1.3 all-to-all-done.small_ref
  27.7 5.4 %shard_map.349 = (bf16[576,768]{1,0:T(8,128)(2,1)S(1)}, bf16[3,576,192]{2,1,0:T(8,128)(2,1)S(1)}, f32[8,576]{1,0:T(8,128)S(1)}, bf16[864,128]{1,0:T(8,128)(2,1)S(1)}, bf16[3,768,192]{2,1,0:T(8,128)(2,1)S(1)}) custom-call(s32[2]{0:T(128)S(1)} %pad_add_fusion.at_ref, bf16[576,768]{1,0:T(8,128)(2,1)S(1)} %bitcast.61, f32[8,768]{1,0:T(8,128)S(1)} %get-tuple-element.120.vec_ref, ...), custom_call_target="tpu_custom_call" | custom-call | tf_op jit(solution)/shard_map/pallas_call | solution.py:41
  33.1 1.3 collective-permute-start.7
  34.5 2.4 %collective-permute-start.8 = (bf16[864,128]{1,0:T(8,128)(2,1)S(1)}, bf16[864,128]{1,0:T(8,128)(2,1)S(1)}, u32[]{:S(2)}, u32[]{:S(2)}) collective-permute-start(bf16[864,128]{1,0:T(8,128)(2,1)S(1)} %get-tuple-element.128.refs_0_), channel_id=1, source_target_pairs={{0,2},{1,3},{2,0},{3,1},{4,6},{5,7},{6,4},{7,5},{8,10},{9,11},{10,... | collective-permute-start | bytes 663560 | tf_op jit(solution)/shard_map/ppermute | solution.py:61
  36.9 7.3 %collective-permute-done.14.refs_8_ = bf16[3,96,768]{2,1,0:T(8,128)(2,1)} collective-permute-done((bf16[3,96,768]{2,1,0:T(8,128)(2,1)S(1)}, bf16[3,96,768]{2,1,0:T(8,128)(2,1)}, u32[]{:S(2)}, u32[]{:S(2)}) %collective-permute-start.14) | collective-permute-done | bytes 442400 | tf_op jit(solution)/shard_map/ppermute | solution.py:61
  47.7 6.2 %collective-permute-done.9.refs_3_ = bf16[864,128]{1,0:T(8,128)(2,1)S(1)} collective-permute-done((bf16[864,128]{1,0:T(8,128)(2,1)S(1)}, bf16[864,128]{1,0:T(8,128)(2,1)S(1)}, u32[]{:S(2)}, u32[]{:S(2)}) %collective-permute-start.9) | collective-permute-done | bytes 221216 | tf_op jit(solution)/shard_map/ppermute | solution.py:61
  54.9 6.4 %shard_map.351 = (bf16[144,768]{1,0:T(8,128)(2,1)S(1)}, bf16[144,768]{1,0:T(8,128)(2,1)S(1)}, bf16[144,768]{1,0:T(8,128)(2,1)S(1)}, bf16[144,768]{1,0:T(8,128)(2...) custom-call(s32[2]{0:T(128)S(1)} %pad_add_fusion.at_ref, ...), custom_call_target="tpu_custom_call" | custom-call | tf_op jit(solution)/shard_map/pallas_call | solution.py:41
  62.3 2.7 %shard_map.353 = (bf16[4,2,96,768]{3,2,1,0:T(8,128)(2,1)S(1)}, bf16[4,2,96,768]{3,2,1,0:T(8,128)(2,1)S(1)}) custom-call(s32[2]{0:T(128)S(1)} %pad_add_fusion.at_ref, bf16[576,768]{1,0:T(8,128)(2,1)S(1)} %get-tuple-element.154.a2_ref, bf16[576,768]{1,0:T(8,128)(2,1)S(1)} %get-tuple-element.155.du_ref, bf16[576,768]{1,0:T(8,128)(2,1)S(1)} %bitcast.66, ...), custom_call_target="tpu_custom_call" | custom-call | tf_op jit(solution)/shard_map/pallas_call | solution.py:41
  65.1 2.2 %collective-permute-done.22.right_ref = bf16[144,768]{1,0:T(8,128)(2,1)S(1)} collective-permute-done((bf16[144,768]{1,0:T(8,128)(2,1)S(1)}, bf16[144,768]{1,0:T(8,128)(2,1)S(1)}, u32[]{:S(2)}, u32[]{:S(2)}) %collective-permute-start.22) | collective-permute-done | bytes 221216 | tf_op jit(solution)/shard_map/ppermute | solution.py:61
  67.9 1.4 collective-permute-start.20
  69.4 1.4 collective-permute-done.24.got_ref
  71.6 1.8 %collective-permute-start.25 = (bf16[2,96,768]{2,1,0:T(8,128)(2,1)S(1)}, bf16[2,96,768]{2,1,0:T(8,128)(2,1)S(1)}, u32[]{:S(2)}, u32[]{:S(2)}) collective-permute-start(bf16[2,96,768]{2,1,0:T(8,128)(2,1)S(1)} %get-tuple-element.163), channel_id=1, source_target_pairs={{0,8},{4,12},{8,0},{12,4},{16,24},{20,28},{24,16},{28,20},{1,9},{5... | collective-permute-start | bytes 884744 | tf_op jit(solution)/shard_map/ppermute | solution.py:61
  73.4 1.5 collective-permute-start.26
  75.8 1.5 shard_map.352
  77.3 1.4 collective-permute-start.31
  78.7 1.9 %collective-permute-start.23 = (bf16[144,768]{1,0:T(8,128)(2,1)S(1)}, bf16[144,768]{1,0:T(8,128)(2,1)S(1)}, u32[]{:S(2)}, u32[]{:S(2)}) collective-permute-start(bf16[144,768]{1,0:T(8,128)(2,1)S(1)} %shard_map.354), channel_id=1, source_target_pairs={{0,2},{1,3},{2,0},{3,1},{4,6},{5,7},{6,4},{7,5},{8,10},{9,11},{10,... | collective-permute-start | bytes 663560 | tf_op jit(solution)/shard_map/ppermute | solution.py:61
  80.6 8.5 %collective-permute-done.31.right_ref = bf16[144,768]{1,0:T(8,128)(2,1)S(1)} collective-permute-done((bf16[144,768]{1,0:T(8,128)(2,1)S(1)}, bf16[144,768]{1,0:T(8,128)(2,1)S(1)}, u32[]{:S(2)}, u32[]{:S(2)}) %collective-permute-start.31) | collective-permute-done | bytes 221216 | tf_op jit(solution)/shard_map/ppermute | solution.py:61
  89.8 1.2 shard_map.356
  91.1 2.9 %collective-permute-start.28 = (bf16[216,128]{1,0:T(8,128)(2,1)S(1)}, bf16[216,128]{1,0:T(8,128)(2,1)S(1)}, u32[]{:S(2)}, u32[]{:S(2)}) collective-permute-start(bf16[216,128]{1,0:T(8,128)(2,1)S(1)} %get-tuple-element.172), channel_id=1, source_target_pairs={{0,1},{1,0},{2,3},{3,2},{4,5},{5,4},{6,7},{7,6},{8,9},{9,8},{10,11... | collective-permute-start | bytes 165896 | tf_op jit(solution)/shard_map/ppermute | solution.py:61
  94.0 1.8 %collective-permute-start.29 = (bf16[216,128]{1,0:T(8,128)(2,1)S(1)}, bf16[216,128]{1,0:T(8,128)(2,1)S(1)}, u32[]{:S(2)}, u32[]{:S(2)}) collective-permute-start(bf16[216,128]{1,0:T(8,128)(2,1)S(1)} %get-tuple-element.173), channel_id=1, source_target_pairs={{0,2},{1,3},{2,0},{3,1},{4,6},{5,7},{6,4},{7,5},{8,10},{9,11},{10,... | collective-permute-start | bytes 165896 | tf_op jit(solution)/shard_map/ppermute | solution.py:61
  96.5 1.6 %multiply_subtract_fusion.1 = (f32[96,768]{1,0:T(8,128)}, f32[96,768]{1,0:T(8,128)}, f32[96,768]{1,0:T(8,128)}, f32[96,768]{1,0:T(8,128)}, f32[96,768]{1,0:T(8,128)}, /*index=5*/f32[96,768]{1,0:T(8,128)}) fusion(f32[768,96]{0,1:T(8,128)S(1)} %copy-done.16, bf16[2,96,768]{2,1,0:T(8,128)(2,1)S(1)} %collective-permute-done.27, ...), kind=kLoop, calls=%fused_computation.15 | loop fusion | flops 3096576 | bytes 5013504 | tf_op jit(solution)/shard_map/sub | solution.py:443
  99.4 2.4 %collective-permute-done.30.refs_3_ = bf16[216,128]{1,0:T(8,128)(2,1)S(1)} collective-permute-done((bf16[216,128]{1,0:T(8,128)(2,1)S(1)}, bf16[216,128]{1,0:T(8,128)(2,1)S(1)}, u32[]{:S(2)}, u32[]{:S(2)}) %collective-permute-start.30) | collective-permute-done | bytes 55328 | tf_op jit(solution)/shard_map/ppermute | solution.py:61
  101.8 6.3 %shard_map.359 = (bf16[144,768]{1,0:T(8,128)(2,1)S(1)}, bf16[144,768]{1,0:T(8,128)(2,1)S(1)}, bf16[144,768]{1,0:T(8,128)(2,1)S(1)}, bf16[144,768]{1,0:T(8,128)(2...) custom-call(s32[2]{0:T(128)S(1)} %pad_add_fusion.at_ref, ...), custom_call_target="tpu_custom_call" | custom-call | tf_op jit(solution)/shard_map/pallas_call | solution.py:41
  108.3 2.6 %collective-permute-done.33.got_ref = bf16[4,96,1344]{2,1,0:T(8,128)(2,1)S(1)} collective-permute-done((bf16[4,96,1344]{2,1,0:T(8,128)(2,1)S(1)}, bf16[4,96,1344]{2,1,0:T(8,128)(2,1)S(1)}, u32[]{:S(2)}, u32[]{:S(2)}) %collective-permute-start.33) | collective-permute-done | bytes 1032224 | tf_op jit(solution)/shard_map/ppermute | solution.py:61
  110.9 1.5 shard_map.360
  113.5 1.1 collective-permute-start.38
  114.6 1.2 collective-permute-start.39
  117.4 1.4 shard_map.366
  118.7 2.6 %all-to-all-start.1 = ((f32[32,8,128]{2,1,0:T(8,128)}), f32[32,8,128]{2,1,0:T(8,128)S(1)}, u32[]{:S(2)}, u32[]{:S(2)}) async-start(f32[32,8,128]{2,1,0:T(8,128)} %shard_map.366), calls=%async_computation.1 | async-start | bytes 262144 | tf_op jit(solution)/shard_map/all_to_all | solution.py:657
  121.3 1.8 %collective-permute-start.35 = (bf16[144,768]{1,0:T(8,128)(2,1)}, bf16[144,768]{1,0:T(8,128)(2,1)}, u32[]{:S(2)}, u32[]{:S(2)}) collective-permute-start(bf16[144,768]{1,0:T(8,128)(2,1)} %copy-done.13), channel_id=1, source_target_pairs={{0,1},{1,0},{2,3},{3,2},{4,5},{5,4},{6,7},{7,6},{8,9},{9,8},{10,11... | collective-permute-start | bytes 663560 | tf_op jit(solution)/shard_map/ppermute | solution.py:61
  123.1 2.5 %collective-permute-start.34 = (bf16[144,768]{1,0:T(8,128)(2,1)S(1)}, bf16[144,768]{1,0:T(8,128)(2,1)S(1)}, u32[]{:S(2)}, u32[]{:S(2)}) collective-permute-start(bf16[144,768]{1,0:T(8,128)(2,1)S(1)} %shard_map.358), channel_id=1, source_target_pairs={{0,2},{1,3},{2,0},{3,1},{4,6},{5,7},{6,4},{7,5},{8,10},{9,11},{10,... | collective-permute-start | bytes 663560 | tf_op jit(solution)/shard_map/ppermute | solution.py:61
  126.3 7.2 %collective-permute-done.34.three_ref = bf16[144,768]{1,0:T(8,128)(2,1)S(1)} collective-permute-done((bf16[144,768]{1,0:T(8,128)(2,1)S(1)}, bf16[144,768]{1,0:T(8,128)(2,1)S(1)}, u32[]{:S(2)}, u32[]{:S(2)}) %collective-permute-start.34) | collective-permute-done | bytes 221216 | tf_op jit(solution)/shard_map/ppermute | solution.py:61
  133.6 3.4 %collective-permute-start.36 = (bf16[144,768]{1,0:T(8,128)(2,1)}, bf16[144,768]{1,0:T(8,128)(2,1)S(1)}, u32[]{:S(2)}, u32[]{:S(2)}) collective-permute-start(bf16[144,768]{1,0:T(8,128)(2,1)} %copy-done.6), channel_id=1, source_target_pairs={{0,2},{1,3},{2,0},{3,1},{4,6},{5,7},{6,4},{7,5},{8,10},{9,11},{10,... | collective-permute-start | bytes 663560 | tf_op jit(solution)/shard_map/ppermute | solution.py:61
  138.9 1.3 shard_map.362
  140.3 2.0 %shard_map.367 = (f32[8,24]{1,0:T(8,128)}, f32[8,24]{1,0:T(8,128)}, f32[8,24]{1,0:T(8,128)}, f32[1,96]{1,0:T(1,128)}, f32[1,96]{1,0:T(1,128)}, /*index=5*/f32[1,96]{1,0:T(1,128)}) custom-call(s32[2]{0:T(128)S(1)} %pad_add_fusion.at_ref, f32[32,8,128]{2,1,0:T(8,128)S(1)} %all-to-all-done.1.got_ref, f32[8,24]{1,0:T(8,128)} %refs_0_.3, f32[8,24]{1,0:T(8,128)} %refs_1_.1, ...), custom_call_target="tpu_custom_call" | custom-call | tf_op jit(solution)/shard_map/pallas_call | solution.py:41
  143.0 2.2 %collective-permute-start.40 = (bf16[96,192]{1,0:T(8,128)(2,1)S(1)}, bf16[96,192]{1,0:T(8,128)(2,1)S(1)}, u32[]{:S(2)}, u32[]{:S(2)}) collective-permute-start(bf16[96,192]{1,0:T(8,128)(2,1)S(1)} %get-tuple-element.201), channel_id=1, source_target_pairs={{0,1},{1,0},{2,3},{3,2},{4,5},{5,4},{6,7},{7,6},{8,9},{9,8},{10,11... | collective-permute-start | bytes 110600 | tf_op jit(solution)/shard_map/ppermute | solution.py:61
  145.2 2.0 %collective-permute-start.41 = (bf16[96,192]{1,0:T(8,128)(2,1)S(1)}, bf16[96,192]{1,0:T(8,128)(2,1)S(1)}, u32[]{:S(2)}, u32[]{:S(2)}) collective-permute-start(bf16[96,192]{1,0:T(8,128)(2,1)S(1)} %get-tuple-element.202), channel_id=1, source_target_pairs={{0,2},{1,3},{2,0},{3,1},{4,6},{5,7},{6,4},{7,5},{8,10},{9,11},{10,... | collective-permute-start | bytes 110600 | tf_op jit(solution)/shard_map/ppermute | solution.py:61
  148.0 1.1 multiply_subtract_fusion
  149.2 2.1 %shard_map.363 = f32[144,768]{1,0:T(8,128)} custom-call(s32[2]{0:T(128)S(1)} %pad_add_fusion.at_ref, bf16[576,768]{1,0:T(8,128)(2,1)S(1)} %bitcast.64, f32[144,768]{1,0:T(8,128)S(1)} %copy-done.5, f32[8,768]{1,0:T(8,128)S(1)} %get-tuple-element.120.vec_ref, bf16[144,768]{1,0:T(8,128)(2,1)S(1)} %copy-done.10, ...), custom_call_target="tpu_custom_call" | custom-call | tf_op jit(solution)/shard_map/pallas_call | solution.py:41
  151.3 1.8 %collective-permute-done.42.refs_3_ = bf16[96,192]{1,0:T(8,128)(2,1)S(1)} collective-permute-done((bf16[96,192]{1,0:T(8,128)(2,1)S(1)}, bf16[96,192]{1,0:T(8,128)(2,1)S(1)}, u32[]{:S(2)}, u32[]{:S(2)}) %collective-permute-start.42) | collective-permute-done | bytes 36896 | tf_op jit(solution)/shard_map/ppermute | solution.py:61
  153.1 2.4 %shard_map.365 = (f32[192,96]{1,0:T(8,128)}, f32[192,96]{1,0:T(8,128)}, f32[192,96]{1,0:T(8,128)}) custom-call(s32[2]{0:T(128)S(1)} %pad_add_fusion.at_ref, bf16[96,192]{1,0:T(8,128)(2,1)S(1)} %get-tuple-element.200.refs_0_, bf16[96,192]{1,0:T(8,128)(2,1)S(1)} %collective-permute-done.40.refs_1_, bf16[96,192]{1,0:T(8,128)(2,1)S(1)} %collective-permute-done.41.refs_2_, ...), custom_call_target="tpu_custom_call" | custom-call | tf_op jit(solution)/shard_map/pallas_call | solution.py:41
  (130 shorter events, 21.4 us)
Async XLA Ops:
  0.7 27.1 %copy-start = (bf16[1,576,768]{2,1,0:T(8,128)(2,1)S(1)}, bf16[1,576,768]{2,1,0:T(8,128)(2,1)}, u32[]{:S(2)}) copy-start(bf16[1,576,768]{2,1,0:T(8,128)(2,1)} %param.20) | copy-start | bytes 2654212
  3.0 8.6 %collective-permute-start.2 = (bf16[3,96,192]{2,1,0:T(8,128)(2,1)S(1)}, bf16[3,96,192]{2,1,0:T(8,128)(2,1)S(1)}, u32[]{:S(2)}, u32[]{:S(2)}) collective-permute-start(bf16[3,96,192]{2,1,0:T(8,128)(2,1)S(1)} %get-tuple-element.124.refs_0_), channel_id=1, source_target_pairs={{0,24},{4,28},{8,16},{12,20},{16,8},{20,12},{24,0},{28,4},{1,25},{... | collective-permute-start | bytes 331784 | tf_op jit(solution)/shard_map/ppermute | solution.py:61
  7.0 11.6 %collective-permute-start.1 = (bf16[3,96,192]{2,1,0:T(8,128)(2,1)S(1)}, bf16[3,96,192]{2,1,0:T(8,128)(2,1)S(1)}, u32[]{:S(2)}, u32[]{:S(2)}) collective-permute-start(bf16[3,96,192]{2,1,0:T(8,128)(2,1)S(1)} %get-tuple-element.124.refs_0_), channel_id=1, source_target_pairs={{0,16},{4,20},{8,24},{12,28},{16,0},{20,4},{24,8},{28,12},{1,17},{... | collective-permute-start | bytes 331784 | tf_op jit(solution)/shard_map/ppermute | solution.py:61
  7.5 11.1 %collective-permute-start = (bf16[3,96,192]{2,1,0:T(8,128)(2,1)S(1)}, bf16[3,96,192]{2,1,0:T(8,128)(2,1)}, u32[]{:S(2)}, u32[]{:S(2)}) collective-permute-start(bf16[3,96,192]{2,1,0:T(8,128)(2,1)S(1)} %get-tuple-element.124.refs_0_), channel_id=1, source_target_pairs={{0,8},{4,12},{8,0},{12,4},{16,24},{20,28},{24,16},{28,20},{1,9},{5... | collective-permute-start | bytes 331784 | tf_op jit(solution)/shard_map/ppermute | solution.py:61
  7.6 11.6 %collective-permute-start.12 = (bf16[96,192]{1,0:T(8,128)(2,1)S(1)}, bf16[96,192]{1,0:T(8,128)(2,1)S(1)}, u32[]{:S(2)}, u32[]{:S(2)}) collective-permute-start(bf16[96,192]{1,0:T(8,128)(2,1)S(1)} %get-tuple-element.130.refs_0_), channel_id=1, source_target_pairs={{0,3},{1,2},{2,1},{3,0},{4,7},{5,6},{6,5},{7,4},{8,11},{9,10},{10,... | collective-permute-start | bytes 110600 | tf_op jit(solution)/shard_map/ppermute | solution.py:61
  11.6 7.6 %collective-permute-start.11 = (bf16[96,192]{1,0:T(8,128)(2,1)S(1)}, bf16[96,192]{1,0:T(8,128)(2,1)S(1)}, u32[]{:S(2)}, u32[]{:S(2)}) collective-permute-start(bf16[96,192]{1,0:T(8,128)(2,1)S(1)} %get-tuple-element.130.refs_0_), channel_id=1, source_target_pairs={{0,2},{1,3},{2,0},{3,1},{4,6},{5,7},{6,4},{7,5},{8,10},{9,11},{10,... | collective-permute-start | bytes 110600 | tf_op jit(solution)/shard_map/ppermute | solution.py:61
  11.6 16.1 %copy-start.26 = (bf16[3,96,192]{2,1,0:T(8,128)(2,1)}, bf16[3,96,192]{2,1,0:T(8,128)(2,1)S(1)}, u32[]{:S(2)}) copy-start(bf16[3,96,192]{2,1,0:T(8,128)(2,1)S(1)} %collective-permute-done.2.refs_6_) | copy-start | bytes 331780
  11.6 7.6 %collective-permute-start.10 = (bf16[96,192]{1,0:T(8,128)(2,1)S(1)}, bf16[96,192]{1,0:T(8,128)(2,1)S(1)}, u32[]{:S(2)}, u32[]{:S(2)}) collective-permute-start(bf16[96,192]{1,0:T(8,128)(2,1)S(1)} %get-tuple-element.130.refs_0_), channel_id=1, source_target_pairs={{0,1},{1,0},{2,3},{3,2},{4,5},{5,4},{6,7},{7,6},{8,9},{9,8},{10,11... | collective-permute-start | bytes 110600 | tf_op jit(solution)/shard_map/ppermute | solution.py:61
  13.2 13.8 %all-to-all-start = ((f32[32,8,128]{2,1,0:T(8,128)}), f32[32,8,128]{2,1,0:T(8,128)S(1)}, u32[]{:S(2)}, u32[]{:S(2)}) async-start(f32[32,8,128]{2,1,0:T(8,128)} %get-tuple-element.119), calls=%async_computation | async-start | bytes 262144 | tf_op jit(solution)/shard_map/all_to_all | solution.py:497
  18.6 5.8 %collective-permute-start.3 = (bf16[3,96,192]{2,1,0:T(8,128)(2,1)S(1)}, bf16[3,96,192]{2,1,0:T(8,128)(2,1)S(1)}, u32[]{:S(2)}, u32[]{:S(2)}) collective-permute-start(bf16[3,96,192]{2,1,0:T(8,128)(2,1)S(1)} %get-tuple-element.124.refs_0_), channel_id=1, source_target_pairs={{0,4},{4,0},{8,12},{12,8},{16,20},{20,16},{24,28},{28,24},{1,5},{5... | collective-permute-start | bytes 331784 | tf_op jit(solution)/shard_map/ppermute | solution.py:61
  18.9 5.5 %collective-permute-start.4 = (bf16[3,96,192]{2,1,0:T(8,128)(2,1)}, bf16[3,96,192]{2,1,0:T(8,128)(2,1)S(1)}, u32[]{:S(2)}, u32[]{:S(2)}) collective-permute-start(bf16[3,96,192]{2,1,0:T(8,128)(2,1)} %collective-permute-done.refs_2_), channel_id=1, source_target_pairs={{0,4},{4,0},{8,12},{12,8},{16,20},{20,16},{24,28},{28,24},{1,5},{5... | collective-permute-start | bytes 331784 | tf_op jit(solution)/shard_map/ppermute | solution.py:61
  20.8 33.0 %copy-start.1 = (bf16[1,576,768]{2,1,0:T(8,128)(2,1)S(1)}, bf16[1,576,768]{2,1,0:T(8,128)(2,1)}, u32[]{:S(2)}) copy-start(bf16[1,576,768]{2,1,0:T(8,128)(2,1)} %param.21) | copy-start | bytes 2654212
  20.8 16.1 %collective-permute-start.15 = (bf16[3,96,768]{2,1,0:T(8,128)(2,1)S(1)}, bf16[3,96,768]{2,1,0:T(8,128)(2,1)S(1)}, u32[]{:S(2)}, u32[]{:S(2)}) collective-permute-start(bf16[3,96,768]{2,1,0:T(8,128)(2,1)S(1)} %shard_map.350.refs_4_), channel_id=1, source_target_pairs={{0,24},{4,28},{8,16},{12,20},{16,8},{20,12},{24,0},{28,4},{1,25},{... | collective-permute-start | bytes 1327112 | tf_op jit(solution)/shard_map/ppermute | solution.py:61
  23.6 20.6 %collective-permute-start.14 = (bf16[3,96,768]{2,1,0:T(8,128)(2,1)S(1)}, bf16[3,96,768]{2,1,0:T(8,128)(2,1)}, u32[]{:S(2)}, u32[]{:S(2)}) collective-permute-start(bf16[3,96,768]{2,1,0:T(8,128)(2,1)S(1)} %shard_map.350.refs_4_), channel_id=1, source_target_pairs={{0,16},{4,20},{8,24},{12,28},{16,0},{20,4},{24,8},{28,12},{1,17},{... | collective-permute-start | bytes 1327112 | tf_op jit(solution)/shard_map/ppermute | solution.py:61
  24.1 20.1 %collective-permute-start.13 = (bf16[3,96,768]{2,1,0:T(8,128)(2,1)S(1)}, bf16[3,96,768]{2,1,0:T(8,128)(2,1)}, u32[]{:S(2)}, u32[]{:S(2)}) collective-permute-start(bf16[3,96,768]{2,1,0:T(8,128)(2,1)S(1)} %shard_map.350.refs_4_), channel_id=1, source_target_pairs={{0,8},{4,12},{8,0},{12,4},{16,24},{20,28},{24,16},{28,20},{1,9},{5... | collective-permute-start | bytes 1327112 | tf_op jit(solution)/shard_map/ppermute | solution.py:61
  24.4 3.3 %collective-permute-start.5 = (bf16[3,96,192]{2,1,0:T(8,128)(2,1)S(1)}, bf16[3,96,192]{2,1,0:T(8,128)(2,1)}, u32[]{:S(2)}, u32[]{:S(2)}) collective-permute-start(bf16[3,96,192]{2,1,0:T(8,128)(2,1)S(1)} %collective-permute-done.1.refs_4_), channel_id=1, source_target_pairs={{0,4},{4,0},{8,12},{12,8},{16,20},{20,16},{24,28},{28,24},{1,5},{5... | collective-permute-start | bytes 331784 | tf_op jit(solution)/shard_map/ppermute | solution.py:61
  25.7 2.0 %collective-permute-start.6 = (bf16[3,96,192]{2,1,0:T(8,128)(2,1)S(1)}, bf16[3,96,192]{2,1,0:T(8,128)(2,1)}, u32[]{:S(2)}, u32[]{:S(2)}) collective-permute-start(bf16[3,96,192]{2,1,0:T(8,128)(2,1)S(1)} %collective-permute-done.2.refs_6_), channel_id=1, source_target_pairs={{0,4},{4,0},{8,12},{12,8},{16,20},{20,16},{24,28},{28,24},{1,5},{5... | collective-permute-start | bytes 331784 | tf_op jit(solution)/shard_map/ppermute | solution.py:61
  33.1 11.6 %collective-permute-start.7 = (bf16[864,128]{1,0:T(8,128)(2,1)S(1)}, bf16[864,128]{1,0:T(8,128)(2,1)S(1)}, u32[]{:S(2)}, u32[]{:S(2)}) collective-permute-start(bf16[864,128]{1,0:T(8,128)(2,1)S(1)} %get-tuple-element.128.refs_0_), channel_id=1, source_target_pairs={{0,1},{1,0},{2,3},{3,2},{4,5},{5,4},{6,7},{7,6},{8,9},{9,8},{10,11... | collective-permute-start | bytes 663560 | tf_op jit(solution)/shard_map/ppermute | solution.py:61
  34.5 12.9 %collective-permute-start.8 = (bf16[864,128]{1,0:T(8,128)(2,1)S(1)}, bf16[864,128]{1,0:T(8,128)(2,1)S(1)}, u32[]{:S(2)}, u32[]{:S(2)}) collective-permute-start(bf16[864,128]{1,0:T(8,128)(2,1)S(1)} %get-tuple-element.128.refs_0_), channel_id=1, source_target_pairs={{0,2},{1,3},{2,0},{3,1},{4,6},{5,7},{6,4},{7,5},{8,10},{9,11},{10,... | collective-permute-start | bytes 663560 | tf_op jit(solution)/shard_map/ppermute | solution.py:61
  44.7 9.1 %collective-permute-start.16 = (bf16[3,96,768]{2,1,0:T(8,128)(2,1)S(1)}, bf16[3,96,768]{2,1,0:T(8,128)(2,1)S(1)}, u32[]{:S(2)}, u32[]{:S(2)}) collective-permute-start(bf16[3,96,768]{2,1,0:T(8,128)(2,1)S(1)} %shard_map.350.refs_4_), channel_id=1, source_target_pairs={{0,4},{4,0},{8,12},{12,8},{16,20},{20,16},{24,28},{28,24},{1,5},{5... | collective-permute-start | bytes 1327112 | tf_op jit(solution)/shard_map/ppermute | solution.py:61
  44.7 9.1 %collective-permute-start.17 = (bf16[3,96,768]{2,1,0:T(8,128)(2,1)}, bf16[3,96,768]{2,1,0:T(8,128)(2,1)S(1)}, u32[]{:S(2)}, u32[]{:S(2)}) collective-permute-start(bf16[3,96,768]{2,1,0:T(8,128)(2,1)} %collective-permute-done.13.refs_6_), channel_id=1, source_target_pairs={{0,4},{4,0},{8,12},{12,8},{16,20},{20,16},{24,28},{28,24},{1,5},{5... | collective-permute-start | bytes 1327112 | tf_op jit(solution)/shard_map/ppermute | solution.py:61
  45.2 8.6 %collective-permute-start.18 = (bf16[3,96,768]{2,1,0:T(8,128)(2,1)}, bf16[3,96,768]{2,1,0:T(8,128)(2,1)S(1)}, u32[]{:S(2)}, u32[]{:S(2)}) collective-permute-start(bf16[3,96,768]{2,1,0:T(8,128)(2,1)} %collective-permute-done.14.refs_8_), channel_id=1, source_target_pairs={{0,4},{4,0},{8,12},{12,8},{16,20},{20,16},{24,28},{28,24},{1,5},{5... | collective-permute-start | bytes 1327112 | tf_op jit(solution)/shard_map/ppermute | solution.py:61
  45.2 8.6 %collective-permute-start.19 = (bf16[3,96,768]{2,1,0:T(8,128)(2,1)S(1)}, bf16[3,96,768]{2,1,0:T(8,128)(2,1)S(1)}, u32[]{:S(2)}, u32[]{:S(2)}) collective-permute-start(bf16[3,96,768]{2,1,0:T(8,128)(2,1)S(1)} %collective-permute-done.15.refs_10_), channel_id=1, source_target_pairs={{0,4},{4,0},{8,12},{12,8},{16,20},{20,16},{24,28},{28,24},{1,5},{5... | collective-permute-start | bytes 1327112 | tf_op jit(solution)/shard_map/ppermute | solution.py:61
  47.4 6.5 %collective-permute-start.9 = (bf16[864,128]{1,0:T(8,128)(2,1)S(1)}, bf16[864,128]{1,0:T(8,128)(2,1)S(1)}, u32[]{:S(2)}, u32[]{:S(2)}) collective-permute-start(bf16[864,128]{1,0:T(8,128)(2,1)S(1)} %collective-permute-done.8.refs_2_), channel_id=1, source_target_pairs={{0,1},{1,0},{2,3},{3,2},{4,5},{5,4},{6,7},{7,6},{8,9},{9,8},{10,11... | collective-permute-start | bytes 663560 | tf_op jit(solution)/shard_map/ppermute | solution.py:61
  61.3 6.0 %collective-permute-start.22 = (bf16[144,768]{1,0:T(8,128)(2,1)S(1)}, bf16[144,768]{1,0:T(8,128)(2,1)S(1)}, u32[]{:S(2)}, u32[]{:S(2)}) collective-permute-start(bf16[144,768]{1,0:T(8,128)(2,1)S(1)} %get-tuple-element.153), channel_id=1, source_target_pairs={{0,1},{1,0},{2,3},{3,2},{4,5},{5,4},{6,7},{7,6},{8,9},{9,8},{10,11... | collective-permute-start | bytes 663560 | tf_op jit(solution)/shard_map/ppermute | solution.py:61
  67.9 2.9 %collective-permute-start.24 = (bf16[4,2,96,768]{3,2,1,0:T(8,128)(2,1)S(1)}, bf16[4,2,96,768]{3,2,1,0:T(8,128)(2,1)S(1)}, u32[]{:S(2)}, u32[]{:S(2)}) collective-permute-start(bf16[4,2,96,768]{3,2,1,0:T(8,128)(2,1)S(1)} %get-tuple-element.161), channel_id=1, source_target_pairs={{0,4},{4,0},{8,12},{12,8},{16,20},{20,16},{24,28},{28,24},{1,5},{5... | collective-permute-start | bytes 3538952 | tf_op jit(solution)/shard_map/ppermute | solution.py:61
  67.9 7.8 %collective-permute-start.20 = (bf16[144,768]{1,0:T(8,128)(2,1)S(1)}, bf16[144,768]{1,0:T(8,128)(2,1)S(1)}, u32[]{:S(2)}, u32[]{:S(2)}) collective-permute-start(bf16[144,768]{1,0:T(8,128)(2,1)S(1)} %get-tuple-element.141), channel_id=1, source_target_pairs={{0,1},{1,0},{2,3},{3,2},{4,5},{5,4},{6,7},{7,6},{8,9},{9,8},{10,11... | collective-permute-start | bytes 663560 | tf_op jit(solution)/shard_map/ppermute | solution.py:61
  71.6 18.1 %collective-permute-start.25 = (bf16[2,96,768]{2,1,0:T(8,128)(2,1)S(1)}, bf16[2,96,768]{2,1,0:T(8,128)(2,1)S(1)}, u32[]{:S(2)}, u32[]{:S(2)}) collective-permute-start(bf16[2,96,768]{2,1,0:T(8,128)(2,1)S(1)} %get-tuple-element.163), channel_id=1, source_target_pairs={{0,8},{4,12},{8,0},{12,4},{16,24},{20,28},{24,16},{28,20},{1,9},{5... | collective-permute-start | bytes 884744 | tf_op jit(solution)/shard_map/ppermute | solution.py:61
  73.4 16.4 %collective-permute-start.26 = (bf16[2,96,768]{2,1,0:T(8,128)(2,1)S(1)}, bf16[2,96,768]{2,1,0:T(8,128)(2,1)S(1)}, u32[]{:S(2)}, u32[]{:S(2)}) collective-permute-start(bf16[2,96,768]{2,1,0:T(8,128)(2,1)S(1)} %get-tuple-element.164), channel_id=1, source_target_pairs={{0,16},{4,20},{8,24},{12,28},{16,0},{20,4},{24,8},{28,12},{1,17},{... | collective-permute-start | bytes 884744 | tf_op jit(solution)/shard_map/ppermute | solution.py:61
  74.9 14.9 %collective-permute-start.27 = (bf16[2,96,768]{2,1,0:T(8,128)(2,1)S(1)}, bf16[2,96,768]{2,1,0:T(8,128)(2,1)S(1)}, u32[]{:S(2)}, u32[]{:S(2)}) collective-permute-start(bf16[2,96,768]{2,1,0:T(8,128)(2,1)S(1)} %get-tuple-element.165), channel_id=1, source_target_pairs={{0,24},{4,28},{8,16},{12,20},{16,8},{20,12},{24,0},{28,4},{1,25},{... | collective-permute-start | bytes 884744 | tf_op jit(solution)/shard_map/ppermute | solution.py:61
  77.3 11.8 %collective-permute-start.31 = (bf16[144,768]{1,0:T(8,128)(2,1)S(1)}, bf16[144,768]{1,0:T(8,128)(2,1)S(1)}, u32[]{:S(2)}, u32[]{:S(2)}) collective-permute-start(bf16[144,768]{1,0:T(8,128)(2,1)S(1)} %get-tuple-element.160), channel_id=1, source_target_pairs={{0,1},{1,0},{2,3},{3,2},{4,5},{5,4},{6,7},{7,6},{8,9},{9,8},{10,11... | collective-permute-start | bytes 663560 | tf_op jit(solution)/shard_map/ppermute | solution.py:61
  78.7 11.0 %collective-permute-start.23 = (bf16[144,768]{1,0:T(8,128)(2,1)S(1)}, bf16[144,768]{1,0:T(8,128)(2,1)S(1)}, u32[]{:S(2)}, u32[]{:S(2)}) collective-permute-start(bf16[144,768]{1,0:T(8,128)(2,1)S(1)} %shard_map.354), channel_id=1, source_target_pairs={{0,2},{1,3},{2,0},{3,1},{4,6},{5,7},{6,4},{7,5},{8,10},{9,11},{10,... | collective-permute-start | bytes 663560 | tf_op jit(solution)/shard_map/ppermute | solution.py:61
  89.1 10.0 %collective-permute-start.21 = (bf16[144,768]{1,0:T(8,128)(2,1)S(1)}, bf16[144,768]{1,0:T(8,128)(2,1)S(1)}, u32[]{:S(2)}, u32[]{:S(2)}) collective-permute-start(bf16[144,768]{1,0:T(8,128)(2,1)S(1)} %get-tuple-element.145), channel_id=1, source_target_pairs={{0,1},{1,0},{2,3},{3,2},{4,5},{5,4},{6,7},{7,6},{8,9},{9,8},{10,11... | collective-permute-start | bytes 663560 | tf_op jit(solution)/shard_map/ppermute | solution.py:61
  91.1 8.1 %collective-permute-start.28 = (bf16[216,128]{1,0:T(8,128)(2,1)S(1)}, bf16[216,128]{1,0:T(8,128)(2,1)S(1)}, u32[]{:S(2)}, u32[]{:S(2)}) collective-permute-start(bf16[216,128]{1,0:T(8,128)(2,1)S(1)} %get-tuple-element.172), channel_id=1, source_target_pairs={{0,1},{1,0},{2,3},{3,2},{4,5},{5,4},{6,7},{7,6},{8,9},{9,8},{10,11... | collective-permute-start | bytes 165896 | tf_op jit(solution)/shard_map/ppermute | solution.py:61
  94.0 5.3 %collective-permute-start.29 = (bf16[216,128]{1,0:T(8,128)(2,1)S(1)}, bf16[216,128]{1,0:T(8,128)(2,1)S(1)}, u32[]{:S(2)}, u32[]{:S(2)}) collective-permute-start(bf16[216,128]{1,0:T(8,128)(2,1)S(1)} %get-tuple-element.173), channel_id=1, source_target_pairs={{0,2},{1,3},{2,0},{3,1},{4,6},{5,7},{6,4},{7,5},{8,10},{9,11},{10,... | collective-permute-start | bytes 165896 | tf_op jit(solution)/shard_map/ppermute | solution.py:61
  95.8 6.0 %collective-permute-start.30 = (bf16[216,128]{1,0:T(8,128)(2,1)S(1)}, bf16[216,128]{1,0:T(8,128)(2,1)S(1)}, u32[]{:S(2)}, u32[]{:S(2)}) collective-permute-start(bf16[216,128]{1,0:T(8,128)(2,1)S(1)} %get-tuple-element.174), channel_id=1, source_target_pairs={{0,3},{1,2},{2,1},{3,0},{4,7},{5,6},{6,5},{7,4},{8,11},{9,10},{10,... | collective-permute-start | bytes 165896 | tf_op jit(solution)/shard_map/ppermute | solution.py:61
  108.1 2.8 %collective-permute-start.33 = (bf16[4,96,1344]{2,1,0:T(8,128)(2,1)S(1)}, bf16[4,96,1344]{2,1,0:T(8,128)(2,1)S(1)}, u32[]{:S(2)}, u32[]{:S(2)}) collective-permute-start(bf16[4,96,1344]{2,1,0:T(8,128)(2,1)S(1)} %get-tuple-element.187), channel_id=1, source_target_pairs={{0,4},{4,0},{8,12},{12,8},{16,20},{20,16},{24,28},{28,24},{1,5},{5... | collective-permute-start | bytes 3096584 | tf_op jit(solution)/shard_map/ppermute | solution.py:61
  108.2 7.8 %collective-permute-start.32 = (bf16[144,768]{1,0:T(8,128)(2,1)S(1)}, bf16[144,768]{1,0:T(8,128)(2,1)S(1)}, u32[]{:S(2)}, u32[]{:S(2)}) collective-permute-start(bf16[144,768]{1,0:T(8,128)(2,1)S(1)} %get-tuple-element.185), channel_id=1, source_target_pairs={{0,1},{1,0},{2,3},{3,2},{4,5},{5,4},{6,7},{7,6},{8,9},{9,8},{10,11... | collective-permute-start | bytes 663560 | tf_op jit(solution)/shard_map/ppermute | solution.py:61
  112.4 29.9 %collective-permute-start.37 = (bf16[96,1344]{1,0:T(8,128)(2,1)}, bf16[96,1344]{1,0:T(8,128)(2,1)S(1)}, u32[]{:S(2)}, u32[]{:S(2)}) collective-permute-start(bf16[96,1344]{1,0:T(8,128)(2,1)} %get-tuple-element.189), channel_id=1, source_target_pairs={{0,8},{4,12},{8,0},{12,4},{16,24},{20,28},{24,16},{28,20},{1,9},{5... | collective-permute-start | bytes 774152 | tf_op jit(solution)/shard_map/ppermute | solution.py:61
  113.5 28.8 %collective-permute-start.38 = (bf16[96,1344]{1,0:T(8,128)(2,1)}, bf16[96,1344]{1,0:T(8,128)(2,1)S(1)}, u32[]{:S(2)}, u32[]{:S(2)}) collective-permute-start(bf16[96,1344]{1,0:T(8,128)(2,1)} %get-tuple-element.190), channel_id=1, source_target_pairs={{0,16},{4,20},{8,24},{12,28},{16,0},{20,4},{24,8},{28,12},{1,17},{... | collective-permute-start | bytes 774152 | tf_op jit(solution)/shard_map/ppermute | solution.py:61
  114.6 27.7 %collective-permute-start.39 = (bf16[96,1344]{1,0:T(8,128)(2,1)}, bf16[96,1344]{1,0:T(8,128)(2,1)S(1)}, u32[]{:S(2)}, u32[]{:S(2)}) collective-permute-start(bf16[96,1344]{1,0:T(8,128)(2,1)} %get-tuple-element.191), channel_id=1, source_target_pairs={{0,24},{4,28},{8,16},{12,20},{16,8},{20,12},{24,0},{28,4},{1,25},{... | collective-permute-start | bytes 774152 | tf_op jit(solution)/shard_map/ppermute | solution.py:61
  118.7 21.5 %all-to-all-start.1 = ((f32[32,8,128]{2,1,0:T(8,128)}), f32[32,8,128]{2,1,0:T(8,128)S(1)}, u32[]{:S(2)}, u32[]{:S(2)}) async-start(f32[32,8,128]{2,1,0:T(8,128)} %shard_map.366), calls=%async_computation.1 | async-start | bytes 262144 | tf_op jit(solution)/shard_map/all_to_all | solution.py:657
  121.3 27.8 %collective-permute-start.35 = (bf16[144,768]{1,0:T(8,128)(2,1)}, bf16[144,768]{1,0:T(8,128)(2,1)}, u32[]{:S(2)}, u32[]{:S(2)}) collective-permute-start(bf16[144,768]{1,0:T(8,128)(2,1)} %copy-done.13), channel_id=1, source_target_pairs={{0,1},{1,0},{2,3},{3,2},{4,5},{5,4},{6,7},{7,6},{8,9},{9,8},{10,11... | collective-permute-start | bytes 663560 | tf_op jit(solution)/shard_map/ppermute | solution.py:61
  123.1 10.5 %collective-permute-start.34 = (bf16[144,768]{1,0:T(8,128)(2,1)S(1)}, bf16[144,768]{1,0:T(8,128)(2,1)S(1)}, u32[]{:S(2)}, u32[]{:S(2)}) collective-permute-start(bf16[144,768]{1,0:T(8,128)(2,1)S(1)} %shard_map.358), channel_id=1, source_target_pairs={{0,2},{1,3},{2,0},{3,1},{4,6},{5,7},{6,4},{7,5},{8,10},{9,11},{10,... | collective-permute-start | bytes 663560 | tf_op jit(solution)/shard_map/ppermute | solution.py:61
  133.6 15.6 %collective-permute-start.36 = (bf16[144,768]{1,0:T(8,128)(2,1)}, bf16[144,768]{1,0:T(8,128)(2,1)S(1)}, u32[]{:S(2)}, u32[]{:S(2)}) collective-permute-start(bf16[144,768]{1,0:T(8,128)(2,1)} %copy-done.6), channel_id=1, source_target_pairs={{0,2},{1,3},{2,0},{3,1},{4,6},{5,7},{6,4},{7,5},{8,10},{9,11},{10,... | collective-permute-start | bytes 663560 | tf_op jit(solution)/shard_map/ppermute | solution.py:61
  143.0 8.3 %collective-permute-start.40 = (bf16[96,192]{1,0:T(8,128)(2,1)S(1)}, bf16[96,192]{1,0:T(8,128)(2,1)S(1)}, u32[]{:S(2)}, u32[]{:S(2)}) collective-permute-start(bf16[96,192]{1,0:T(8,128)(2,1)S(1)} %get-tuple-element.201), channel_id=1, source_target_pairs={{0,1},{1,0},{2,3},{3,2},{4,5},{5,4},{6,7},{7,6},{8,9},{9,8},{10,11... | collective-permute-start | bytes 110600 | tf_op jit(solution)/shard_map/ppermute | solution.py:61
  145.2 6.1 %collective-permute-start.41 = (bf16[96,192]{1,0:T(8,128)(2,1)S(1)}, bf16[96,192]{1,0:T(8,128)(2,1)S(1)}, u32[]{:S(2)}, u32[]{:S(2)}) collective-permute-start(bf16[96,192]{1,0:T(8,128)(2,1)S(1)} %get-tuple-element.202), channel_id=1, source_target_pairs={{0,2},{1,3},{2,0},{3,1},{4,6},{5,7},{6,4},{7,5},{8,10},{9,11},{10,... | collective-permute-start | bytes 110600 | tf_op jit(solution)/shard_map/ppermute | solution.py:61
  147.2 5.9 %collective-permute-start.42 = (bf16[96,192]{1,0:T(8,128)(2,1)S(1)}, bf16[96,192]{1,0:T(8,128)(2,1)S(1)}, u32[]{:S(2)}, u32[]{:S(2)}) collective-permute-start(bf16[96,192]{1,0:T(8,128)(2,1)S(1)} %get-tuple-element.203), channel_id=1, source_target_pairs={{0,3},{1,2},{2,1},{3,0},{4,7},{5,6},{6,5},{7,4},{8,11},{9,10},{10,... | collective-permute-start | bytes 110600 | tf_op jit(solution)/shard_map/ppermute | solution.py:61
  (27 other events, 149.7 us)

commit v4 on v3

--- a/solution.py
+++ b/solution.py
@@ -189,9 +189,38 @@
 def ranks_kernel(at_ref, *refs):
     parts, out_refs = refs[:-4], refs[-4:]
     width = out_refs[0].shape[1]
-    total = sum(ref[:, : 4 * width].astype(wide) for ref in parts)
+    total = sum(ref[...].astype(wide) for ref in parts)
+    height = total.shape[0]
     for j, ref in enumerate(out_refs):
-        ref[...] = total[:, j * width : (j + 1) * width].astype(low)
+        ref[0:height, :] = total[:, j * width : (j + 1) * width].astype(low)
+        if ref.shape[0] > height:
+            small = total[0:16, 4 * width : 4 * width + 96]
+            cols = 96 // 4
+            vec = jnp.zeros((16, cols), wide)
+            bias = jnp.zeros((1, 96), wide)
+            for other in range(4):
+                here = ((at_ref[1] ^ j) == other).astype(wide)
+                vec += small[:, other * cols : (other + 1) * cols] * here
+                bias += small[8 + other : 9 + other, :] * here
+            ref[height:, :] = jnp.concatenate(
+                [vec, jnp.zeros((16, width - cols - 96), wide), jnp.broadcast_to(bias, (16, 96))], axis=1
+            ).astype(low)
+
+
+def last_kernel(at_ref, *refs):
+    parts, ins, outs, bufs, (in_sems, out_sems) = refs[:4], refs[4:13], refs[13:22], refs[22:31], refs[31:]
+    copies = fetch(list(zip(ins, bufs)), in_sems)
+    total = sum(ref[...].astype(wide) for ref in parts)
+    height, cols, ends = bufs[0].shape[1], bufs[3].shape[1], bufs[6].shape[1]
+    small = total[height : height + 8]
+    grads = (total[0:height].T, small[:, :cols], small[0:1, total.shape[1] - ends :])
+    for copy in copies:
+        copy.wait()
+    states = []
+    for j, (rate, decay) in enumerate(((0.3, 0.1), (0.5, 0.0), (0.7, 0.0))):
+        weight, first, second = (buf[...] for buf in bufs[3 * j : 3 * j + 3])
+        states += adamw(weight, grads[j], first, second, rate, decay)
+    stored(states, bufs, outs, out_sems)
 
 
 def output_kernel(at_ref, own_ref, vec_ref, one_ref, two_ref, three_ref, out_ref):
@@ -367,6 +396,8 @@
 
 
 def attend_back_kernel(fast, at_ref, x_ref, a1_ref, qkv_ref, lse_ref, w_ref, out_grad_ref, *refs):
+    if fast:
+        (two_ref, gbo_ref, gub_ref), refs = refs[:3], refs[3:]
     chunks, dn1_refs = refs[:4], refs[4:8]
     grad_refs, (sums_ref, qvsum_ref) = refs[8:-7], refs[-7:-5]
     do_ref, dqt_ref, d_ref, g_ref, dn1_ref = refs[-5:]
@@ -402,12 +433,30 @@
     normed, _ = norm_parts(x_ref[...].astype(wide))
     sums_ref[0:1, :] = jnp.sum(dn1 * normed, axis=0, keepdims=True)
     sums_ref[1:2, :] = jnp.sum(dn1, axis=0, keepdims=True)
-    grad = jnp.concatenate([out_grad_ref[...], dot(a1_ref[...].T, d_ref[...]).astype(low)], axis=1)
-    if fast:
-        g_ref[...] = grad
-        cut_blocks(at_ref, g_ref, *grad_refs)
-    else:
-        grad_refs[0][...] = grad
+    g_ref[:, :width] = out_grad_ref[...]
+    g_ref[:, g_ref.shape[1] - 3 * heads_width :] = dot(a1_ref[...].T, d_ref[...]).astype(low)
+    if not fast:
+        grad_refs[0][...] = g_ref[...]
+        return
+    height = width // 8
+    ends = gub_ref.shape[1] // 8
+    for j in range(8):
+        span, half = slice(j * height, (j + 1) * height), j % 2
+        here = (at_ref[1] == j // 2).astype(wide)
+        rows_in = [
+            sums_ref[0:2, span],
+            two_ref[0:2, span],
+            qvsum_ref[0:2, half * height : (half + 1) * height] * here,
+            gbo_ref[0:1, span],
+            two_ref[2:3, span],
+        ]
+        rows_in += [gub_ref[0:1, (4 * half + k) * ends : (4 * half + k + 1) * ends] * here for k in range(4)]
+        rows_in += [jnp.zeros((4, height), wide)]
+        small = jnp.concatenate(rows_in, axis=0)
+        g_ref[j * height : j * height + 16, width : width + 128] = jnp.concatenate(
+            [small, jnp.zeros((16, 128 - height), wide)], axis=1
+        ).astype(low)
+    cut_blocks(at_ref, g_ref, *grad_refs)
 
 
 def cut_blocks(at_ref, source, keep_refs, send_refs):
@@ -591,7 +640,7 @@
     mlp = kernel_call(
         mlp_out_kernel,
         [block] * 4,
-        (at, after(g, dn2_got[1]), w_full),
+        (at, after(g, dn2_pair), w_full),
         [pltpu.VMEM((rows, width), wide)],
     )
     dn2_got = lax.optimization_barrier((dn2_got, mlp, mlp_sums))[0]
@@ -618,16 +667,18 @@
     )
     mlp_three, mlp_one = flip(mlp[3], "tensor", 1), flip(mlp[1], "tensor", 1)
     (mlp_two,) = kernel_call(add_kernel, [block], (at, mlp[2], mlp_three))
+    mlp_two = flip(mlp_two, "tensor", 2)
     do_got = lax.optimization_barrier((do_got, out_grad, mlp_one, mlp_two, up_state, down_state))[0]
     down_state = [value.T for value in down_state]
 
-    lanes = width + 3 * heads_width
+    lanes = width + 3 * heads_width + (128 if fast else 0)
+    extra = (sums_two, gbo, gub) if fast else ()
     cut = (4, height, lanes)
     grads = [(cut, low)] * 2 if fast else [((width, lanes), low)]
     *dn1, sums_one, qv_sums = kernel_call(
         functools.partial(attend_back_kernel, fast),
         [*[block] * 4, *grads, ((8, width), wide), ((8, heads_width), wide)],
-        (at, x, a1, qkv, lse, qkv_full, out_grad, *do_got),
+        (at, x, a1, qkv, lse, qkv_full, out_grad, *extra, *do_got),
         [
             pltpu.VMEM((rows, heads_width), low),
             pltpu.VMEM((heads_width, rows), wide),
@@ -646,39 +697,50 @@
         dn1_got, dn1_pair = rank_sum(at, dn1)
         sums = summed_on_arrival(grads[0], 0)
 
-    sums_one, mlp_two = lax.optimization_barrier((sums_one, mlp_two, dn1_pair))[:2]
-    (tiles,) = kernel_call(
-        functools.partial(sums_pack_kernel, cols, ends),
-        [((devices, 8, 128), wide)],
-        (at, sums_one, sums_two, qv_sums, gbo, gub),
-    )
-    (output,) = kernel_call(output_kernel, [block], (at, own, vec, mlp[0], mlp_one, flip(mlp_two, "tensor", 2)))
-    out_sums = to_ranks(kernel_call(ranks_kernel, [((height, heads_width), low)] * 4, (at, *sums)))
-    tiles = lax.all_to_all(tiles, both_axes, 0, 0, tiled=True)
-    small_state = (vectors, vector_first, vector_second, up_bias[None], bias_first[None], bias_second[None])
-    *vec_state, bias_new, bias_m, bias_s = kernel_call(
-        small_adam_kernel,
-        [(value.shape, wide) for value in small_state],
-        (at, tiles, *small_state),
-        [pltpu.VMEM(value.shape, wide) for value in small_state] + [pltpu.SemaphoreType.DMA((6,))] * 2,
-        hbm=range(2, 8),
-        hbm_outs=True,
-    )
-
+    (output,) = kernel_call(output_kernel, [block], (at, own, vec, mlp[0], mlp_one, mlp_two))
     qkv_sums = [
-        jnp.stack([part[:, width + j * heads_width : width + (j + 1) * heads_width] for j in range(3)]) for part in sums
+        jnp.stack([part[:, lanes - j * heads_width : lanes - (j - 1) * heads_width] for j in (3, 2, 1)]) for part in sums
     ]
     qkv_state = update(qkv_sums, qkv_weight, qkv_first, qkv_second, 0.08, 0.1)
+
+    tall = height + (16 if fast else 0)
+    out_sums = to_ranks(kernel_call(ranks_kernel, [((tall, heads_width), low)] * 4, (at, *sums)))
     out_state = (out_weight, out_first, out_second)
-    sems = pltpu.SemaphoreType.DMA((3,))
-    out_state = kernel_call(
-        functools.partial(adam_kernel, 4, True, ((0.3, 0.1),)),
-        [(value.shape, wide) for value in out_state],
-        (at, *out_sums, *out_state),
-        [pltpu.VMEM(value.shape, wide) for value in out_state] + [sems, sems],
-        hbm=range(5, 8),
-        hbm_outs=True,
-    )
+    small_state = (vectors, vector_first, vector_second, up_bias[None], bias_first[None], bias_second[None])
+    if fast:
+        states = out_state + small_state
+        *last, bias_new, bias_m, bias_s = kernel_call(
+            last_kernel,
+            [(value.shape, wide) for value in states],
+            (at, *out_sums, *states),
+            [pltpu.VMEM(value.shape, wide) for value in states] + [pltpu.SemaphoreType.DMA((9,))] * 2,
+            hbm=range(5, 14),
+            hbm_outs=True,
+        )
+        out_state, vec_state = last[:3], last[3:]
+    else:
+        (tiles,) = kernel_call(
+            functools.partial(sums_pack_kernel, cols, ends),
+            [((devices, 8, 128), wide)],
+            (at, sums_one, sums_two, qv_sums, gbo, gub),
+        )
+        tiles = lax.all_to_all(tiles, both_axes, 0, 0, tiled=True)
+        *vec_state, bias_new, bias_m, bias_s = kernel_call(
+            small_adam_kernel,
+            [(value.shape, wide) for value in small_state],
+            (at, tiles, *small_state),
+            [pltpu.VMEM(value.shape, wide) for value in small_state] + [pltpu.SemaphoreType.DMA((6,))] * 2,
+            hbm=range(2, 8),
+            hbm_outs=True,
+        )
+        out_state = kernel_call(
+            functools.partial(adam_kernel, 4, True, ((0.3, 0.1),)),
+            [(value.shape, wide) for value in out_state],
+            (at, *out_sums, *out_state),
+            [pltpu.VMEM(value.shape, wide) for value in out_state] + [pltpu.SemaphoreType.DMA((3,))] * 2,
+            hbm=range(5, 8),
+            hbm_outs=True,
+        )
 
     dn1_got = lax.optimization_barrier((dn1_got, output, qkv_state))[0]
     (input_own,) = kernel_call(

time: 156 us -> 143 us (0.917)
  starting transfers between devices: 58.1 us -> 51.2 us
  local copies, waits for them, and re-layouts: 6.75 us -> 1.78 us
  Pallas kernels: 43.1 us -> 39.2 us
  waiting for transfers between devices: 43.4 us -> 46.8 us
    unnamed x60 -> x30, local copies, waits for them, and re-layouts: 5.75 us -> 1.43 us
    ppermute x43, starting transfers between devices: 50.2 us -> 45.9 us  [flip(): return lax.ppermute(value, axis, [(i, i ^ mask) for i in range(size)])]
    pallas_call x21 -> x19, Pallas kernels: 43.1 us -> 39.2 us  [kernel_call(): pl.pallas_call(body, out_shape=[jax.ShapeDtypeStruct(s, d) for s, d in ou...]
    ppermute x43, waiting for transfers between devices: 42.1 us -> 45.5 us  [flip(): return lax.ppermute(value, axis, [(i, i ^ mask) for i in range(size)])]
    all_to_all x1 -> x0, starting transfers between devices: 2.57 us -> none  [body(): tiles = lax.all_to_all(tiles, both_axes, 0, 0, tiled=True)]
  transfers between devices with their start and end apart: 45 -> 44, of which waited for: 15 -> 18; matrix products, arithmetic and copies ran while one was open for 2% -> 2% of each run, Pallas kernels for 16% -> 14%
where the time goes in v4:
time: 143 us
  starting transfers between devices  51.2 us (36%)
  waiting for transfers between devices  46.8 us (33%)
  Pallas kernels  39.2 us (27%)
  other arithmetic  2.79 us (2%)
  local copies, waits for them, and re-layouts  1.78 us (1%)
    ppermute x43, starting transfers between devices, flip(): return lax.ppermute(value, axis, [(i, i ^ mask) for i in range(size)])  45.9 us
    ppermute x43, waiting for transfers between devices, flip(): return lax.ppermute(value, axis, [(i, i ^ mask) for i in range(size)])  45.5 us
    pallas_call x19, Pallas kernels, kernel_call(): pl.pallas_call(body, out_shape=[jax.ShapeDtypeStruct(s, d) for s, d in ou...  39.2 us
    all_to_all x1, starting transfers between devices, body(): small = lax.all_to_all(tiles, both_axes, 0, 0, tiled=True)  5.32 us
  transfers between devices with their start and end apart: 44, of which 18 were waited for; matrix products, arithmetic and copies ran while one was open for 2% of the time, Pallas kernels for 14%

profile of v4, /device:TPU:0, one launch (start us, length us, event | category | flops | bytes accessed | tf_op | source)
XLA Modules:
  0.0 143.0 jit_solution(4651841768490418021)
XLA Ops:
  0.7 2.2 %shard_map.347 = (f32[32,8,128]{2,1,0:T(8,128)}, bf16[3,96,192]{2,1,0:T(8,128)(2,1)S(1)}, bf16[96,192]{1,0:T(8,128)(2,1)S(1)}) custom-call(s32[2]{0:T(128)S(1)} %pad_add_fusion.at_ref, f32[8,24]{1,0:T(8,128)} %refs_7_.1, f32[1,96]{1,0:T(1,128)} %bitcast.74, f32[3,96,192]{2,1,0:T(8,128)} %refs_2_.1, f32[192,96]{1,0:T(8,128)} %refs_4_.1), custom_call_target="tpu_custom_call" | custom-call | tf_op jit(solution)/shard_map/pallas_call | solution.py:41
  3.0 4.0 %collective-permute-start.2 = (bf16[3,96,192]{2,1,0:T(8,128)(2,1)S(1)}, bf16[3,96,192]{2,1,0:T(8,128)(2,1)S(1)}, u32[]{:S(2)}, u32[]{:S(2)}) collective-permute-start(bf16[3,96,192]{2,1,0:T(8,128)(2,1)S(1)} %get-tuple-element.120.refs_0_), channel_id=1, source_target_pairs={{0,24},{4,28},{8,16},{12,20},{16,8},{20,12},{24,0},{28,4},{1,25},{... | collective-permute-start | bytes 331784 | tf_op jit(solution)/shard_map/ppermute | solution.py:61
  7.6 4.0 %collective-permute-start.12 = (bf16[96,192]{1,0:T(8,128)(2,1)S(1)}, bf16[96,192]{1,0:T(8,128)(2,1)S(1)}, u32[]{:S(2)}, u32[]{:S(2)}) collective-permute-start(bf16[96,192]{1,0:T(8,128)(2,1)S(1)} %get-tuple-element.126.refs_0_), channel_id=1, source_target_pairs={{0,3},{1,2},{2,1},{3,0},{4,7},{5,6},{6,5},{7,4},{8,11},{9,10},{10,... | collective-permute-start | bytes 110600 | tf_op jit(solution)/shard_map/ppermute | solution.py:61
  11.6 1.6 %collective-permute-start.10 = (bf16[96,192]{1,0:T(8,128)(2,1)S(1)}, bf16[96,192]{1,0:T(8,128)(2,1)S(1)}, u32[]{:S(2)}, u32[]{:S(2)}) collective-permute-start(bf16[96,192]{1,0:T(8,128)(2,1)S(1)} %get-tuple-element.126.refs_0_), channel_id=1, source_target_pairs={{0,1},{1,0},{2,3},{3,2},{4,5},{5,4},{6,7},{7,6},{8,9},{9,8},{10,11... | collective-permute-start | bytes 110600 | tf_op jit(solution)/shard_map/ppermute | solution.py:61
  13.2 5.3 %all-to-all-start = ((f32[32,8,128]{2,1,0:T(8,128)}), f32[32,8,128]{2,1,0:T(8,128)S(1)}, u32[]{:S(2)}, u32[]{:S(2)}) async-start(f32[32,8,128]{2,1,0:T(8,128)} %get-tuple-element.115), calls=%async_computation | async-start | bytes 262144 | tf_op jit(solution)/shard_map/all_to_all | solution.py:546
  19.2 1.6 %shard_map.350.refs_4_ = bf16[3,96,768]{2,1,0:T(8,128)(2,1)S(1)} custom-call(s32[2]{0:T(128)S(1)} %pad_add_fusion.at_ref, f32[96,768]{1,0:T(8,128)} %up_ref, f32[96,768]{1,0:T(8,128)} %bitcast.68, bf16[96,192]{1,0:T(8,128)(2,1)S(1)} %get-tuple-element.126.refs_0_, bf16[96,192]{1,0:T(8,128)(2,1)S(1)} %collective-permute-done.10.refs_1_, ...), custom_call_target="tpu_custom_call" | custom-call | tf_op jit(solution)/shard_map/pallas_call | solution.py:41
  20.9 2.7 %collective-permute-start.15 = (bf16[3,96,768]{2,1,0:T(8,128)(2,1)S(1)}, bf16[3,96,768]{2,1,0:T(8,128)(2,1)S(1)}, u32[]{:S(2)}, u32[]{:S(2)}) collective-permute-start(bf16[3,96,768]{2,1,0:T(8,128)(2,1)S(1)} %shard_map.350.refs_4_), channel_id=1, source_target_pairs={{0,24},{4,28},{8,16},{12,20},{16,8},{20,12},{24,0},{28,4},{1,25},{... | collective-permute-start | bytes 1327112 | tf_op jit(solution)/shard_map/ppermute | solution.py:61
  25.8 1.2 all-to-all-done.small_ref
  27.7 5.4 %shard_map.349 = (bf16[576,768]{1,0:T(8,128)(2,1)S(1)}, bf16[3,576,192]{2,1,0:T(8,128)(2,1)S(1)}, f32[8,576]{1,0:T(8,128)S(1)}, bf16[864,128]{1,0:T(8,128)(2,1)S(1)}, bf16[3,768,192]{2,1,0:T(8,128)(2,1)S(1)}) custom-call(s32[2]{0:T(128)S(1)} %pad_add_fusion.at_ref, bf16[576,768]{1,0:T(8,128)(2,1)S(1)} %bitcast.61, f32[8,768]{1,0:T(8,128)S(1)} %get-tuple-element.116.vec_ref, ...), custom_call_target="tpu_custom_call" | custom-call | tf_op jit(solution)/shard_map/pallas_call | solution.py:41
  33.1 1.4 collective-permute-start.7
  34.5 2.4 %collective-permute-start.8 = (bf16[864,128]{1,0:T(8,128)(2,1)S(1)}, bf16[864,128]{1,0:T(8,128)(2,1)S(1)}, u32[]{:S(2)}, u32[]{:S(2)}) collective-permute-start(bf16[864,128]{1,0:T(8,128)(2,1)S(1)} %get-tuple-element.124.refs_0_), channel_id=1, source_target_pairs={{0,2},{1,3},{2,0},{3,1},{4,6},{5,7},{6,4},{7,5},{8,10},{9,11},{10,... | collective-permute-start | bytes 663560 | tf_op jit(solution)/shard_map/ppermute | solution.py:61
  36.9 7.2 %collective-permute-done.14.refs_8_ = bf16[3,96,768]{2,1,0:T(8,128)(2,1)S(1)} collective-permute-done((bf16[3,96,768]{2,1,0:T(8,128)(2,1)S(1)}, bf16[3,96,768]{2,1,0:T(8,128)(2,1)S(1)}, u32[]{:S(2)}, u32[]{:S(2)}) %collective-permute-start.14) | collective-permute-done | bytes 442400 | tf_op jit(solution)/shard_map/ppermute | solution.py:61
  45.8 1.6 %collective-permute-done.8.refs_2_ = bf16[864,128]{1,0:T(8,128)(2,1)S(1)} collective-permute-done((bf16[864,128]{1,0:T(8,128)(2,1)S(1)}, bf16[864,128]{1,0:T(8,128)(2,1)S(1)}, u32[]{:S(2)}, u32[]{:S(2)}) %collective-permute-start.8) | collective-permute-done | bytes 221216 | tf_op jit(solution)/shard_map/ppermute | solution.py:61
  47.7 5.6 %collective-permute-done.9.refs_3_ = bf16[864,128]{1,0:T(8,128)(2,1)S(1)} collective-permute-done((bf16[864,128]{1,0:T(8,128)(2,1)S(1)}, bf16[864,128]{1,0:T(8,128)(2,1)S(1)}, u32[]{:S(2)}, u32[]{:S(2)}) %collective-permute-start.9) | collective-permute-done | bytes 221216 | tf_op jit(solution)/shard_map/ppermute | solution.py:61
  53.4 6.3 %shard_map.351 = (bf16[144,768]{1,0:T(8,128)(2,1)S(1)}, bf16[144,768]{1,0:T(8,128)(2,1)S(1)}, bf16[144,768]{1,0:T(8,128)(2,1)S(1)}, bf16[144,768]{1,0:T(8,128)(2...) custom-call(s32[2]{0:T(128)S(1)} %pad_add_fusion.at_ref, ...), custom_call_target="tpu_custom_call" | custom-call | tf_op jit(solution)/shard_map/pallas_call | solution.py:41
  59.7 1.1 collective-permute-start.20
  60.7 2.7 %shard_map.352 = (bf16[4,2,96,768]{3,2,1,0:T(8,128)(2,1)S(1)}, bf16[4,2,96,768]{3,2,1,0:T(8,128)(2,1)S(1)}) custom-call(s32[2]{0:T(128)S(1)} %pad_add_fusion.at_ref, bf16[576,768]{1,0:T(8,128)(2,1)S(1)} %get-tuple-element.139.a2_ref, bf16[576,768]{1,0:T(8,128)(2,1)S(1)} %get-tuple-element.140.du_ref, bf16[576,768]{1,0:T(8,128)(2,1)S(1)} %bitcast.66, ...), custom_call_target="tpu_custom_call" | custom-call | tf_op jit(solution)/shard_map/pallas_call | solution.py:41
  63.4 2.2 %collective-permute-done.20.right_ref = bf16[144,768]{1,0:T(8,128)(2,1)S(1)} collective-permute-done((bf16[144,768]{1,0:T(8,128)(2,1)S(1)}, bf16[144,768]{1,0:T(8,128)(2,1)S(1)}, u32[]{:S(2)}, u32[]{:S(2)}) %collective-permute-start.20) | collective-permute-done | bytes 221216 | tf_op jit(solution)/shard_map/ppermute | solution.py:61
  66.3 1.5 %shard_map.354 = (bf16[144,768]{1,0:T(8,128)(2,1)S(1)}, bf16[144,768]{1,0:T(8,128)(2,1)S(1)}, bf16[144,768]{1,0:T(8,128)(2,1)S(1)}, bf16[144,768]{1,0:T(8,128)(2,1)S(1)}) custom-call(s32[2]{0:T(128)S(1)} %pad_add_fusion.at_ref, bf16[576,768]{1,0:T(8,128)(2,1)S(1)} %get-tuple-element.144.g_ref, bf16[3,768,768]{2,1,0:T(8,128)(2,1)S(1)} %get-tuple-element.145.w_ref), custom_call_target="tpu_custom_call" | custom-call | tf_op jit(solution)/shard_map/pallas_call | solution.py:41
  67.8 1.1 collective-permute-start.22
  70.0 1.6 %collective-permute-start.27 = (bf16[2,96,768]{2,1,0:T(8,128)(2,1)S(1)}, bf16[2,96,768]{2,1,0:T(8,128)(2,1)S(1)}, u32[]{:S(2)}, u32[]{:S(2)}) collective-permute-start(bf16[2,96,768]{2,1,0:T(8,128)(2,1)S(1)} %get-tuple-element.155), channel_id=1, source_target_pairs={{0,8},{4,12},{8,0},{12,4},{16,24},{20,28},{24,16},{28,20},{1,9},{5... | collective-permute-start | bytes 884744 | tf_op jit(solution)/shard_map/ppermute | solution.py:61
  71.6 1.5 %collective-permute-start.28 = (bf16[2,96,768]{2,1,0:T(8,128)(2,1)S(1)}, bf16[2,96,768]{2,1,0:T(8,128)(2,1)S(1)}, u32[]{:S(2)}, u32[]{:S(2)}) collective-permute-start(bf16[2,96,768]{2,1,0:T(8,128)(2,1)S(1)} %get-tuple-element.156), channel_id=1, source_target_pairs={{0,16},{4,20},{8,24},{12,28},{16,0},{20,4},{24,8},{28,12},{1,17},{... | collective-permute-start | bytes 884744 | tf_op jit(solution)/shard_map/ppermute | solution.py:61
  74.5 1.5 %collective-permute-done.22.right_ref = bf16[144,768]{1,0:T(8,128)(2,1)S(1)} collective-permute-done((bf16[144,768]{1,0:T(8,128)(2,1)S(1)}, bf16[144,768]{1,0:T(8,128)(2,1)S(1)}, u32[]{:S(2)}, u32[]{:S(2)}) %collective-permute-start.22) | collective-permute-done | bytes 221216 | tf_op jit(solution)/shard_map/ppermute | solution.py:61
  76.0 1.4 collective-permute-start.25
  78.0 5.1 %collective-permute-done.24.refs_1_ = bf16[144,768]{1,0:T(8,128)(2,1)S(1)} collective-permute-done((bf16[144,768]{1,0:T(8,128)(2,1)S(1)}, bf16[144,768]{1,0:T(8,128)(2,1)S(1)}, u32[]{:S(2)}, u32[]{:S(2)}) %collective-permute-start.24) | collective-permute-done | bytes 221216 | tf_op jit(solution)/shard_map/ppermute | solution.py:61
  83.1 5.5 %collective-permute-done.25.refs_2_ = bf16[144,768]{1,0:T(8,128)(2,1)S(1)} collective-permute-done((bf16[144,768]{1,0:T(8,128)(2,1)S(1)}, bf16[144,768]{1,0:T(8,128)(2,1)S(1)}, u32[]{:S(2)}, u32[]{:S(2)}) %collective-permute-start.25) | collective-permute-done | bytes 221216 | tf_op jit(solution)/shard_map/ppermute | solution.py:61
  88.7 1.2 shard_map.358
  89.9 3.4 %collective-permute-start.30 = (bf16[216,128]{1,0:T(8,128)(2,1)S(1)}, bf16[216,128]{1,0:T(8,128)(2,1)S(1)}, u32[]{:S(2)}, u32[]{:S(2)}) collective-permute-start(bf16[216,128]{1,0:T(8,128)(2,1)S(1)} %get-tuple-element.172), channel_id=1, source_target_pairs={{0,1},{1,0},{2,3},{3,2},{4,5},{5,4},{6,7},{7,6},{8,9},{9,8},{10,11... | collective-permute-start | bytes 165896 | tf_op jit(solution)/shard_map/ppermute | solution.py:61
  93.3 2.4 %collective-permute-start.32 = (bf16[216,128]{1,0:T(8,128)(2,1)S(1)}, bf16[216,128]{1,0:T(8,128)(2,1)S(1)}, u32[]{:S(2)}, u32[]{:S(2)}) collective-permute-start(bf16[216,128]{1,0:T(8,128)(2,1)S(1)} %get-tuple-element.174), channel_id=1, source_target_pairs={{0,3},{1,2},{2,1},{3,0},{4,7},{5,6},{6,5},{7,4},{8,11},{9,10},{10,... | collective-permute-start | bytes 165896 | tf_op jit(solution)/shard_map/ppermute | solution.py:61
  95.8 1.6 %multiply_subtract_fusion.1 = (f32[96,768]{1,0:T(8,128)}, f32[96,768]{1,0:T(8,128)}, f32[96,768]{1,0:T(8,128)}, f32[96,768]{1,0:T(8,128)}, f32[96,768]{1,0:T(8,128)}, /*index=5*/f32[96,768]{1,0:T(8,128)}) fusion(f32[768,96]{0,1:T(8,128)S(1)} %copy-done.4, bf16[2,96,768]{2,1,0:T(8,128)(2,1)S(1)} %collective-permute-done.29, ...), kind=kLoop, calls=%fused_computation.15 | loop fusion | flops 3096576 | bytes 5013504 | tf_op jit(solution)/shard_map/sub | solution.py:492
  97.4 1.1 shard_map.359.out_grad_ref
  98.5 4.2 %collective-permute-done.23.three_ref = bf16[144,768]{1,0:T(8,128)(2,1)S(1)} collective-permute-done((bf16[144,768]{1,0:T(8,128)(2,1)S(1)}, bf16[144,768]{1,0:T(8,128)(2,1)S(1)}, u32[]{:S(2)}, u32[]{:S(2)}) %collective-permute-start.23) | collective-permute-done | bytes 221216 | tf_op jit(solution)/shard_map/ppermute | solution.py:61
  103.3 6.8 %shard_map.360 = (bf16[144,768]{1,0:T(8,128)(2,1)S(1)}, bf16[144,768]{1,0:T(8,128)(2,1)S(1)}, bf16[144,768]{1,0:T(8,128)(2,1)S(1)}, bf16[144,768]{1,0:T(8,128)(2...) custom-call(s32[2]{0:T(128)S(1)} %pad_add_fusion.at_ref, ...), custom_call_target="tpu_custom_call" | custom-call | tf_op jit(solution)/shard_map/pallas_call | solution.py:41
  110.1 1.1 collective-permute-start.34
  111.2 1.7 %collective-permute-done.35.got_ref = bf16[4,96,1472]{2,1,0:T(8,128)(2,1)S(1)} collective-permute-done((bf16[4,96,1472]{2,1,0:T(8,128)(2,1)S(1)}, bf16[4,96,1472]{2,1,0:T(8,128)(2,1)S(1)}, u32[]{:S(2)}, u32[]{:S(2)}) %collective-permute-start.35) | collective-permute-done | bytes 1130528 | tf_op jit(solution)/shard_map/ppermute | solution.py:61
  113.7 1.7 %collective-permute-start.37 = (bf16[96,1472]{1,0:T(8,128)(2,1)S(1)}, bf16[96,1472]{1,0:T(8,128)(2,1)S(1)}, u32[]{:S(2)}, u32[]{:S(2)}) collective-permute-start(bf16[96,1472]{1,0:T(8,128)(2,1)S(1)} %get-tuple-element.190), channel_id=1, source_target_pairs={{0,8},{4,12},{8,0},{12,4},{16,24},{20,28},{24,16},{28,20},{1,9},{5... | collective-permute-start | bytes 847880 | tf_op jit(solution)/shard_map/ppermute | solution.py:61
  115.5 1.5 %collective-permute-start.38 = (bf16[96,1472]{1,0:T(8,128)(2,1)S(1)}, bf16[96,1472]{1,0:T(8,128)(2,1)S(1)}, u32[]{:S(2)}, u32[]{:S(2)}) collective-permute-start(bf16[96,1472]{1,0:T(8,128)(2,1)S(1)} %get-tuple-element.191), channel_id=1, source_target_pairs={{0,16},{4,20},{8,24},{12,28},{16,0},{20,4},{24,8},{28,12},{1,17},{... | collective-permute-start | bytes 847880 | tf_op jit(solution)/shard_map/ppermute | solution.py:61
  117.3 1.3 shard_map.356
  118.6 1.1 collective-permute-start.33
  120.4 2.2 %collective-permute-start.36 = (bf16[144,768]{1,0:T(8,128)(2,1)S(1)}, bf16[144,768]{1,0:T(8,128)(2,1)S(1)}, u32[]{:S(2)}, u32[]{:S(2)}) collective-permute-start(bf16[144,768]{1,0:T(8,128)(2,1)S(1)} %shard_map.362), channel_id=1, source_target_pairs={{0,2},{1,3},{2,0},{3,1},{4,6},{5,7},{6,4},{7,5},{8,10},{9,11},{10,... | collective-permute-start | bytes 663560 | tf_op jit(solution)/shard_map/ppermute | solution.py:61
  123.6 6.9 %collective-permute-done.38.refs_2_ = bf16[96,1472]{1,0:T(8,128)(2,1)S(1)} collective-permute-done((bf16[96,1472]{1,0:T(8,128)(2,1)S(1)}, bf16[96,1472]{1,0:T(8,128)(2,1)S(1)}, u32[]{:S(2)}, u32[]{:S(2)}) %collective-permute-start.38) | collective-permute-done | bytes 282656 | tf_op jit(solution)/shard_map/ppermute | solution.py:61
  131.2 1.2 collective-permute-start.40
  132.5 1.9 %collective-permute-start.41 = (bf16[112,192]{1,0:T(8,128)(2,1)S(1)}, bf16[112,192]{1,0:T(8,128)(2,1)S(1)}, u32[]{:S(2)}, u32[]{:S(2)}) collective-permute-start(bf16[112,192]{1,0:T(8,128)(2,1)S(1)} %get-tuple-element.199), channel_id=1, source_target_pairs={{0,2},{1,3},{2,0},{3,1},{4,6},{5,7},{6,4},{7,5},{8,10},{9,11},{10,... | collective-permute-start | bytes 129032 | tf_op jit(solution)/shard_map/ppermute | solution.py:61
  134.3 1.3 collective-permute-start.42
  136.0 1.1 multiply_subtract_fusion
  137.1 1.7 %shard_map.363 = f32[144,768]{1,0:T(8,128)} custom-call(s32[2]{0:T(128)S(1)} %pad_add_fusion.at_ref, bf16[576,768]{1,0:T(8,128)(2,1)S(1)} %bitcast.64, f32[144,768]{1,0:T(8,128)S(1)} %get-tuple-element.161.dh_ref, f32[8,768]{1,0:T(8,128)S(1)} %get-tuple-element.116.vec_ref, bf16[144,768]{1,0:T(8,128)(2,1)S(1)} %get-tuple-element.194.refs_0_, ...), custom_call_target="tpu_custom_call" | custom-call | tf_op jit(solution)/shard_map/pallas_call | solution.py:41
  138.9 1.4 %collective-permute-done.42.refs_3_ = bf16[112,192]{1,0:T(8,128)(2,1)S(1)} collective-permute-done((bf16[112,192]{1,0:T(8,128)(2,1)S(1)}, bf16[112,192]{1,0:T(8,128)(2,1)S(1)}, u32[]{:S(2)}, u32[]{:S(2)}) %collective-permute-start.42) | collective-permute-done | bytes 43040 | tf_op jit(solution)/shard_map/ppermute | solution.py:61
  140.3 2.5 %shard_map.365 = (f32[192,96]{1,0:T(8,128)}, f32[192,96]{1,0:T(8,128)}, f32[192,96]{1,0:T(8,128)}, f32[8,24]{1,0:T(8,128)}, f32[8,24]{1,0:T(8,128)}, /*index=5*/...) custom-call(s32[2]{0:T(128)S(1)} %pad_add_fusion.at_ref, ...), custom_call_target="tpu_custom_call" | custom-call | tf_op jit(solution)/shard_map/pallas_call | solution.py:41
  (96 shorter events, 14.4 us)
Async XLA Ops:
  0.7 27.1 %copy-start = (bf16[1,576,768]{2,1,0:T(8,128)(2,1)S(1)}, bf16[1,576,768]{2,1,0:T(8,128)(2,1)}, u32[]{:S(2)}) copy-start(bf16[1,576,768]{2,1,0:T(8,128)(2,1)} %param.20) | copy-start | bytes 2654212
  3.0 8.6 %collective-permute-start.2 = (bf16[3,96,192]{2,1,0:T(8,128)(2,1)S(1)}, bf16[3,96,192]{2,1,0:T(8,128)(2,1)S(1)}, u32[]{:S(2)}, u32[]{:S(2)}) collective-permute-start(bf16[3,96,192]{2,1,0:T(8,128)(2,1)S(1)} %get-tuple-element.120.refs_0_), channel_id=1, source_target_pairs={{0,24},{4,28},{8,16},{12,20},{16,8},{20,12},{24,0},{28,4},{1,25},{... | collective-permute-start | bytes 331784 | tf_op jit(solution)/shard_map/ppermute | solution.py:61
  7.0 11.6 %collective-permute-start.1 = (bf16[3,96,192]{2,1,0:T(8,128)(2,1)S(1)}, bf16[3,96,192]{2,1,0:T(8,128)(2,1)S(1)}, u32[]{:S(2)}, u32[]{:S(2)}) collective-permute-start(bf16[3,96,192]{2,1,0:T(8,128)(2,1)S(1)} %get-tuple-element.120.refs_0_), channel_id=1, source_target_pairs={{0,16},{4,20},{8,24},{12,28},{16,0},{20,4},{24,8},{28,12},{1,17},{... | collective-permute-start | bytes 331784 | tf_op jit(solution)/shard_map/ppermute | solution.py:61
  7.5 11.1 %collective-permute-start = (bf16[3,96,192]{2,1,0:T(8,128)(2,1)S(1)}, bf16[3,96,192]{2,1,0:T(8,128)(2,1)}, u32[]{:S(2)}, u32[]{:S(2)}) collective-permute-start(bf16[3,96,192]{2,1,0:T(8,128)(2,1)S(1)} %get-tuple-element.120.refs_0_), channel_id=1, source_target_pairs={{0,8},{4,12},{8,0},{12,4},{16,24},{20,28},{24,16},{28,20},{1,9},{5... | collective-permute-start | bytes 331784 | tf_op jit(solution)/shard_map/ppermute | solution.py:61
  7.6 11.6 %collective-permute-start.12 = (bf16[96,192]{1,0:T(8,128)(2,1)S(1)}, bf16[96,192]{1,0:T(8,128)(2,1)S(1)}, u32[]{:S(2)}, u32[]{:S(2)}) collective-permute-start(bf16[96,192]{1,0:T(8,128)(2,1)S(1)} %get-tuple-element.126.refs_0_), channel_id=1, source_target_pairs={{0,3},{1,2},{2,1},{3,0},{4,7},{5,6},{6,5},{7,4},{8,11},{9,10},{10,... | collective-permute-start | bytes 110600 | tf_op jit(solution)/shard_map/ppermute | solution.py:61
  11.6 7.6 %collective-permute-start.11 = (bf16[96,192]{1,0:T(8,128)(2,1)S(1)}, bf16[96,192]{1,0:T(8,128)(2,1)S(1)}, u32[]{:S(2)}, u32[]{:S(2)}) collective-permute-start(bf16[96,192]{1,0:T(8,128)(2,1)S(1)} %get-tuple-element.126.refs_0_), channel_id=1, source_target_pairs={{0,2},{1,3},{2,0},{3,1},{4,6},{5,7},{6,4},{7,5},{8,10},{9,11},{10,... | collective-permute-start | bytes 110600 | tf_op jit(solution)/shard_map/ppermute | solution.py:61
  11.6 16.1 %copy-start.11 = (bf16[3,96,192]{2,1,0:T(8,128)(2,1)}, bf16[3,96,192]{2,1,0:T(8,128)(2,1)S(1)}, u32[]{:S(2)}) copy-start(bf16[3,96,192]{2,1,0:T(8,128)(2,1)S(1)} %collective-permute-done.2.refs_6_) | copy-start | bytes 331780
  11.6 7.6 %collective-permute-start.10 = (bf16[96,192]{1,0:T(8,128)(2,1)S(1)}, bf16[96,192]{1,0:T(8,128)(2,1)S(1)}, u32[]{:S(2)}, u32[]{:S(2)}) collective-permute-start(bf16[96,192]{1,0:T(8,128)(2,1)S(1)} %get-tuple-element.126.refs_0_), channel_id=1, source_target_pairs={{0,1},{1,0},{2,3},{3,2},{4,5},{5,4},{6,7},{7,6},{8,9},{9,8},{10,11... | collective-permute-start | bytes 110600 | tf_op jit(solution)/shard_map/ppermute | solution.py:61
  13.2 13.8 %all-to-all-start = ((f32[32,8,128]{2,1,0:T(8,128)}), f32[32,8,128]{2,1,0:T(8,128)S(1)}, u32[]{:S(2)}, u32[]{:S(2)}) async-start(f32[32,8,128]{2,1,0:T(8,128)} %get-tuple-element.115), calls=%async_computation | async-start | bytes 262144 | tf_op jit(solution)/shard_map/all_to_all | solution.py:546
  18.6 5.8 %collective-permute-start.3 = (bf16[3,96,192]{2,1,0:T(8,128)(2,1)S(1)}, bf16[3,96,192]{2,1,0:T(8,128)(2,1)S(1)}, u32[]{:S(2)}, u32[]{:S(2)}) collective-permute-start(bf16[3,96,192]{2,1,0:T(8,128)(2,1)S(1)} %get-tuple-element.120.refs_0_), channel_id=1, source_target_pairs={{0,4},{4,0},{8,12},{12,8},{16,20},{20,16},{24,28},{28,24},{1,5},{5... | collective-permute-start | bytes 331784 | tf_op jit(solution)/shard_map/ppermute | solution.py:61
  18.9 5.5 %collective-permute-start.4 = (bf16[3,96,192]{2,1,0:T(8,128)(2,1)}, bf16[3,96,192]{2,1,0:T(8,128)(2,1)S(1)}, u32[]{:S(2)}, u32[]{:S(2)}) collective-permute-start(bf16[3,96,192]{2,1,0:T(8,128)(2,1)} %collective-permute-done.refs_2_), channel_id=1, source_target_pairs={{0,4},{4,0},{8,12},{12,8},{16,20},{20,16},{24,28},{28,24},{1,5},{5... | collective-permute-start | bytes 331784 | tf_op jit(solution)/shard_map/ppermute | solution.py:61
  20.9 32.5 %copy-start.1 = (bf16[1,576,768]{2,1,0:T(8,128)(2,1)S(1)}, bf16[1,576,768]{2,1,0:T(8,128)(2,1)}, u32[]{:S(2)}) copy-start(bf16[1,576,768]{2,1,0:T(8,128)(2,1)} %param.21) | copy-start | bytes 2654212
  20.9 16.0 %collective-permute-start.15 = (bf16[3,96,768]{2,1,0:T(8,128)(2,1)S(1)}, bf16[3,96,768]{2,1,0:T(8,128)(2,1)S(1)}, u32[]{:S(2)}, u32[]{:S(2)}) collective-permute-start(bf16[3,96,768]{2,1,0:T(8,128)(2,1)S(1)} %shard_map.350.refs_4_), channel_id=1, source_target_pairs={{0,24},{4,28},{8,16},{12,20},{16,8},{20,12},{24,0},{28,4},{1,25},{... | collective-permute-start | bytes 1327112 | tf_op jit(solution)/shard_map/ppermute | solution.py:61
  23.6 20.5 %collective-permute-start.14 = (bf16[3,96,768]{2,1,0:T(8,128)(2,1)S(1)}, bf16[3,96,768]{2,1,0:T(8,128)(2,1)S(1)}, u32[]{:S(2)}, u32[]{:S(2)}) collective-permute-start(bf16[3,96,768]{2,1,0:T(8,128)(2,1)S(1)} %shard_map.350.refs_4_), channel_id=1, source_target_pairs={{0,16},{4,20},{8,24},{12,28},{16,0},{20,4},{24,8},{28,12},{1,17},{... | collective-permute-start | bytes 1327112 | tf_op jit(solution)/shard_map/ppermute | solution.py:61
  24.2 20.1 %collective-permute-start.13 = (bf16[3,96,768]{2,1,0:T(8,128)(2,1)S(1)}, bf16[3,96,768]{2,1,0:T(8,128)(2,1)}, u32[]{:S(2)}, u32[]{:S(2)}) collective-permute-start(bf16[3,96,768]{2,1,0:T(8,128)(2,1)S(1)} %shard_map.350.refs_4_), channel_id=1, source_target_pairs={{0,8},{4,12},{8,0},{12,4},{16,24},{20,28},{24,16},{28,20},{1,9},{5... | collective-permute-start | bytes 1327112 | tf_op jit(solution)/shard_map/ppermute | solution.py:61
  24.4 3.2 %collective-permute-start.5 = (bf16[3,96,192]{2,1,0:T(8,128)(2,1)}, bf16[3,96,192]{2,1,0:T(8,128)(2,1)}, u32[]{:S(2)}, u32[]{:S(2)}) collective-permute-start(bf16[3,96,192]{2,1,0:T(8,128)(2,1)} %copy-done.12), channel_id=1, source_target_pairs={{0,4},{4,0},{8,12},{12,8},{16,20},{20,16},{24,28},{28,24},{1,5},{5... | collective-permute-start | bytes 331784 | tf_op jit(solution)/shard_map/ppermute | solution.py:61
  25.8 1.9 %collective-permute-start.6 = (bf16[3,96,192]{2,1,0:T(8,128)(2,1)S(1)}, bf16[3,96,192]{2,1,0:T(8,128)(2,1)}, u32[]{:S(2)}, u32[]{:S(2)}) collective-permute-start(bf16[3,96,192]{2,1,0:T(8,128)(2,1)S(1)} %collective-permute-done.2.refs_6_), channel_id=1, source_target_pairs={{0,4},{4,0},{8,12},{12,8},{16,20},{20,16},{24,28},{28,24},{1,5},{5... | collective-permute-start | bytes 331784 | tf_op jit(solution)/shard_map/ppermute | solution.py:61
  33.1 11.6 %collective-permute-start.7 = (bf16[864,128]{1,0:T(8,128)(2,1)S(1)}, bf16[864,128]{1,0:T(8,128)(2,1)S(1)}, u32[]{:S(2)}, u32[]{:S(2)}) collective-permute-start(bf16[864,128]{1,0:T(8,128)(2,1)S(1)} %get-tuple-element.124.refs_0_), channel_id=1, source_target_pairs={{0,1},{1,0},{2,3},{3,2},{4,5},{5,4},{6,7},{7,6},{8,9},{9,8},{10,11... | collective-permute-start | bytes 663560 | tf_op jit(solution)/shard_map/ppermute | solution.py:61
  34.5 12.9 %collective-permute-start.8 = (bf16[864,128]{1,0:T(8,128)(2,1)S(1)}, bf16[864,128]{1,0:T(8,128)(2,1)S(1)}, u32[]{:S(2)}, u32[]{:S(2)}) collective-permute-start(bf16[864,128]{1,0:T(8,128)(2,1)S(1)} %get-tuple-element.124.refs_0_), channel_id=1, source_target_pairs={{0,2},{1,3},{2,0},{3,1},{4,6},{5,7},{6,4},{7,5},{8,10},{9,11},{10,... | collective-permute-start | bytes 663560 | tf_op jit(solution)/shard_map/ppermute | solution.py:61
  44.8 8.6 %collective-permute-start.16 = (bf16[3,96,768]{2,1,0:T(8,128)(2,1)S(1)}, bf16[3,96,768]{2,1,0:T(8,128)(2,1)S(1)}, u32[]{:S(2)}, u32[]{:S(2)}) collective-permute-start(bf16[3,96,768]{2,1,0:T(8,128)(2,1)S(1)} %shard_map.350.refs_4_), channel_id=1, source_target_pairs={{0,4},{4,0},{8,12},{12,8},{16,20},{20,16},{24,28},{28,24},{1,5},{5... | collective-permute-start | bytes 1327112 | tf_op jit(solution)/shard_map/ppermute | solution.py:61
  44.8 8.6 %collective-permute-start.17 = (bf16[3,96,768]{2,1,0:T(8,128)(2,1)}, bf16[3,96,768]{2,1,0:T(8,128)(2,1)S(1)}, u32[]{:S(2)}, u32[]{:S(2)}) collective-permute-start(bf16[3,96,768]{2,1,0:T(8,128)(2,1)} %collective-permute-done.13.refs_6_), channel_id=1, source_target_pairs={{0,4},{4,0},{8,12},{12,8},{16,20},{20,16},{24,28},{28,24},{1,5},{5... | collective-permute-start | bytes 1327112 | tf_op jit(solution)/shard_map/ppermute | solution.py:61
  45.3 8.1 %collective-permute-start.18 = (bf16[3,96,768]{2,1,0:T(8,128)(2,1)S(1)}, bf16[3,96,768]{2,1,0:T(8,128)(2,1)S(1)}, u32[]{:S(2)}, u32[]{:S(2)}) collective-permute-start(bf16[3,96,768]{2,1,0:T(8,128)(2,1)S(1)} %collective-permute-done.14.refs_8_), channel_id=1, source_target_pairs={{0,4},{4,0},{8,12},{12,8},{16,20},{20,16},{24,28},{28,24},{1,5},{5... | collective-permute-start | bytes 1327112 | tf_op jit(solution)/shard_map/ppermute | solution.py:61
  45.3 8.1 %collective-permute-start.19 = (bf16[3,96,768]{2,1,0:T(8,128)(2,1)S(1)}, bf16[3,96,768]{2,1,0:T(8,128)(2,1)S(1)}, u32[]{:S(2)}, u32[]{:S(2)}) collective-permute-start(bf16[3,96,768]{2,1,0:T(8,128)(2,1)S(1)} %collective-permute-done.15.refs_10_), channel_id=1, source_target_pairs={{0,4},{4,0},{8,12},{12,8},{16,20},{20,16},{24,28},{28,24},{1,5},{5... | collective-permute-start | bytes 1327112 | tf_op jit(solution)/shard_map/ppermute | solution.py:61
  47.4 5.9 %collective-permute-start.9 = (bf16[864,128]{1,0:T(8,128)(2,1)S(1)}, bf16[864,128]{1,0:T(8,128)(2,1)S(1)}, u32[]{:S(2)}, u32[]{:S(2)}) collective-permute-start(bf16[864,128]{1,0:T(8,128)(2,1)S(1)} %collective-permute-done.8.refs_2_), channel_id=1, source_target_pairs={{0,1},{1,0},{2,3},{3,2},{4,5},{5,4},{6,7},{7,6},{8,9},{9,8},{10,11... | collective-permute-start | bytes 663560 | tf_op jit(solution)/shard_map/ppermute | solution.py:61
  59.7 6.0 %collective-permute-start.20 = (bf16[144,768]{1,0:T(8,128)(2,1)S(1)}, bf16[144,768]{1,0:T(8,128)(2,1)S(1)}, u32[]{:S(2)}, u32[]{:S(2)}) collective-permute-start(bf16[144,768]{1,0:T(8,128)(2,1)S(1)} %get-tuple-element.138), channel_id=1, source_target_pairs={{0,1},{1,0},{2,3},{3,2},{4,5},{5,4},{6,7},{7,6},{8,9},{9,8},{10,11... | collective-permute-start | bytes 663560 | tf_op jit(solution)/shard_map/ppermute | solution.py:61
  66.3 2.9 %collective-permute-start.26 = (bf16[4,2,96,768]{3,2,1,0:T(8,128)(2,1)S(1)}, bf16[4,2,96,768]{3,2,1,0:T(8,128)(2,1)S(1)}, u32[]{:S(2)}, u32[]{:S(2)}) collective-permute-start(bf16[4,2,96,768]{3,2,1,0:T(8,128)(2,1)S(1)} %get-tuple-element.153), channel_id=1, source_target_pairs={{0,4},{4,0},{8,12},{12,8},{16,20},{20,16},{24,28},{28,24},{1,5},{5... | collective-permute-start | bytes 3538952 | tf_op jit(solution)/shard_map/ppermute | solution.py:61
  67.8 8.2 %collective-permute-start.22 = (bf16[144,768]{1,0:T(8,128)(2,1)S(1)}, bf16[144,768]{1,0:T(8,128)(2,1)S(1)}, u32[]{:S(2)}, u32[]{:S(2)}) collective-permute-start(bf16[144,768]{1,0:T(8,128)(2,1)S(1)} %get-tuple-element.149), channel_id=1, source_target_pairs={{0,1},{1,0},{2,3},{3,2},{4,5},{5,4},{6,7},{7,6},{8,9},{9,8},{10,11... | collective-permute-start | bytes 663560 | tf_op jit(solution)/shard_map/ppermute | solution.py:61
  70.0 18.6 %collective-permute-start.27 = (bf16[2,96,768]{2,1,0:T(8,128)(2,1)S(1)}, bf16[2,96,768]{2,1,0:T(8,128)(2,1)S(1)}, u32[]{:S(2)}, u32[]{:S(2)}) collective-permute-start(bf16[2,96,768]{2,1,0:T(8,128)(2,1)S(1)} %get-tuple-element.155), channel_id=1, source_target_pairs={{0,8},{4,12},{8,0},{12,4},{16,24},{20,28},{24,16},{28,20},{1,9},{5... | collective-permute-start | bytes 884744 | tf_op jit(solution)/shard_map/ppermute | solution.py:61
  71.6 17.0 %collective-permute-start.28 = (bf16[2,96,768]{2,1,0:T(8,128)(2,1)S(1)}, bf16[2,96,768]{2,1,0:T(8,128)(2,1)S(1)}, u32[]{:S(2)}, u32[]{:S(2)}) collective-permute-start(bf16[2,96,768]{2,1,0:T(8,128)(2,1)S(1)} %get-tuple-element.156), channel_id=1, source_target_pairs={{0,16},{4,20},{8,24},{12,28},{16,0},{20,4},{24,8},{28,12},{1,17},{... | collective-permute-start | bytes 884744 | tf_op jit(solution)/shard_map/ppermute | solution.py:61
  73.1 15.5 %collective-permute-start.29 = (bf16[2,96,768]{2,1,0:T(8,128)(2,1)S(1)}, bf16[2,96,768]{2,1,0:T(8,128)(2,1)S(1)}, u32[]{:S(2)}, u32[]{:S(2)}) collective-permute-start(bf16[2,96,768]{2,1,0:T(8,128)(2,1)S(1)} %get-tuple-element.157), channel_id=1, source_target_pairs={{0,24},{4,28},{8,16},{12,20},{16,8},{20,12},{24,0},{28,4},{1,25},{... | collective-permute-start | bytes 884744 | tf_op jit(solution)/shard_map/ppermute | solution.py:61
  73.5 9.6 %collective-permute-start.24 = (bf16[144,768]{1,0:T(8,128)(2,1)S(1)}, bf16[144,768]{1,0:T(8,128)(2,1)S(1)}, u32[]{:S(2)}, u32[]{:S(2)}) collective-permute-start(bf16[144,768]{1,0:T(8,128)(2,1)S(1)} %get-tuple-element.152), channel_id=1, source_target_pairs={{0,1},{1,0},{2,3},{3,2},{4,5},{5,4},{6,7},{7,6},{8,9},{9,8},{10,11... | collective-permute-start | bytes 663560 | tf_op jit(solution)/shard_map/ppermute | solution.py:61
  76.0 12.6 %collective-permute-start.25 = (bf16[144,768]{1,0:T(8,128)(2,1)S(1)}, bf16[144,768]{1,0:T(8,128)(2,1)S(1)}, u32[]{:S(2)}, u32[]{:S(2)}) collective-permute-start(bf16[144,768]{1,0:T(8,128)(2,1)S(1)} %shard_map.353), channel_id=1, source_target_pairs={{0,2},{1,3},{2,0},{3,1},{4,6},{5,7},{6,4},{7,5},{8,10},{9,11},{10,... | collective-permute-start | bytes 663560 | tf_op jit(solution)/shard_map/ppermute | solution.py:61
  83.1 15.3 %collective-permute-start.21 = (bf16[144,768]{1,0:T(8,128)(2,1)S(1)}, bf16[144,768]{1,0:T(8,128)(2,1)S(1)}, u32[]{:S(2)}, u32[]{:S(2)}) collective-permute-start(bf16[144,768]{1,0:T(8,128)(2,1)S(1)} %get-tuple-element.147), channel_id=1, source_target_pairs={{0,1},{1,0},{2,3},{3,2},{4,5},{5,4},{6,7},{7,6},{8,9},{9,8},{10,11... | collective-permute-start | bytes 663560 | tf_op jit(solution)/shard_map/ppermute | solution.py:61
  88.6 14.1 %collective-permute-start.23 = (bf16[144,768]{1,0:T(8,128)(2,1)S(1)}, bf16[144,768]{1,0:T(8,128)(2,1)S(1)}, u32[]{:S(2)}, u32[]{:S(2)}) collective-permute-start(bf16[144,768]{1,0:T(8,128)(2,1)S(1)} %shard_map.355), channel_id=1, source_target_pairs={{0,2},{1,3},{2,0},{3,1},{4,6},{5,7},{6,4},{7,5},{8,10},{9,11},{10,... | collective-permute-start | bytes 663560 | tf_op jit(solution)/shard_map/ppermute | solution.py:61
  89.9 12.7 %collective-permute-start.30 = (bf16[216,128]{1,0:T(8,128)(2,1)S(1)}, bf16[216,128]{1,0:T(8,128)(2,1)S(1)}, u32[]{:S(2)}, u32[]{:S(2)}) collective-permute-start(bf16[216,128]{1,0:T(8,128)(2,1)S(1)} %get-tuple-element.172), channel_id=1, source_target_pairs={{0,1},{1,0},{2,3},{3,2},{4,5},{5,4},{6,7},{7,6},{8,9},{9,8},{10,11... | collective-permute-start | bytes 165896 | tf_op jit(solution)/shard_map/ppermute | solution.py:61
  93.3 9.9 %collective-permute-start.31 = (bf16[216,128]{1,0:T(8,128)(2,1)S(1)}, bf16[216,128]{1,0:T(8,128)(2,1)S(1)}, u32[]{:S(2)}, u32[]{:S(2)}) collective-permute-start(bf16[216,128]{1,0:T(8,128)(2,1)S(1)} %get-tuple-element.173), channel_id=1, source_target_pairs={{0,2},{1,3},{2,0},{3,1},{4,6},{5,7},{6,4},{7,5},{8,10},{9,11},{10,... | collective-permute-start | bytes 165896 | tf_op jit(solution)/shard_map/ppermute | solution.py:61
  93.3 9.9 %collective-permute-start.32 = (bf16[216,128]{1,0:T(8,128)(2,1)S(1)}, bf16[216,128]{1,0:T(8,128)(2,1)S(1)}, u32[]{:S(2)}, u32[]{:S(2)}) collective-permute-start(bf16[216,128]{1,0:T(8,128)(2,1)S(1)} %get-tuple-element.174), channel_id=1, source_target_pairs={{0,3},{1,2},{2,1},{3,0},{4,7},{5,6},{6,5},{7,4},{8,11},{9,10},{10,... | collective-permute-start | bytes 165896 | tf_op jit(solution)/shard_map/ppermute | solution.py:61
  110.1 2.8 %collective-permute-start.35 = (bf16[4,96,1472]{2,1,0:T(8,128)(2,1)S(1)}, bf16[4,96,1472]{2,1,0:T(8,128)(2,1)S(1)}, u32[]{:S(2)}, u32[]{:S(2)}) collective-permute-start(bf16[4,96,1472]{2,1,0:T(8,128)(2,1)S(1)} %get-tuple-element.188), channel_id=1, source_target_pairs={{0,4},{4,0},{8,12},{12,8},{16,20},{20,16},{24,28},{28,24},{1,5},{5... | collective-permute-start | bytes 3391496 | tf_op jit(solution)/shard_map/ppermute | solution.py:61
  110.1 9.7 %collective-permute-start.34 = (bf16[144,768]{1,0:T(8,128)(2,1)S(1)}, bf16[144,768]{1,0:T(8,128)(2,1)S(1)}, u32[]{:S(2)}, u32[]{:S(2)}) collective-permute-start(bf16[144,768]{1,0:T(8,128)(2,1)S(1)} %get-tuple-element.186), channel_id=1, source_target_pairs={{0,1},{1,0},{2,3},{3,2},{4,5},{5,4},{6,7},{7,6},{8,9},{9,8},{10,11... | collective-permute-start | bytes 663560 | tf_op jit(solution)/shard_map/ppermute | solution.py:61
  113.7 9.9 %collective-permute-start.37 = (bf16[96,1472]{1,0:T(8,128)(2,1)S(1)}, bf16[96,1472]{1,0:T(8,128)(2,1)S(1)}, u32[]{:S(2)}, u32[]{:S(2)}) collective-permute-start(bf16[96,1472]{1,0:T(8,128)(2,1)S(1)} %get-tuple-element.190), channel_id=1, source_target_pairs={{0,8},{4,12},{8,0},{12,4},{16,24},{20,28},{24,16},{28,20},{1,9},{5... | collective-permute-start | bytes 847880 | tf_op jit(solution)/shard_map/ppermute | solution.py:61
  115.5 15.1 %collective-permute-start.38 = (bf16[96,1472]{1,0:T(8,128)(2,1)S(1)}, bf16[96,1472]{1,0:T(8,128)(2,1)S(1)}, u32[]{:S(2)}, u32[]{:S(2)}) collective-permute-start(bf16[96,1472]{1,0:T(8,128)(2,1)S(1)} %get-tuple-element.191), channel_id=1, source_target_pairs={{0,16},{4,20},{8,24},{12,28},{16,0},{20,4},{24,8},{28,12},{1,17},{... | collective-permute-start | bytes 847880 | tf_op jit(solution)/shard_map/ppermute | solution.py:61
  117.0 13.6 %collective-permute-start.39 = (bf16[96,1472]{1,0:T(8,128)(2,1)S(1)}, bf16[96,1472]{1,0:T(8,128)(2,1)S(1)}, u32[]{:S(2)}, u32[]{:S(2)}) collective-permute-start(bf16[96,1472]{1,0:T(8,128)(2,1)S(1)} %get-tuple-element.192), channel_id=1, source_target_pairs={{0,24},{4,28},{8,16},{12,20},{16,8},{20,12},{24,0},{28,4},{1,25},{... | collective-permute-start | bytes 847880 | tf_op jit(solution)/shard_map/ppermute | solution.py:61
  118.6 18.5 %collective-permute-start.33 = (bf16[144,768]{1,0:T(8,128)(2,1)S(1)}, bf16[144,768]{1,0:T(8,128)(2,1)S(1)}, u32[]{:S(2)}, u32[]{:S(2)}) collective-permute-start(bf16[144,768]{1,0:T(8,128)(2,1)S(1)} %get-tuple-element.184), channel_id=1, source_target_pairs={{0,1},{1,0},{2,3},{3,2},{4,5},{5,4},{6,7},{7,6},{8,9},{9,8},{10,11... | collective-permute-start | bytes 663560 | tf_op jit(solution)/shard_map/ppermute | solution.py:61
  120.4 16.7 %collective-permute-start.36 = (bf16[144,768]{1,0:T(8,128)(2,1)S(1)}, bf16[144,768]{1,0:T(8,128)(2,1)S(1)}, u32[]{:S(2)}, u32[]{:S(2)}) collective-permute-start(bf16[144,768]{1,0:T(8,128)(2,1)S(1)} %shard_map.362), channel_id=1, source_target_pairs={{0,2},{1,3},{2,0},{3,1},{4,6},{5,7},{6,4},{7,5},{8,10},{9,11},{10,... | collective-permute-start | bytes 663560 | tf_op jit(solution)/shard_map/ppermute | solution.py:61
  122.6 13.3 %copy-start.9 = (f32[3,96,192]{2,1,0:T(8,128)S(1)}, f32[3,96,192]{2,1,0:T(8,128)}, u32[]{:S(2)}) copy-start(f32[3,96,192]{2,1,0:T(8,128)} %param.28) | copy-start | bytes 663556
  131.2 7.6 %collective-permute-start.40 = (bf16[112,192]{1,0:T(8,128)(2,1)S(1)}, bf16[112,192]{1,0:T(8,128)(2,1)S(1)}, u32[]{:S(2)}, u32[]{:S(2)}) collective-permute-start(bf16[112,192]{1,0:T(8,128)(2,1)S(1)} %get-tuple-element.198), channel_id=1, source_target_pairs={{0,1},{1,0},{2,3},{3,2},{4,5},{5,4},{6,7},{7,6},{8,9},{9,8},{10,11... | collective-permute-start | bytes 129032 | tf_op jit(solution)/shard_map/ppermute | solution.py:61
  132.5 6.4 %collective-permute-start.41 = (bf16[112,192]{1,0:T(8,128)(2,1)S(1)}, bf16[112,192]{1,0:T(8,128)(2,1)S(1)}, u32[]{:S(2)}, u32[]{:S(2)}) collective-permute-start(bf16[112,192]{1,0:T(8,128)(2,1)S(1)} %get-tuple-element.199), channel_id=1, source_target_pairs={{0,2},{1,3},{2,0},{3,1},{4,6},{5,7},{6,4},{7,5},{8,10},{9,11},{10,... | collective-permute-start | bytes 129032 | tf_op jit(solution)/shard_map/ppermute | solution.py:61
  134.3 6.0 %collective-permute-start.42 = (bf16[112,192]{1,0:T(8,128)(2,1)S(1)}, bf16[112,192]{1,0:T(8,128)(2,1)S(1)}, u32[]{:S(2)}, u32[]{:S(2)}) collective-permute-start(bf16[112,192]{1,0:T(8,128)(2,1)S(1)} %get-tuple-element.200), channel_id=1, source_target_pairs={{0,3},{1,2},{2,1},{3,0},{4,7},{5,6},{6,5},{7,4},{8,11},{9,10},{10,... | collective-permute-start | bytes 129032 | tf_op jit(solution)/shard_map/ppermute | solution.py:61
  (11 other events, 71.4 us)

commit v5 on v4

--- a/solution.py
+++ b/solution.py
@@ -306,7 +306,7 @@
     a1_ref[...] = a1
     for copy in copies:
         copy.wait()
-    q = (dot(a1, w_ref[0]) + qv_ref[4:5, :]).astype(low)
+    q = ((dot(a1, w_ref[0]) + qv_ref[4:5, :]) * score_scale).astype(low)
     k = dot(a1, w_ref[1]).astype(low)
     v = (dot(a1, w_ref[2]) + qv_ref[5:6, :]).astype(low)
     qkv_ref[0] = q
@@ -315,7 +315,7 @@
     vt = v.T
     for head in range(q.shape[1] // HD):
         cols = slice(head * HD, (head + 1) * HD)
-        scores = dot(k[:, cols], q[:, cols], NT) * score_scale
+        scores = dot(k[:, cols], q[:, cols], NT)
         top = jnp.max(scores, axis=0, keepdims=True)
         expos = jnp.exp(scores - top)
         summed = jnp.sum(expos, axis=0, keepdims=True)
@@ -328,16 +328,18 @@
     o_ref[rows:, :] = side_part
 
 
-def mlp_kernel(n_parts, at_ref, x_ref, c_ref, vec_ref, ub_ref, *refs):
-    heads, parts = refs[:4], refs[4 : 4 + n_parts]
-    dn2_refs = refs[4 + n_parts : 8 + n_parts]
-    (a2_ref, g_ref, du_ref, own_ref, stat_ref, sums_ref, gub_ref, oo_ref,
-     w_ref, h_ref, n_ref, s_ref, o_ref, sems) = refs[8 + n_parts :]
+def ready_kernel(at_ref, c_ref, *refs):
+    parts, (w_ref, dg_ref, sems) = refs[:-3], refs[-3:]
+    for copy in place_rows(at_ref, parts, w_ref, sems):
+        copy.wait()
+    dg_ref[...] = dot(c_ref[...], w_ref[1])
+
+
+def mlp_kernel(at_ref, x_ref, c_ref, vec_ref, ub_ref, w_ref, dg_ref, *refs):
+    heads, dn2_refs = refs[:4], refs[4:8]
+    a2_ref, g_ref, du_ref, own_ref, stat_ref, sums_ref, gub_ref, oo_ref, h_ref, n_ref, s_ref, o_ref = refs[8:]
     part_rows = dn2_refs[0].shape[0]
-    copies = place_rows(at_ref, parts, w_ref, sems)
     o_ref[...] = jnp.concatenate([unpack_heads(ref[...]) for ref in heads], axis=1)
-    for copy in copies:
-        copy.wait()
     hidden_state = x_ref[...].astype(wide) + dot(o_ref[...], w_ref[2], NT) + vec_ref[6:7, :]
     h_ref[...] = hidden_state
     normed, inverse = norm_parts(hidden_state)
@@ -347,11 +349,12 @@
     a2_ref[...] = a2
     pre = dot(a2, w_ref[0]) + ub_ref[...]
     square = pre * pre
-    tangent = jnp.tanh(gelu_coef * pre * (1.0 + 0.044715 * square))
-    half = 0.5 * (1.0 + tangent)
-    g_ref[...] = (pre * half).astype(low)
-    slope = half + 0.5 * pre * (1.0 - tangent * tangent) * gelu_coef * (1.0 + 3.0 * 0.044715 * square)
-    du = (dot(c_ref[...], w_ref[1]) * slope).astype(low)
+    tangent = jnp.tanh(pre * (gelu_coef + (0.044715 * gelu_coef) * square))
+    half = 0.5 + 0.5 * tangent
+    active = pre * half
+    g_ref[...] = active.astype(low)
+    slope = half + active * (1.0 - half) * (2.0 * gelu_coef + (6.0 * 0.044715 * gelu_coef) * square)
+    du = (dg_ref[...] * slope).astype(low)
     du_ref[...] = du
     gub_ref[...] = jnp.sum(du.astype(wide), axis=0, keepdims=True)
     own = rank_rows(at_ref, 0, part_rows)
@@ -395,7 +398,7 @@
         ref[part_rows:, :] = side_part
 
 
-def attend_back_kernel(fast, at_ref, x_ref, a1_ref, qkv_ref, lse_ref, w_ref, out_grad_ref, *refs):
+def attend_back_kernel(fast, at_ref, x_ref, a1_ref, qkv_ref, lse_ref, w_ref, *refs):
     if fast:
         (two_ref, gbo_ref, gub_ref), refs = refs[:3], refs[3:]
     chunks, dn1_refs = refs[:4], refs[4:8]
@@ -410,7 +413,7 @@
     heads_width = q.shape[1]
     for head in range(q.shape[1] // HD):
         cols = slice(head * HD, (head + 1) * HD)
-        scores = dot(k[:, cols], q[:, cols], NT) * score_scale
+        scores = dot(k[:, cols], q[:, cols], NT)
         probs = jnp.exp(scores - lse_ref[head : head + 1, :])
         grad_probs = dot(v[:, cols], do[:, cols], NT)
         d_ref[:, 2 * heads_width + head * HD : 2 * heads_width + (head + 1) * HD] = dot(
@@ -418,8 +421,8 @@
         ).astype(low)
         both = probs * grad_probs
         grad_scores = (both - probs * jnp.sum(both, axis=0, keepdims=True)).astype(low)
-        d_ref[:, heads_width + head * HD : heads_width + (head + 1) * HD] = (
-            dot(grad_scores, q[:, cols]) * score_scale
+        d_ref[:, heads_width + head * HD : heads_width + (head + 1) * HD] = dot(
+            grad_scores, q[:, cols]
         ).astype(low)
         dqt_ref[cols, :] = dot(kt[cols, :], grad_scores) * score_scale
     d_ref[:, :heads_width] = dqt_ref[...].T.astype(low)
@@ -433,7 +436,6 @@
     normed, _ = norm_parts(x_ref[...].astype(wide))
     sums_ref[0:1, :] = jnp.sum(dn1 * normed, axis=0, keepdims=True)
     sums_ref[1:2, :] = jnp.sum(dn1, axis=0, keepdims=True)
-    g_ref[:, :width] = out_grad_ref[...]
     g_ref[:, g_ref.shape[1] - 3 * heads_width :] = dot(a1_ref[...].T, d_ref[...]).astype(low)
     if not fast:
         grad_refs[0][...] = g_ref[...]
@@ -453,7 +455,7 @@
         rows_in += [gub_ref[0:1, (4 * half + k) * ends : (4 * half + k + 1) * ends] * here for k in range(4)]
         rows_in += [jnp.zeros((4, height), wide)]
         small = jnp.concatenate(rows_in, axis=0)
-        g_ref[j * height : j * height + 16, width : width + 128] = jnp.concatenate(
+        g_ref[j * height : j * height + 16, 0:128] = jnp.concatenate(
             [small, jnp.zeros((16, 128 - height), wide)], axis=1
         ).astype(low)
     cut_blocks(at_ref, g_ref, *grad_refs)
@@ -468,6 +470,18 @@
 
 def weight_grad_kernel(at_ref, left_ref, right_ref, out_ref):
     out_ref[...] = dot(left_ref[...].T, right_ref[...]).astype(low)
+
+
+def out_grad_kernel(at_ref, left_ref, right_ref, keep_ref, send_ref, grad_ref):
+    grad_ref[...] = dot(left_ref[...].T, right_ref[...]).astype(low)
+    cut_blocks(at_ref, grad_ref, keep_ref, send_ref)
+
+
+def pair_quad_kernel(at_ref, keep_ref, got_ref, more_keep_ref, more_got_ref, *out_refs):
+    first = keep_ref.shape[2]
+    for j, ref in enumerate(out_refs):
+        ref[:, :first] = (keep_ref[j].astype(wide) + got_ref[j].astype(wide)).astype(ref.dtype)
+        ref[:, first:] = (more_keep_ref[j].astype(wide) + more_got_ref[j].astype(wide)).astype(ref.dtype)
 
 
 def mlp_grad_kernel(at_ref, a2_ref, du_ref, c_ref, g_ref, keep_ref, send_ref, grad_ref):
@@ -585,14 +599,21 @@
     )
     o_parts = rank_gather(o_mine)
     if fast:
-        chips = lax.optimization_barrier((*chips, o_parts[1]))[:4]
+        chips = lax.optimization_barrier((*chips, o_parts[1], o_parts[2]))[:4]
         rest_parts = cores_of(chips)
     else:
         rest_parts = [lax.all_gather(shard, "fsdp", axis=1, tiled=True)]
 
     block = ((part_rows, width), low)
-    *dn2, a2, g, du, own, stat, sums_two, gub, o_own, w_full = kernel_call(
-        functools.partial(mlp_kernel, n),
+    w_full, dg = kernel_call(
+        ready_kernel,
+        [((3, width, width), low), ((rows, hidden), wide)],
+        (at, c, *rest_parts),
+        [pltpu.SemaphoreType.DMA((n,))],
+        free=range(2, 2 + n),
+    )
+    *dn2, a2, g, du, own, stat, sums_two, gub, o_own = kernel_call(
+        mlp_kernel,
         [
             *[block] * 4,
             ((rows, width), low),
@@ -603,17 +624,14 @@
             ((8, width), wide),
             ((1, hidden), wide),
             block,
-            ((3, width, hidden), low),
         ],
-        (at, x, c, vec, up_local, *o_parts, *rest_parts),
+        (at, x, c, vec, up_local, w_full, dg, *o_parts),
         [
             pltpu.VMEM((rows, width), wide),
             pltpu.VMEM((rows, width), wide),
             pltpu.VMEM((rows, 128), wide),
             pltpu.VMEM((rows, width), low),
-            pltpu.SemaphoreType.DMA((n,)),
         ],
-        free=range(9, 9 + n),
     )
 
     def over_cores(keep, send):
@@ -655,7 +673,12 @@
         (at, own, stat, c, vec, w_full, *dn2_got),
     )
     do_got = to_ranks(do)
-    (out_grad,) = kernel_call(weight_grad_kernel, [((width, width), low)], (at, dz, o_own))
+    if fast:
+        out_grad = kernel_call(
+            out_grad_kernel, [((4, height, width), low)] * 2, (at, dz, o_own), [pltpu.VMEM((width, width), low)]
+        )
+    else:
+        out_grad = kernel_call(weight_grad_kernel, [((width, width), low)], (at, dz, o_own))
 
     def update(sums, weight, first, second, rate, decay):
         return adamw(weight, sum(part.astype(wide) for part in sums), first, second, rate, decay)
@@ -671,14 +694,14 @@
     do_got = lax.optimization_barrier((do_got, out_grad, mlp_one, mlp_two, up_state, down_state))[0]
     down_state = [value.T for value in down_state]
 
-    lanes = width + 3 * heads_width + (128 if fast else 0)
+    lanes = 3 * heads_width + (128 if fast else 0)
     extra = (sums_two, gbo, gub) if fast else ()
     cut = (4, height, lanes)
     grads = [(cut, low)] * 2 if fast else [((width, lanes), low)]
     *dn1, sums_one, qv_sums = kernel_call(
         functools.partial(attend_back_kernel, fast),
         [*[block] * 4, *grads, ((8, width), wide), ((8, heads_width), wide)],
-        (at, x, a1, qkv, lse, qkv_full, out_grad, *extra, *do_got),
+        (at, x, a1, qkv, lse, qkv_full, *extra, *do_got),
         [
             pltpu.VMEM((rows, heads_width), low),
             pltpu.VMEM((heads_width, rows), wide),
@@ -690,14 +713,17 @@
     dn1, grads = dn1[:4], dn1[4:]
 
     if fast:
-        sums = over_cores(*grads)
+        full = (height, width + lanes)
+        arrived = (out_grad[0], flip(out_grad[1], "fsdp", 1), grads[0], flip(grads[1], "fsdp", 1))
+        sums = kernel_call(pair_quad_kernel, [(full, wide)] + [(full, low)] * 3, (at, *arrived))
         dn1_got, dn1_pair = rank_sum(at, dn1, *sums)
         sums = over_chips(*sums)
     else:
         dn1_got, dn1_pair = rank_sum(at, dn1)
-        sums = summed_on_arrival(grads[0], 0)
-
-    (output,) = kernel_call(output_kernel, [block], (at, own, vec, mlp[0], mlp_one, mlp_two))
+        sums = summed_on_arrival(jnp.concatenate([out_grad[0], grads[0]], axis=1), 0)
+
+    (output,) = kernel_call(output_kernel, [block], (at, after(own, dn1_pair), vec, mlp[0], mlp_one, mlp_two))
+    lanes += width
     qkv_sums = [
         jnp.stack([part[:, lanes - j * heads_width : lanes - (j - 1) * heads_width] for j in (3, 2, 1)]) for part in sums
     ]

time: 143 us -> 140 us (0.979)
  waiting for transfers between devices: 46.8 us -> 37.9 us
  starting transfers between devices: 51.2 us -> 57.2 us
    ppermute x43 -> x44, waiting for transfers between devices: 45.5 us -> 36.6 us  [flip(): return lax.ppermute(value, axis, [(i, i ^ mask) for i in range(size)])]
    ppermute x43 -> x44, starting transfers between devices: 45.9 us -> 51.9 us  [flip(): return lax.ppermute(value, axis, [(i, i ^ mask) for i in range(size)])]
    pallas_call x19 -> x20, Pallas kernels: 39.2 us -> 39.2 us  [kernel_call(): pl.pallas_call(body, out_shape=[jax.ShapeDtypeStruct(s, d) for s, d in ou...]
  transfers between devices with their start and end apart: 44 -> 45, of which waited for: 18 -> 20; matrix products, arithmetic and copies ran while one was open for 2% -> 2% of each run, Pallas kernels for 14% -> 21%
where the time goes in v5:
time: 140 us
  starting transfers between devices  57.2 us (41%)
  Pallas kernels  39.2 us (28%)
  waiting for transfers between devices  37.9 us (27%)
  other arithmetic  2.81 us (2%)
  local copies, waits for them, and re-layouts  1.72 us (1%)
    ppermute x44, starting transfers between devices, flip(): return lax.ppermute(value, axis, [(i, i ^ mask) for i in range(size)])  51.9 us
    pallas_call x20, Pallas kernels, kernel_call(): pl.pallas_call(body, out_shape=[jax.ShapeDtypeStruct(s, d) for s, d in ou...  39.2 us
    ppermute x44, waiting for transfers between devices, flip(): return lax.ppermute(value, axis, [(i, i ^ mask) for i in range(size)])  36.6 us
    all_to_all x1, starting transfers between devices, body(): small = lax.all_to_all(tiles, both_axes, 0, 0, tiled=True)  5.32 us
  transfers between devices with their start and end apart: 45, of which 20 were waited for; matrix products, arithmetic and copies ran while one was open for 2% of the time, Pallas kernels for 21%

profile of v5, /device:TPU:0, one launch (start us, length us, event | category | flops | bytes accessed | tf_op | source)
XLA Modules:
  0.0 140.1 jit_solution(2090248841444730685)
XLA Ops:
  0.7 2.2 %shard_map.347 = (f32[32,8,128]{2,1,0:T(8,128)}, bf16[3,96,192]{2,1,0:T(8,128)(2,1)S(1)}, bf16[96,192]{1,0:T(8,128)(2,1)S(1)}) custom-call(s32[2]{0:T(128)S(1)} %pad_add_fusion.at_ref, f32[8,24]{1,0:T(8,128)} %refs_7_.1, f32[1,96]{1,0:T(1,128)} %bitcast.75, f32[3,96,192]{2,1,0:T(8,128)} %refs_2_.1, f32[192,96]{1,0:T(8,128)} %refs_4_.1), custom_call_target="tpu_custom_call" | custom-call | tf_op jit(solution)/shard_map/pallas_call | solution.py:41
  3.0 4.0 %collective-permute-start.2 = (bf16[3,96,192]{2,1,0:T(8,128)(2,1)S(1)}, bf16[3,96,192]{2,1,0:T(8,128)(2,1)S(1)}, u32[]{:S(2)}, u32[]{:S(2)}) collective-permute-start(bf16[3,96,192]{2,1,0:T(8,128)(2,1)S(1)} %get-tuple-element.131.refs_0_), channel_id=1, source_target_pairs={{0,24},{4,28},{8,16},{12,20},{16,8},{20,12},{24,0},{28,4},{1,25},{... | collective-permute-start | bytes 331784 | tf_op jit(solution)/shard_map/ppermute | solution.py:61
  7.6 4.0 %collective-permute-start.5 = (bf16[96,192]{1,0:T(8,128)(2,1)S(1)}, bf16[96,192]{1,0:T(8,128)(2,1)S(1)}, u32[]{:S(2)}, u32[]{:S(2)}) collective-permute-start(bf16[96,192]{1,0:T(8,128)(2,1)S(1)} %get-tuple-element.125.refs_0_), channel_id=1, source_target_pairs={{0,3},{1,2},{2,1},{3,0},{4,7},{5,6},{6,5},{7,4},{8,11},{9,10},{10,... | collective-permute-start | bytes 110600 | tf_op jit(solution)/shard_map/ppermute | solution.py:61
  11.6 1.6 %collective-permute-start.3 = (bf16[96,192]{1,0:T(8,128)(2,1)S(1)}, bf16[96,192]{1,0:T(8,128)(2,1)S(1)}, u32[]{:S(2)}, u32[]{:S(2)}) collective-permute-start(bf16[96,192]{1,0:T(8,128)(2,1)S(1)} %get-tuple-element.125.refs_0_), channel_id=1, source_target_pairs={{0,1},{1,0},{2,3},{3,2},{4,5},{5,4},{6,7},{7,6},{8,9},{9,8},{10,11... | collective-permute-start | bytes 110600 | tf_op jit(solution)/shard_map/ppermute | solution.py:61
  13.2 5.3 %all-to-all-start = ((f32[32,8,128]{2,1,0:T(8,128)}), f32[32,8,128]{2,1,0:T(8,128)S(1)}, u32[]{:S(2)}, u32[]{:S(2)}) async-start(f32[32,8,128]{2,1,0:T(8,128)} %get-tuple-element.119), calls=%async_computation | async-start | bytes 262144 | tf_op jit(solution)/shard_map/all_to_all | solution.py:560
  19.2 1.6 %shard_map.349.refs_0_ = bf16[3,96,768]{2,1,0:T(8,128)(2,1)S(1)} custom-call(s32[2]{0:T(128)S(1)} %pad_add_fusion.at_ref, f32[96,768]{1,0:T(8,128)} %up_ref, f32[96,768]{1,0:T(8,128)} %bitcast.69, bf16[96,192]{1,0:T(8,128)(2,1)S(1)} %get-tuple-element.125.refs_0_, bf16[96,192]{1,0:T(8,128)(2,1)S(1)} %collective-permute-done.3.refs_1_, ...), custom_call_target="tpu_custom_call" | custom-call | tf_op jit(solution)/shard_map/pallas_call | solution.py:41
  20.8 2.7 %collective-permute-start.8 = (bf16[3,96,768]{2,1,0:T(8,128)(2,1)S(1)}, bf16[3,96,768]{2,1,0:T(8,128)(2,1)S(1)}, u32[]{:S(2)}, u32[]{:S(2)}) collective-permute-start(bf16[3,96,768]{2,1,0:T(8,128)(2,1)S(1)} %shard_map.349.refs_0_), channel_id=1, source_target_pairs={{0,24},{4,28},{8,16},{12,20},{16,8},{20,12},{24,0},{28,4},{1,25},{... | collective-permute-start | bytes 1327112 | tf_op jit(solution)/shard_map/ppermute | solution.py:61
  25.7 1.3 all-to-all-done.small_ref
  27.7 5.3 %shard_map.350 = (bf16[576,768]{1,0:T(8,128)(2,1)S(1)}, bf16[3,576,192]{2,1,0:T(8,128)(2,1)S(1)}, f32[8,576]{1,0:T(8,128)S(1)}, bf16[864,128]{1,0:T(8,128)(2,1)S(1)}, bf16[3,768,192]{2,1,0:T(8,128)(2,1)S(1)}) custom-call(s32[2]{0:T(128)S(1)} %pad_add_fusion.at_ref, bf16[576,768]{1,0:T(8,128)(2,1)S(1)} %bitcast.65, f32[8,768]{1,0:T(8,128)S(1)} %get-tuple-element.120.vec_ref, ...), custom_call_target="tpu_custom_call" | custom-call | tf_op jit(solution)/shard_map/pallas_call | solution.py:41
  33.0 2.2 %collective-permute-start.14 = (bf16[864,128]{1,0:T(8,128)(2,1)S(1)}, bf16[864,128]{1,0:T(8,128)(2,1)S(1)}, u32[]{:S(2)}, u32[]{:S(2)}) collective-permute-start(bf16[864,128]{1,0:T(8,128)(2,1)S(1)} %get-tuple-element.134.refs_0_), channel_id=1, source_target_pairs={{0,2},{1,3},{2,0},{3,1},{4,6},{5,7},{6,4},{7,5},{8,10},{9,11},{10,... | collective-permute-start | bytes 663560 | tf_op jit(solution)/shard_map/ppermute | solution.py:61
  35.2 1.5 %collective-permute-start.13 = (bf16[864,128]{1,0:T(8,128)(2,1)S(1)}, bf16[864,128]{1,0:T(8,128)(2,1)S(1)}, u32[]{:S(2)}, u32[]{:S(2)}) collective-permute-start(bf16[864,128]{1,0:T(8,128)(2,1)S(1)} %get-tuple-element.134.refs_0_), channel_id=1, source_target_pairs={{0,1},{1,0},{2,3},{3,2},{4,5},{5,4},{6,7},{7,6},{8,9},{9,8},{10,11... | collective-permute-start | bytes 663560 | tf_op jit(solution)/shard_map/ppermute | solution.py:61
  36.7 7.3 %collective-permute-done.7.refs_4_ = bf16[3,96,768]{2,1,0:T(8,128)(2,1)S(1)} collective-permute-done((bf16[3,96,768]{2,1,0:T(8,128)(2,1)S(1)}, bf16[3,96,768]{2,1,0:T(8,128)(2,1)S(1)}, u32[]{:S(2)}, u32[]{:S(2)}) %collective-permute-start.7) | collective-permute-done | bytes 442400 | tf_op jit(solution)/shard_map/ppermute | solution.py:61
  44.2 1.6 %collective-permute-done.14.refs_2_ = bf16[864,128]{1,0:T(8,128)(2,1)S(1)} collective-permute-done((bf16[864,128]{1,0:T(8,128)(2,1)S(1)}, bf16[864,128]{1,0:T(8,128)(2,1)S(1)}, u32[]{:S(2)}, u32[]{:S(2)}) %collective-permute-start.14) | collective-permute-done | bytes 221216 | tf_op jit(solution)/shard_map/ppermute | solution.py:61
  46.9 1.6 %collective-permute-start.19 = (bf16[864,128]{1,0:T(8,128)(2,1)S(1)}, bf16[864,128]{1,0:T(8,128)(2,1)S(1)}, u32[]{:S(2)}, u32[]{:S(2)}) collective-permute-start(bf16[864,128]{1,0:T(8,128)(2,1)S(1)} %collective-permute-done.14.refs_2_), channel_id=1, source_target_pairs={{0,1},{1,0},{2,3},{3,2},{4,5},{5,4},{6,7},{7,6},{8,9},{9,8},{10,11... | collective-permute-start | bytes 663560 | tf_op jit(solution)/shard_map/ppermute | solution.py:61
  49.6 2.7 %shard_map.351 = (bf16[3,768,768]{2,1,0:T(8,128)(2,1)S(1)}, f32[576,768]{1,0:T(8,128)S(1)}) custom-call(s32[2]{0:T(128)S(1)} %pad_add_fusion.at_ref, bf16[576,768]{1,0:T(8,128)(2,1)S(1)} %bitcast.61, bf16[3,96,768]{2,1,0:T(8,128)(2,1)S(1)} %shard_map.349.refs_0_, bf16[3,96,768]{2,1,0:T(8,128)(2,1)S(1)} %collective-permute-done.15.refs_1_, ...), custom_call_target="tpu_custom_call" | custom-call | tf_op jit(solution)/shard_map/pallas_call | solution.py:41
  52.3 2.0 %collective-permute-done.19.refs_3_ = bf16[864,128]{1,0:T(8,128)(2,1)S(1)} collective-permute-done((bf16[864,128]{1,0:T(8,128)(2,1)S(1)}, bf16[864,128]{1,0:T(8,128)(2,1)S(1)}, u32[]{:S(2)}, u32[]{:S(2)}) %collective-permute-start.19) | collective-permute-done | bytes 221216 | tf_op jit(solution)/shard_map/ppermute | solution.py:61
  54.3 4.3 %shard_map.352 = (bf16[144,768]{1,0:T(8,128)(2,1)S(1)}, bf16[144,768]{1,0:T(8,128)(2,1)S(1)}, bf16[144,768]{1,0:T(8,128)(2,1)S(1)}, bf16[144,768]{1,0:T(8,128)(2...) custom-call(s32[2]{0:T(128)S(1)} %pad_add_fusion.at_ref, ...), custom_call_target="tpu_custom_call" | custom-call | tf_op jit(solution)/shard_map/pallas_call | solution.py:41
  58.6 1.7 %collective-permute-start.21 = (bf16[144,768]{1,0:T(8,128)(2,1)S(1)}, bf16[144,768]{1,0:T(8,128)(2,1)S(1)}, u32[]{:S(2)}, u32[]{:S(2)}) collective-permute-start(bf16[144,768]{1,0:T(8,128)(2,1)S(1)} %get-tuple-element.151), channel_id=1, source_target_pairs={{0,1},{1,0},{2,3},{3,2},{4,5},{5,4},{6,7},{7,6},{8,9},{9,8},{10,11... | collective-permute-start | bytes 663560 | tf_op jit(solution)/shard_map/ppermute | solution.py:61
  60.2 2.7 %shard_map.353 = (bf16[4,2,96,768]{3,2,1,0:T(8,128)(2,1)S(1)}, bf16[4,2,96,768]{3,2,1,0:T(8,128)(2,1)S(1)}) custom-call(s32[2]{0:T(128)S(1)} %pad_add_fusion.at_ref, bf16[576,768]{1,0:T(8,128)(2,1)S(1)} %get-tuple-element.152.a2_ref, bf16[576,768]{1,0:T(8,128)(2,1)S(1)} %get-tuple-element.153.du_ref, bf16[576,768]{1,0:T(8,128)(2,1)S(1)} %bitcast.63, ...), custom_call_target="tpu_custom_call" | custom-call | tf_op jit(solution)/shard_map/pallas_call | solution.py:41
  63.0 2.2 %collective-permute-done.21.right_ref = bf16[144,768]{1,0:T(8,128)(2,1)S(1)} collective-permute-done((bf16[144,768]{1,0:T(8,128)(2,1)S(1)}, bf16[144,768]{1,0:T(8,128)(2,1)S(1)}, u32[]{:S(2)}, u32[]{:S(2)}) %collective-permute-start.21) | collective-permute-done | bytes 221216 | tf_op jit(solution)/shard_map/ppermute | solution.py:61
  65.8 1.7 %collective-permute-start.20 = (bf16[144,768]{1,0:T(8,128)(2,1)S(1)}, bf16[144,768]{1,0:T(8,128)(2,1)S(1)}, u32[]{:S(2)}, u32[]{:S(2)}) collective-permute-start(bf16[144,768]{1,0:T(8,128)(2,1)S(1)} %get-tuple-element.149), channel_id=1, source_target_pairs={{0,1},{1,0},{2,3},{3,2},{4,5},{5,4},{6,7},{7,6},{8,9},{9,8},{10,11... | collective-permute-start | bytes 663560 | tf_op jit(solution)/shard_map/ppermute | solution.py:61
  67.5 1.5 %shard_map.355 = (bf16[144,768]{1,0:T(8,128)(2,1)S(1)}, bf16[144,768]{1,0:T(8,128)(2,1)S(1)}, bf16[144,768]{1,0:T(8,128)(2,1)S(1)}, bf16[144,768]{1,0:T(8,128)(2,1)S(1)}) custom-call(s32[2]{0:T(128)S(1)} %pad_add_fusion.at_ref, bf16[576,768]{1,0:T(8,128)(2,1)S(1)} %get-tuple-element.158.g_ref, bf16[3,768,768]{2,1,0:T(8,128)(2,1)S(1)} %get-tuple-element.139.w_ref), custom_call_target="tpu_custom_call" | custom-call | tf_op jit(solution)/shard_map/pallas_call | solution.py:41
  70.3 1.8 %collective-permute-start.24 = (bf16[2,96,768]{2,1,0:T(8,128)(2,1)S(1)}, bf16[2,96,768]{2,1,0:T(8,128)(2,1)S(1)}, u32[]{:S(2)}, u32[]{:S(2)}) collective-permute-start(bf16[2,96,768]{2,1,0:T(8,128)(2,1)S(1)} %get-tuple-element.165), channel_id=1, source_target_pairs={{0,8},{4,12},{8,0},{12,4},{16,24},{20,28},{24,16},{28,20},{1,9},{5... | collective-permute-start | bytes 884744 | tf_op jit(solution)/shard_map/ppermute | solution.py:61
  72.1 1.5 %collective-permute-start.25 = (bf16[2,96,768]{2,1,0:T(8,128)(2,1)S(1)}, bf16[2,96,768]{2,1,0:T(8,128)(2,1)S(1)}, u32[]{:S(2)}, u32[]{:S(2)}) collective-permute-start(bf16[2,96,768]{2,1,0:T(8,128)(2,1)S(1)} %get-tuple-element.166), channel_id=1, source_target_pairs={{0,16},{4,20},{8,24},{12,28},{16,0},{20,4},{24,8},{28,12},{1,17},{... | collective-permute-start | bytes 884744 | tf_op jit(solution)/shard_map/ppermute | solution.py:61
  74.1 2.6 %collective-permute-start.22 = (bf16[144,768]{1,0:T(8,128)(2,1)S(1)}, bf16[144,768]{1,0:T(8,128)(2,1)S(1)}, u32[]{:S(2)}, u32[]{:S(2)}) collective-permute-start(bf16[144,768]{1,0:T(8,128)(2,1)S(1)} %shard_map.354), channel_id=1, source_target_pairs={{0,2},{1,3},{2,0},{3,1},{4,6},{5,7},{6,4},{7,5},{8,10},{9,11},{10,... | collective-permute-start | bytes 663560 | tf_op jit(solution)/shard_map/ppermute | solution.py:61
  76.7 5.4 %collective-permute-done.31.right_ref = bf16[144,768]{1,0:T(8,128)(2,1)S(1)} collective-permute-done((bf16[144,768]{1,0:T(8,128)(2,1)S(1)}, bf16[144,768]{1,0:T(8,128)(2,1)S(1)}, u32[]{:S(2)}, u32[]{:S(2)}) %collective-permute-start.31) | collective-permute-done | bytes 221216 | tf_op jit(solution)/shard_map/ppermute | solution.py:61
  82.6 3.9 %collective-permute-done.22.refs_2_ = bf16[144,768]{1,0:T(8,128)(2,1)S(1)} collective-permute-done((bf16[144,768]{1,0:T(8,128)(2,1)S(1)}, bf16[144,768]{1,0:T(8,128)(2,1)S(1)}, u32[]{:S(2)}, u32[]{:S(2)}) %collective-permute-start.22) | collective-permute-done | bytes 221216 | tf_op jit(solution)/shard_map/ppermute | solution.py:61
  87.0 1.2 shard_map.357
  88.2 3.6 %collective-permute-start.27 = (bf16[216,128]{1,0:T(8,128)(2,1)S(1)}, bf16[216,128]{1,0:T(8,128)(2,1)S(1)}, u32[]{:S(2)}, u32[]{:S(2)}) collective-permute-start(bf16[216,128]{1,0:T(8,128)(2,1)S(1)} %get-tuple-element.174), channel_id=1, source_target_pairs={{0,1},{1,0},{2,3},{3,2},{4,5},{5,4},{6,7},{7,6},{8,9},{9,8},{10,11... | collective-permute-start | bytes 165896 | tf_op jit(solution)/shard_map/ppermute | solution.py:61
  92.0 2.3 %collective-permute-start.29 = (bf16[216,128]{1,0:T(8,128)(2,1)S(1)}, bf16[216,128]{1,0:T(8,128)(2,1)S(1)}, u32[]{:S(2)}, u32[]{:S(2)}) collective-permute-start(bf16[216,128]{1,0:T(8,128)(2,1)S(1)} %get-tuple-element.176), channel_id=1, source_target_pairs={{0,3},{1,2},{2,1},{3,0},{4,7},{5,6},{6,5},{7,4},{8,11},{9,10},{10,... | collective-permute-start | bytes 165896 | tf_op jit(solution)/shard_map/ppermute | solution.py:61
  94.3 1.1 shard_map.358
  95.6 1.6 %multiply_subtract_fusion.1 = (f32[96,768]{1,0:T(8,128)}, f32[96,768]{1,0:T(8,128)}, f32[96,768]{1,0:T(8,128)}, f32[96,768]{1,0:T(8,128)}, f32[96,768]{1,0:T(8,128)}, /*index=5*/f32[96,768]{1,0:T(8,128)}) fusion(f32[768,96]{0,1:T(8,128)S(1)} %copy-done.4, bf16[2,96,768]{2,1,0:T(8,128)(2,1)S(1)} %collective-permute-done.26, ...), kind=kLoop, calls=%fused_computation.15 | loop fusion | flops 3096576 | bytes 5013504 | tf_op jit(solution)/shard_map/sub | solution.py:506
  97.2 3.4 %collective-permute-done.32.three_ref = bf16[144,768]{1,0:T(8,128)(2,1)S(1)} collective-permute-done((bf16[144,768]{1,0:T(8,128)(2,1)S(1)}, bf16[144,768]{1,0:T(8,128)(2,1)S(1)}, u32[]{:S(2)}, u32[]{:S(2)}) %collective-permute-start.32) | collective-permute-done | bytes 221216 | tf_op jit(solution)/shard_map/ppermute | solution.py:61
  101.2 6.1 %shard_map.360 = (bf16[144,768]{1,0:T(8,128)(2,1)S(1)}, bf16[144,768]{1,0:T(8,128)(2,1)S(1)}, bf16[144,768]{1,0:T(8,128)(2,1)S(1)}, bf16[144,768]{1,0:T(8,128)(2...) custom-call(s32[2]{0:T(128)S(1)} %pad_add_fusion.at_ref, ...), custom_call_target="tpu_custom_call" | custom-call | tf_op jit(solution)/shard_map/pallas_call | solution.py:41
  107.4 1.5 %collective-permute-start.33 = (bf16[144,768]{1,0:T(8,128)(2,1)S(1)}, bf16[144,768]{1,0:T(8,128)(2,1)S(1)}, u32[]{:S(2)}, u32[]{:S(2)}) collective-permute-start(bf16[144,768]{1,0:T(8,128)(2,1)S(1)} %get-tuple-element.190), channel_id=1, source_target_pairs={{0,1},{1,0},{2,3},{3,2},{4,5},{5,4},{6,7},{7,6},{8,9},{9,8},{10,11... | collective-permute-start | bytes 663560 | tf_op jit(solution)/shard_map/ppermute | solution.py:61
  110.2 1.5 %collective-permute-start.38 = (bf16[96,1472]{1,0:T(8,128)(2,1)S(1)}, bf16[96,1472]{1,0:T(8,128)(2,1)S(1)}, u32[]{:S(2)}, u32[]{:S(2)}) collective-permute-start(bf16[96,1472]{1,0:T(8,128)(2,1)S(1)} %get-tuple-element.194), channel_id=1, source_target_pairs={{0,8},{4,12},{8,0},{12,4},{16,24},{20,28},{24,16},{28,20},{1,9},{5... | collective-permute-start | bytes 847880 | tf_op jit(solution)/shard_map/ppermute | solution.py:61
  111.7 1.5 %collective-permute-start.39 = (bf16[96,1472]{1,0:T(8,128)(2,1)S(1)}, bf16[96,1472]{1,0:T(8,128)(2,1)S(1)}, u32[]{:S(2)}, u32[]{:S(2)}) collective-permute-start(bf16[96,1472]{1,0:T(8,128)(2,1)S(1)} %get-tuple-element.195), channel_id=1, source_target_pairs={{0,16},{4,20},{8,24},{12,28},{16,0},{20,4},{24,8},{28,12},{1,17},{... | collective-permute-start | bytes 847880 | tf_op jit(solution)/shard_map/ppermute | solution.py:61
  113.7 1.5 %collective-permute-start.36 = (bf16[144,768]{1,0:T(8,128)(2,1)S(1)}, bf16[144,768]{1,0:T(8,128)(2,1)S(1)}, u32[]{:S(2)}, u32[]{:S(2)}) collective-permute-start(bf16[144,768]{1,0:T(8,128)(2,1)S(1)} %get-tuple-element.201), channel_id=1, source_target_pairs={{0,1},{1,0},{2,3},{3,2},{4,5},{5,4},{6,7},{7,6},{8,9},{9,8},{10,11... | collective-permute-start | bytes 663560 | tf_op jit(solution)/shard_map/ppermute | solution.py:61
  115.8 3.5 %collective-permute-start.37 = (bf16[144,768]{1,0:T(8,128)(2,1)S(1)}, bf16[144,768]{1,0:T(8,128)(2,1)S(1)}, u32[]{:S(2)}, u32[]{:S(2)}) collective-permute-start(bf16[144,768]{1,0:T(8,128)(2,1)S(1)} %shard_map.362), channel_id=1, source_target_pairs={{0,2},{1,3},{2,0},{3,1},{4,6},{5,7},{6,4},{7,5},{8,10},{9,11},{10,... | collective-permute-start | bytes 663560 | tf_op jit(solution)/shard_map/ppermute | solution.py:61
  119.3 1.3 shard_map.363
  120.8 6.0 %collective-permute-done.39.refs_2_ = bf16[96,1472]{1,0:T(8,128)(2,1)S(1)} collective-permute-done((bf16[96,1472]{1,0:T(8,128)(2,1)S(1)}, bf16[96,1472]{1,0:T(8,128)(2,1)S(1)}, u32[]{:S(2)}, u32[]{:S(2)}) %collective-permute-start.39) | collective-permute-done | bytes 282656 | tf_op jit(solution)/shard_map/ppermute | solution.py:61
  127.5 1.6 %collective-permute-start.41 = (bf16[112,192]{1,0:T(8,128)(2,1)S(1)}, bf16[112,192]{1,0:T(8,128)(2,1)S(1)}, u32[]{:S(2)}, u32[]{:S(2)}) collective-permute-start(bf16[112,192]{1,0:T(8,128)(2,1)S(1)} %get-tuple-element.206), channel_id=1, source_target_pairs={{0,1},{1,0},{2,3},{3,2},{4,5},{5,4},{6,7},{7,6},{8,9},{9,8},{10,11... | collective-permute-start | bytes 129032 | tf_op jit(solution)/shard_map/ppermute | solution.py:61
  129.0 2.4 %collective-permute-start.42 = (bf16[112,192]{1,0:T(8,128)(2,1)S(1)}, bf16[112,192]{1,0:T(8,128)(2,1)S(1)}, u32[]{:S(2)}, u32[]{:S(2)}) collective-permute-start(bf16[112,192]{1,0:T(8,128)(2,1)S(1)} %get-tuple-element.207), channel_id=1, source_target_pairs={{0,2},{1,3},{2,0},{3,1},{4,6},{5,7},{6,4},{7,5},{8,10},{9,11},{10,... | collective-permute-start | bytes 129032 | tf_op jit(solution)/shard_map/ppermute | solution.py:61
  131.4 1.0 collective-permute-start.43
  132.7 1.1 multiply_subtract_fusion
  133.9 1.7 %shard_map.364 = f32[144,768]{1,0:T(8,128)} custom-call(s32[2]{0:T(128)S(1)} %pad_add_fusion.at_ref, bf16[576,768]{1,0:T(8,128)(2,1)S(1)} %bitcast.68, f32[144,768]{1,0:T(8,128)S(1)} %get-tuple-element.199.dh_ref, f32[8,768]{1,0:T(8,128)S(1)} %get-tuple-element.120.vec_ref, bf16[144,768]{1,0:T(8,128)(2,1)S(1)} %get-tuple-element.202.refs_0_, ...), custom_call_target="tpu_custom_call" | custom-call | tf_op jit(solution)/shard_map/pallas_call | solution.py:41
  135.9 1.5 %collective-permute-done.43.refs_3_ = bf16[112,192]{1,0:T(8,128)(2,1)S(1)} collective-permute-done((bf16[112,192]{1,0:T(8,128)(2,1)S(1)}, bf16[112,192]{1,0:T(8,128)(2,1)S(1)}, u32[]{:S(2)}, u32[]{:S(2)}) %collective-permute-start.43) | collective-permute-done | bytes 43040 | tf_op jit(solution)/shard_map/ppermute | solution.py:61
  137.4 2.5 %shard_map.366 = (f32[192,96]{1,0:T(8,128)}, f32[192,96]{1,0:T(8,128)}, f32[192,96]{1,0:T(8,128)}, f32[8,24]{1,0:T(8,128)}, f32[8,24]{1,0:T(8,128)}, /*index=5*/...) custom-call(s32[2]{0:T(128)S(1)} %pad_add_fusion.at_ref, ...), custom_call_target="tpu_custom_call" | custom-call | tf_op jit(solution)/shard_map/pallas_call | solution.py:41
  (97 shorter events, 14.7 us)
Async XLA Ops:
  0.7 27.1 %copy-start.1 = (bf16[1,576,768]{2,1,0:T(8,128)(2,1)S(1)}, bf16[1,576,768]{2,1,0:T(8,128)(2,1)}, u32[]{:S(2)}) copy-start(bf16[1,576,768]{2,1,0:T(8,128)(2,1)} %param.20) | copy-start | bytes 2654212
  3.0 8.6 %collective-permute-start.2 = (bf16[3,96,192]{2,1,0:T(8,128)(2,1)S(1)}, bf16[3,96,192]{2,1,0:T(8,128)(2,1)S(1)}, u32[]{:S(2)}, u32[]{:S(2)}) collective-permute-start(bf16[3,96,192]{2,1,0:T(8,128)(2,1)S(1)} %get-tuple-element.131.refs_0_), channel_id=1, source_target_pairs={{0,24},{4,28},{8,16},{12,20},{16,8},{20,12},{24,0},{28,4},{1,25},{... | collective-permute-start | bytes 331784 | tf_op jit(solution)/shard_map/ppermute | solution.py:61
  7.0 11.6 %collective-permute-start.1 = (bf16[3,96,192]{2,1,0:T(8,128)(2,1)S(1)}, bf16[3,96,192]{2,1,0:T(8,128)(2,1)}, u32[]{:S(2)}, u32[]{:S(2)}) collective-permute-start(bf16[3,96,192]{2,1,0:T(8,128)(2,1)S(1)} %get-tuple-element.131.refs_0_), channel_id=1, source_target_pairs={{0,16},{4,20},{8,24},{12,28},{16,0},{20,4},{24,8},{28,12},{1,17},{... | collective-permute-start | bytes 331784 | tf_op jit(solution)/shard_map/ppermute | solution.py:61
  7.5 11.1 %collective-permute-start = (bf16[3,96,192]{2,1,0:T(8,128)(2,1)S(1)}, bf16[3,96,192]{2,1,0:T(8,128)(2,1)}, u32[]{:S(2)}, u32[]{:S(2)}) collective-permute-start(bf16[3,96,192]{2,1,0:T(8,128)(2,1)S(1)} %get-tuple-element.131.refs_0_), channel_id=1, source_target_pairs={{0,8},{4,12},{8,0},{12,4},{16,24},{20,28},{24,16},{28,20},{1,9},{5... | collective-permute-start | bytes 331784 | tf_op jit(solution)/shard_map/ppermute | solution.py:61
  7.6 11.6 %collective-permute-start.5 = (bf16[96,192]{1,0:T(8,128)(2,1)S(1)}, bf16[96,192]{1,0:T(8,128)(2,1)S(1)}, u32[]{:S(2)}, u32[]{:S(2)}) collective-permute-start(bf16[96,192]{1,0:T(8,128)(2,1)S(1)} %get-tuple-element.125.refs_0_), channel_id=1, source_target_pairs={{0,3},{1,2},{2,1},{3,0},{4,7},{5,6},{6,5},{7,4},{8,11},{9,10},{10,... | collective-permute-start | bytes 110600 | tf_op jit(solution)/shard_map/ppermute | solution.py:61
  11.6 7.6 %collective-permute-start.4 = (bf16[96,192]{1,0:T(8,128)(2,1)S(1)}, bf16[96,192]{1,0:T(8,128)(2,1)S(1)}, u32[]{:S(2)}, u32[]{:S(2)}) collective-permute-start(bf16[96,192]{1,0:T(8,128)(2,1)S(1)} %get-tuple-element.125.refs_0_), channel_id=1, source_target_pairs={{0,2},{1,3},{2,0},{3,1},{4,6},{5,7},{6,4},{7,5},{8,10},{9,11},{10,... | collective-permute-start | bytes 110600 | tf_op jit(solution)/shard_map/ppermute | solution.py:61
  11.6 16.1 %copy-start.11 = (bf16[3,96,192]{2,1,0:T(8,128)(2,1)}, bf16[3,96,192]{2,1,0:T(8,128)(2,1)S(1)}, u32[]{:S(2)}) copy-start(bf16[3,96,192]{2,1,0:T(8,128)(2,1)S(1)} %collective-permute-done.2.refs_6_) | copy-start | bytes 331780
  11.6 7.6 %collective-permute-start.3 = (bf16[96,192]{1,0:T(8,128)(2,1)S(1)}, bf16[96,192]{1,0:T(8,128)(2,1)S(1)}, u32[]{:S(2)}, u32[]{:S(2)}) collective-permute-start(bf16[96,192]{1,0:T(8,128)(2,1)S(1)} %get-tuple-element.125.refs_0_), channel_id=1, source_target_pairs={{0,1},{1,0},{2,3},{3,2},{4,5},{5,4},{6,7},{7,6},{8,9},{9,8},{10,11... | collective-permute-start | bytes 110600 | tf_op jit(solution)/shard_map/ppermute | solution.py:61
  13.2 13.8 %all-to-all-start = ((f32[32,8,128]{2,1,0:T(8,128)}), f32[32,8,128]{2,1,0:T(8,128)S(1)}, u32[]{:S(2)}, u32[]{:S(2)}) async-start(f32[32,8,128]{2,1,0:T(8,128)} %get-tuple-element.119), calls=%async_computation | async-start | bytes 262144 | tf_op jit(solution)/shard_map/all_to_all | solution.py:560
  18.6 5.8 %collective-permute-start.9 = (bf16[3,96,192]{2,1,0:T(8,128)(2,1)S(1)}, bf16[3,96,192]{2,1,0:T(8,128)(2,1)S(1)}, u32[]{:S(2)}, u32[]{:S(2)}) collective-permute-start(bf16[3,96,192]{2,1,0:T(8,128)(2,1)S(1)} %get-tuple-element.131.refs_0_), channel_id=1, source_target_pairs={{0,4},{4,0},{8,12},{12,8},{16,20},{20,16},{24,28},{28,24},{1,5},{5... | collective-permute-start | bytes 331784 | tf_op jit(solution)/shard_map/ppermute | solution.py:61
  18.9 5.5 %collective-permute-start.10 = (bf16[3,96,192]{2,1,0:T(8,128)(2,1)}, bf16[3,96,192]{2,1,0:T(8,128)(2,1)S(1)}, u32[]{:S(2)}, u32[]{:S(2)}) collective-permute-start(bf16[3,96,192]{2,1,0:T(8,128)(2,1)} %collective-permute-done.refs_2_), channel_id=1, source_target_pairs={{0,4},{4,0},{8,12},{12,8},{16,20},{20,16},{24,28},{28,24},{1,5},{5... | collective-permute-start | bytes 331784 | tf_op jit(solution)/shard_map/ppermute | solution.py:61
  20.8 28.8 %copy-start = (bf16[1,576,768]{2,1,0:T(8,128)(2,1)S(1)}, bf16[1,576,768]{2,1,0:T(8,128)(2,1)}, u32[]{:S(2)}) copy-start(bf16[1,576,768]{2,1,0:T(8,128)(2,1)} %param.21) | copy-start | bytes 2654212
  20.8 15.9 %collective-permute-start.8 = (bf16[3,96,768]{2,1,0:T(8,128)(2,1)S(1)}, bf16[3,96,768]{2,1,0:T(8,128)(2,1)S(1)}, u32[]{:S(2)}, u32[]{:S(2)}) collective-permute-start(bf16[3,96,768]{2,1,0:T(8,128)(2,1)S(1)} %shard_map.349.refs_0_), channel_id=1, source_target_pairs={{0,24},{4,28},{8,16},{12,20},{16,8},{20,12},{24,0},{28,4},{1,25},{... | collective-permute-start | bytes 1327112 | tf_op jit(solution)/shard_map/ppermute | solution.py:61
  23.6 20.5 %collective-permute-start.7 = (bf16[3,96,768]{2,1,0:T(8,128)(2,1)S(1)}, bf16[3,96,768]{2,1,0:T(8,128)(2,1)S(1)}, u32[]{:S(2)}, u32[]{:S(2)}) collective-permute-start(bf16[3,96,768]{2,1,0:T(8,128)(2,1)S(1)} %shard_map.349.refs_0_), channel_id=1, source_target_pairs={{0,16},{4,20},{8,24},{12,28},{16,0},{20,4},{24,8},{28,12},{1,17},{... | collective-permute-start | bytes 1327112 | tf_op jit(solution)/shard_map/ppermute | solution.py:61
  24.1 20.1 %collective-permute-start.6 = (bf16[3,96,768]{2,1,0:T(8,128)(2,1)S(1)}, bf16[3,96,768]{2,1,0:T(8,128)(2,1)}, u32[]{:S(2)}, u32[]{:S(2)}) collective-permute-start(bf16[3,96,768]{2,1,0:T(8,128)(2,1)S(1)} %shard_map.349.refs_0_), channel_id=1, source_target_pairs={{0,8},{4,12},{8,0},{12,4},{16,24},{20,28},{24,16},{28,20},{1,9},{5... | collective-permute-start | bytes 1327112 | tf_op jit(solution)/shard_map/ppermute | solution.py:61
  24.4 3.3 %collective-permute-start.11 = (bf16[3,96,192]{2,1,0:T(8,128)(2,1)}, bf16[3,96,192]{2,1,0:T(8,128)(2,1)}, u32[]{:S(2)}, u32[]{:S(2)}) collective-permute-start(bf16[3,96,192]{2,1,0:T(8,128)(2,1)} %collective-permute-done.1.refs_4_), channel_id=1, source_target_pairs={{0,4},{4,0},{8,12},{12,8},{16,20},{20,16},{24,28},{28,24},{1,5},{5... | collective-permute-start | bytes 331784 | tf_op jit(solution)/shard_map/ppermute | solution.py:61
  25.7 2.0 %collective-permute-start.12 = (bf16[3,96,192]{2,1,0:T(8,128)(2,1)S(1)}, bf16[3,96,192]{2,1,0:T(8,128)(2,1)}, u32[]{:S(2)}, u32[]{:S(2)}) collective-permute-start(bf16[3,96,192]{2,1,0:T(8,128)(2,1)S(1)} %collective-permute-done.2.refs_6_), channel_id=1, source_target_pairs={{0,4},{4,0},{8,12},{12,8},{16,20},{20,16},{24,28},{28,24},{1,5},{5... | collective-permute-start | bytes 331784 | tf_op jit(solution)/shard_map/ppermute | solution.py:61
  33.0 12.8 %collective-permute-start.14 = (bf16[864,128]{1,0:T(8,128)(2,1)S(1)}, bf16[864,128]{1,0:T(8,128)(2,1)S(1)}, u32[]{:S(2)}, u32[]{:S(2)}) collective-permute-start(bf16[864,128]{1,0:T(8,128)(2,1)S(1)} %get-tuple-element.134.refs_0_), channel_id=1, source_target_pairs={{0,2},{1,3},{2,0},{3,1},{4,6},{5,7},{6,4},{7,5},{8,10},{9,11},{10,... | collective-permute-start | bytes 663560 | tf_op jit(solution)/shard_map/ppermute | solution.py:61
  35.2 10.7 %collective-permute-start.13 = (bf16[864,128]{1,0:T(8,128)(2,1)S(1)}, bf16[864,128]{1,0:T(8,128)(2,1)S(1)}, u32[]{:S(2)}, u32[]{:S(2)}) collective-permute-start(bf16[864,128]{1,0:T(8,128)(2,1)S(1)} %get-tuple-element.134.refs_0_), channel_id=1, source_target_pairs={{0,1},{1,0},{2,3},{3,2},{4,5},{5,4},{6,7},{7,6},{8,9},{9,8},{10,11... | collective-permute-start | bytes 663560 | tf_op jit(solution)/shard_map/ppermute | solution.py:61
  45.9 2.6 %collective-permute-start.15 = (bf16[3,96,768]{2,1,0:T(8,128)(2,1)S(1)}, bf16[3,96,768]{2,1,0:T(8,128)(2,1)S(1)}, u32[]{:S(2)}, u32[]{:S(2)}) collective-permute-start(bf16[3,96,768]{2,1,0:T(8,128)(2,1)S(1)} %shard_map.349.refs_0_), channel_id=1, source_target_pairs={{0,4},{4,0},{8,12},{12,8},{16,20},{20,16},{24,28},{28,24},{1,5},{5... | collective-permute-start | bytes 1327112 | tf_op jit(solution)/shard_map/ppermute | solution.py:61
  45.9 2.9 %collective-permute-start.16 = (bf16[3,96,768]{2,1,0:T(8,128)(2,1)}, bf16[3,96,768]{2,1,0:T(8,128)(2,1)S(1)}, u32[]{:S(2)}, u32[]{:S(2)}) collective-permute-start(bf16[3,96,768]{2,1,0:T(8,128)(2,1)} %collective-permute-done.6.refs_2_), channel_id=1, source_target_pairs={{0,4},{4,0},{8,12},{12,8},{16,20},{20,16},{24,28},{28,24},{1,5},{5... | collective-permute-start | bytes 1327112 | tf_op jit(solution)/shard_map/ppermute | solution.py:61
  46.4 2.5 %collective-permute-start.17 = (bf16[3,96,768]{2,1,0:T(8,128)(2,1)S(1)}, bf16[3,96,768]{2,1,0:T(8,128)(2,1)S(1)}, u32[]{:S(2)}, u32[]{:S(2)}) collective-permute-start(bf16[3,96,768]{2,1,0:T(8,128)(2,1)S(1)} %collective-permute-done.7.refs_4_), channel_id=1, source_target_pairs={{0,4},{4,0},{8,12},{12,8},{16,20},{20,16},{24,28},{28,24},{1,5},{5... | collective-permute-start | bytes 1327112 | tf_op jit(solution)/shard_map/ppermute | solution.py:61
  46.4 3.2 %collective-permute-start.18 = (bf16[3,96,768]{2,1,0:T(8,128)(2,1)S(1)}, bf16[3,96,768]{2,1,0:T(8,128)(2,1)S(1)}, u32[]{:S(2)}, u32[]{:S(2)}) collective-permute-start(bf16[3,96,768]{2,1,0:T(8,128)(2,1)S(1)} %collective-permute-done.8.refs_6_), channel_id=1, source_target_pairs={{0,4},{4,0},{8,12},{12,8},{16,20},{20,16},{24,28},{28,24},{1,5},{5... | collective-permute-start | bytes 1327112 | tf_op jit(solution)/shard_map/ppermute | solution.py:61
  46.9 7.3 %collective-permute-start.19 = (bf16[864,128]{1,0:T(8,128)(2,1)S(1)}, bf16[864,128]{1,0:T(8,128)(2,1)S(1)}, u32[]{:S(2)}, u32[]{:S(2)}) collective-permute-start(bf16[864,128]{1,0:T(8,128)(2,1)S(1)} %collective-permute-done.14.refs_2_), channel_id=1, source_target_pairs={{0,1},{1,0},{2,3},{3,2},{4,5},{5,4},{6,7},{7,6},{8,9},{9,8},{10,11... | collective-permute-start | bytes 663560 | tf_op jit(solution)/shard_map/ppermute | solution.py:61
  58.6 6.6 %collective-permute-start.21 = (bf16[144,768]{1,0:T(8,128)(2,1)S(1)}, bf16[144,768]{1,0:T(8,128)(2,1)S(1)}, u32[]{:S(2)}, u32[]{:S(2)}) collective-permute-start(bf16[144,768]{1,0:T(8,128)(2,1)S(1)} %get-tuple-element.151), channel_id=1, source_target_pairs={{0,1},{1,0},{2,3},{3,2},{4,5},{5,4},{6,7},{7,6},{8,9},{9,8},{10,11... | collective-permute-start | bytes 663560 | tf_op jit(solution)/shard_map/ppermute | solution.py:61
  65.7 3.8 %collective-permute-start.23 = (bf16[4,2,96,768]{3,2,1,0:T(8,128)(2,1)S(1)}, bf16[4,2,96,768]{3,2,1,0:T(8,128)(2,1)S(1)}, u32[]{:S(2)}, u32[]{:S(2)}) collective-permute-start(bf16[4,2,96,768]{3,2,1,0:T(8,128)(2,1)S(1)} %get-tuple-element.163), channel_id=1, source_target_pairs={{0,4},{4,0},{8,12},{12,8},{16,20},{20,16},{24,28},{28,24},{1,5},{5... | collective-permute-start | bytes 3538952 | tf_op jit(solution)/shard_map/ppermute | solution.py:61
  65.8 8.3 %collective-permute-start.20 = (bf16[144,768]{1,0:T(8,128)(2,1)S(1)}, bf16[144,768]{1,0:T(8,128)(2,1)S(1)}, u32[]{:S(2)}, u32[]{:S(2)}) collective-permute-start(bf16[144,768]{1,0:T(8,128)(2,1)S(1)} %get-tuple-element.149), channel_id=1, source_target_pairs={{0,1},{1,0},{2,3},{3,2},{4,5},{5,4},{6,7},{7,6},{8,9},{9,8},{10,11... | collective-permute-start | bytes 663560 | tf_op jit(solution)/shard_map/ppermute | solution.py:61
  69.0 13.0 %collective-permute-start.31 = (bf16[144,768]{1,0:T(8,128)(2,1)S(1)}, bf16[144,768]{1,0:T(8,128)(2,1)S(1)}, u32[]{:S(2)}, u32[]{:S(2)}) collective-permute-start(bf16[144,768]{1,0:T(8,128)(2,1)S(1)} %get-tuple-element.162), channel_id=1, source_target_pairs={{0,1},{1,0},{2,3},{3,2},{4,5},{5,4},{6,7},{7,6},{8,9},{9,8},{10,11... | collective-permute-start | bytes 663560 | tf_op jit(solution)/shard_map/ppermute | solution.py:61
  70.3 16.2 %collective-permute-start.24 = (bf16[2,96,768]{2,1,0:T(8,128)(2,1)S(1)}, bf16[2,96,768]{2,1,0:T(8,128)(2,1)S(1)}, u32[]{:S(2)}, u32[]{:S(2)}) collective-permute-start(bf16[2,96,768]{2,1,0:T(8,128)(2,1)S(1)} %get-tuple-element.165), channel_id=1, source_target_pairs={{0,8},{4,12},{8,0},{12,4},{16,24},{20,28},{24,16},{28,20},{1,9},{5... | collective-permute-start | bytes 884744 | tf_op jit(solution)/shard_map/ppermute | solution.py:61
  72.1 14.8 %collective-permute-start.25 = (bf16[2,96,768]{2,1,0:T(8,128)(2,1)S(1)}, bf16[2,96,768]{2,1,0:T(8,128)(2,1)S(1)}, u32[]{:S(2)}, u32[]{:S(2)}) collective-permute-start(bf16[2,96,768]{2,1,0:T(8,128)(2,1)S(1)} %get-tuple-element.166), channel_id=1, source_target_pairs={{0,16},{4,20},{8,24},{12,28},{16,0},{20,4},{24,8},{28,12},{1,17},{... | collective-permute-start | bytes 884744 | tf_op jit(solution)/shard_map/ppermute | solution.py:61
  73.6 13.4 %collective-permute-start.26 = (bf16[2,96,768]{2,1,0:T(8,128)(2,1)S(1)}, bf16[2,96,768]{2,1,0:T(8,128)(2,1)S(1)}, u32[]{:S(2)}, u32[]{:S(2)}) collective-permute-start(bf16[2,96,768]{2,1,0:T(8,128)(2,1)S(1)} %get-tuple-element.167), channel_id=1, source_target_pairs={{0,24},{4,28},{8,16},{12,20},{16,8},{20,12},{24,0},{28,4},{1,25},{... | collective-permute-start | bytes 884744 | tf_op jit(solution)/shard_map/ppermute | solution.py:61
  74.1 12.4 %collective-permute-start.22 = (bf16[144,768]{1,0:T(8,128)(2,1)S(1)}, bf16[144,768]{1,0:T(8,128)(2,1)S(1)}, u32[]{:S(2)}, u32[]{:S(2)}) collective-permute-start(bf16[144,768]{1,0:T(8,128)(2,1)S(1)} %shard_map.354), channel_id=1, source_target_pairs={{0,2},{1,3},{2,0},{3,1},{4,6},{5,7},{6,4},{7,5},{8,10},{9,11},{10,... | collective-permute-start | bytes 663560 | tf_op jit(solution)/shard_map/ppermute | solution.py:61
  82.0 13.4 %collective-permute-start.30 = (bf16[144,768]{1,0:T(8,128)(2,1)S(1)}, bf16[144,768]{1,0:T(8,128)(2,1)S(1)}, u32[]{:S(2)}, u32[]{:S(2)}) collective-permute-start(bf16[144,768]{1,0:T(8,128)(2,1)S(1)} %get-tuple-element.160), channel_id=1, source_target_pairs={{0,1},{1,0},{2,3},{3,2},{4,5},{5,4},{6,7},{7,6},{8,9},{9,8},{10,11... | collective-permute-start | bytes 663560 | tf_op jit(solution)/shard_map/ppermute | solution.py:61
  86.5 14.1 %collective-permute-start.32 = (bf16[144,768]{1,0:T(8,128)(2,1)S(1)}, bf16[144,768]{1,0:T(8,128)(2,1)S(1)}, u32[]{:S(2)}, u32[]{:S(2)}) collective-permute-start(bf16[144,768]{1,0:T(8,128)(2,1)S(1)} %shard_map.359), channel_id=1, source_target_pairs={{0,2},{1,3},{2,0},{3,1},{4,6},{5,7},{6,4},{7,5},{8,10},{9,11},{10,... | collective-permute-start | bytes 663560 | tf_op jit(solution)/shard_map/ppermute | solution.py:61
  88.2 12.4 %collective-permute-start.27 = (bf16[216,128]{1,0:T(8,128)(2,1)S(1)}, bf16[216,128]{1,0:T(8,128)(2,1)S(1)}, u32[]{:S(2)}, u32[]{:S(2)}) collective-permute-start(bf16[216,128]{1,0:T(8,128)(2,1)S(1)} %get-tuple-element.174), channel_id=1, source_target_pairs={{0,1},{1,0},{2,3},{3,2},{4,5},{5,4},{6,7},{7,6},{8,9},{9,8},{10,11... | collective-permute-start | bytes 165896 | tf_op jit(solution)/shard_map/ppermute | solution.py:61
  91.9 9.3 %collective-permute-start.28 = (bf16[216,128]{1,0:T(8,128)(2,1)S(1)}, bf16[216,128]{1,0:T(8,128)(2,1)S(1)}, u32[]{:S(2)}, u32[]{:S(2)}) collective-permute-start(bf16[216,128]{1,0:T(8,128)(2,1)S(1)} %get-tuple-element.175), channel_id=1, source_target_pairs={{0,2},{1,3},{2,0},{3,1},{4,6},{5,7},{6,4},{7,5},{8,10},{9,11},{10,... | collective-permute-start | bytes 165896 | tf_op jit(solution)/shard_map/ppermute | solution.py:61
  92.0 9.1 %collective-permute-start.29 = (bf16[216,128]{1,0:T(8,128)(2,1)S(1)}, bf16[216,128]{1,0:T(8,128)(2,1)S(1)}, u32[]{:S(2)}, u32[]{:S(2)}) collective-permute-start(bf16[216,128]{1,0:T(8,128)(2,1)S(1)} %get-tuple-element.176), channel_id=1, source_target_pairs={{0,3},{1,2},{2,1},{3,0},{4,7},{5,6},{6,5},{7,4},{8,11},{9,10},{10,... | collective-permute-start | bytes 165896 | tf_op jit(solution)/shard_map/ppermute | solution.py:61
  95.5 13.5 %collective-permute-start.34 = (bf16[4,96,768]{2,1,0:T(8,128)(2,1)S(1)}, bf16[4,96,768]{2,1,0:T(8,128)(2,1)S(1)}, u32[]{:S(2)}, u32[]{:S(2)}) collective-permute-start(bf16[4,96,768]{2,1,0:T(8,128)(2,1)S(1)} %get-tuple-element.180), channel_id=1, source_target_pairs={{0,4},{4,0},{8,12},{12,8},{16,20},{20,16},{24,28},{28,24},{1,5},{5... | collective-permute-start | bytes 1769480 | tf_op jit(solution)/shard_map/ppermute | solution.py:61
  107.3 2.1 %collective-permute-start.35 = (bf16[4,96,704]{2,1,0:T(8,128)(2,1)S(1)}, bf16[4,96,704]{2,1,0:T(8,128)(2,1)S(1)}, u32[]{:S(2)}, u32[]{:S(2)}) collective-permute-start(bf16[4,96,704]{2,1,0:T(8,128)(2,1)S(1)} %get-tuple-element.192), channel_id=1, source_target_pairs={{0,4},{4,0},{8,12},{12,8},{16,20},{20,16},{24,28},{28,24},{1,5},{5... | collective-permute-start | bytes 1622024 | tf_op jit(solution)/shard_map/ppermute | solution.py:61
  107.4 7.8 %collective-permute-start.33 = (bf16[144,768]{1,0:T(8,128)(2,1)S(1)}, bf16[144,768]{1,0:T(8,128)(2,1)S(1)}, u32[]{:S(2)}, u32[]{:S(2)}) collective-permute-start(bf16[144,768]{1,0:T(8,128)(2,1)S(1)} %get-tuple-element.190), channel_id=1, source_target_pairs={{0,1},{1,0},{2,3},{3,2},{4,5},{5,4},{6,7},{7,6},{8,9},{9,8},{10,11... | collective-permute-start | bytes 663560 | tf_op jit(solution)/shard_map/ppermute | solution.py:61
  110.2 10.6 %collective-permute-start.38 = (bf16[96,1472]{1,0:T(8,128)(2,1)S(1)}, bf16[96,1472]{1,0:T(8,128)(2,1)S(1)}, u32[]{:S(2)}, u32[]{:S(2)}) collective-permute-start(bf16[96,1472]{1,0:T(8,128)(2,1)S(1)} %get-tuple-element.194), channel_id=1, source_target_pairs={{0,8},{4,12},{8,0},{12,4},{16,24},{20,28},{24,16},{28,20},{1,9},{5... | collective-permute-start | bytes 847880 | tf_op jit(solution)/shard_map/ppermute | solution.py:61
  111.7 15.1 %collective-permute-start.39 = (bf16[96,1472]{1,0:T(8,128)(2,1)S(1)}, bf16[96,1472]{1,0:T(8,128)(2,1)S(1)}, u32[]{:S(2)}, u32[]{:S(2)}) collective-permute-start(bf16[96,1472]{1,0:T(8,128)(2,1)S(1)} %get-tuple-element.195), channel_id=1, source_target_pairs={{0,16},{4,20},{8,24},{12,28},{16,0},{20,4},{24,8},{28,12},{1,17},{... | collective-permute-start | bytes 847880 | tf_op jit(solution)/shard_map/ppermute | solution.py:61
  113.2 13.6 %collective-permute-start.40 = (bf16[96,1472]{1,0:T(8,128)(2,1)S(1)}, bf16[96,1472]{1,0:T(8,128)(2,1)S(1)}, u32[]{:S(2)}, u32[]{:S(2)}) collective-permute-start(bf16[96,1472]{1,0:T(8,128)(2,1)S(1)} %get-tuple-element.196), channel_id=1, source_target_pairs={{0,24},{4,28},{8,16},{12,20},{16,8},{20,12},{24,0},{28,4},{1,25},{... | collective-permute-start | bytes 847880 | tf_op jit(solution)/shard_map/ppermute | solution.py:61
  113.7 20.1 %collective-permute-start.36 = (bf16[144,768]{1,0:T(8,128)(2,1)S(1)}, bf16[144,768]{1,0:T(8,128)(2,1)S(1)}, u32[]{:S(2)}, u32[]{:S(2)}) collective-permute-start(bf16[144,768]{1,0:T(8,128)(2,1)S(1)} %get-tuple-element.201), channel_id=1, source_target_pairs={{0,1},{1,0},{2,3},{3,2},{4,5},{5,4},{6,7},{7,6},{8,9},{9,8},{10,11... | collective-permute-start | bytes 663560 | tf_op jit(solution)/shard_map/ppermute | solution.py:61
  115.8 18.0 %collective-permute-start.37 = (bf16[144,768]{1,0:T(8,128)(2,1)S(1)}, bf16[144,768]{1,0:T(8,128)(2,1)S(1)}, u32[]{:S(2)}, u32[]{:S(2)}) collective-permute-start(bf16[144,768]{1,0:T(8,128)(2,1)S(1)} %shard_map.362), channel_id=1, source_target_pairs={{0,2},{1,3},{2,0},{3,1},{4,6},{5,7},{6,4},{7,5},{8,10},{9,11},{10,... | collective-permute-start | bytes 663560 | tf_op jit(solution)/shard_map/ppermute | solution.py:61
  127.5 8.1 %collective-permute-start.41 = (bf16[112,192]{1,0:T(8,128)(2,1)S(1)}, bf16[112,192]{1,0:T(8,128)(2,1)S(1)}, u32[]{:S(2)}, u32[]{:S(2)}) collective-permute-start(bf16[112,192]{1,0:T(8,128)(2,1)S(1)} %get-tuple-element.206), channel_id=1, source_target_pairs={{0,1},{1,0},{2,3},{3,2},{4,5},{5,4},{6,7},{7,6},{8,9},{9,8},{10,11... | collective-permute-start | bytes 129032 | tf_op jit(solution)/shard_map/ppermute | solution.py:61
  129.0 6.9 %collective-permute-start.42 = (bf16[112,192]{1,0:T(8,128)(2,1)S(1)}, bf16[112,192]{1,0:T(8,128)(2,1)S(1)}, u32[]{:S(2)}, u32[]{:S(2)}) collective-permute-start(bf16[112,192]{1,0:T(8,128)(2,1)S(1)} %get-tuple-element.207), channel_id=1, source_target_pairs={{0,2},{1,3},{2,0},{3,1},{4,6},{5,7},{6,4},{7,5},{8,10},{9,11},{10,... | collective-permute-start | bytes 129032 | tf_op jit(solution)/shard_map/ppermute | solution.py:61
  131.4 6.0 %collective-permute-start.43 = (bf16[112,192]{1,0:T(8,128)(2,1)S(1)}, bf16[112,192]{1,0:T(8,128)(2,1)S(1)}, u32[]{:S(2)}, u32[]{:S(2)}) collective-permute-start(bf16[112,192]{1,0:T(8,128)(2,1)S(1)} %get-tuple-element.208), channel_id=1, source_target_pairs={{0,3},{1,2},{2,1},{3,0},{4,7},{5,6},{6,5},{7,4},{8,11},{9,10},{10,... | collective-permute-start | bytes 129032 | tf_op jit(solution)/shard_map/ppermute | solution.py:61
  (11 other events, 89.1 us)

commit v6 on v5

--- a/solution.py
+++ b/solution.py
@@ -208,17 +208,14 @@
 
 
 def last_kernel(at_ref, *refs):
-    parts, ins, outs, bufs, (in_sems, out_sems) = refs[:4], refs[4:13], refs[13:22], refs[22:31], refs[31:]
-    copies = fetch(list(zip(ins, bufs)), in_sems)
+    parts, ins, outs, bufs, out_sems = refs[:4], refs[4:13], refs[13:22], refs[22:31], refs[31]
     total = sum(ref[...].astype(wide) for ref in parts)
     height, cols, ends = bufs[0].shape[1], bufs[3].shape[1], bufs[6].shape[1]
     small = total[height : height + 8]
     grads = (total[0:height].T, small[:, :cols], small[0:1, total.shape[1] - ends :])
-    for copy in copies:
-        copy.wait()
     states = []
     for j, (rate, decay) in enumerate(((0.3, 0.1), (0.5, 0.0), (0.7, 0.0))):
-        weight, first, second = (buf[...] for buf in bufs[3 * j : 3 * j + 3])
+        weight, first, second = (ref[...] for ref in ins[3 * j : 3 * j + 3])
         states += adamw(weight, grads[j], first, second, rate, decay)
     stored(states, bufs, outs, out_sems)
 
@@ -491,11 +488,15 @@
 
 
 def input_kernel(at_ref, x_ref, dh_ref, vec_ref, *refs):
-    chunks, out_ref = refs[:3], refs[3]
+    count = (len(refs) - 4) // 2 if len(refs) > 4 else 0
+    chunks, ins, out_ref, outs = refs[:3], refs[3 : 3 + count], refs[3 + count], refs[4 + count : 4 + 2 * count]
+    copies = fetch(list(zip(ins, outs)), refs[-1]) if count else []
     part_rows = dh_ref.shape[0]
     normed, inverse = norm_parts(x_ref[rank_rows(at_ref, 0, part_rows), :].astype(wide))
     grad = sum(ref[...].astype(wide) for ref in chunks)
     out_ref[...] = dh_ref[...] + norm_backward(grad, normed, inverse, vec_ref[0:1, :])
+    for copy in copies:
+        copy.wait()
 
 
 def adamw(weight, gradient, first, second, rate, decay):
@@ -733,14 +734,21 @@
     out_sums = to_ranks(kernel_call(ranks_kernel, [((tall, heads_width), low)] * 4, (at, *sums)))
     out_state = (out_weight, out_first, out_second)
     small_state = (vectors, vector_first, vector_second, up_bias[None], bias_first[None], bias_second[None])
+    dn1_got = lax.optimization_barrier((dn1_got, output, qkv_state))[0]
+    states = out_state + small_state if fast else ()
+    input_own, *brought = kernel_call(
+        input_kernel,
+        [((part_rows, width), wide)] + [(value.shape, wide) for value in states],
+        (at, x, dh, vec, *dn1_got, *states),
+        [pltpu.SemaphoreType.DMA((9,))] if fast else [],
+        hbm=range(7, 7 + len(states)),
+    )
     if fast:
-        states = out_state + small_state
         *last, bias_new, bias_m, bias_s = kernel_call(
             last_kernel,
             [(value.shape, wide) for value in states],
-            (at, *out_sums, *states),
-            [pltpu.VMEM(value.shape, wide) for value in states] + [pltpu.SemaphoreType.DMA((9,))] * 2,
-            hbm=range(5, 14),
+            (at, *out_sums, *brought),
+            [pltpu.VMEM(value.shape, wide) for value in states] + [pltpu.SemaphoreType.DMA((9,))],
             hbm_outs=True,
         )
         out_state, vec_state = last[:3], last[3:]
@@ -768,12 +776,6 @@
             hbm_outs=True,
         )
 
-    dn1_got = lax.optimization_barrier((dn1_got, output, qkv_state))[0]
-    (input_own,) = kernel_call(
-        input_kernel,
-        [((part_rows, width), wide)],
-        (at, x, dh, vec, *dn1_got),
-    )
     return (
         output[None],
         input_own[None],

time: 140 us -> 139 us (level)
  transfers between devices with their start and end apart: 45 -> 45, of which waited for: 20 -> 19; matrix products, arithmetic and copies ran while one was open for 2% -> 2% of each run, Pallas kernels for 21% -> 22%
where the time goes in v6:
time: 139 us
  starting transfers between devices  57.2 us (41%)
  Pallas kernels  39.1 us (28%)
  waiting for transfers between devices  37 us (27%)
  other arithmetic  2.81 us (2%)
  local copies, waits for them, and re-layouts  1.72 us (1%)
    ppermute x44, starting transfers between devices, flip(): return lax.ppermute(value, axis, [(i, i ^ mask) for i in range(size)])  51.9 us
    pallas_call x20, Pallas kernels, kernel_call(): pl.pallas_call(body, out_shape=[jax.ShapeDtypeStruct(s, d) for s, d in ou...  39.1 us
    ppermute x44, waiting for transfers between devices, flip(): return lax.ppermute(value, axis, [(i, i ^ mask) for i in range(size)])  35.7 us
    all_to_all x1, starting transfers between devices, body(): small = lax.all_to_all(tiles, both_axes, 0, 0, tiled=True)  5.32 us
  transfers between devices with their start and end apart: 45, of which 19 were waited for; matrix products, arithmetic and copies ran while one was open for 2% of the time, Pallas kernels for 22%

profile of v6, /device:TPU:0, one launch (start us, length us, event | category | flops | bytes accessed | tf_op | source)
XLA Modules:
  0.0 139.1 jit_solution(1842060487526211186)
XLA Ops:
  0.7 2.2 %shard_map.347 = (f32[32,8,128]{2,1,0:T(8,128)}, bf16[3,96,192]{2,1,0:T(8,128)(2,1)S(1)}, bf16[96,192]{1,0:T(8,128)(2,1)S(1)}) custom-call(s32[2]{0:T(128)S(1)} %pad_add_fusion.at_ref, f32[8,24]{1,0:T(8,128)} %refs_6_.1, f32[1,96]{1,0:T(1,128)} %bitcast.74, f32[3,96,192]{2,1,0:T(8,128)} %refs_2_.1, f32[192,96]{1,0:T(8,128)} %refs_3_.3), custom_call_target="tpu_custom_call" | custom-call | tf_op jit(solution)/shard_map/pallas_call | solution.py:41
  3.0 4.0 %collective-permute-start.2 = (bf16[3,96,192]{2,1,0:T(8,128)(2,1)S(1)}, bf16[3,96,192]{2,1,0:T(8,128)(2,1)S(1)}, u32[]{:S(2)}, u32[]{:S(2)}) collective-permute-start(bf16[3,96,192]{2,1,0:T(8,128)(2,1)S(1)} %get-tuple-element.141.refs_0_), channel_id=1, source_target_pairs={{0,24},{4,28},{8,16},{12,20},{16,8},{20,12},{24,0},{28,4},{1,25},{... | collective-permute-start | bytes 331784 | tf_op jit(solution)/shard_map/ppermute | solution.py:61
  7.6 4.0 %collective-permute-start.5 = (bf16[96,192]{1,0:T(8,128)(2,1)S(1)}, bf16[96,192]{1,0:T(8,128)(2,1)S(1)}, u32[]{:S(2)}, u32[]{:S(2)}) collective-permute-start(bf16[96,192]{1,0:T(8,128)(2,1)S(1)} %get-tuple-element.135.refs_0_), channel_id=1, source_target_pairs={{0,3},{1,2},{2,1},{3,0},{4,7},{5,6},{6,5},{7,4},{8,11},{9,10},{10,... | collective-permute-start | bytes 110600 | tf_op jit(solution)/shard_map/ppermute | solution.py:61
  11.6 1.6 %collective-permute-start.3 = (bf16[96,192]{1,0:T(8,128)(2,1)S(1)}, bf16[96,192]{1,0:T(8,128)(2,1)S(1)}, u32[]{:S(2)}, u32[]{:S(2)}) collective-permute-start(bf16[96,192]{1,0:T(8,128)(2,1)S(1)} %get-tuple-element.135.refs_0_), channel_id=1, source_target_pairs={{0,1},{1,0},{2,3},{3,2},{4,5},{5,4},{6,7},{7,6},{8,9},{9,8},{10,11... | collective-permute-start | bytes 110600 | tf_op jit(solution)/shard_map/ppermute | solution.py:61
  13.2 5.3 %all-to-all-start = ((f32[32,8,128]{2,1,0:T(8,128)}), f32[32,8,128]{2,1,0:T(8,128)S(1)}, u32[]{:S(2)}, u32[]{:S(2)}) async-start(f32[32,8,128]{2,1,0:T(8,128)} %get-tuple-element.129), calls=%async_computation | async-start | bytes 262144 | tf_op jit(solution)/shard_map/all_to_all | solution.py:561
  19.2 1.6 %shard_map.349.refs_0_ = bf16[3,96,768]{2,1,0:T(8,128)(2,1)S(1)} custom-call(s32[2]{0:T(128)S(1)} %pad_add_fusion.at_ref, f32[96,768]{1,0:T(8,128)} %up_ref, f32[96,768]{1,0:T(8,128)} %bitcast.69, bf16[96,192]{1,0:T(8,128)(2,1)S(1)} %get-tuple-element.135.refs_0_, bf16[96,192]{1,0:T(8,128)(2,1)S(1)} %collective-permute-done.3.refs_1_, ...), custom_call_target="tpu_custom_call" | custom-call | tf_op jit(solution)/shard_map/pallas_call | solution.py:41
  20.8 2.7 %collective-permute-start.8 = (bf16[3,96,768]{2,1,0:T(8,128)(2,1)S(1)}, bf16[3,96,768]{2,1,0:T(8,128)(2,1)S(1)}, u32[]{:S(2)}, u32[]{:S(2)}) collective-permute-start(bf16[3,96,768]{2,1,0:T(8,128)(2,1)S(1)} %shard_map.349.refs_0_), channel_id=1, source_target_pairs={{0,24},{4,28},{8,16},{12,20},{16,8},{20,12},{24,0},{28,4},{1,25},{... | collective-permute-start | bytes 1327112 | tf_op jit(solution)/shard_map/ppermute | solution.py:61
  25.7 1.3 all-to-all-done.small_ref
  27.7 5.3 %shard_map.350 = (bf16[576,768]{1,0:T(8,128)(2,1)S(1)}, bf16[3,576,192]{2,1,0:T(8,128)(2,1)S(1)}, f32[8,576]{1,0:T(8,128)S(1)}, bf16[864,128]{1,0:T(8,128)(2,1)S(1)}, bf16[3,768,192]{2,1,0:T(8,128)(2,1)S(1)}) custom-call(s32[2]{0:T(128)S(1)} %pad_add_fusion.at_ref, bf16[576,768]{1,0:T(8,128)(2,1)S(1)} %bitcast.65, f32[8,768]{1,0:T(8,128)S(1)} %get-tuple-element.130.vec_ref, ...), custom_call_target="tpu_custom_call" | custom-call | tf_op jit(solution)/shard_map/pallas_call | solution.py:41
  33.0 2.2 %collective-permute-start.14 = (bf16[864,128]{1,0:T(8,128)(2,1)S(1)}, bf16[864,128]{1,0:T(8,128)(2,1)S(1)}, u32[]{:S(2)}, u32[]{:S(2)}) collective-permute-start(bf16[864,128]{1,0:T(8,128)(2,1)S(1)} %get-tuple-element.144.refs_0_), channel_id=1, source_target_pairs={{0,2},{1,3},{2,0},{3,1},{4,6},{5,7},{6,4},{7,5},{8,10},{9,11},{10,... | collective-permute-start | bytes 663560 | tf_op jit(solution)/shard_map/ppermute | solution.py:61
  35.2 1.5 %collective-permute-start.13 = (bf16[864,128]{1,0:T(8,128)(2,1)S(1)}, bf16[864,128]{1,0:T(8,128)(2,1)S(1)}, u32[]{:S(2)}, u32[]{:S(2)}) collective-permute-start(bf16[864,128]{1,0:T(8,128)(2,1)S(1)} %get-tuple-element.144.refs_0_), channel_id=1, source_target_pairs={{0,1},{1,0},{2,3},{3,2},{4,5},{5,4},{6,7},{7,6},{8,9},{9,8},{10,11... | collective-permute-start | bytes 663560 | tf_op jit(solution)/shard_map/ppermute | solution.py:61
  36.7 7.3 %collective-permute-done.7.refs_4_ = bf16[3,96,768]{2,1,0:T(8,128)(2,1)S(1)} collective-permute-done((bf16[3,96,768]{2,1,0:T(8,128)(2,1)S(1)}, bf16[3,96,768]{2,1,0:T(8,128)(2,1)S(1)}, u32[]{:S(2)}, u32[]{:S(2)}) %collective-permute-start.7) | collective-permute-done | bytes 442400 | tf_op jit(solution)/shard_map/ppermute | solution.py:61
  44.2 1.6 %collective-permute-done.14.refs_2_ = bf16[864,128]{1,0:T(8,128)(2,1)S(1)} collective-permute-done((bf16[864,128]{1,0:T(8,128)(2,1)S(1)}, bf16[864,128]{1,0:T(8,128)(2,1)S(1)}, u32[]{:S(2)}, u32[]{:S(2)}) %collective-permute-start.14) | collective-permute-done | bytes 221216 | tf_op jit(solution)/shard_map/ppermute | solution.py:61
  46.9 1.6 %collective-permute-start.19 = (bf16[864,128]{1,0:T(8,128)(2,1)S(1)}, bf16[864,128]{1,0:T(8,128)(2,1)S(1)}, u32[]{:S(2)}, u32[]{:S(2)}) collective-permute-start(bf16[864,128]{1,0:T(8,128)(2,1)S(1)} %collective-permute-done.14.refs_2_), channel_id=1, source_target_pairs={{0,1},{1,0},{2,3},{3,2},{4,5},{5,4},{6,7},{7,6},{8,9},{9,8},{10,11... | collective-permute-start | bytes 663560 | tf_op jit(solution)/shard_map/ppermute | solution.py:61
  49.6 2.7 %shard_map.351 = (bf16[3,768,768]{2,1,0:T(8,128)(2,1)S(1)}, f32[576,768]{1,0:T(8,128)S(1)}) custom-call(s32[2]{0:T(128)S(1)} %pad_add_fusion.at_ref, bf16[576,768]{1,0:T(8,128)(2,1)S(1)} %bitcast.61, bf16[3,96,768]{2,1,0:T(8,128)(2,1)S(1)} %shard_map.349.refs_0_, bf16[3,96,768]{2,1,0:T(8,128)(2,1)S(1)} %collective-permute-done.15.refs_1_, ...), custom_call_target="tpu_custom_call" | custom-call | tf_op jit(solution)/shard_map/pallas_call | solution.py:41
  52.3 2.0 %collective-permute-done.19.refs_3_ = bf16[864,128]{1,0:T(8,128)(2,1)S(1)} collective-permute-done((bf16[864,128]{1,0:T(8,128)(2,1)S(1)}, bf16[864,128]{1,0:T(8,128)(2,1)S(1)}, u32[]{:S(2)}, u32[]{:S(2)}) %collective-permute-start.19) | collective-permute-done | bytes 221216 | tf_op jit(solution)/shard_map/ppermute | solution.py:61
  54.3 4.3 %shard_map.352 = (bf16[144,768]{1,0:T(8,128)(2,1)S(1)}, bf16[144,768]{1,0:T(8,128)(2,1)S(1)}, bf16[144,768]{1,0:T(8,128)(2,1)S(1)}, bf16[144,768]{1,0:T(8,128)(2...) custom-call(s32[2]{0:T(128)S(1)} %pad_add_fusion.at_ref, ...), custom_call_target="tpu_custom_call" | custom-call | tf_op jit(solution)/shard_map/pallas_call | solution.py:41
  58.6 1.7 %collective-permute-start.21 = (bf16[144,768]{1,0:T(8,128)(2,1)S(1)}, bf16[144,768]{1,0:T(8,128)(2,1)S(1)}, u32[]{:S(2)}, u32[]{:S(2)}) collective-permute-start(bf16[144,768]{1,0:T(8,128)(2,1)S(1)} %get-tuple-element.161), channel_id=1, source_target_pairs={{0,1},{1,0},{2,3},{3,2},{4,5},{5,4},{6,7},{7,6},{8,9},{9,8},{10,11... | collective-permute-start | bytes 663560 | tf_op jit(solution)/shard_map/ppermute | solution.py:61
  60.2 2.7 %shard_map.353 = (bf16[4,2,96,768]{3,2,1,0:T(8,128)(2,1)S(1)}, bf16[4,2,96,768]{3,2,1,0:T(8,128)(2,1)S(1)}) custom-call(s32[2]{0:T(128)S(1)} %pad_add_fusion.at_ref, bf16[576,768]{1,0:T(8,128)(2,1)S(1)} %get-tuple-element.162.a2_ref, bf16[576,768]{1,0:T(8,128)(2,1)S(1)} %get-tuple-element.163.du_ref, bf16[576,768]{1,0:T(8,128)(2,1)S(1)} %bitcast.63, ...), custom_call_target="tpu_custom_call" | custom-call | tf_op jit(solution)/shard_map/pallas_call | solution.py:41
  63.0 2.2 %collective-permute-done.21.right_ref = bf16[144,768]{1,0:T(8,128)(2,1)S(1)} collective-permute-done((bf16[144,768]{1,0:T(8,128)(2,1)S(1)}, bf16[144,768]{1,0:T(8,128)(2,1)S(1)}, u32[]{:S(2)}, u32[]{:S(2)}) %collective-permute-start.21) | collective-permute-done | bytes 221216 | tf_op jit(solution)/shard_map/ppermute | solution.py:61
  65.8 1.7 %collective-permute-start.20 = (bf16[144,768]{1,0:T(8,128)(2,1)S(1)}, bf16[144,768]{1,0:T(8,128)(2,1)S(1)}, u32[]{:S(2)}, u32[]{:S(2)}) collective-permute-start(bf16[144,768]{1,0:T(8,128)(2,1)S(1)} %get-tuple-element.159), channel_id=1, source_target_pairs={{0,1},{1,0},{2,3},{3,2},{4,5},{5,4},{6,7},{7,6},{8,9},{9,8},{10,11... | collective-permute-start | bytes 663560 | tf_op jit(solution)/shard_map/ppermute | solution.py:61
  67.5 1.5 %shard_map.355 = (bf16[144,768]{1,0:T(8,128)(2,1)S(1)}, bf16[144,768]{1,0:T(8,128)(2,1)S(1)}, bf16[144,768]{1,0:T(8,128)(2,1)S(1)}, bf16[144,768]{1,0:T(8,128)(2,1)S(1)}) custom-call(s32[2]{0:T(128)S(1)} %pad_add_fusion.at_ref, bf16[576,768]{1,0:T(8,128)(2,1)S(1)} %get-tuple-element.168.g_ref, bf16[3,768,768]{2,1,0:T(8,128)(2,1)S(1)} %get-tuple-element.149.w_ref), custom_call_target="tpu_custom_call" | custom-call | tf_op jit(solution)/shard_map/pallas_call | solution.py:41
  70.3 1.8 %collective-permute-start.24 = (bf16[2,96,768]{2,1,0:T(8,128)(2,1)S(1)}, bf16[2,96,768]{2,1,0:T(8,128)(2,1)S(1)}, u32[]{:S(2)}, u32[]{:S(2)}) collective-permute-start(bf16[2,96,768]{2,1,0:T(8,128)(2,1)S(1)} %get-tuple-element.175), channel_id=1, source_target_pairs={{0,8},{4,12},{8,0},{12,4},{16,24},{20,28},{24,16},{28,20},{1,9},{5... | collective-permute-start | bytes 884744 | tf_op jit(solution)/shard_map/ppermute | solution.py:61
  72.1 1.5 %collective-permute-start.25 = (bf16[2,96,768]{2,1,0:T(8,128)(2,1)S(1)}, bf16[2,96,768]{2,1,0:T(8,128)(2,1)S(1)}, u32[]{:S(2)}, u32[]{:S(2)}) collective-permute-start(bf16[2,96,768]{2,1,0:T(8,128)(2,1)S(1)} %get-tuple-element.176), channel_id=1, source_target_pairs={{0,16},{4,20},{8,24},{12,28},{16,0},{20,4},{24,8},{28,12},{1,17},{... | collective-permute-start | bytes 884744 | tf_op jit(solution)/shard_map/ppermute | solution.py:61
  74.1 2.6 %collective-permute-start.22 = (bf16[144,768]{1,0:T(8,128)(2,1)S(1)}, bf16[144,768]{1,0:T(8,128)(2,1)S(1)}, u32[]{:S(2)}, u32[]{:S(2)}) collective-permute-start(bf16[144,768]{1,0:T(8,128)(2,1)S(1)} %shard_map.354), channel_id=1, source_target_pairs={{0,2},{1,3},{2,0},{3,1},{4,6},{5,7},{6,4},{7,5},{8,10},{9,11},{10,... | collective-permute-start | bytes 663560 | tf_op jit(solution)/shard_map/ppermute | solution.py:61
  76.7 5.4 %collective-permute-done.31.right_ref = bf16[144,768]{1,0:T(8,128)(2,1)S(1)} collective-permute-done((bf16[144,768]{1,0:T(8,128)(2,1)S(1)}, bf16[144,768]{1,0:T(8,128)(2,1)S(1)}, u32[]{:S(2)}, u32[]{:S(2)}) %collective-permute-start.31) | collective-permute-done | bytes 221216 | tf_op jit(solution)/shard_map/ppermute | solution.py:61
  82.6 3.9 %collective-permute-done.22.refs_2_ = bf16[144,768]{1,0:T(8,128)(2,1)S(1)} collective-permute-done((bf16[144,768]{1,0:T(8,128)(2,1)S(1)}, bf16[144,768]{1,0:T(8,128)(2,1)S(1)}, u32[]{:S(2)}, u32[]{:S(2)}) %collective-permute-start.22) | collective-permute-done | bytes 221216 | tf_op jit(solution)/shard_map/ppermute | solution.py:61
  87.0 1.2 shard_map.357
  88.2 3.6 %collective-permute-start.27 = (bf16[216,128]{1,0:T(8,128)(2,1)S(1)}, bf16[216,128]{1,0:T(8,128)(2,1)S(1)}, u32[]{:S(2)}, u32[]{:S(2)}) collective-permute-start(bf16[216,128]{1,0:T(8,128)(2,1)S(1)} %get-tuple-element.184), channel_id=1, source_target_pairs={{0,1},{1,0},{2,3},{3,2},{4,5},{5,4},{6,7},{7,6},{8,9},{9,8},{10,11... | collective-permute-start | bytes 165896 | tf_op jit(solution)/shard_map/ppermute | solution.py:61
  92.0 2.3 %collective-permute-start.29 = (bf16[216,128]{1,0:T(8,128)(2,1)S(1)}, bf16[216,128]{1,0:T(8,128)(2,1)S(1)}, u32[]{:S(2)}, u32[]{:S(2)}) collective-permute-start(bf16[216,128]{1,0:T(8,128)(2,1)S(1)} %get-tuple-element.186), channel_id=1, source_target_pairs={{0,3},{1,2},{2,1},{3,0},{4,7},{5,6},{6,5},{7,4},{8,11},{9,10},{10,... | collective-permute-start | bytes 165896 | tf_op jit(solution)/shard_map/ppermute | solution.py:61
  94.3 1.1 shard_map.358
  95.6 1.6 %multiply_subtract_fusion.1 = (f32[96,768]{1,0:T(8,128)}, f32[96,768]{1,0:T(8,128)}, f32[96,768]{1,0:T(8,128)}, f32[96,768]{1,0:T(8,128)}, f32[96,768]{1,0:T(8,128)}, /*index=5*/f32[96,768]{1,0:T(8,128)}) fusion(f32[768,96]{0,1:T(8,128)S(1)} %copy-done.4, bf16[2,96,768]{2,1,0:T(8,128)(2,1)S(1)} %collective-permute-done.26, ...), kind=kLoop, calls=%fused_computation.15 | loop fusion | flops 3096576 | bytes 5013504 | tf_op jit(solution)/shard_map/sub | solution.py:507
  97.2 3.4 %collective-permute-done.32.three_ref = bf16[144,768]{1,0:T(8,128)(2,1)S(1)} collective-permute-done((bf16[144,768]{1,0:T(8,128)(2,1)S(1)}, bf16[144,768]{1,0:T(8,128)(2,1)S(1)}, u32[]{:S(2)}, u32[]{:S(2)}) %collective-permute-start.32) | collective-permute-done | bytes 221216 | tf_op jit(solution)/shard_map/ppermute | solution.py:61
  101.2 6.1 %shard_map.360 = (bf16[144,768]{1,0:T(8,128)(2,1)S(1)}, bf16[144,768]{1,0:T(8,128)(2,1)S(1)}, bf16[144,768]{1,0:T(8,128)(2,1)S(1)}, bf16[144,768]{1,0:T(8,128)(2...) custom-call(s32[2]{0:T(128)S(1)} %pad_add_fusion.at_ref, ...), custom_call_target="tpu_custom_call" | custom-call | tf_op jit(solution)/shard_map/pallas_call | solution.py:41
  107.4 1.5 %collective-permute-start.33 = (bf16[144,768]{1,0:T(8,128)(2,1)S(1)}, bf16[144,768]{1,0:T(8,128)(2,1)S(1)}, u32[]{:S(2)}, u32[]{:S(2)}) collective-permute-start(bf16[144,768]{1,0:T(8,128)(2,1)S(1)} %get-tuple-element.200), channel_id=1, source_target_pairs={{0,1},{1,0},{2,3},{3,2},{4,5},{5,4},{6,7},{7,6},{8,9},{9,8},{10,11... | collective-permute-start | bytes 663560 | tf_op jit(solution)/shard_map/ppermute | solution.py:61
  110.2 1.5 %collective-permute-start.38 = (bf16[96,1472]{1,0:T(8,128)(2,1)S(1)}, bf16[96,1472]{1,0:T(8,128)(2,1)S(1)}, u32[]{:S(2)}, u32[]{:S(2)}) collective-permute-start(bf16[96,1472]{1,0:T(8,128)(2,1)S(1)} %get-tuple-element.204), channel_id=1, source_target_pairs={{0,8},{4,12},{8,0},{12,4},{16,24},{20,28},{24,16},{28,20},{1,9},{5... | collective-permute-start | bytes 847880 | tf_op jit(solution)/shard_map/ppermute | solution.py:61
  111.7 1.5 %collective-permute-start.39 = (bf16[96,1472]{1,0:T(8,128)(2,1)S(1)}, bf16[96,1472]{1,0:T(8,128)(2,1)S(1)}, u32[]{:S(2)}, u32[]{:S(2)}) collective-permute-start(bf16[96,1472]{1,0:T(8,128)(2,1)S(1)} %get-tuple-element.205), channel_id=1, source_target_pairs={{0,16},{4,20},{8,24},{12,28},{16,0},{20,4},{24,8},{28,12},{1,17},{... | collective-permute-start | bytes 847880 | tf_op jit(solution)/shard_map/ppermute | solution.py:61
  113.7 1.5 %collective-permute-start.36 = (bf16[144,768]{1,0:T(8,128)(2,1)S(1)}, bf16[144,768]{1,0:T(8,128)(2,1)S(1)}, u32[]{:S(2)}, u32[]{:S(2)}) collective-permute-start(bf16[144,768]{1,0:T(8,128)(2,1)S(1)} %get-tuple-element.211), channel_id=1, source_target_pairs={{0,1},{1,0},{2,3},{3,2},{4,5},{5,4},{6,7},{7,6},{8,9},{9,8},{10,11... | collective-permute-start | bytes 663560 | tf_op jit(solution)/shard_map/ppermute | solution.py:61
  115.8 3.5 %collective-permute-start.37 = (bf16[144,768]{1,0:T(8,128)(2,1)S(1)}, bf16[144,768]{1,0:T(8,128)(2,1)S(1)}, u32[]{:S(2)}, u32[]{:S(2)}) collective-permute-start(bf16[144,768]{1,0:T(8,128)(2,1)S(1)} %shard_map.362), channel_id=1, source_target_pairs={{0,2},{1,3},{2,0},{3,1},{4,6},{5,7},{6,4},{7,5},{8,10},{9,11},{10,... | collective-permute-start | bytes 663560 | tf_op jit(solution)/shard_map/ppermute | solution.py:61
  119.3 1.3 shard_map.363
  120.8 6.0 %collective-permute-done.39.refs_2_ = bf16[96,1472]{1,0:T(8,128)(2,1)S(1)} collective-permute-done((bf16[96,1472]{1,0:T(8,128)(2,1)S(1)}, bf16[96,1472]{1,0:T(8,128)(2,1)S(1)}, u32[]{:S(2)}, u32[]{:S(2)}) %collective-permute-start.39) | collective-permute-done | bytes 282656 | tf_op jit(solution)/shard_map/ppermute | solution.py:61
  127.5 1.6 %collective-permute-start.41 = (bf16[112,192]{1,0:T(8,128)(2,1)S(1)}, bf16[112,192]{1,0:T(8,128)(2,1)S(1)}, u32[]{:S(2)}, u32[]{:S(2)}) collective-permute-start(bf16[112,192]{1,0:T(8,128)(2,1)S(1)} %get-tuple-element.217), channel_id=1, source_target_pairs={{0,1},{1,0},{2,3},{3,2},{4,5},{5,4},{6,7},{7,6},{8,9},{9,8},{10,11... | collective-permute-start | bytes 129032 | tf_op jit(solution)/shard_map/ppermute | solution.py:61
  129.0 2.4 %collective-permute-start.42 = (bf16[112,192]{1,0:T(8,128)(2,1)S(1)}, bf16[112,192]{1,0:T(8,128)(2,1)S(1)}, u32[]{:S(2)}, u32[]{:S(2)}) collective-permute-start(bf16[112,192]{1,0:T(8,128)(2,1)S(1)} %get-tuple-element.218), channel_id=1, source_target_pairs={{0,2},{1,3},{2,0},{3,1},{4,6},{5,7},{6,4},{7,5},{8,10},{9,11},{10,... | collective-permute-start | bytes 129032 | tf_op jit(solution)/shard_map/ppermute | solution.py:61
  131.4 1.0 collective-permute-start.43
  132.7 1.1 multiply_subtract_fusion
  133.9 2.6 %shard_map.364 = (f32[144,768]{1,0:T(8,128)}, f32[192,96]{1,0:T(8,128)S(1)}, f32[192,96]{1,0:T(8,128)S(1)}, f32[192,96]{1,0:T(8,128)S(1)}, f32[8,24]{1,0:T(8,128...) custom-call(s32[2]{0:T(128)S(1)} %pad_add_fusion.at_ref, ...), custom_call_target="tpu_custom_call" | custom-call | tf_op jit(solution)/shard_map/pallas_call | solution.py:41
  136.5 0.9 collective-permute-done.43.refs_3_
  137.4 1.5 %shard_map.366 = (f32[192,96]{1,0:T(8,128)}, f32[192,96]{1,0:T(8,128)}, f32[192,96]{1,0:T(8,128)}, f32[8,24]{1,0:T(8,128)}, f32[8,24]{1,0:T(8,128)}, /*index=5*/...) custom-call(s32[2]{0:T(128)S(1)} %pad_add_fusion.at_ref, ...), custom_call_target="tpu_custom_call" | custom-call | tf_op jit(solution)/shard_map/pallas_call | solution.py:41
  (97 shorter events, 14.4 us)
Async XLA Ops:
  0.7 27.1 %copy-start.1 = (bf16[1,576,768]{2,1,0:T(8,128)(2,1)S(1)}, bf16[1,576,768]{2,1,0:T(8,128)(2,1)}, u32[]{:S(2)}) copy-start(bf16[1,576,768]{2,1,0:T(8,128)(2,1)} %param.20) | copy-start | bytes 2654212
  3.0 8.6 %collective-permute-start.2 = (bf16[3,96,192]{2,1,0:T(8,128)(2,1)S(1)}, bf16[3,96,192]{2,1,0:T(8,128)(2,1)S(1)}, u32[]{:S(2)}, u32[]{:S(2)}) collective-permute-start(bf16[3,96,192]{2,1,0:T(8,128)(2,1)S(1)} %get-tuple-element.141.refs_0_), channel_id=1, source_target_pairs={{0,24},{4,28},{8,16},{12,20},{16,8},{20,12},{24,0},{28,4},{1,25},{... | collective-permute-start | bytes 331784 | tf_op jit(solution)/shard_map/ppermute | solution.py:61
  7.0 11.6 %collective-permute-start.1 = (bf16[3,96,192]{2,1,0:T(8,128)(2,1)S(1)}, bf16[3,96,192]{2,1,0:T(8,128)(2,1)}, u32[]{:S(2)}, u32[]{:S(2)}) collective-permute-start(bf16[3,96,192]{2,1,0:T(8,128)(2,1)S(1)} %get-tuple-element.141.refs_0_), channel_id=1, source_target_pairs={{0,16},{4,20},{8,24},{12,28},{16,0},{20,4},{24,8},{28,12},{1,17},{... | collective-permute-start | bytes 331784 | tf_op jit(solution)/shard_map/ppermute | solution.py:61
  7.5 11.1 %collective-permute-start = (bf16[3,96,192]{2,1,0:T(8,128)(2,1)S(1)}, bf16[3,96,192]{2,1,0:T(8,128)(2,1)}, u32[]{:S(2)}, u32[]{:S(2)}) collective-permute-start(bf16[3,96,192]{2,1,0:T(8,128)(2,1)S(1)} %get-tuple-element.141.refs_0_), channel_id=1, source_target_pairs={{0,8},{4,12},{8,0},{12,4},{16,24},{20,28},{24,16},{28,20},{1,9},{5... | collective-permute-start | bytes 331784 | tf_op jit(solution)/shard_map/ppermute | solution.py:61
  7.6 11.6 %collective-permute-start.5 = (bf16[96,192]{1,0:T(8,128)(2,1)S(1)}, bf16[96,192]{1,0:T(8,128)(2,1)S(1)}, u32[]{:S(2)}, u32[]{:S(2)}) collective-permute-start(bf16[96,192]{1,0:T(8,128)(2,1)S(1)} %get-tuple-element.135.refs_0_), channel_id=1, source_target_pairs={{0,3},{1,2},{2,1},{3,0},{4,7},{5,6},{6,5},{7,4},{8,11},{9,10},{10,... | collective-permute-start | bytes 110600 | tf_op jit(solution)/shard_map/ppermute | solution.py:61
  11.6 7.6 %collective-permute-start.4 = (bf16[96,192]{1,0:T(8,128)(2,1)S(1)}, bf16[96,192]{1,0:T(8,128)(2,1)S(1)}, u32[]{:S(2)}, u32[]{:S(2)}) collective-permute-start(bf16[96,192]{1,0:T(8,128)(2,1)S(1)} %get-tuple-element.135.refs_0_), channel_id=1, source_target_pairs={{0,2},{1,3},{2,0},{3,1},{4,6},{5,7},{6,4},{7,5},{8,10},{9,11},{10,... | collective-permute-start | bytes 110600 | tf_op jit(solution)/shard_map/ppermute | solution.py:61
  11.6 16.1 %copy-start.11 = (bf16[3,96,192]{2,1,0:T(8,128)(2,1)}, bf16[3,96,192]{2,1,0:T(8,128)(2,1)S(1)}, u32[]{:S(2)}) copy-start(bf16[3,96,192]{2,1,0:T(8,128)(2,1)S(1)} %collective-permute-done.2.refs_6_) | copy-start | bytes 331780
  11.6 7.6 %collective-permute-start.3 = (bf16[96,192]{1,0:T(8,128)(2,1)S(1)}, bf16[96,192]{1,0:T(8,128)(2,1)S(1)}, u32[]{:S(2)}, u32[]{:S(2)}) collective-permute-start(bf16[96,192]{1,0:T(8,128)(2,1)S(1)} %get-tuple-element.135.refs_0_), channel_id=1, source_target_pairs={{0,1},{1,0},{2,3},{3,2},{4,5},{5,4},{6,7},{7,6},{8,9},{9,8},{10,11... | collective-permute-start | bytes 110600 | tf_op jit(solution)/shard_map/ppermute | solution.py:61
  13.2 13.8 %all-to-all-start = ((f32[32,8,128]{2,1,0:T(8,128)}), f32[32,8,128]{2,1,0:T(8,128)S(1)}, u32[]{:S(2)}, u32[]{:S(2)}) async-start(f32[32,8,128]{2,1,0:T(8,128)} %get-tuple-element.129), calls=%async_computation | async-start | bytes 262144 | tf_op jit(solution)/shard_map/all_to_all | solution.py:561
  18.6 5.8 %collective-permute-start.9 = (bf16[3,96,192]{2,1,0:T(8,128)(2,1)S(1)}, bf16[3,96,192]{2,1,0:T(8,128)(2,1)S(1)}, u32[]{:S(2)}, u32[]{:S(2)}) collective-permute-start(bf16[3,96,192]{2,1,0:T(8,128)(2,1)S(1)} %get-tuple-element.141.refs_0_), channel_id=1, source_target_pairs={{0,4},{4,0},{8,12},{12,8},{16,20},{20,16},{24,28},{28,24},{1,5},{5... | collective-permute-start | bytes 331784 | tf_op jit(solution)/shard_map/ppermute | solution.py:61
  18.9 5.5 %collective-permute-start.10 = (bf16[3,96,192]{2,1,0:T(8,128)(2,1)}, bf16[3,96,192]{2,1,0:T(8,128)(2,1)S(1)}, u32[]{:S(2)}, u32[]{:S(2)}) collective-permute-start(bf16[3,96,192]{2,1,0:T(8,128)(2,1)} %collective-permute-done.refs_2_), channel_id=1, source_target_pairs={{0,4},{4,0},{8,12},{12,8},{16,20},{20,16},{24,28},{28,24},{1,5},{5... | collective-permute-start | bytes 331784 | tf_op jit(solution)/shard_map/ppermute | solution.py:61
  20.8 28.8 %copy-start = (bf16[1,576,768]{2,1,0:T(8,128)(2,1)S(1)}, bf16[1,576,768]{2,1,0:T(8,128)(2,1)}, u32[]{:S(2)}) copy-start(bf16[1,576,768]{2,1,0:T(8,128)(2,1)} %param.21) | copy-start | bytes 2654212
  20.8 15.9 %collective-permute-start.8 = (bf16[3,96,768]{2,1,0:T(8,128)(2,1)S(1)}, bf16[3,96,768]{2,1,0:T(8,128)(2,1)S(1)}, u32[]{:S(2)}, u32[]{:S(2)}) collective-permute-start(bf16[3,96,768]{2,1,0:T(8,128)(2,1)S(1)} %shard_map.349.refs_0_), channel_id=1, source_target_pairs={{0,24},{4,28},{8,16},{12,20},{16,8},{20,12},{24,0},{28,4},{1,25},{... | collective-permute-start | bytes 1327112 | tf_op jit(solution)/shard_map/ppermute | solution.py:61
  23.6 20.5 %collective-permute-start.7 = (bf16[3,96,768]{2,1,0:T(8,128)(2,1)S(1)}, bf16[3,96,768]{2,1,0:T(8,128)(2,1)S(1)}, u32[]{:S(2)}, u32[]{:S(2)}) collective-permute-start(bf16[3,96,768]{2,1,0:T(8,128)(2,1)S(1)} %shard_map.349.refs_0_), channel_id=1, source_target_pairs={{0,16},{4,20},{8,24},{12,28},{16,0},{20,4},{24,8},{28,12},{1,17},{... | collective-permute-start | bytes 1327112 | tf_op jit(solution)/shard_map/ppermute | solution.py:61
  24.1 20.1 %collective-permute-start.6 = (bf16[3,96,768]{2,1,0:T(8,128)(2,1)S(1)}, bf16[3,96,768]{2,1,0:T(8,128)(2,1)}, u32[]{:S(2)}, u32[]{:S(2)}) collective-permute-start(bf16[3,96,768]{2,1,0:T(8,128)(2,1)S(1)} %shard_map.349.refs_0_), channel_id=1, source_target_pairs={{0,8},{4,12},{8,0},{12,4},{16,24},{20,28},{24,16},{28,20},{1,9},{5... | collective-permute-start | bytes 1327112 | tf_op jit(solution)/shard_map/ppermute | solution.py:61
  24.4 3.3 %collective-permute-start.11 = (bf16[3,96,192]{2,1,0:T(8,128)(2,1)}, bf16[3,96,192]{2,1,0:T(8,128)(2,1)}, u32[]{:S(2)}, u32[]{:S(2)}) collective-permute-start(bf16[3,96,192]{2,1,0:T(8,128)(2,1)} %collective-permute-done.1.refs_4_), channel_id=1, source_target_pairs={{0,4},{4,0},{8,12},{12,8},{16,20},{20,16},{24,28},{28,24},{1,5},{5... | collective-permute-start | bytes 331784 | tf_op jit(solution)/shard_map/ppermute | solution.py:61
  25.7 2.0 %collective-permute-start.12 = (bf16[3,96,192]{2,1,0:T(8,128)(2,1)S(1)}, bf16[3,96,192]{2,1,0:T(8,128)(2,1)}, u32[]{:S(2)}, u32[]{:S(2)}) collective-permute-start(bf16[3,96,192]{2,1,0:T(8,128)(2,1)S(1)} %collective-permute-done.2.refs_6_), channel_id=1, source_target_pairs={{0,4},{4,0},{8,12},{12,8},{16,20},{20,16},{24,28},{28,24},{1,5},{5... | collective-permute-start | bytes 331784 | tf_op jit(solution)/shard_map/ppermute | solution.py:61
  33.0 12.8 %collective-permute-start.14 = (bf16[864,128]{1,0:T(8,128)(2,1)S(1)}, bf16[864,128]{1,0:T(8,128)(2,1)S(1)}, u32[]{:S(2)}, u32[]{:S(2)}) collective-permute-start(bf16[864,128]{1,0:T(8,128)(2,1)S(1)} %get-tuple-element.144.refs_0_), channel_id=1, source_target_pairs={{0,2},{1,3},{2,0},{3,1},{4,6},{5,7},{6,4},{7,5},{8,10},{9,11},{10,... | collective-permute-start | bytes 663560 | tf_op jit(solution)/shard_map/ppermute | solution.py:61
  35.2 10.7 %collective-permute-start.13 = (bf16[864,128]{1,0:T(8,128)(2,1)S(1)}, bf16[864,128]{1,0:T(8,128)(2,1)S(1)}, u32[]{:S(2)}, u32[]{:S(2)}) collective-permute-start(bf16[864,128]{1,0:T(8,128)(2,1)S(1)} %get-tuple-element.144.refs_0_), channel_id=1, source_target_pairs={{0,1},{1,0},{2,3},{3,2},{4,5},{5,4},{6,7},{7,6},{8,9},{9,8},{10,11... | collective-permute-start | bytes 663560 | tf_op jit(solution)/shard_map/ppermute | solution.py:61
  45.9 2.6 %collective-permute-start.15 = (bf16[3,96,768]{2,1,0:T(8,128)(2,1)S(1)}, bf16[3,96,768]{2,1,0:T(8,128)(2,1)S(1)}, u32[]{:S(2)}, u32[]{:S(2)}) collective-permute-start(bf16[3,96,768]{2,1,0:T(8,128)(2,1)S(1)} %shard_map.349.refs_0_), channel_id=1, source_target_pairs={{0,4},{4,0},{8,12},{12,8},{16,20},{20,16},{24,28},{28,24},{1,5},{5... | collective-permute-start | bytes 1327112 | tf_op jit(solution)/shard_map/ppermute | solution.py:61
  45.9 2.9 %collective-permute-start.16 = (bf16[3,96,768]{2,1,0:T(8,128)(2,1)}, bf16[3,96,768]{2,1,0:T(8,128)(2,1)S(1)}, u32[]{:S(2)}, u32[]{:S(2)}) collective-permute-start(bf16[3,96,768]{2,1,0:T(8,128)(2,1)} %collective-permute-done.6.refs_2_), channel_id=1, source_target_pairs={{0,4},{4,0},{8,12},{12,8},{16,20},{20,16},{24,28},{28,24},{1,5},{5... | collective-permute-start | bytes 1327112 | tf_op jit(solution)/shard_map/ppermute | solution.py:61
  46.4 2.5 %collective-permute-start.17 = (bf16[3,96,768]{2,1,0:T(8,128)(2,1)S(1)}, bf16[3,96,768]{2,1,0:T(8,128)(2,1)S(1)}, u32[]{:S(2)}, u32[]{:S(2)}) collective-permute-start(bf16[3,96,768]{2,1,0:T(8,128)(2,1)S(1)} %collective-permute-done.7.refs_4_), channel_id=1, source_target_pairs={{0,4},{4,0},{8,12},{12,8},{16,20},{20,16},{24,28},{28,24},{1,5},{5... | collective-permute-start | bytes 1327112 | tf_op jit(solution)/shard_map/ppermute | solution.py:61
  46.4 3.2 %collective-permute-start.18 = (bf16[3,96,768]{2,1,0:T(8,128)(2,1)S(1)}, bf16[3,96,768]{2,1,0:T(8,128)(2,1)S(1)}, u32[]{:S(2)}, u32[]{:S(2)}) collective-permute-start(bf16[3,96,768]{2,1,0:T(8,128)(2,1)S(1)} %collective-permute-done.8.refs_6_), channel_id=1, source_target_pairs={{0,4},{4,0},{8,12},{12,8},{16,20},{20,16},{24,28},{28,24},{1,5},{5... | collective-permute-start | bytes 1327112 | tf_op jit(solution)/shard_map/ppermute | solution.py:61
  46.9 7.3 %collective-permute-start.19 = (bf16[864,128]{1,0:T(8,128)(2,1)S(1)}, bf16[864,128]{1,0:T(8,128)(2,1)S(1)}, u32[]{:S(2)}, u32[]{:S(2)}) collective-permute-start(bf16[864,128]{1,0:T(8,128)(2,1)S(1)} %collective-permute-done.14.refs_2_), channel_id=1, source_target_pairs={{0,1},{1,0},{2,3},{3,2},{4,5},{5,4},{6,7},{7,6},{8,9},{9,8},{10,11... | collective-permute-start | bytes 663560 | tf_op jit(solution)/shard_map/ppermute | solution.py:61
  58.6 6.6 %collective-permute-start.21 = (bf16[144,768]{1,0:T(8,128)(2,1)S(1)}, bf16[144,768]{1,0:T(8,128)(2,1)S(1)}, u32[]{:S(2)}, u32[]{:S(2)}) collective-permute-start(bf16[144,768]{1,0:T(8,128)(2,1)S(1)} %get-tuple-element.161), channel_id=1, source_target_pairs={{0,1},{1,0},{2,3},{3,2},{4,5},{5,4},{6,7},{7,6},{8,9},{9,8},{10,11... | collective-permute-start | bytes 663560 | tf_op jit(solution)/shard_map/ppermute | solution.py:61
  65.7 3.8 %collective-permute-start.23 = (bf16[4,2,96,768]{3,2,1,0:T(8,128)(2,1)S(1)}, bf16[4,2,96,768]{3,2,1,0:T(8,128)(2,1)S(1)}, u32[]{:S(2)}, u32[]{:S(2)}) collective-permute-start(bf16[4,2,96,768]{3,2,1,0:T(8,128)(2,1)S(1)} %get-tuple-element.173), channel_id=1, source_target_pairs={{0,4},{4,0},{8,12},{12,8},{16,20},{20,16},{24,28},{28,24},{1,5},{5... | collective-permute-start | bytes 3538952 | tf_op jit(solution)/shard_map/ppermute | solution.py:61
  65.8 8.3 %collective-permute-start.20 = (bf16[144,768]{1,0:T(8,128)(2,1)S(1)}, bf16[144,768]{1,0:T(8,128)(2,1)S(1)}, u32[]{:S(2)}, u32[]{:S(2)}) collective-permute-start(bf16[144,768]{1,0:T(8,128)(2,1)S(1)} %get-tuple-element.159), channel_id=1, source_target_pairs={{0,1},{1,0},{2,3},{3,2},{4,5},{5,4},{6,7},{7,6},{8,9},{9,8},{10,11... | collective-permute-start | bytes 663560 | tf_op jit(solution)/shard_map/ppermute | solution.py:61
  69.0 13.0 %collective-permute-start.31 = (bf16[144,768]{1,0:T(8,128)(2,1)S(1)}, bf16[144,768]{1,0:T(8,128)(2,1)S(1)}, u32[]{:S(2)}, u32[]{:S(2)}) collective-permute-start(bf16[144,768]{1,0:T(8,128)(2,1)S(1)} %get-tuple-element.172), channel_id=1, source_target_pairs={{0,1},{1,0},{2,3},{3,2},{4,5},{5,4},{6,7},{7,6},{8,9},{9,8},{10,11... | collective-permute-start | bytes 663560 | tf_op jit(solution)/shard_map/ppermute | solution.py:61
  70.3 16.2 %collective-permute-start.24 = (bf16[2,96,768]{2,1,0:T(8,128)(2,1)S(1)}, bf16[2,96,768]{2,1,0:T(8,128)(2,1)S(1)}, u32[]{:S(2)}, u32[]{:S(2)}) collective-permute-start(bf16[2,96,768]{2,1,0:T(8,128)(2,1)S(1)} %get-tuple-element.175), channel_id=1, source_target_pairs={{0,8},{4,12},{8,0},{12,4},{16,24},{20,28},{24,16},{28,20},{1,9},{5... | collective-permute-start | bytes 884744 | tf_op jit(solution)/shard_map/ppermute | solution.py:61
  72.1 14.8 %collective-permute-start.25 = (bf16[2,96,768]{2,1,0:T(8,128)(2,1)S(1)}, bf16[2,96,768]{2,1,0:T(8,128)(2,1)S(1)}, u32[]{:S(2)}, u32[]{:S(2)}) collective-permute-start(bf16[2,96,768]{2,1,0:T(8,128)(2,1)S(1)} %get-tuple-element.176), channel_id=1, source_target_pairs={{0,16},{4,20},{8,24},{12,28},{16,0},{20,4},{24,8},{28,12},{1,17},{... | collective-permute-start | bytes 884744 | tf_op jit(solution)/shard_map/ppermute | solution.py:61
  73.6 13.4 %collective-permute-start.26 = (bf16[2,96,768]{2,1,0:T(8,128)(2,1)S(1)}, bf16[2,96,768]{2,1,0:T(8,128)(2,1)S(1)}, u32[]{:S(2)}, u32[]{:S(2)}) collective-permute-start(bf16[2,96,768]{2,1,0:T(8,128)(2,1)S(1)} %get-tuple-element.177), channel_id=1, source_target_pairs={{0,24},{4,28},{8,16},{12,20},{16,8},{20,12},{24,0},{28,4},{1,25},{... | collective-permute-start | bytes 884744 | tf_op jit(solution)/shard_map/ppermute | solution.py:61
  74.1 12.4 %collective-permute-start.22 = (bf16[144,768]{1,0:T(8,128)(2,1)S(1)}, bf16[144,768]{1,0:T(8,128)(2,1)S(1)}, u32[]{:S(2)}, u32[]{:S(2)}) collective-permute-start(bf16[144,768]{1,0:T(8,128)(2,1)S(1)} %shard_map.354), channel_id=1, source_target_pairs={{0,2},{1,3},{2,0},{3,1},{4,6},{5,7},{6,4},{7,5},{8,10},{9,11},{10,... | collective-permute-start | bytes 663560 | tf_op jit(solution)/shard_map/ppermute | solution.py:61
  82.0 13.4 %collective-permute-start.30 = (bf16[144,768]{1,0:T(8,128)(2,1)S(1)}, bf16[144,768]{1,0:T(8,128)(2,1)S(1)}, u32[]{:S(2)}, u32[]{:S(2)}) collective-permute-start(bf16[144,768]{1,0:T(8,128)(2,1)S(1)} %get-tuple-element.170), channel_id=1, source_target_pairs={{0,1},{1,0},{2,3},{3,2},{4,5},{5,4},{6,7},{7,6},{8,9},{9,8},{10,11... | collective-permute-start | bytes 663560 | tf_op jit(solution)/shard_map/ppermute | solution.py:61
  86.5 14.1 %collective-permute-start.32 = (bf16[144,768]{1,0:T(8,128)(2,1)S(1)}, bf16[144,768]{1,0:T(8,128)(2,1)S(1)}, u32[]{:S(2)}, u32[]{:S(2)}) collective-permute-start(bf16[144,768]{1,0:T(8,128)(2,1)S(1)} %shard_map.359), channel_id=1, source_target_pairs={{0,2},{1,3},{2,0},{3,1},{4,6},{5,7},{6,4},{7,5},{8,10},{9,11},{10,... | collective-permute-start | bytes 663560 | tf_op jit(solution)/shard_map/ppermute | solution.py:61
  88.2 12.4 %collective-permute-start.27 = (bf16[216,128]{1,0:T(8,128)(2,1)S(1)}, bf16[216,128]{1,0:T(8,128)(2,1)S(1)}, u32[]{:S(2)}, u32[]{:S(2)}) collective-permute-start(bf16[216,128]{1,0:T(8,128)(2,1)S(1)} %get-tuple-element.184), channel_id=1, source_target_pairs={{0,1},{1,0},{2,3},{3,2},{4,5},{5,4},{6,7},{7,6},{8,9},{9,8},{10,11... | collective-permute-start | bytes 165896 | tf_op jit(solution)/shard_map/ppermute | solution.py:61
  91.9 9.3 %collective-permute-start.28 = (bf16[216,128]{1,0:T(8,128)(2,1)S(1)}, bf16[216,128]{1,0:T(8,128)(2,1)S(1)}, u32[]{:S(2)}, u32[]{:S(2)}) collective-permute-start(bf16[216,128]{1,0:T(8,128)(2,1)S(1)} %get-tuple-element.185), channel_id=1, source_target_pairs={{0,2},{1,3},{2,0},{3,1},{4,6},{5,7},{6,4},{7,5},{8,10},{9,11},{10,... | collective-permute-start | bytes 165896 | tf_op jit(solution)/shard_map/ppermute | solution.py:61
  92.0 9.1 %collective-permute-start.29 = (bf16[216,128]{1,0:T(8,128)(2,1)S(1)}, bf16[216,128]{1,0:T(8,128)(2,1)S(1)}, u32[]{:S(2)}, u32[]{:S(2)}) collective-permute-start(bf16[216,128]{1,0:T(8,128)(2,1)S(1)} %get-tuple-element.186), channel_id=1, source_target_pairs={{0,3},{1,2},{2,1},{3,0},{4,7},{5,6},{6,5},{7,4},{8,11},{9,10},{10,... | collective-permute-start | bytes 165896 | tf_op jit(solution)/shard_map/ppermute | solution.py:61
  95.5 13.5 %collective-permute-start.34 = (bf16[4,96,768]{2,1,0:T(8,128)(2,1)S(1)}, bf16[4,96,768]{2,1,0:T(8,128)(2,1)S(1)}, u32[]{:S(2)}, u32[]{:S(2)}) collective-permute-start(bf16[4,96,768]{2,1,0:T(8,128)(2,1)S(1)} %get-tuple-element.190), channel_id=1, source_target_pairs={{0,4},{4,0},{8,12},{12,8},{16,20},{20,16},{24,28},{28,24},{1,5},{5... | collective-permute-start | bytes 1769480 | tf_op jit(solution)/shard_map/ppermute | solution.py:61
  107.3 2.1 %collective-permute-start.35 = (bf16[4,96,704]{2,1,0:T(8,128)(2,1)S(1)}, bf16[4,96,704]{2,1,0:T(8,128)(2,1)S(1)}, u32[]{:S(2)}, u32[]{:S(2)}) collective-permute-start(bf16[4,96,704]{2,1,0:T(8,128)(2,1)S(1)} %get-tuple-element.202), channel_id=1, source_target_pairs={{0,4},{4,0},{8,12},{12,8},{16,20},{20,16},{24,28},{28,24},{1,5},{5... | collective-permute-start | bytes 1622024 | tf_op jit(solution)/shard_map/ppermute | solution.py:61
  107.4 7.8 %collective-permute-start.33 = (bf16[144,768]{1,0:T(8,128)(2,1)S(1)}, bf16[144,768]{1,0:T(8,128)(2,1)S(1)}, u32[]{:S(2)}, u32[]{:S(2)}) collective-permute-start(bf16[144,768]{1,0:T(8,128)(2,1)S(1)} %get-tuple-element.200), channel_id=1, source_target_pairs={{0,1},{1,0},{2,3},{3,2},{4,5},{5,4},{6,7},{7,6},{8,9},{9,8},{10,11... | collective-permute-start | bytes 663560 | tf_op jit(solution)/shard_map/ppermute | solution.py:61
  110.2 10.6 %collective-permute-start.38 = (bf16[96,1472]{1,0:T(8,128)(2,1)S(1)}, bf16[96,1472]{1,0:T(8,128)(2,1)S(1)}, u32[]{:S(2)}, u32[]{:S(2)}) collective-permute-start(bf16[96,1472]{1,0:T(8,128)(2,1)S(1)} %get-tuple-element.204), channel_id=1, source_target_pairs={{0,8},{4,12},{8,0},{12,4},{16,24},{20,28},{24,16},{28,20},{1,9},{5... | collective-permute-start | bytes 847880 | tf_op jit(solution)/shard_map/ppermute | solution.py:61
  111.7 15.1 %collective-permute-start.39 = (bf16[96,1472]{1,0:T(8,128)(2,1)S(1)}, bf16[96,1472]{1,0:T(8,128)(2,1)S(1)}, u32[]{:S(2)}, u32[]{:S(2)}) collective-permute-start(bf16[96,1472]{1,0:T(8,128)(2,1)S(1)} %get-tuple-element.205), channel_id=1, source_target_pairs={{0,16},{4,20},{8,24},{12,28},{16,0},{20,4},{24,8},{28,12},{1,17},{... | collective-permute-start | bytes 847880 | tf_op jit(solution)/shard_map/ppermute | solution.py:61
  113.2 13.6 %collective-permute-start.40 = (bf16[96,1472]{1,0:T(8,128)(2,1)S(1)}, bf16[96,1472]{1,0:T(8,128)(2,1)S(1)}, u32[]{:S(2)}, u32[]{:S(2)}) collective-permute-start(bf16[96,1472]{1,0:T(8,128)(2,1)S(1)} %get-tuple-element.206), channel_id=1, source_target_pairs={{0,24},{4,28},{8,16},{12,20},{16,8},{20,12},{24,0},{28,4},{1,25},{... | collective-permute-start | bytes 847880 | tf_op jit(solution)/shard_map/ppermute | solution.py:61
  113.7 20.1 %collective-permute-start.36 = (bf16[144,768]{1,0:T(8,128)(2,1)S(1)}, bf16[144,768]{1,0:T(8,128)(2,1)S(1)}, u32[]{:S(2)}, u32[]{:S(2)}) collective-permute-start(bf16[144,768]{1,0:T(8,128)(2,1)S(1)} %get-tuple-element.211), channel_id=1, source_target_pairs={{0,1},{1,0},{2,3},{3,2},{4,5},{5,4},{6,7},{7,6},{8,9},{9,8},{10,11... | collective-permute-start | bytes 663560 | tf_op jit(solution)/shard_map/ppermute | solution.py:61
  115.8 18.0 %collective-permute-start.37 = (bf16[144,768]{1,0:T(8,128)(2,1)S(1)}, bf16[144,768]{1,0:T(8,128)(2,1)S(1)}, u32[]{:S(2)}, u32[]{:S(2)}) collective-permute-start(bf16[144,768]{1,0:T(8,128)(2,1)S(1)} %shard_map.362), channel_id=1, source_target_pairs={{0,2},{1,3},{2,0},{3,1},{4,6},{5,7},{6,4},{7,5},{8,10},{9,11},{10,... | collective-permute-start | bytes 663560 | tf_op jit(solution)/shard_map/ppermute | solution.py:61
  127.5 9.0 %collective-permute-start.41 = (bf16[112,192]{1,0:T(8,128)(2,1)S(1)}, bf16[112,192]{1,0:T(8,128)(2,1)S(1)}, u32[]{:S(2)}, u32[]{:S(2)}) collective-permute-start(bf16[112,192]{1,0:T(8,128)(2,1)S(1)} %get-tuple-element.217), channel_id=1, source_target_pairs={{0,1},{1,0},{2,3},{3,2},{4,5},{5,4},{6,7},{7,6},{8,9},{9,8},{10,11... | collective-permute-start | bytes 129032 | tf_op jit(solution)/shard_map/ppermute | solution.py:61
  129.0 7.5 %collective-permute-start.42 = (bf16[112,192]{1,0:T(8,128)(2,1)S(1)}, bf16[112,192]{1,0:T(8,128)(2,1)S(1)}, u32[]{:S(2)}, u32[]{:S(2)}) collective-permute-start(bf16[112,192]{1,0:T(8,128)(2,1)S(1)} %get-tuple-element.218), channel_id=1, source_target_pairs={{0,2},{1,3},{2,0},{3,1},{4,6},{5,7},{6,4},{7,5},{8,10},{9,11},{10,... | collective-permute-start | bytes 129032 | tf_op jit(solution)/shard_map/ppermute | solution.py:61
  131.4 6.0 %collective-permute-start.43 = (bf16[112,192]{1,0:T(8,128)(2,1)S(1)}, bf16[112,192]{1,0:T(8,128)(2,1)S(1)}, u32[]{:S(2)}, u32[]{:S(2)}) collective-permute-start(bf16[112,192]{1,0:T(8,128)(2,1)S(1)} %get-tuple-element.219), channel_id=1, source_target_pairs={{0,3},{1,2},{2,1},{3,0},{4,7},{5,6},{6,5},{7,4},{8,11},{9,10},{10,... | collective-permute-start | bytes 129032 | tf_op jit(solution)/shard_map/ppermute | solution.py:61
  (11 other events, 89.1 us)
